TPU v7x, 128 devices: a whole 4x4x4 slice. The times are simulated.
128 devices in a mesh: dp: 128 (over y, z, x, core).
Axes of the slice: x: 4, y: 4, z: 4, core: 2. Of those that a mesh axis runs over, the one named last changes fastest.
Arguments:
- query_rows: bfloat16 [16384, 1152], P('dp'), may hold values from -30 to 30
- key_rows: bfloat16 [16384, 1152], P('dp'), may hold values from -30 to 30
- value_rows: bfloat16 [16384, 1152], P('dp'), may hold values from -6 to 6
- residual: bfloat16 [16384, 1152], P('dp'), may hold values from -4 to 4
- token_clip: int32 [16384], P('dp'), may hold values from 0 to 31, never falling along the last dimension, each value on 1 to 897 neighbouring positions
- clip_gate: float32 [32, 1152], replicated, may hold values from -4 to 4
- out_weight: bfloat16 [1152, 1152], replicated, may hold values from -0.1875 to 0.1875
- out_bias: float32 [1152], replicated, may hold values from -3 to 3
- out_grad: bfloat16 [16384, 1152], P('dp'), may hold values from -24 to 24
Outputs:
- block_out: bfloat16 [16384, 1152], P('dp')
- query_grad: bfloat16 [16384, 1152], P('dp')
- key_grad: bfloat16 [16384, 1152], P('dp')
- value_grad: bfloat16 [16384, 1152], P('dp')
- weight_grad: float32 [1152, 1152], P(None, 'dp')
Inputs may be any that keep to these rules, and one draw needn't show every extreme that they name: `token_clip`: clip numbers never fall along the rows; each clip has 1 to 897 tokens, and one clip has exactly that many.
All inputs are finite; a program needn't handle non-finite values.
Results may differ from a plain program's by a relative error of at most 0.03.
Values may be sent and summed in bfloat16 or wider, within the bound.
No kernel may reach another device: no remote copies, remote signals or barrier semaphores. Data moves between devices by JAX's collectives and lax.ppermute only.
A program may use at most 128 MiB of HBM per device.

v0:
```python
import math

import jax
import jax.numpy as jnp
from jax import lax
from jax.sharding import PartitionSpec as P

HEADS = 16
HEAD_DIM = 72
REACH = 7


def passed_along(shard, axis, by):
    count = lax.axis_size(axis)
    pairs = [(i, i + by) for i in range(count) if 0 <= i + by < count]
    return lax.ppermute(shard, axis, pairs)


def head_split(values_in):
    return values_in.reshape(values_in.shape[0], HEADS, HEAD_DIM)


def score_block(query_part, key_part, query_tags, key_tags):
    raw_scores = jnp.einsum(
        "qhd,khd->hqk", query_part, key_part, preferred_element_type=jnp.float32
    ) * (1.0 / math.sqrt(HEAD_DIM))
    same_clip = query_tags[:, None] == key_tags[None, :]
    return jnp.where(same_clip[None], raw_scores, -1e30)


def neighbour_keys(payload):
    arrived = []
    for direction in (1, -1):
        moving = payload
        for distance in range(REACH):
            moving = passed_along((moving[0], moving[1], moving[2]), "dp", direction)
            arrived.append(moving)
    return arrived


def neighbour_queries(payload):
    arrived = []
    for direction in (1, -1):
        moving = payload
        for distance in range(REACH):
            moving = (
                passed_along(moving[0].astype(jnp.float32), "dp", direction).astype(jnp.bfloat16),
                passed_along(moving[1].astype(jnp.float32), "dp", direction).astype(jnp.bfloat16),
                passed_along(moving[2], "dp", direction),
                passed_along(moving[3], "dp", direction),
                passed_along(moving[4], "dp", direction),
            )
            arrived.append(moving)
    return arrived


def stacked(own_entry, arrived, member):
    pieces = [own_entry[member]] + [entry[member] for entry in arrived]
    pieces.append(jnp.zeros_like(own_entry[member]))
    return jnp.concatenate(pieces, 0)


def grouped(values_in, group_count):
    return values_in.reshape((group_count, values_in.shape[0] // group_count) + values_in.shape[1:])


def count_groups(rows_here, slot_total):
    blocks_each = min(slot_total, max(1, 512 // rows_here))
    while slot_total % blocks_each != 0:
        blocks_each -= 1
    return slot_total // blocks_each


def shards(
    query_rows,
    key_rows,
    value_rows,
    residual,
    token_clip,
    clip_gate,
    out_weight,
    out_bias,
    out_grad,
):
    rows_here = query_rows.shape[0]
    model_width = query_rows.shape[1]
    scale_factor = 1.0 / math.sqrt(HEAD_DIM)
    own_tags = token_clip + 1
    query_heads = head_split(query_rows)
    key_heads = head_split(key_rows)
    value_heads = head_split(value_rows)
    slot_total = 2 * REACH + 2
    group_count = count_groups(rows_here, slot_total)
    own_entry = (key_rows, value_rows, own_tags)
    arrived = neighbour_keys(own_entry)
    key_stack = grouped(head_split(stacked(own_entry, arrived, 0)), group_count)
    value_stack = grouped(head_split(stacked(own_entry, arrived, 1)), group_count)
    tag_stack = grouped(stacked(own_entry, arrived, 2), group_count)

    def soft_step(running, inputs):
        key_part, value_part, tag_part = inputs
        run_max, totals, accumulated = running
        scores = score_block(query_heads, key_part, own_tags, tag_part)
        new_max = jnp.maximum(run_max, jnp.max(scores, axis=2))
        fade = jnp.exp(run_max - new_max)
        weights = jnp.exp(scores - new_max[:, :, None])
        totals = totals * fade + jnp.sum(weights, axis=2)
        accumulated = accumulated * fade.T[:, :, None] + jnp.einsum(
            "hqk,khd->qhd",
            weights.astype(jnp.bfloat16),
            value_part,
            preferred_element_type=jnp.float32,
        )
        return ((new_max, totals, accumulated), None)

    start_sums = (
        jnp.full((HEADS, rows_here), -1e30, jnp.float32),
        jnp.zeros((HEADS, rows_here), jnp.float32),
        jnp.zeros((rows_here, HEADS, HEAD_DIM), jnp.float32),
    )
    (row_max, totals, accumulated), ignored = lax.scan(
        soft_step, start_sums, (key_stack, value_stack, tag_stack)
    )
    attended = accumulated / totals.T[:, :, None]
    log_sum = (row_max + jnp.log(totals)).T
    mixed = attended.reshape(rows_here, model_width).astype(jnp.bfloat16)
    onehot = (
        token_clip[:, None] == jnp.arange(clip_gate.shape[0], dtype=jnp.int32)[None, :]
    ).astype(jnp.float32)
    gate_rows = jnp.dot(onehot, clip_gate, precision=lax.Precision.HIGHEST)
    projected = jnp.dot(mixed, out_weight, preferred_element_type=jnp.float32) + out_bias
    block_out = (residual.astype(jnp.float32) + gate_rows * projected).astype(jnp.bfloat16)
    branch_grad = (out_grad.astype(jnp.float32) * gate_rows).astype(jnp.bfloat16)
    mixed_grad = jnp.einsum(
        "te,de->td", branch_grad, out_weight, preferred_element_type=jnp.float32
    ).astype(jnp.bfloat16)
    grad_heads = head_split(mixed_grad)
    row_delta = jnp.sum(
        grad_heads.astype(jnp.float32) * head_split(mixed).astype(jnp.float32), axis=2
    )

    def query_step(running, inputs):
        key_part, value_part, tag_part = inputs
        prob_rows = jnp.exp(
            score_block(query_heads, key_part, own_tags, tag_part) - log_sum.T[:, :, None]
        )
        prob_grad = jnp.einsum(
            "qhd,khd->hqk", grad_heads, value_part, preferred_element_type=jnp.float32
        )
        score_grad = (prob_rows * (prob_grad - row_delta.T[:, :, None])).astype(jnp.bfloat16)
        return (
            running
            + jnp.einsum("hqk,khd->qhd", score_grad, key_part, preferred_element_type=jnp.float32),
            None,
        )

    start_query = jnp.zeros((rows_here, HEADS, HEAD_DIM), jnp.float32)
    query_acc, ignored = lax.scan(query_step, start_query, (key_stack, value_stack, tag_stack))
    query_grad = (query_acc * scale_factor).reshape(rows_here, model_width).astype(jnp.bfloat16)
    own_visit = (query_rows, mixed_grad, log_sum, row_delta, own_tags)
    visitors = neighbour_queries(own_visit)
    query_stack = grouped(head_split(stacked(own_visit, visitors, 0)), group_count)
    grad_stack = grouped(head_split(stacked(own_visit, visitors, 1)), group_count)
    lse_stack = grouped(stacked(own_visit, visitors, 2), group_count)
    delta_stack = grouped(stacked(own_visit, visitors, 3), group_count)
    visit_tags = grouped(stacked(own_visit, visitors, 4), group_count)

    def key_step(running, inputs):
        query_part, grad_part, lse_part, delta_part, tag_part = inputs
        key_acc, value_acc = running
        prob_rows = jnp.exp(
            score_block(query_part, key_heads, tag_part, own_tags) - lse_part.T[:, :, None]
        )
        value_acc = value_acc + jnp.einsum(
            "hqk,qhd->khd",
            prob_rows.astype(jnp.bfloat16),
            grad_part,
            preferred_element_type=jnp.float32,
        )
        prob_grad = jnp.einsum(
            "qhd,khd->hqk", grad_part, value_heads, preferred_element_type=jnp.float32
        )
        score_grad = (prob_rows * (prob_grad - delta_part.T[:, :, None])).astype(jnp.bfloat16)
        key_acc = key_acc + jnp.einsum(
            "hqk,qhd->khd", score_grad, query_part, preferred_element_type=jnp.float32
        )
        return ((key_acc, value_acc), None)

    start_keys = (
        jnp.zeros((rows_here, HEADS, HEAD_DIM), jnp.float32),
        jnp.zeros((rows_here, HEADS, HEAD_DIM), jnp.float32),
    )
    (key_acc, value_acc), ignored = lax.scan(
        key_step, start_keys, (query_stack, grad_stack, lse_stack, delta_stack, visit_tags)
    )
    key_grad = (key_acc * scale_factor).reshape(rows_here, model_width).astype(jnp.bfloat16)
    value_grad = value_acc.reshape(rows_here, model_width).astype(jnp.bfloat16)
    column_share = lax.psum_scatter(
        jnp.einsum("tc,td->cd", branch_grad, mixed, preferred_element_type=jnp.float32),
        "dp",
        scatter_dimension=0,
        tiled=True,
    )
    weight_grad = column_share.T
    return (block_out, query_grad, key_grad, value_grad, weight_grad)


def solution(mesh):
    in_specs = (
        P("dp", None),
        P("dp", None),
        P("dp", None),
        P("dp", None),
        P("dp"),
        P(),
        P(),
        P(),
        P("dp", None),
    )
    out_specs = (P("dp", None), P("dp", None), P("dp", None), P("dp", None), P(None, "dp"))
    return jax.shard_map(shards, mesh=mesh, in_specs=in_specs, out_specs=out_specs, check_vma=False)
```

profile of v0, /device:TPU:8, one launch (start us, length us, event | category | flops | bytes accessed | tf_op | source)
XLA Modules:
  0.0 851.3 jit_solution(10493224799260607871)
XLA Ops:
  10.0 7.9 collective-permute-start.7
  19.8 7.9 collective-permute-start.21
  47.6 7.9 collective-permute-start.8
  57.4 7.9 collective-permute-start.9
  67.3 7.9 collective-permute-start.10
  77.1 7.9 collective-permute-start.11
  86.9 7.9 collective-permute-start.12
  96.8 7.9 collective-permute-start.35
  111.1 8.2 collective-permute-start.49
  176.8 7.9 collective-permute-start.77
  199.8 7.8 collective-permute-start.50
  212.7 7.4 collective-permute-start.23
  222.8 7.8 collective-permute-start.37
  235.8 7.4 collective-permute-start.79
  245.8 7.8 collective-permute-start.24
  258.8 7.4 collective-permute-start.52
  268.9 7.8 collective-permute-start.80
  281.8 7.4 collective-permute-start.39
  291.9 7.8 collective-permute-start.53
  304.8 7.4 collective-permute-start.26
  315.8 7.9 collective-permute-start.40
  331.7 7.4 collective-permute-start.27
  350.6 7.9 collective-permute-start.41
  368.4 17.4 %reshape.145 = bf16[4,512,16,72]{3,2,1,0:T(8,128)(2,1)} reshape(bf16[2048,1152]{1,0:T(8,128)(2,1)} %constant_dynamic-update-slice_fusion.1) | data formatting | bytes 9437184 | tf_op jit(solution)/shard_map/reshape;reshape | solution.py:64
  385.8 13.0 %copy.55 = bf16[4,512,16,72]{1,3,2,0:T(8,128)(2,1)} copy(bf16[4,512,16,72]{3,2,1,0:T(8,128)(2,1)} %reshape.145) | data formatting | bytes 9437184
  403.0 17.4 %reshape.146 = bf16[4,512,16,72]{3,2,1,0:T(8,128)(2,1)} reshape(bf16[2048,1152]{1,0:T(8,128)(2,1)} %constant_dynamic-update-slice_fusion.17) | data formatting | bytes 9437184 | tf_op jit(solution)/shard_map/reshape;reshape | solution.py:64
  420.4 13.1 %copy.56 = bf16[4,512,16,72]{1,3,2,0:T(8,128)(2,1)} copy(bf16[4,512,16,72]{3,2,1,0:T(8,128)(2,1)} %reshape.146) | data formatting | bytes 9437184
  433.5 48.8 %while.39 = (s32[]{:T(128)}, f32[16,128]{1,0:T(8,128)S(1)}, f32[16,128]{1,0:T(8,128)S(1)}, f32[128,16,72]{0,2,1:T(8,128)}, s32[128]{0:T(128)S(1)}, /*index=5*/s3...) while((s32[]{:T(128)}, f32[16,128]{1,0:T(8,128)S(1)}, ...), condition=%wide.region_3.4_spmd.clone, body=%wide.region_0.3_spmd.clone.sunk | while | flops 314044416 | bytes 16816780 | solution.py:121
  484.9 40.2 %while.40 = (s32[]{:T(128)}, f32[128,16,72]{0,2,1:T(8,128)}, bf16[4,512,16,72]{1,3,2,0:T(8,128)(2,1)}, s32[128]{0:T(128)S(1)}, s32[4,512]{1,0:T(4,128)S(1)}, /*i...) while((s32[]{:T(128)}, f32[128,16,72]{0,2,1:T(8,128)}, ...), condition=%wide.region_6.7_spmd.clone, body=%wide.region_5.6_spmd.clone.sunk | while | flops 459636736 | bytes 13852814 | solution.py:158
  527.6 7.4 collective-permute-start.63
  551.4 8.1 collective-permute-start.91
  577.4 17.4 %reshape.143 = bf16[4,512,16,72]{3,2,1,0:T(8,128)(2,1)} reshape(bf16[2048,1152]{1,0:T(8,128)(2,1)} %constant_dynamic-update-slice_fusion.33) | data formatting | bytes 9437184 | tf_op jit(solution)/shard_map/reshape;reshape | solution.py:64
  594.9 13.1 %copy.64 = bf16[4,512,16,72]{1,3,2,0:T(8,128)(2,1)} copy(bf16[4,512,16,72]{3,2,1,0:T(8,128)(2,1)} %reshape.143) | data formatting | bytes 9437184
  608.0 17.4 %reshape.144 = bf16[4,512,16,72]{3,2,1,0:T(8,128)(2,1)} reshape(bf16[2048,1152]{1,0:T(8,128)(2,1)} %constant_dynamic-update-slice_fusion.63) | data formatting | bytes 9437184 | tf_op jit(solution)/shard_map/reshape;reshape | solution.py:64
  625.4 13.1 %copy.66 = bf16[4,512,16,72]{1,3,2,0:T(8,128)(2,1)} copy(bf16[4,512,16,72]{3,2,1,0:T(8,128)(2,1)} %reshape.144) | data formatting | bytes 9437184
  641.2 7.8 collective-permute-start.64
  651.6 7.8 collective-permute-start.92
  662.0 7.8 collective-permute-start.65
  672.4 7.8 collective-permute-start.93
  682.8 7.8 collective-permute-start.66
  693.2 7.8 collective-permute-start.94
  703.6 7.8 collective-permute-start.67
  714.0 7.8 collective-permute-start.95
  724.4 7.8 collective-permute-start.68
  734.8 7.8 collective-permute-start.96
  745.2 7.8 collective-permute-start.69
  755.6 7.8 collective-permute-start.97
  776.3 62.5 %while.41 = (s32[]{:T(128)}, f32[128,16,72]{0,2,1:T(8,128)}, f32[128,16,72]{0,2,1:T(8,128)}, bf16[4,512,16,72]{1,3,2,0:T(8,128)(2,1)}, s32[4,512]{1,0:T(4,128)S(...) while((s32[]{:T(128)}, f32[128,16,72]{0,2,1:T(8,128)}, ...), condition=%wide.region_8.9_spmd.clone, body=%wide.region_7.8_spmd.clone.sunk | while | flops 615120896 | bytes 20816032 | solution.py:193
  (427 shorter events, 425.7 us)
Async XLA Ops:
  7.2 835.8 %all-reduce.3.cloned.1.call-start = ((), (), s32[]{:S(2)}) async-start(), calls=%async_computation | async-start | bytes 10616832
  8.0 37.6 %collective-permute-start = (s32[128]{0:T(128)S(1)}, s32[128]{0:T(128)S(1)}, u32[]{:S(2)}, u32[]{:S(2)}) collective-permute-start(s32[128]{0:T(128)S(1)} %get-tuple-element.712), channel_id=1, source_target_pairs={{0,1},{1,2},{2,3},{3,4},{4,5},{5,6},{6,7},{7,8},{8,9},{9,10},{10,1... | collective-permute-start | bytes 1544 | tf_op jit(solution)/shard_map/ppermute | solution.py:16
  10.0 37.6 %collective-permute-start.7 = (s32[128]{0:T(128)S(1)}, s32[128]{0:T(128)S(1)}, u32[]{:S(2)}, u32[]{:S(2)}) collective-permute-start(s32[128]{0:T(128)S(1)} %get-tuple-element.712), channel_id=1, source_target_pairs={{1,0},{2,1},{3,2},{4,3},{5,4},{6,5},{7,6},{8,7},{9,8},{10,9},{11,1... | collective-permute-start | bytes 1544 | tf_op jit(solution)/shard_map/ppermute | solution.py:16
  17.8 93.3 %collective-permute-start.14 = (bf16[128,1152]{1,0:T(8,128)(2,1)}, bf16[128,1152]{1,0:T(8,128)(2,1)}, u32[]{:S(2)}, u32[]{:S(2)}) collective-permute-start(bf16[128,1152]{1,0:T(8,128)(2,1)} %param.16), channel_id=1, source_target_pairs={{0,1},{1,2},{2,3},{3,4},{4,5},{5,6},{6,7},{7,8},{8,9},{9,10},{10,1... | collective-permute-start | bytes 884744 | tf_op jit(solution)/shard_map/ppermute | solution.py:16
  19.8 157.0 %collective-permute-start.21 = (bf16[128,1152]{1,0:T(8,128)(2,1)}, bf16[128,1152]{1,0:T(8,128)(2,1)}, u32[]{:S(2)}, u32[]{:S(2)}) collective-permute-start(bf16[128,1152]{1,0:T(8,128)(2,1)} %param.16), channel_id=1, source_target_pairs={{1,0},{2,1},{3,2},{4,3},{5,4},{6,5},{7,6},{8,7},{9,8},{10,9},{11,1... | collective-permute-start | bytes 884744 | tf_op jit(solution)/shard_map/ppermute | solution.py:16
  27.6 93.4 %collective-permute-start.28 = (bf16[128,1152]{1,0:T(8,128)(2,1)}, bf16[128,1152]{1,0:T(8,128)(2,1)}, u32[]{:S(2)}, u32[]{:S(2)}) collective-permute-start(bf16[128,1152]{1,0:T(8,128)(2,1)} %param.17), channel_id=1, source_target_pairs={{0,1},{1,2},{2,3},{3,4},{4,5},{5,6},{6,7},{7,8},{8,9},{9,10},{10,1... | collective-permute-start | bytes 884744 | tf_op jit(solution)/shard_map/ppermute | solution.py:16
  96.8 87.9 %collective-permute-start.35 = (bf16[128,1152]{1,0:T(8,128)(2,1)}, bf16[128,1152]{1,0:T(8,128)(2,1)}, u32[]{:S(2)}, u32[]{:S(2)}) collective-permute-start(bf16[128,1152]{1,0:T(8,128)(2,1)} %param.17), channel_id=1, source_target_pairs={{1,0},{2,1},{3,2},{4,3},{5,4},{6,5},{7,6},{8,7},{9,8},{10,9},{11,1... | collective-permute-start | bytes 884744 | tf_op jit(solution)/shard_map/ppermute | solution.py:16
  111.1 78.6 %collective-permute-start.49 = (bf16[128,1152]{1,0:T(8,128)(2,1)}, bf16[128,1152]{1,0:T(8,128)(2,1)S(1)}, u32[]{:S(2)}, u32[]{:S(2)}) collective-permute-start(bf16[128,1152]{1,0:T(8,128)(2,1)} %param.15), channel_id=1, source_target_pairs={{1,0},{2,1},{3,2},{4,3},{5,4},{6,5},{7,6},{8,7},{9,8},{10,9},{11,1... | collective-permute-start | bytes 884744 | tf_op jit(solution)/shard_map/ppermute | solution.py:16
  174.1 23.0 %collective-permute-start.17 = (bf16[128,1152]{1,0:T(8,128)(2,1)S(1)}, bf16[128,1152]{1,0:T(8,128)(2,1)S(1)}, u32[]{:S(2)}, u32[]{:S(2)}) collective-permute-start(bf16[128,1152]{1,0:T(8,128)(2,1)S(1)} %collective-permute-done.16), channel_id=1, source_target_pairs={{0,1},{1,2},{2,3},{3,4},{4,5},{5,6},{6,7},{7,8},{8,9},{9,10},{10,1... | collective-permute-start | bytes 884744 | tf_op jit(solution)/shard_map/ppermute | solution.py:16
  176.8 23.0 %collective-permute-start.77 = (bf16[128,1152]{1,0:T(8,128)(2,1)S(1)}, bf16[128,1152]{1,0:T(8,128)(2,1)S(1)}, u32[]{:S(2)}, u32[]{:S(2)}) collective-permute-start(bf16[128,1152]{1,0:T(8,128)(2,1)S(1)} %copy-done.6), channel_id=1, source_target_pairs={{1,0},{2,1},{3,2},{4,3},{5,4},{6,5},{7,6},{8,7},{9,8},{10,9},{11,1... | collective-permute-start | bytes 884744 | tf_op jit(solution)/shard_map/ppermute | solution.py:16
  184.6 23.0 %collective-permute-start.22 = (bf16[128,1152]{1,0:T(8,128)(2,1)}, bf16[128,1152]{1,0:T(8,128)(2,1)S(1)}, u32[]{:S(2)}, u32[]{:S(2)}) collective-permute-start(bf16[128,1152]{1,0:T(8,128)(2,1)} %collective-permute-done.21), channel_id=1, source_target_pairs={{1,0},{2,1},{3,2},{4,3},{5,4},{6,5},{7,6},{8,7},{9,8},{10,9},{11,1... | collective-permute-start | bytes 884744 | tf_op jit(solution)/shard_map/ppermute | solution.py:16
  186.6 23.0 %collective-permute-start.31 = (bf16[128,1152]{1,0:T(8,128)(2,1)S(1)}, bf16[128,1152]{1,0:T(8,128)(2,1)S(1)}, u32[]{:S(2)}, u32[]{:S(2)}) collective-permute-start(bf16[128,1152]{1,0:T(8,128)(2,1)S(1)} %collective-permute-done.30), channel_id=1, source_target_pairs={{0,1},{1,2},{2,3},{3,4},{4,5},{5,6},{6,7},{7,8},{8,9},{9,10},{10,1... | collective-permute-start | bytes 884744 | tf_op jit(solution)/shard_map/ppermute | solution.py:16
  189.7 23.0 %collective-permute-start.36 = (bf16[128,1152]{1,0:T(8,128)(2,1)}, bf16[128,1152]{1,0:T(8,128)(2,1)S(1)}, u32[]{:S(2)}, u32[]{:S(2)}) collective-permute-start(bf16[128,1152]{1,0:T(8,128)(2,1)} %collective-permute-done.35), channel_id=1, source_target_pairs={{1,0},{2,1},{3,2},{4,3},{5,4},{6,5},{7,6},{8,7},{9,8},{10,9},{11,1... | collective-permute-start | bytes 884744 | tf_op jit(solution)/shard_map/ppermute | solution.py:16
  197.1 23.0 %collective-permute-start.45 = (bf16[128,1152]{1,0:T(8,128)(2,1)S(1)}, bf16[128,1152]{1,0:T(8,128)(2,1)S(1)}, u32[]{:S(2)}, u32[]{:S(2)}) collective-permute-start(bf16[128,1152]{1,0:T(8,128)(2,1)S(1)} %collective-permute-done.44), channel_id=1, source_target_pairs={{0,1},{1,2},{2,3},{3,4},{4,5},{5,6},{6,7},{7,8},{8,9},{9,10},{10,1... | collective-permute-start | bytes 884744 | tf_op jit(solution)/shard_map/ppermute | solution.py:16
  199.8 23.0 %collective-permute-start.50 = (bf16[128,1152]{1,0:T(8,128)(2,1)S(1)}, bf16[128,1152]{1,0:T(8,128)(2,1)S(1)}, u32[]{:S(2)}, u32[]{:S(2)}) collective-permute-start(bf16[128,1152]{1,0:T(8,128)(2,1)S(1)} %collective-permute-done.49), channel_id=1, source_target_pairs={{1,0},{2,1},{3,2},{4,3},{5,4},{6,5},{7,6},{8,7},{9,8},{10,9},{11,1... | collective-permute-start | bytes 884744 | tf_op jit(solution)/shard_map/ppermute | solution.py:16
  209.6 23.0 %collective-permute-start.73 = (bf16[128,1152]{1,0:T(8,128)(2,1)S(1)}, bf16[128,1152]{1,0:T(8,128)(2,1)S(1)}, u32[]{:S(2)}, u32[]{:S(2)}) collective-permute-start(bf16[128,1152]{1,0:T(8,128)(2,1)S(1)} %collective-permute-done.72), channel_id=1, source_target_pairs={{0,1},{1,2},{2,3},{3,4},{4,5},{5,6},{6,7},{7,8},{8,9},{9,10},{10,1... | collective-permute-start | bytes 884744 | tf_op jit(solution)/shard_map/ppermute | solution.py:16
  212.7 23.0 %collective-permute-start.23 = (bf16[128,1152]{1,0:T(8,128)(2,1)S(1)}, bf16[128,1152]{1,0:T(8,128)(2,1)S(1)}, u32[]{:S(2)}, u32[]{:S(2)}) collective-permute-start(bf16[128,1152]{1,0:T(8,128)(2,1)S(1)} %collective-permute-done.22), channel_id=1, source_target_pairs={{1,0},{2,1},{3,2},{4,3},{5,4},{6,5},{7,6},{8,7},{9,8},{10,9},{11,1... | collective-permute-start | bytes 884744 | tf_op jit(solution)/shard_map/ppermute | solution.py:16
  220.1 23.0 %collective-permute-start.18 = (bf16[128,1152]{1,0:T(8,128)(2,1)S(1)}, bf16[128,1152]{1,0:T(8,128)(2,1)S(1)}, u32[]{:S(2)}, u32[]{:S(2)}) collective-permute-start(bf16[128,1152]{1,0:T(8,128)(2,1)S(1)} %collective-permute-done.17), channel_id=1, source_target_pairs={{0,1},{1,2},{2,3},{3,4},{4,5},{5,6},{6,7},{7,8},{8,9},{9,10},{10,1... | collective-permute-start | bytes 884744 | tf_op jit(solution)/shard_map/ppermute | solution.py:16
  222.8 23.0 %collective-permute-start.37 = (bf16[128,1152]{1,0:T(8,128)(2,1)S(1)}, bf16[128,1152]{1,0:T(8,128)(2,1)S(1)}, u32[]{:S(2)}, u32[]{:S(2)}) collective-permute-start(bf16[128,1152]{1,0:T(8,128)(2,1)S(1)} %collective-permute-done.36), channel_id=1, source_target_pairs={{1,0},{2,1},{3,2},{4,3},{5,4},{6,5},{7,6},{8,7},{9,8},{10,9},{11,1... | collective-permute-start | bytes 884744 | tf_op jit(solution)/shard_map/ppermute | solution.py:16
  230.7 23.0 %collective-permute-start.51 = (bf16[128,1152]{1,0:T(8,128)(2,1)S(1)}, bf16[128,1152]{1,0:T(8,128)(2,1)S(1)}, u32[]{:S(2)}, u32[]{:S(2)}) collective-permute-start(bf16[128,1152]{1,0:T(8,128)(2,1)S(1)} %collective-permute-done.50), channel_id=1, source_target_pairs={{1,0},{2,1},{3,2},{4,3},{5,4},{6,5},{7,6},{8,7},{9,8},{10,9},{11,1... | collective-permute-start | bytes 884744 | tf_op jit(solution)/shard_map/ppermute | solution.py:16
  232.6 23.0 %collective-permute-start.32 = (bf16[128,1152]{1,0:T(8,128)(2,1)S(1)}, bf16[128,1152]{1,0:T(8,128)(2,1)S(1)}, u32[]{:S(2)}, u32[]{:S(2)}) collective-permute-start(bf16[128,1152]{1,0:T(8,128)(2,1)S(1)} %collective-permute-done.31), channel_id=1, source_target_pairs={{0,1},{1,2},{2,3},{3,4},{4,5},{5,6},{6,7},{7,8},{8,9},{9,10},{10,1... | collective-permute-start | bytes 884744 | tf_op jit(solution)/shard_map/ppermute | solution.py:16
  235.8 23.0 %collective-permute-start.79 = (bf16[128,1152]{1,0:T(8,128)(2,1)S(1)}, bf16[128,1152]{1,0:T(8,128)(2,1)S(1)}, u32[]{:S(2)}, u32[]{:S(2)}) collective-permute-start(bf16[128,1152]{1,0:T(8,128)(2,1)S(1)} %collective-permute-done.78), channel_id=1, source_target_pairs={{1,0},{2,1},{3,2},{4,3},{5,4},{6,5},{7,6},{8,7},{9,8},{10,9},{11,1... | collective-permute-start | bytes 884744 | tf_op jit(solution)/shard_map/ppermute | solution.py:16
  243.2 23.0 %collective-permute-start.46 = (bf16[128,1152]{1,0:T(8,128)(2,1)S(1)}, bf16[128,1152]{1,0:T(8,128)(2,1)S(1)}, u32[]{:S(2)}, u32[]{:S(2)}) collective-permute-start(bf16[128,1152]{1,0:T(8,128)(2,1)S(1)} %collective-permute-done.45), channel_id=1, source_target_pairs={{0,1},{1,2},{2,3},{3,4},{4,5},{5,6},{6,7},{7,8},{8,9},{9,10},{10,1... | collective-permute-start | bytes 884744 | tf_op jit(solution)/shard_map/ppermute | solution.py:16
  245.8 23.1 %collective-permute-start.24 = (bf16[128,1152]{1,0:T(8,128)(2,1)S(1)}, bf16[128,1152]{1,0:T(8,128)(2,1)S(1)}, u32[]{:S(2)}, u32[]{:S(2)}) collective-permute-start(bf16[128,1152]{1,0:T(8,128)(2,1)S(1)} %collective-permute-done.23), channel_id=1, source_target_pairs={{1,0},{2,1},{3,2},{4,3},{5,4},{6,5},{7,6},{8,7},{9,8},{10,9},{11,1... | collective-permute-start | bytes 884744 | tf_op jit(solution)/shard_map/ppermute | solution.py:16
  253.7 23.0 %collective-permute-start.38 = (bf16[128,1152]{1,0:T(8,128)(2,1)S(1)}, bf16[128,1152]{1,0:T(8,128)(2,1)S(1)}, u32[]{:S(2)}, u32[]{:S(2)}) collective-permute-start(bf16[128,1152]{1,0:T(8,128)(2,1)S(1)} %collective-permute-done.37), channel_id=1, source_target_pairs={{1,0},{2,1},{3,2},{4,3},{5,4},{6,5},{7,6},{8,7},{9,8},{10,9},{11,1... | collective-permute-start | bytes 884744 | tf_op jit(solution)/shard_map/ppermute | solution.py:16
  255.6 23.0 %collective-permute-start.74 = (bf16[128,1152]{1,0:T(8,128)(2,1)S(1)}, bf16[128,1152]{1,0:T(8,128)(2,1)S(1)}, u32[]{:S(2)}, u32[]{:S(2)}) collective-permute-start(bf16[128,1152]{1,0:T(8,128)(2,1)S(1)} %collective-permute-done.73), channel_id=1, source_target_pairs={{0,1},{1,2},{2,3},{3,4},{4,5},{5,6},{6,7},{7,8},{8,9},{9,10},{10,1... | collective-permute-start | bytes 884744 | tf_op jit(solution)/shard_map/ppermute | solution.py:16
  258.8 23.0 %collective-permute-start.52 = (bf16[128,1152]{1,0:T(8,128)(2,1)S(1)}, bf16[128,1152]{1,0:T(8,128)(2,1)S(1)}, u32[]{:S(2)}, u32[]{:S(2)}) collective-permute-start(bf16[128,1152]{1,0:T(8,128)(2,1)S(1)} %collective-permute-done.51), channel_id=1, source_target_pairs={{1,0},{2,1},{3,2},{4,3},{5,4},{6,5},{7,6},{8,7},{9,8},{10,9},{11,1... | collective-permute-start | bytes 884744 | tf_op jit(solution)/shard_map/ppermute | solution.py:16
  266.2 23.0 %collective-permute-start.19 = (bf16[128,1152]{1,0:T(8,128)(2,1)S(1)}, bf16[128,1152]{1,0:T(8,128)(2,1)S(1)}, u32[]{:S(2)}, u32[]{:S(2)}) collective-permute-start(bf16[128,1152]{1,0:T(8,128)(2,1)S(1)} %collective-permute-done.18), channel_id=1, source_target_pairs={{0,1},{1,2},{2,3},{3,4},{4,5},{5,6},{6,7},{7,8},{8,9},{9,10},{10,1... | collective-permute-start | bytes 884744 | tf_op jit(solution)/shard_map/ppermute | solution.py:16
  268.9 23.0 %collective-permute-start.80 = (bf16[128,1152]{1,0:T(8,128)(2,1)S(1)}, bf16[128,1152]{1,0:T(8,128)(2,1)S(1)}, u32[]{:S(2)}, u32[]{:S(2)}) collective-permute-start(bf16[128,1152]{1,0:T(8,128)(2,1)S(1)} %collective-permute-done.79), channel_id=1, source_target_pairs={{1,0},{2,1},{3,2},{4,3},{5,4},{6,5},{7,6},{8,7},{9,8},{10,9},{11,1... | collective-permute-start | bytes 884744 | tf_op jit(solution)/shard_map/ppermute | solution.py:16
  281.8 23.0 %collective-permute-start.39 = (bf16[128,1152]{1,0:T(8,128)(2,1)S(1)}, bf16[128,1152]{1,0:T(8,128)(2,1)S(1)}, u32[]{:S(2)}, u32[]{:S(2)}) collective-permute-start(bf16[128,1152]{1,0:T(8,128)(2,1)S(1)} %collective-permute-done.38), channel_id=1, source_target_pairs={{1,0},{2,1},{3,2},{4,3},{5,4},{6,5},{7,6},{8,7},{9,8},{10,9},{11,1... | collective-permute-start | bytes 884744 | tf_op jit(solution)/shard_map/ppermute | solution.py:16
  289.2 23.0 %collective-permute-start.47 = (bf16[128,1152]{1,0:T(8,128)(2,1)S(1)}, bf16[128,1152]{1,0:T(8,128)(2,1)}, u32[]{:S(2)}, u32[]{:S(2)}) collective-permute-start(bf16[128,1152]{1,0:T(8,128)(2,1)S(1)} %collective-permute-done.46), channel_id=1, source_target_pairs={{0,1},{1,2},{2,3},{3,4},{4,5},{5,6},{6,7},{7,8},{8,9},{9,10},{10,1... | collective-permute-start | bytes 884744 | tf_op jit(solution)/shard_map/ppermute | solution.py:16
  291.9 24.0 %collective-permute-start.53 = (bf16[128,1152]{1,0:T(8,128)(2,1)S(1)}, bf16[128,1152]{1,0:T(8,128)(2,1)S(1)}, u32[]{:S(2)}, u32[]{:S(2)}) collective-permute-start(bf16[128,1152]{1,0:T(8,128)(2,1)S(1)} %collective-permute-done.52), channel_id=1, source_target_pairs={{1,0},{2,1},{3,2},{4,3},{5,4},{6,5},{7,6},{8,7},{9,8},{10,9},{11,1... | collective-permute-start | bytes 884744 | tf_op jit(solution)/shard_map/ppermute | solution.py:16
  299.7 24.0 %collective-permute-start.81 = (bf16[128,1152]{1,0:T(8,128)(2,1)S(1)}, bf16[128,1152]{1,0:T(8,128)(2,1)S(1)}, u32[]{:S(2)}, u32[]{:S(2)}) collective-permute-start(bf16[128,1152]{1,0:T(8,128)(2,1)S(1)} %collective-permute-done.80), channel_id=1, source_target_pairs={{1,0},{2,1},{3,2},{4,3},{5,4},{6,5},{7,6},{8,7},{9,8},{10,9},{11,1... | collective-permute-start | bytes 884744 | tf_op jit(solution)/shard_map/ppermute | solution.py:16
  301.7 24.0 %collective-permute-start.75 = (bf16[128,1152]{1,0:T(8,128)(2,1)S(1)}, bf16[128,1152]{1,0:T(8,128)(2,1)}, u32[]{:S(2)}, u32[]{:S(2)}) collective-permute-start(bf16[128,1152]{1,0:T(8,128)(2,1)S(1)} %collective-permute-done.74), channel_id=1, source_target_pairs={{0,1},{1,2},{2,3},{3,4},{4,5},{5,6},{6,7},{7,8},{8,9},{9,10},{10,1... | collective-permute-start | bytes 884744 | tf_op jit(solution)/shard_map/ppermute | solution.py:16
  304.8 24.5 %collective-permute-start.26 = (bf16[128,1152]{1,0:T(8,128)(2,1)S(1)}, bf16[128,1152]{1,0:T(8,128)(2,1)S(1)}, u32[]{:S(2)}, u32[]{:S(2)}) collective-permute-start(bf16[128,1152]{1,0:T(8,128)(2,1)S(1)} %collective-permute-done.25), channel_id=1, source_target_pairs={{1,0},{2,1},{3,2},{4,3},{5,4},{6,5},{7,6},{8,7},{9,8},{10,9},{11,1... | collective-permute-start | bytes 884744 | tf_op jit(solution)/shard_map/ppermute | solution.py:16
  315.8 32.8 %collective-permute-start.40 = (bf16[128,1152]{1,0:T(8,128)(2,1)S(1)}, bf16[128,1152]{1,0:T(8,128)(2,1)}, u32[]{:S(2)}, u32[]{:S(2)}) collective-permute-start(bf16[128,1152]{1,0:T(8,128)(2,1)S(1)} %collective-permute-done.39), channel_id=1, source_target_pairs={{1,0},{2,1},{3,2},{4,3},{5,4},{6,5},{7,6},{8,7},{9,8},{10,9},{11,1... | collective-permute-start | bytes 884744 | tf_op jit(solution)/shard_map/ppermute | solution.py:16
  323.7 26.8 %collective-permute-start.54 = (bf16[128,1152]{1,0:T(8,128)(2,1)S(1)}, bf16[128,1152]{1,0:T(8,128)(2,1)}, u32[]{:S(2)}, u32[]{:S(2)}) collective-permute-start(bf16[128,1152]{1,0:T(8,128)(2,1)S(1)} %collective-permute-done.53), channel_id=1, source_target_pairs={{1,0},{2,1},{3,2},{4,3},{5,4},{6,5},{7,6},{8,7},{9,8},{10,9},{11,1... | collective-permute-start | bytes 884744 | tf_op jit(solution)/shard_map/ppermute | solution.py:16
  325.7 32.8 %collective-permute-start.82 = (bf16[128,1152]{1,0:T(8,128)(2,1)S(1)}, bf16[128,1152]{1,0:T(8,128)(2,1)}, u32[]{:S(2)}, u32[]{:S(2)}) collective-permute-start(bf16[128,1152]{1,0:T(8,128)(2,1)S(1)} %collective-permute-done.81), channel_id=1, source_target_pairs={{1,0},{2,1},{3,2},{4,3},{5,4},{6,5},{7,6},{8,7},{9,8},{10,9},{11,1... | collective-permute-start | bytes 884744 | tf_op jit(solution)/shard_map/ppermute | solution.py:16
  329.3 31.6 %collective-permute-start.34 = (bf16[128,1152]{1,0:T(8,128)(2,1)S(1)}, bf16[128,1152]{1,0:T(8,128)(2,1)S(1)}, u32[]{:S(2)}, u32[]{:S(2)}) collective-permute-start(bf16[128,1152]{1,0:T(8,128)(2,1)S(1)} %collective-permute-done.33), channel_id=1, source_target_pairs={{0,1},{1,2},{2,3},{3,4},{4,5},{5,6},{6,7},{7,8},{8,9},{9,10},{10,1... | collective-permute-start | bytes 884744 | tf_op jit(solution)/shard_map/ppermute | solution.py:16
  345.2 182.3 %collective-permute-start.48 = (bf16[128,1152]{1,0:T(8,128)(2,1)}, bf16[128,1152]{1,0:T(8,128)(2,1)}, u32[]{:S(2)}, u32[]{:S(2)}) collective-permute-start(bf16[128,1152]{1,0:T(8,128)(2,1)} %collective-permute-done.47), channel_id=1, source_target_pairs={{0,1},{1,2},{2,3},{3,4},{4,5},{5,6},{6,7},{7,8},{8,9},{9,10},{10,1... | collective-permute-start | bytes 884744 | tf_op jit(solution)/shard_map/ppermute | solution.py:16
  348.6 202.7 %collective-permute-start.76 = (bf16[128,1152]{1,0:T(8,128)(2,1)}, bf16[128,1152]{1,0:T(8,128)(2,1)}, u32[]{:S(2)}, u32[]{:S(2)}) collective-permute-start(bf16[128,1152]{1,0:T(8,128)(2,1)} %collective-permute-done.75), channel_id=1, source_target_pairs={{0,1},{1,2},{2,3},{3,4},{4,5},{5,6},{6,7},{7,8},{8,9},{9,10},{10,1... | collective-permute-start | bytes 884744 | tf_op jit(solution)/shard_map/ppermute | solution.py:16
  350.6 50.0 %collective-permute-start.41 = (bf16[128,1152]{1,0:T(8,128)(2,1)}, bf16[128,1152]{1,0:T(8,128)(2,1)}, u32[]{:S(2)}, u32[]{:S(2)}) collective-permute-start(bf16[128,1152]{1,0:T(8,128)(2,1)} %collective-permute-done.40), channel_id=1, source_target_pairs={{1,0},{2,1},{3,2},{4,3},{5,4},{6,5},{7,6},{8,7},{9,8},{10,9},{11,1... | collective-permute-start | bytes 884744 | tf_op jit(solution)/shard_map/ppermute | solution.py:16
  358.5 188.6 %collective-permute-start.55 = (bf16[128,1152]{1,0:T(8,128)(2,1)}, bf16[128,1152]{1,0:T(8,128)(2,1)}, u32[]{:S(2)}, u32[]{:S(2)}) collective-permute-start(bf16[128,1152]{1,0:T(8,128)(2,1)} %collective-permute-done.54), channel_id=1, source_target_pairs={{1,0},{2,1},{3,2},{4,3},{5,4},{6,5},{7,6},{8,7},{9,8},{10,9},{11,1... | collective-permute-start | bytes 884744 | tf_op jit(solution)/shard_map/ppermute | solution.py:16
  360.9 206.3 %collective-permute-start.83 = (bf16[128,1152]{1,0:T(8,128)(2,1)}, bf16[128,1152]{1,0:T(8,128)(2,1)}, u32[]{:S(2)}, u32[]{:S(2)}) collective-permute-start(bf16[128,1152]{1,0:T(8,128)(2,1)} %collective-permute-done.82), channel_id=1, source_target_pairs={{1,0},{2,1},{3,2},{4,3},{5,4},{6,5},{7,6},{8,7},{9,8},{10,9},{11,1... | collective-permute-start | bytes 884744 | tf_op jit(solution)/shard_map/ppermute | solution.py:16
  525.1 113.4 %collective-permute-start.56 = (f32[128,16]{0,1:T(8,128)S(1)}, f32[128,16]{0,1:T(8,128)S(1)}, u32[]{:S(2)}, u32[]{:S(2)}) collective-permute-start(f32[128,16]{0,1:T(8,128)S(1)} %bitcast.202), channel_id=1, source_target_pairs={{0,1},{1,2},{2,3},{3,4},{4,5},{5,6},{6,7},{7,8},{8,9},{9,10},{10,1... | collective-permute-start | bytes 24584 | tf_op jit(solution)/shard_map/ppermute | solution.py:16
  527.6 113.5 %collective-permute-start.63 = (f32[128,16]{0,1:T(8,128)S(1)}, f32[128,16]{0,1:T(8,128)S(1)}, u32[]{:S(2)}, u32[]{:S(2)}) collective-permute-start(f32[128,16]{0,1:T(8,128)S(1)} %bitcast.203), channel_id=1, source_target_pairs={{1,0},{2,1},{3,2},{4,3},{5,4},{6,5},{7,6},{8,7},{9,8},{10,9},{11,1... | collective-permute-start | bytes 24584 | tf_op jit(solution)/shard_map/ppermute | solution.py:16
  547.0 102.0 %collective-permute-start.84 = (f32[128,16]{0,1:T(8,128)S(1)}, f32[128,16]{0,1:T(8,128)S(1)}, u32[]{:S(2)}, u32[]{:S(2)}) collective-permute-start(f32[128,16]{0,1:T(8,128)S(1)} %get-tuple-element.845), channel_id=1, source_target_pairs={{0,1},{1,2},{2,3},{3,4},{4,5},{5,6},{6,7},{7,8},{8,9},{9,10},{10,1... | collective-permute-start | bytes 24584 | tf_op jit(solution)/shard_map/ppermute | solution.py:16
  551.4 100.2 %collective-permute-start.91 = (f32[128,16]{0,1:T(8,128)S(1)}, f32[128,16]{0,1:T(8,128)S(1)}, u32[]{:S(2)}, u32[]{:S(2)}) collective-permute-start(f32[128,16]{0,1:T(8,128)S(1)} %get-tuple-element.845), channel_id=1, source_target_pairs={{1,0},{2,1},{3,2},{4,3},{5,4},{6,5},{7,6},{8,7},{9,8},{10,9},{11,1... | collective-permute-start | bytes 24584 | tf_op jit(solution)/shard_map/ppermute | solution.py:16
  (75 other events, 2384.9 us)
Sparse Core Ops, SparseCore 0:
  638.6 152.7 all-reduce.2
where the time goes:
time: 858 us; the launch traced here: 851 us
  starting transfers between devices  415 us (48%)
  local copies, waits for them, and re-layouts  223 us (26%)
  matrix products  147 us (17%)
  waiting for transfers between devices  29.9 us (3%)
  other arithmetic  20.8 us (2%)
  between operations  15.6 us (2%)
    ppermute x98, starting transfers between devices, passed_along(): return lax.ppermute(shard, axis, pairs)  415 us
    unnamed x160, local copies, waits for them, and re-layouts  143 us
    another operation x4, local copies, waits for them, and re-layouts, grouped(): values_in.reshape((group_count, values_in.shape[0] // group_count) + valu...  69.6 us
    dot_general x12, matrix products, score_block(): jnp.einsum('qhd,khd->hqk', query_part, key_part, preferred_element_type=j...  49.6 us
    ppermute x98, waiting for transfers between devices, passed_along(): return lax.ppermute(shard, axis, pairs)  29.9 us
    dot_general x4, matrix products, key_step(): jnp.einsum('hqk,qhd->khd', score_grad, query_part, preferred_element_type...  27.5 us
    dot_general x4, matrix products, query_step(): jnp.einsum('hqk,khd->qhd', score_grad, key_part, preferred_element_type=j...  23.2 us
    dot_general x4, matrix products, soft_step(): jnp.einsum('hqk,khd->qhd', weights.astype(jnp.bfloat16), value_part, pref...  18.7 us
  transfers between devices with their start and end apart: 99, of which 9 were waited for; matrix products, arithmetic and copies ran while one was open for 45% of the time, Pallas kernels for 0%

commit v1 on v0

v1 whole, which is shorter than its diff:
```python
import math

import jax
import jax.numpy as jnp
from jax import lax
from jax.experimental import pallas as pl
from jax.experimental.pallas import tpu as pltpu
from jax.sharding import Mesh, PartitionSpec as P

HEADS = 16
HEAD_DIM = 72
WIDTH = HEADS * HEAD_DIM
TOK = 128
GROUPS = 8
EDGE = 4
SPAN = HEADS + 2 * EDGE
TILE = 256
TILES = SPAN * TOK // TILE
CHUNK = 4 * HEAD_DIM + 16
CLIPS = 32
SCALE = 1.0 / math.sqrt(HEAD_DIM)
SCALE2 = SCALE / math.log(2.0)
FAR = -1e30
BF = jnp.bfloat16
F32 = jnp.float32
VMEM_BYTES = 56 * 1024 * 1024

WHOLE = pl.BlockSpec(memory_space=pltpu.VMEM)


def params():
    return pltpu.CompilerParams(vmem_limit_bytes=VMEM_BYTES)


def mm(left, right):
    return jnp.dot(left, right, preferred_element_type=F32)


def pack_body(query, key, value, out_grad, tags, gate, weight, bg_ref, chunk_ref):
    clip = tags[...]
    onehot = (lax.broadcasted_iota(jnp.int32, (CLIPS, TOK), 0) + 1 == clip).astype(F32)
    gate_rows = lax.dot_general(
        onehot, gate[...], (((0,), (0,)), ((), ())), precision=lax.Precision.HIGHEST, preferred_element_type=F32
    )
    branch = (out_grad[...].astype(F32) * gate_rows).astype(BF)
    bg_ref[...] = branch
    grad_t = lax.dot_general(weight[...], branch, (((1,), (1,)), ((), ())), preferred_element_type=F32)
    query_t = query[...].astype(F32).T
    key_t = key[...].astype(F32).T
    value_t = value[...].astype(F32).T
    tag_rows = jnp.broadcast_to(clip.astype(F32), (16, TOK))
    for head in range(HEADS):
        rows = slice(head * HEAD_DIM, (head + 1) * HEAD_DIM)
        whole = jnp.concatenate([query_t[rows], key_t[rows], value_t[rows], grad_t[rows], tag_rows], 0)
        chunk_ref[head] = whole.astype(BF)


def pack(query, key, value, out_grad, tags, gate, weight):
    return pl.pallas_call(
        pack_body,
        out_shape=(jax.ShapeDtypeStruct((TOK, WIDTH), BF), jax.ShapeDtypeStruct((HEADS, CHUNK, TOK), BF)),
        in_specs=[WHOLE] * 7,
        out_specs=(WHOLE, WHOLE),
        compiler_params=params(),
        name="pack",
    )(query, key, value, out_grad, tags, gate, weight)


def window_block(block, left, main, right):
    if block < EDGE:
        return left[block]
    if block < EDGE + HEADS:
        return main[block - EDGE]
    return right[block - EDGE - HEADS]


def clip_row(block, left, main, right):
    row = window_block(block, left, main, right)[4 * HEAD_DIM :].astype(F32)[0:1]
    if block >= EDGE + HEADS:
        row = jnp.where(row == 0.0, 100.0, row)
    return row


def owned_clips(clips):
    ids = lax.broadcasted_iota(jnp.int32, (CLIPS, TOK), 0).astype(F32) + 1.0
    middle = jnp.zeros((CLIPS, TOK), F32)
    for row in clips:
        middle += (row < ids).astype(F32) + (row <= ids).astype(F32)
    middle = jnp.sum(middle, axis=1, keepdims=True)
    inside = (middle >= 2.0 * EDGE * TOK) & (middle < 2.0 * (EDGE + HEADS) * TOK)
    held = jnp.where(inside, 1.0, 0.0)
    return [jnp.sum(jnp.where(ids == row, held, 0.0), axis=0, keepdims=True) for row in clips]


def tile_bounds(clips, owned, low_ref, high_ref):
    per = TILE // TOK
    for tile in range(TILES):
        low, high = None, None
        for block in range(tile * per, (tile + 1) * per):
            least = jnp.where(owned[block] > 0.0, clips[block], 1000.0)
            most = jnp.where(owned[block] > 0.0, clips[block], -1.0)
            low = least if low is None else jnp.minimum(low, least)
            high = most if high is None else jnp.maximum(high, most)
        low_ref[tile] = jnp.min(low).astype(jnp.int32)
        high_ref[tile] = jnp.max(high).astype(jnp.int32)


def key_range(tile, low_ref, high_ref):
    low, high = low_ref[tile], high_ref[tile]
    first, count = jnp.int32(0), jnp.int32(0)
    for other in range(TILES):
        meets = (high_ref[other] >= low) & (low_ref[other] <= high)
        before = high_ref[other] < low
        ahead = (high_ref[other] < 0) & (other < tile)
        first = first + jnp.where(before & (high_ref[other] >= 0), 1, 0) + jnp.where(ahead, 1, 0)
        count = count + jnp.where(meets, 1, 0)
    count = jnp.where(high < 0, 0, count)
    return first, first + count


def spread(piece, extra):
    rows = [piece] + extra
    have = sum(part.shape[0] for part in rows)
    if have < TOK:
        rows.append(jnp.zeros((TOK - have, TOK), F32))
    return jnp.concatenate(rows, 0)


def masks(row):
    ids = lax.broadcasted_iota(jnp.int32, (CLIPS, TOK), 0).astype(F32) + 1.0
    same = ids == row
    return jnp.where(same, 1.0, 0.0), jnp.where(same, 0.0, FAR)


def place(block):
    per = TILE // TOK
    return block // per, slice((block % per) * TOK, (block % per + 1) * TOK)


def forward_body(left, main, right, mixed_ref, stat_ref, query_t, key_n, value_t, out_t, low_ref, high_ref):
    clips = [clip_row(block, left, main, right) for block in range(SPAN)]
    owned = owned_clips(clips)
    tile_bounds(clips, owned, low_ref, high_ref)
    ones = jnp.ones((8, TOK), F32)
    for block in range(SPAN):
        whole = window_block(block, left, main, right).astype(F32)
        tile, part = place(block)
        near, far = masks(clips[block])
        query_t[tile, :, part] = spread(whole[0:72], [near]).astype(BF)
        key_n[tile, part, :] = spread(whole[72:144], [far]).T.astype(BF)
        value_t[tile, :, part] = spread(whole[144:216], [ones]).astype(BF)

    def query_step(tile, carry):
        first, last = key_range(tile, low_ref, high_ref)
        queries = query_t[tile]
        out_t[...] = jnp.zeros_like(out_t)

        def key_step(other, top):
            scores = mm(key_n[other], queries)
            new_top = jnp.maximum(top, jnp.max(scores, axis=0, keepdims=True))
            fade = jnp.exp2((top - new_top) * SCALE2)
            weights = jnp.exp2((scores - new_top) * SCALE2).astype(BF)
            out_t[...] = out_t[...] * fade + mm(value_t[other, 0:80, :], weights)
            return new_top

        top = lax.fori_loop(first, last, key_step, jnp.full((1, TILE), 2.0 * FAR, F32))
        sums = out_t[72:73, :]
        held = sums > 0.0
        sums = jnp.where(held, sums, 1.0)
        mixed = (out_t[0:72, :] / sums).astype(BF)
        log_sum = top * SCALE2 + jnp.log2(sums)
        for part in range(TILE // TOK):
            cols = slice(part * TOK, (part + 1) * TOK)
            block = tile * (TILE // TOK) + part
            mixed_ref[block] = mixed[:, cols]
            stat_ref[block] = jnp.broadcast_to(log_sum[:, cols], (8, TOK))
        return carry

    lax.fori_loop(0, TILES, query_step, 0)
    for block in range(SPAN):
        mixed_ref[block] = jnp.where(owned[block] > 0.0, mixed_ref[block].astype(F32), 0.0).astype(BF)


def forward(left, main, right):
    return pl.pallas_call(
        forward_body,
        out_shape=(
            jax.ShapeDtypeStruct((SPAN, HEAD_DIM, TOK), BF),
            jax.ShapeDtypeStruct((SPAN, 8, TOK), F32),
        ),
        in_specs=[WHOLE] * 3,
        out_specs=(WHOLE, WHOLE),
        scratch_shapes=[
            pltpu.VMEM((TILES, TOK, TILE), BF),
            pltpu.VMEM((TILES, TILE, TOK), BF),
            pltpu.VMEM((TILES, TOK, TILE), BF),
            pltpu.VMEM((80, TILE), F32),
            pltpu.SMEM((TILES,), jnp.int32),
            pltpu.SMEM((TILES,), jnp.int32),
        ],
        compiler_params=params(),
        name="forward",
    )(left, main, right)


def backward_body(
    left, main, right, mixed, stat, out_ref,
    query_t, query_n, key_t, key_n, value_n, grad_t, grad_n, stats, dq, dk, dv, low_ref, high_ref,
):
    clips = [clip_row(block, left, main, right) for block in range(SPAN)]
    owned = owned_clips(clips)
    tile_bounds(clips, owned, low_ref, high_ref)
    for block in range(SPAN):
        whole = window_block(block, left, main, right).astype(F32)
        tile, part = place(block)
        near, far = masks(clips[block])
        asked = spread(whole[0:72], [near])
        query_t[tile, :, part] = asked.astype(BF)
        query_n[tile, part, :] = asked.T.astype(BF)
        held = spread(whole[72:144], [far])
        key_t[tile, :, part] = held.astype(BF)
        key_n[tile, part, :] = held.T.astype(BF)
        value_n[tile, part, :] = spread(whole[144:216], []).T.astype(BF)
        grad = spread(whole[216:288], [])
        grad_t[tile, :, part] = grad.astype(BF)
        grad_n[tile, part, :] = grad.T.astype(BF)
        delta = jnp.sum(whole[216:288] * mixed[block].astype(F32), axis=0, keepdims=True)
        stats[tile, :, part] = jnp.concatenate([stat[block][0:1], delta, jnp.zeros((6, TOK), F32)], 0)
    dk[...] = jnp.zeros_like(dk)
    dv[...] = jnp.zeros_like(dv)

    def query_step(tile, carry):
        first, last = key_range(tile, low_ref, high_ref)
        log_sum = stats[tile, 0:1, :]
        delta = stats[tile, 1:2, :]
        dq[tile] = jnp.zeros((80, TILE), F32)

        def key_step(other, inner):
            scores = mm(key_n[other], query_t[tile])
            prob = jnp.exp2(scores * SCALE2 - log_sum)
            pull = mm(value_n[other], grad_t[tile])
            dv[other] += mm(prob.astype(BF), grad_n[tile])
            score_grad = (prob * (pull - delta)).astype(BF)
            dk[other] += mm(score_grad, query_n[tile])
            dq[tile] += mm(key_t[other, 0:80, :], score_grad)
            return inner

        return lax.fori_loop(first, last, key_step, carry)

    lax.fori_loop(0, TILES, query_step, 0)
    for block in range(SPAN):
        tile, part = place(block)
        held = owned[block] > 0.0
        pieces = [
            dq[tile, 0:72, part] * SCALE,
            dk[tile, part, :].T[0:72] * SCALE,
            dv[tile, part, :].T[0:72],
        ]
        out_ref[block] = jnp.where(held, jnp.concatenate(pieces, 0), 0.0).astype(BF)


def backward(left, main, right, mixed, stat):
    t_form = pltpu.VMEM((TILES, TOK, TILE), BF)
    n_form = pltpu.VMEM((TILES, TILE, TOK), BF)
    return pl.pallas_call(
        backward_body,
        out_shape=jax.ShapeDtypeStruct((SPAN, 3 * HEAD_DIM, TOK), BF),
        in_specs=[WHOLE] * 5,
        out_specs=WHOLE,
        scratch_shapes=[
            t_form, n_form, t_form, n_form, n_form, t_form, n_form,
            pltpu.VMEM((TILES, 8, TILE), F32),
            pltpu.VMEM((TILES, 80, TILE), F32),
            pltpu.VMEM((TILES, TILE, TOK), F32),
            pltpu.VMEM((TILES, TILE, TOK), F32),
            pltpu.SMEM((TILES,), jnp.int32),
            pltpu.SMEM((TILES,), jnp.int32),
        ],
        compiler_params=params(),
        name="backward",
    )(left, main, right, mixed, stat)


def unpack_body(packed, residual, tags, gate, weight, bias, out_ref, dq_ref, dk_ref, dv_ref):
    clip = tags[...]
    onehot = (lax.broadcasted_iota(jnp.int32, (CLIPS, TOK), 0) + 1 == clip).astype(F32)
    gate_rows = lax.dot_general(
        onehot, gate[...], (((0,), (0,)), ((), ())), precision=lax.Precision.HIGHEST, preferred_element_type=F32
    )
    whole = [packed[head].astype(F32) for head in range(HEADS)]
    mixed = jnp.concatenate([part[0:72] for part in whole], 0).T.astype(BF)
    projected = mm(mixed, weight[...]) + bias[...]
    out_ref[...] = (residual[...].astype(F32) + gate_rows * projected).astype(BF)
    for ref, start in ((dq_ref, 72), (dk_ref, 144), (dv_ref, 216)):
        ref[...] = jnp.concatenate([part[start : start + 72] for part in whole], 0).T.astype(BF)


def unpack(packed, residual, tags, gate, weight, bias):
    shape = jax.ShapeDtypeStruct((TOK, WIDTH), BF)
    return pl.pallas_call(
        unpack_body,
        out_shape=(shape,) * 4,
        in_specs=[WHOLE] * 6,
        out_specs=(WHOLE,) * 4,
        compiler_params=params(),
        name="unpack",
    )(packed, residual, tags, gate, weight, bias)


def from_neighbour(values, by):
    total = GROUPS * HEADS
    pairs = [(i, i + by * HEADS) for i in range(total) if 0 <= i + by * HEADS < total]
    return lax.ppermute(values, ("g", "r"), pairs)


def shards(query, key, value, residual, token_clip, gate, weight, bias, out_grad):
    tags = (token_clip + 1).reshape(1, TOK)
    branch, chunk = pack(query, key, value, out_grad, tags, gate, weight)
    gathered = lax.all_gather(branch, "r", axis=0, tiled=False)
    main = lax.all_to_all(chunk, "r", 0, 0, tiled=True)
    left = from_neighbour(main[HEADS - EDGE :], 1)
    right = from_neighbour(main[:EDGE], -1)
    mixed_window, stat = forward(left, main, right)
    mixed_from_left = from_neighbour(mixed_window[EDGE + HEADS :], 1)
    mixed_from_right = from_neighbour(mixed_window[:EDGE], -1)
    grads_window = backward(left, main, right, mixed_window, stat)
    grads_from_left = from_neighbour(grads_window[EDGE + HEADS :], 1)
    grads_from_right = from_neighbour(grads_window[:EDGE], -1)

    def joined(window, from_left, from_right):
        middle = jnp.zeros((HEADS - 2 * EDGE,) + from_left.shape[1:], BF)
        return window[EDGE : EDGE + HEADS] + jnp.concatenate([from_left, middle, from_right], 0)

    mixed = joined(mixed_window, mixed_from_left, mixed_from_right)
    grads = joined(grads_window, grads_from_left, grads_from_right)
    packed = lax.all_to_all(jnp.concatenate([mixed, grads], 1), "r", 0, 0, tiled=True)
    block_out, dq, dk, dv = unpack(packed, residual, tags, gate, weight, bias.reshape(1, WIDTH))

    term = jnp.einsum("bct,btd->cd", mixed, gathered, preferred_element_type=F32)
    share = WIDTH // GROUPS
    term = term.reshape(HEAD_DIM, GROUPS, share).transpose(1, 0, 2)
    term = jnp.sum(lax.all_to_all(term, "g", 0, 0, tiled=True), 0)
    final = share // HEADS
    term = term.reshape(HEAD_DIM, HEADS, final).transpose(1, 0, 2)
    weight_grad = lax.all_to_all(term, "r", 0, 0, tiled=True).reshape(WIDTH, final)
    return (block_out, dq, dk, dv, weight_grad)


def solution(mesh):
    split = Mesh(mesh.devices.reshape(GROUPS, HEADS), ("g", "r"))
    both = ("g", "r")
    in_specs = (
        P(both, None), P(both, None), P(both, None), P(both, None), P(both), P(), P(), P(), P(both, None),
    )
    out_specs = (P(both, None),) * 4 + (P(None, both),)
    return jax.shard_map(shards, mesh=split, in_specs=in_specs, out_specs=out_specs, check_vma=False)
```

time: 858 us -> 202 us (0.24)
  the two profiles are of different devices: /device:TPU:8 before, /device:TPU:1 now
where the time goes in v1:
time: 202 us; the launch traced here: 204 us
  starting transfers between devices  55.9 us (28%)
  waiting for transfers between devices  43.4 us (21%)
  Pallas kernels  43.1 us (21%)
  blocking collectives  32.7 us (16%)
  between operations  14.3 us (7%)
  local copies, waits for them, and re-layouts  7.85 us (4%)
  other arithmetic  3.4 us (2%)
  matrix products  3.29 us (2%)
    all_to_all x1, blocking collectives, shards(): main = lax.all_to_all(chunk, 'r', 0, 0, tiled=True)  32.7 us
    ppermute x6, starting transfers between devices, from_neighbour(): return lax.ppermute(values, ('g', 'r'), pairs)  28.8 us
    ppermute x6, waiting for transfers between devices, from_neighbour(): return lax.ppermute(values, ('g', 'r'), pairs)  18.2 us
    pallas_call x1, Pallas kernels, backward(): pl.pallas_call(backward_body, out_shape=jax.ShapeDtypeStruct((SPAN, 3 * H...  17.6 us
    pallas_call x1, Pallas kernels, forward(): pl.pallas_call(forward_body, out_shape=(jax.ShapeDtypeStruct((SPAN, HEAD_...  16.6 us
    all_to_all x1, waiting for transfers between devices, shards(): lax.all_to_all(jnp.concatenate([mixed, grads], 1), 'r', 0, 0, tiled=True)  16.4 us
    all_to_all x1, starting transfers between devices, shards(): term = jnp.sum(lax.all_to_all(term, 'g', 0, 0, tiled=True), 0)  16 us
    all_to_all x1, waiting for transfers between devices, shards(): term = jnp.sum(lax.all_to_all(term, 'g', 0, 0, tiled=True), 0)  7.7 us
  transfers between devices with their start and end apart: 10, of which 4 were waited for; matrix products, arithmetic and copies ran while one was open for 5% of the time, Pallas kernels for 19%

profile of v1, /device:TPU:1, one launch (start us, length us, event | category | flops | bytes accessed | tf_op | source)
XLA Modules:
  0.0 203.9 jit_solution(14873700930831245207)
XLA Ops:
  7.2 0.0 all-gather.3.cloned.1.call-start
  7.2 1.2 add_bitcast_fusion.tags
  8.4 4.6 %pack.1 = (bf16[128,1152]{1,0:T(8,128)(2,1)}, bf16[16,304,128]{2,1,0:T(8,128)(2,1)}) custom-call(bf16[128,1152]{1,0:T(8,128)(2,1)} %query.1, bf16[128,1152]{1,0:T(8,128)(2,1)} %key.1, bf16[128,1152]{1,0:T(8,128)(2,1)} %value.1, bf16[128,1152]{1,0:T(8,128)(2,1)} %out_grad.1, s32[1,128]{1,0:T(1,128)} %add_bitcast_fusion.tags, f32[32,1152]{1,0:T(8,128)} %gate.3, ...), custom_call_target="tpu_custom_call" | custom-call | tf_op jit(solution)/shard_map/pack/pallas_call | solution.py:59
  13.1 0.0 all-gather.3.cloned.1.call-update
  13.1 32.7 %all_to_all.20.main = bf16[16,304,128]{2,1,0:T(8,128)(2,1)S(1)} all-to-all(bf16[16,304,128]{2,1,0:T(8,128)(2,1)} %get-tuple-element.13), channel_id=1, replica_groups=mesh['g'=8,'r'=16] {'r'}, dimensions={0} | all-to-all | bytes 2490368 | tf_op jit(solution)/shard_map/all_to_all | solution.py:320
  45.8 5.7 %collective-permute-start = (bf16[4,304,128]{2,1,0:T(8,128)(2,1)S(1)}, bf16[4,304,128]{2,1,0:T(8,128)(2,1)S(1)}, u32[]{:S(2)}, u32[]{:S(2)}) collective-permute-start(bf16[4,304,128]{2,1,0:T(8,128)(2,1)S(1)} %get-tuple-element.24), channel_id=1, source_target_pairs={{0,16},{1,17},{2,18},{3,19},{4,20},{5,21},{6,22},{7,23},{8,24},{9,... | collective-permute-start | bytes 933896 | tf_op jit(solution)/shard_map/ppermute | solution.py:313
  51.5 1.3 collective-permute-start.1
  52.8 0.1 pad.6.clone
  52.8 18.2 %collective-permute-done.left = bf16[4,304,128]{2,1,0:T(8,128)(2,1)S(1)} collective-permute-done((bf16[4,304,128]{2,1,0:T(8,128)(2,1)S(1)}, bf16[4,304,128]{2,1,0:T(8,128)(2,1)S(1)}, u32[]{:S(2)}, u32[]{:S(2)}) %collective-permute-start) | collective-permute-done | bytes 311328 | tf_op jit(solution)/shard_map/ppermute | solution.py:313
  71.0 0.0 collective-permute-done.1.right
  71.0 0.0 copy-done
  71.0 0.7 copy-done.4
  71.7 0.7 copy-done.5
  72.5 16.6 %forward.1 = (bf16[24,72,128]{2,1,0:T(8,128)(2,1)}, f32[24,8,128]{2,1,0:T(8,128)}) custom-call(bf16[4,304,128]{2,1,0:T(8,128)(2,1)} %copy-done.4, bf16[16,304,128]{2,1,0:T(8,128)(2,1)} %copy-done, bf16[4,304,128]{2,1,0:T(8,128)(2,1)} %copy-done.5), custom_call_target="tpu_custom_call" | custom-call | tf_op jit(solution)/shard_map/forward/pallas_call | solution.py:185
  89.1 0.9 fusion.2
  90.1 9.7 %collective-permute-start.2 = (bf16[4,72,128]{2,1,0:T(8,128)(2,1)S(1)}, bf16[4,72,128]{2,1,0:T(8,128)(2,1)S(1)}, u32[]{:S(2)}, u32[]{:S(2)}) collective-permute-start(bf16[4,72,128]{2,1,0:T(8,128)(2,1)S(1)} %get-tuple-element.25), channel_id=1, source_target_pairs={{0,16},{1,17},{2,18},{3,19},{4,20},{5,21},{6,22},{7,23},{8,24},{9,... | collective-permute-start | bytes 221192 | tf_op jit(solution)/shard_map/ppermute | solution.py:313
  99.8 1.3 collective-permute-start.3
  101.1 0.0 copy-start.3
  101.1 17.6 %backward.1 = bf16[24,216,128]{2,1,0:T(8,128)(2,1)} custom-call(bf16[4,304,128]{2,1,0:T(8,128)(2,1)} %copy-done.4, bf16[16,304,128]{2,1,0:T(8,128)(2,1)} %copy-done, bf16[4,304,128]{2,1,0:T(8,128)(2,1)} %copy-done.5, bf16[24,72,128]{2,1,0:T(8,128)(2,1)} %get-tuple-element.14.mixed, f32[24,8,128]{2,1,0:T(8,128)} %get-tuple-element.15.stat), custom_call_target="tpu_custom_call" | custom-call | tf_op jit(solution)/shard_map/backward/pallas_call | solution.py:265
  118.7 1.1 fusion
  119.8 9.6 %collective-permute-start.4 = (bf16[4,216,128]{2,1,0:T(8,128)(2,1)S(1)}, bf16[4,216,128]{2,1,0:T(8,128)(2,1)S(1)}, u32[]{:S(2)}, u32[]{:S(2)}) collective-permute-start(bf16[4,216,128]{2,1,0:T(8,128)(2,1)S(1)} %get-tuple-element.21), channel_id=1, source_target_pairs={{0,16},{1,17},{2,18},{3,19},{4,20},{5,21},{6,22},{7,23},{8,24},{9,... | collective-permute-start | bytes 663560 | tf_op jit(solution)/shard_map/ppermute | solution.py:313
  129.4 1.3 collective-permute-start.5
  130.7 0.0 collective-permute-done.2
  130.7 0.0 collective-permute-done.3
  130.7 0.0 copy-done.3
  130.7 0.1 maximum_add_fusion
  130.8 0.0 all-gather.3.cloned.1.call-done
  130.8 3.3 %convolution_bitcast_fusion = f32[72,1152]{1,0:T(8,128)S(1)} fusion(bf16[16,72,128]{2,1,0:T(8,128)(2,1)S(1)} %maximum_add_fusion, bf16[16,128,1152]{2,1,0:T(8,128)(2,1)} %bitcast.19), kind=kOutput, calls=%fused_computation | convolution fusion | flops 339738624 | bytes 5345280 | tf_op jit(solution)/shard_map/bct,btd->cd/dot_general | solution.py:339
  134.1 0.4 reshape.27
  134.5 1.0 copy.21
  135.5 16.0 %all-to-all-start.2 = ((f32[8,72,144]{2,1,0:T(8,128)}), f32[8,72,144]{2,1,0:T(8,128)S(1)}, u32[]{:S(2)}, u32[]{:S(2)}) async-start(f32[8,72,144]{2,1,0:T(8,128)} %bitcast.18), calls=%async_computation.2 | async-start | bytes 1179648 | tf_op jit(solution)/shard_map/all_to_all | solution.py:342
  151.5 0.0 collective-permute-done.4
  151.5 0.0 collective-permute-done.5
  151.5 0.2 slice_add_fusion
  151.7 1.1 pad_maximum_fusion
  152.8 7.7 %all-to-all-done.2 = f32[8,72,144]{2,1,0:T(8,128)S(1)} async-done(((f32[8,72,144]{2,1,0:T(8,128)}), f32[8,72,144]{2,1,0:T(8,128)S(1)}, u32[]{:S(2)}, u32[]{:S(2)}) %all-to-all-start.2) | async-done | bytes 331808 | tf_op jit(solution)/shard_map/all_to_all | solution.py:342
  160.5 7.1 %all-to-all-start.1 = ((bf16[16,288,128]{2,1,0:T(8,128)(2,1)}), bf16[16,288,128]{2,1,0:T(8,128)(2,1)S(1)}, u32[]{:S(2)}, u32[]{:S(2)}) async-start(bf16[16,288,128]{2,1,0:T(8,128)(2,1)} %pad_maximum_fusion), calls=%async_computation.1 | async-start | bytes 2359296 | tf_op jit(solution)/shard_map/all_to_all | solution.py:336
  167.7 0.1 copy.17
  167.8 0.8 reshape.32
  168.6 16.4 %all-to-all-done.1.packed = bf16[16,288,128]{2,1,0:T(8,128)(2,1)S(1)} async-done(((bf16[16,288,128]{2,1,0:T(8,128)(2,1)}), bf16[16,288,128]{2,1,0:T(8,128)(2,1)S(1)}, u32[]{:S(2)}, u32[]{:S(2)}) %all-to-all-start.1) | async-done | bytes 1179680 | tf_op jit(solution)/shard_map/all_to_all | solution.py:336
  185.0 4.0 %all-to-all-start.3 = ((f32[16,1,648]{2,1,0:T(1,128)}), f32[16,1,648]{2,1,0:T(1,128)S(1)}, u32[]{:S(2)}, u32[]{:S(2)}) async-start(f32[16,1,648]{2,1,0:T(1,128)} %reshape.32), calls=%async_computation.3 | async-start | bytes 98304 | tf_op jit(solution)/shard_map/all_to_all | solution.py:345
  189.0 0.6 reshape.26.bias
  189.6 4.2 %unpack.1 = (bf16[128,1152]{1,0:T(8,128)(2,1)}, bf16[128,1152]{1,0:T(8,128)(2,1)}, bf16[128,1152]{1,0:T(8,128)(2,1)}, bf16[128,1152]{1,0:T(8,128)(2,1)}) custom-call(bf16[16,288,128]{2,1,0:T(8,128)(2,1)} %copy-done.2, bf16[128,1152]{1,0:T(8,128)(2,1)} %residual.1, s32[1,128]{1,0:T(1,128)} %add_bitcast_fusion.tags, f32[32,1152]{1,0:T(8,128)} %gate.3, ...), custom_call_target="tpu_custom_call" | custom-call | tf_op jit(solution)/shard_map/unpack/pallas_call | solution.py:300
  193.8 1.0 all-to-all-done.3
  194.9 0.5 broadcast.4
  195.4 0.8 reduce
  196.1 0.1 reshape.33
  196.3 0.7 reshape.29
  (15 shorter events, 0.2 us)
Async XLA Ops:
  7.2 123.7 %all-gather.3.cloned.1.call-start = ((), (), s32[]{:S(2)}) async-start(), calls=%async_computation.4 | async-start | bytes 5013504 | tf_op jit(solution)/shard_map/all_gather | solution.py:319
  45.7 25.3 %copy-start = (bf16[16,304,128]{2,1,0:T(8,128)(2,1)}, bf16[16,304,128]{2,1,0:T(8,128)(2,1)S(1)}, u32[]{:S(2)}) copy-start(bf16[16,304,128]{2,1,0:T(8,128)(2,1)S(1)} %all_to_all.20.main) | copy-start | bytes 3735556
  45.8 25.2 %collective-permute-start = (bf16[4,304,128]{2,1,0:T(8,128)(2,1)S(1)}, bf16[4,304,128]{2,1,0:T(8,128)(2,1)S(1)}, u32[]{:S(2)}, u32[]{:S(2)}) collective-permute-start(bf16[4,304,128]{2,1,0:T(8,128)(2,1)S(1)} %get-tuple-element.24), channel_id=1, source_target_pairs={{0,16},{1,17},{2,18},{3,19},{4,20},{5,21},{6,22},{7,23},{8,24},{9,... | collective-permute-start | bytes 933896 | tf_op jit(solution)/shard_map/ppermute | solution.py:313
  51.5 19.6 %collective-permute-start.1 = (bf16[4,304,128]{2,1,0:T(8,128)(2,1)S(1)}, bf16[4,304,128]{2,1,0:T(8,128)(2,1)S(1)}, u32[]{:S(2)}, u32[]{:S(2)}) collective-permute-start(bf16[4,304,128]{2,1,0:T(8,128)(2,1)S(1)} %get-tuple-element.23), channel_id=1, source_target_pairs={{16,0},{17,1},{18,2},{19,3},{20,4},{21,5},{22,6},{23,7},{24,8},{25... | collective-permute-start | bytes 933896 | tf_op jit(solution)/shard_map/ppermute | solution.py:313
  71.0 0.7 copy-start.4
  71.7 0.7 copy-start.5
  90.1 40.6 %collective-permute-start.2 = (bf16[4,72,128]{2,1,0:T(8,128)(2,1)S(1)}, bf16[4,72,128]{2,1,0:T(8,128)(2,1)S(1)}, u32[]{:S(2)}, u32[]{:S(2)}) collective-permute-start(bf16[4,72,128]{2,1,0:T(8,128)(2,1)S(1)} %get-tuple-element.25), channel_id=1, source_target_pairs={{0,16},{1,17},{2,18},{3,19},{4,20},{5,21},{6,22},{7,23},{8,24},{9,... | collective-permute-start | bytes 221192 | tf_op jit(solution)/shard_map/ppermute | solution.py:313
  99.8 30.9 %collective-permute-start.3 = (bf16[4,72,128]{2,1,0:T(8,128)(2,1)S(1)}, bf16[4,72,128]{2,1,0:T(8,128)(2,1)S(1)}, u32[]{:S(2)}, u32[]{:S(2)}) collective-permute-start(bf16[4,72,128]{2,1,0:T(8,128)(2,1)S(1)} %get-tuple-element.26), channel_id=1, source_target_pairs={{16,0},{17,1},{18,2},{19,3},{20,4},{21,5},{22,6},{23,7},{24,8},{25... | collective-permute-start | bytes 221192 | tf_op jit(solution)/shard_map/ppermute | solution.py:313
  101.1 29.6 %copy-start.3 = (bf16[24,72,128]{2,1,0:T(8,128)(2,1)S(1)}, bf16[24,72,128]{2,1,0:T(8,128)(2,1)}, u32[]{:S(2)}) copy-start(bf16[24,72,128]{2,1,0:T(8,128)(2,1)} %get-tuple-element.14.mixed) | copy-start | bytes 1327108
  119.8 31.7 %collective-permute-start.4 = (bf16[4,216,128]{2,1,0:T(8,128)(2,1)S(1)}, bf16[4,216,128]{2,1,0:T(8,128)(2,1)S(1)}, u32[]{:S(2)}, u32[]{:S(2)}) collective-permute-start(bf16[4,216,128]{2,1,0:T(8,128)(2,1)S(1)} %get-tuple-element.21), channel_id=1, source_target_pairs={{0,16},{1,17},{2,18},{3,19},{4,20},{5,21},{6,22},{7,23},{8,24},{9,... | collective-permute-start | bytes 663560 | tf_op jit(solution)/shard_map/ppermute | solution.py:313
  129.4 22.1 %collective-permute-start.5 = (bf16[4,216,128]{2,1,0:T(8,128)(2,1)S(1)}, bf16[4,216,128]{2,1,0:T(8,128)(2,1)S(1)}, u32[]{:S(2)}, u32[]{:S(2)}) collective-permute-start(bf16[4,216,128]{2,1,0:T(8,128)(2,1)S(1)} %get-tuple-element.22), channel_id=1, source_target_pairs={{16,0},{17,1},{18,2},{19,3},{20,4},{21,5},{22,6},{23,7},{24,8},{25... | collective-permute-start | bytes 663560 | tf_op jit(solution)/shard_map/ppermute | solution.py:313
  134.5 17.0 %copy-start.1 = (bf16[24,216,128]{2,1,0:T(8,128)(2,1)S(1)}, bf16[24,216,128]{2,1,0:T(8,128)(2,1)}, u32[]{:S(2)}) copy-start(bf16[24,216,128]{2,1,0:T(8,128)(2,1)} %backward.1) | copy-start | bytes 3981316
  135.5 25.0 %all-to-all-start.2 = ((f32[8,72,144]{2,1,0:T(8,128)}), f32[8,72,144]{2,1,0:T(8,128)S(1)}, u32[]{:S(2)}, u32[]{:S(2)}) async-start(f32[8,72,144]{2,1,0:T(8,128)} %bitcast.18), calls=%async_computation.2 | async-start | bytes 1179648 | tf_op jit(solution)/shard_map/all_to_all | solution.py:342
  160.5 24.5 %all-to-all-start.1 = ((bf16[16,288,128]{2,1,0:T(8,128)(2,1)}), bf16[16,288,128]{2,1,0:T(8,128)(2,1)S(1)}, u32[]{:S(2)}, u32[]{:S(2)}) async-start(bf16[16,288,128]{2,1,0:T(8,128)(2,1)} %pad_maximum_fusion), calls=%async_computation.1 | async-start | bytes 2359296 | tf_op jit(solution)/shard_map/all_to_all | solution.py:336
  167.6 21.4 %copy-start.6 = (f32[1152]{0:T(1024)S(1)}, f32[1152]{0:T(1024)}, u32[]{:S(2)}) copy-start(f32[1152]{0:T(1024)} %param.16) | copy-start | bytes 13828
  185.0 4.6 %copy-start.2 = (bf16[16,288,128]{2,1,0:T(8,128)(2,1)}, bf16[16,288,128]{2,1,0:T(8,128)(2,1)S(1)}, u32[]{:S(2)}) copy-start(bf16[16,288,128]{2,1,0:T(8,128)(2,1)S(1)} %all-to-all-done.1.packed) | copy-start | bytes 3538948
  185.0 9.9 %all-to-all-start.3 = ((f32[16,1,648]{2,1,0:T(1,128)}), f32[16,1,648]{2,1,0:T(1,128)S(1)}, u32[]{:S(2)}, u32[]{:S(2)}) async-start(f32[16,1,648]{2,1,0:T(1,128)} %reshape.32), calls=%async_computation.3 | async-start | bytes 98304 | tf_op jit(solution)/shard_map/all_to_all | solution.py:345
Sparse Core Ops, SparseCore 0:
  13.2 61.5 all-gather.2

commit v2 on v1

v2 whole, which is shorter than its diff:
```python
import math

import jax
import jax.numpy as jnp
from jax import lax
from jax.experimental import pallas as pl
from jax.experimental.pallas import tpu as pltpu
from jax.sharding import Mesh, PartitionSpec as P

HEADS = 16
HEAD_DIM = 72
WIDTH = HEADS * HEAD_DIM
TOK = 128
GROUPS = 8
EDGE = 7
SPAN = HEADS + 2 * EDGE
TILE = 256
TILES = HEADS * TOK // TILE
PART = TILE // TOK
STEP = 4
ROOM = SPAN + STEP - 1
CHUNKS = 5
SHARED = 2 * HEAD_DIM + 16
CHUNK = SHARED + 2 * HEAD_DIM
GRADS = 4 * HEAD_DIM
SHARE = WIDTH // GROUPS
FINAL = SHARE // HEADS
CLIPS = 32
SCALE = 1.0 / math.sqrt(HEAD_DIM)
SCALE2 = SCALE / math.log(2.0)
FAR = -1e30
BF = jnp.bfloat16
F32 = jnp.float32
VMEM_BYTES = 56 * 1024 * 1024

WHOLE = pl.BlockSpec(memory_space=pltpu.VMEM)


def params():
    return pltpu.CompilerParams(vmem_limit_bytes=VMEM_BYTES)


def mm(left, right):
    return jnp.dot(left, right, preferred_element_type=F32)


def pack_body(query, key, value, out_grad, tags, gate, weight, bg_ref, chunk_ref):
    clip = tags[...]
    onehot = (lax.broadcasted_iota(jnp.int32, (CLIPS, TOK), 0) + 1 == clip).astype(F32)
    gate_rows = lax.dot_general(
        onehot, gate[...], (((0,), (0,)), ((), ())), precision=lax.Precision.HIGHEST, preferred_element_type=F32
    )
    branch = (out_grad[...].astype(F32) * gate_rows).astype(BF)
    bg_ref[...] = branch
    grad_t = lax.dot_general(weight[...], branch, (((1,), (1,)), ((), ())), preferred_element_type=F32)
    query_t = query[...].astype(F32).T
    key_t = key[...].astype(F32).T
    value_t = value[...].astype(F32).T
    tag_rows = jnp.broadcast_to(clip.astype(F32), (16, TOK))
    for head in range(HEADS):
        rows = slice(head * HEAD_DIM, (head + 1) * HEAD_DIM)
        whole = jnp.concatenate([key_t[rows], value_t[rows], tag_rows, query_t[rows], grad_t[rows]], 0)
        chunk_ref[head] = whole.astype(BF)


def pack(query, key, value, out_grad, tags, gate, weight):
    return pl.pallas_call(
        pack_body,
        out_shape=(jax.ShapeDtypeStruct((TOK, WIDTH), BF), jax.ShapeDtypeStruct((HEADS, CHUNK, TOK), BF)),
        in_specs=[WHOLE] * 7,
        out_specs=(WHOLE, WHOLE),
        compiler_params=params(),
        name="pack",
    )(query, key, value, out_grad, tags, gate, weight)


def filled(piece, extra):
    rows = [piece] + extra
    have = sum(part.shape[0] for part in rows)
    if have < TOK:
        rows.append(jnp.zeros((TOK - have, TOK), F32))
    return jnp.concatenate(rows, 0)


def lay_out_keys(block, left, main, right, key_n, key_t, value_n, value_t):
    if block < EDGE:
        whole = left[block]
    elif block < EDGE + HEADS:
        whole = main[block - EDGE, 0:SHARED]
    else:
        whole = right[block - EDGE - HEADS]
    whole = whole.astype(F32)
    clip = whole[2 * HEAD_DIM : 2 * HEAD_DIM + 1]
    ids = lax.broadcasted_iota(jnp.int32, (CLIPS, TOK), 0).astype(F32) + 1.0
    rows = slice(block * TOK, (block + 1) * TOK)
    held = filled(whole[0:HEAD_DIM], [jnp.where(ids == clip, 0.0, FAR)])
    key_n[rows, :] = held.T.astype(BF)
    key_t[block] = held[0:80].astype(BF)
    held = filled(whole[HEAD_DIM : 2 * HEAD_DIM], [jnp.ones((8, TOK), F32)])
    value_n[rows, :] = held.T.astype(BF)
    value_t[block] = held[0:80].astype(BF)
    return clip


def lay_out_queries(block, main, clip, query_t, query_n, grad_t, grad_n):
    whole = main[block, SHARED:].astype(F32)
    ids = lax.broadcasted_iota(jnp.int32, (CLIPS, TOK), 0).astype(F32) + 1.0
    tile, cols = block // PART, slice((block % PART) * TOK, (block % PART + 1) * TOK)
    held = filled(whole[0:HEAD_DIM], [jnp.where(ids == clip, 1.0, 0.0)])
    query_t[tile, :, cols] = held.astype(BF)
    query_n[tile, cols, :] = held.T.astype(BF)
    held = filled(whole[HEAD_DIM:], [])
    grad_t[tile, :, cols] = held.astype(BF)
    grad_n[tile, cols, :] = held.T.astype(BF)


def key_ranges(clips, first_ref, count_ref):
    clips = [jnp.where(row == 0.0, 100.0, row) if at >= EDGE + HEADS else row for at, row in enumerate(clips)]
    clips = jnp.concatenate(clips + [jnp.full((32 - SPAN, TOK), 100.0, F32)], 0)
    least = jnp.min(clips, axis=1, keepdims=True)
    most = jnp.max(clips, axis=1, keepdims=True)
    for tile in range(TILES):
        start = EDGE + tile * PART
        low, high = least[start : start + 1], most[start + PART - 1 : start + PART]
        first = jnp.sum(jnp.where(most < low, 1.0, 0.0)).astype(jnp.int32)
        end = jnp.sum(jnp.where(least <= high, 1.0, 0.0)).astype(jnp.int32)
        first_ref[tile] = first
        count_ref[tile] = (end - first + STEP - 1) // STEP


def attend_body(
    left, main, right, own_ref, back_ref, ahead_ref,
    key_n, key_t, value_n, value_t, query_t, query_n, grad_t, grad_n, held, dk, dv, first_ref, count_ref,
):
    clips = [lay_out_keys(block, left, main, right, key_n, key_t, value_n, value_t) for block in range(SPAN)]
    for block in range(HEADS):
        lay_out_queries(block, main, clips[EDGE + block], query_t, query_n, grad_t, grad_n)
    rows = slice(SPAN * TOK, ROOM * TOK)
    lane = lax.broadcasted_iota(jnp.int32, ((ROOM - SPAN) * TOK, TOK), 1)
    key_n[rows, :] = jnp.where((lane >= HEAD_DIM) & (lane < HEAD_DIM + CLIPS), FAR, 0.0).astype(BF)
    value_n[rows, :] = jnp.zeros(((ROOM - SPAN) * TOK, TOK), BF)
    for block in range(SPAN, ROOM):
        key_t[block] = jnp.zeros((80, TOK), BF)
        value_t[block] = jnp.zeros((80, TOK), BF)
    key_ranges(clips, first_ref, count_ref)
    dk[...] = jnp.zeros_like(dk)
    dv[...] = jnp.zeros_like(dv)

    def side_by_side(ref, start):
        return jnp.concatenate([ref[start + at] for at in range(STEP)], 1)

    def query_step(tile, carry):
        first, count = first_ref[tile], count_ref[tile]

        def blocks(step):
            start = first + step * STEP
            return start, pl.ds(pl.multiple_of(start * TOK, TOK), STEP * TOK)

        def score_step(step, top):
            scores = mm(key_n[blocks(step)[1], :], query_t[tile])
            held[step] = scores
            return jnp.maximum(top, jnp.max(scores, axis=0, keepdims=True))

        top = lax.fori_loop(0, count, score_step, jnp.full((1, TILE), 2.0 * FAR, F32))

        def value_step(step, total):
            weights = jnp.exp2((held[step] - top) * SCALE2)
            held[step] = weights
            return total + mm(side_by_side(value_t, blocks(step)[0]), weights.astype(BF))

        total = lax.fori_loop(0, count, value_step, jnp.zeros((80, TILE), F32))
        inverse = 1.0 / total[HEAD_DIM : HEAD_DIM + 1]
        mixed = (total[0:HEAD_DIM] * inverse).astype(BF)
        grad = grad_t[tile]
        delta = jnp.sum(mixed.astype(F32) * grad[0:HEAD_DIM].astype(F32), axis=0, keepdims=True)

        def grad_step(step, total):
            start, rows = blocks(step)
            prob = held[step] * inverse
            pull = mm(value_n[rows, :], grad)
            dv[rows, :] += mm(prob.astype(BF), grad_n[tile])
            score_grad = (prob * (pull - delta)).astype(BF)
            dk[rows, :] += mm(score_grad, query_n[tile])
            return total + mm(side_by_side(key_t, start), score_grad)

        total = lax.fori_loop(0, count, grad_step, jnp.zeros((80, TILE), F32))
        pair = jnp.concatenate([mixed.astype(F32), total[0:HEAD_DIM] * SCALE], 0).astype(BF)
        for part in range(PART):
            own_ref[tile * PART + part, 0 : 2 * HEAD_DIM] = pair[:, part * TOK : (part + 1) * TOK]
        return carry

    lax.fori_loop(0, TILES, query_step, 0)
    for block in range(SPAN):
        rows = slice(block * TOK, (block + 1) * TOK)
        pair = jnp.concatenate([dk[rows, :].T[0:HEAD_DIM] * SCALE, dv[rows, :].T[0:HEAD_DIM]], 0).astype(BF)
        if block < EDGE:
            back_ref[block] = pair
        elif block < EDGE + HEADS:
            own_ref[block - EDGE, 2 * HEAD_DIM :] = pair
        else:
            ahead_ref[block - EDGE - HEADS] = pair


def attend(left, main, right):
    halo = jax.ShapeDtypeStruct((EDGE, 2 * HEAD_DIM, TOK), BF)
    row_form = pltpu.VMEM((ROOM * TOK, TOK), BF)
    column_form = pltpu.VMEM((ROOM, 80, TOK), BF)
    return pl.pallas_call(
        attend_body,
        out_shape=(jax.ShapeDtypeStruct((HEADS, GRADS, TOK), BF), halo, halo),
        in_specs=[WHOLE] * 3,
        out_specs=(WHOLE,) * 3,
        scratch_shapes=[
            row_form, column_form, row_form, column_form,
            pltpu.VMEM((TILES, TOK, TILE), BF), pltpu.VMEM((TILES, TILE, TOK), BF),
            pltpu.VMEM((TILES, TOK, TILE), BF), pltpu.VMEM((TILES, TILE, TOK), BF),
            pltpu.VMEM((CHUNKS, STEP * TOK, TILE), F32),
            pltpu.VMEM((ROOM * TOK, TOK), F32),
            pltpu.VMEM((ROOM * TOK, TOK), F32),
            pltpu.SMEM((TILES,), jnp.int32),
            pltpu.SMEM((TILES,), jnp.int32),
        ],
        compiler_params=params(),
        name="attend",
    )(left, main, right)


def weight_term_body(own, branch, out_ref, total):
    step = pl.program_id(0)
    mixed = jnp.concatenate([own[part, 0:80] for part in range(PART)], 1)

    @pl.when(step == 0)
    def _():
        total[...] = jnp.zeros_like(total)

    total[...] += mm(mixed, branch[...].reshape(TILE, WIDTH))

    @pl.when(step == TILES - 1)
    def _():
        whole = jnp.concatenate([total[0:HEAD_DIM], jnp.zeros((TOK - HEAD_DIM, WIDTH), F32)], 0)
        out_ref[...] = whole.T.astype(BF).reshape(GROUPS, SHARE, TOK)


def weight_term(own, branch):
    return pl.pallas_call(
        weight_term_body,
        grid=(TILES,),
        out_shape=jax.ShapeDtypeStruct((GROUPS, SHARE, TOK), BF),
        in_specs=[
            pl.BlockSpec((PART, GRADS, TOK), lambda i: (i, 0, 0)),
            pl.BlockSpec((PART, TOK, WIDTH), lambda i: (i, 0, 0)),
        ],
        out_specs=pl.BlockSpec((GROUPS, SHARE, TOK), lambda i: (0, 0, 0)),
        scratch_shapes=[pltpu.VMEM((80, WIDTH), F32)],
        compiler_params=params(),
        name="weight_term",
    )(own, branch)


def join_body(own, from_left, from_right, terms, out_ref, total):
    total[0:SHARE] = sum(terms[group].astype(F32) for group in range(GROUPS))
    total[SHARE:] = jnp.zeros((8, TOK), F32)
    for block in range(HEADS):
        whole = own[block].astype(F32)
        if block < EDGE or block >= HEADS - EDGE:
            other = from_left[block] if block < EDGE else from_right[block - HEADS + EDGE]
            pair = whole[2 * HEAD_DIM :] + other.astype(F32)
            whole = jnp.concatenate([whole[0 : 2 * HEAD_DIM], pair], 0)
        tail = total[block * FINAL : block * FINAL + 16, :]
        out_ref[block] = jnp.concatenate([whole, tail], 0).astype(BF)


def join(own, from_left, from_right, terms):
    return pl.pallas_call(
        join_body,
        out_shape=jax.ShapeDtypeStruct((HEADS, GRADS + 16, TOK), BF),
        in_specs=[WHOLE] * 4,
        out_specs=WHOLE,
        scratch_shapes=[pltpu.VMEM((SHARE + 8, TOK), F32)],
        compiler_params=params(),
        name="join",
    )(own, from_left, from_right, terms)


def unpack_body(packed, residual, tags, gate, weight, bias, out_ref, dq_ref, dk_ref, dv_ref, dw_ref):
    clip = tags[...]
    onehot = (lax.broadcasted_iota(jnp.int32, (CLIPS, TOK), 0) + 1 == clip).astype(F32)
    gate_rows = lax.dot_general(
        onehot, gate[...], (((0,), (0,)), ((), ())), precision=lax.Precision.HIGHEST, preferred_element_type=F32
    )
    whole = [packed[head].astype(F32) for head in range(HEADS)]
    mixed = jnp.concatenate([part[0:72] for part in whole], 0).T.astype(BF)
    projected = mm(mixed, weight[...]) + bias[...]
    out_ref[...] = (residual[...].astype(F32) + gate_rows * projected).astype(BF)
    for ref, start in ((dq_ref, 72), (dk_ref, 144), (dv_ref, 216)):
        ref[...] = jnp.concatenate([part[start : start + 72] for part in whole], 0).T.astype(BF)
    dw_ref[...] = jnp.concatenate([part[GRADS:].T[0:72] for part in whole], 0)[:, 0:FINAL]


def unpack(packed, residual, tags, gate, weight, bias):
    shape = jax.ShapeDtypeStruct((TOK, WIDTH), BF)
    return pl.pallas_call(
        unpack_body,
        out_shape=(shape,) * 4 + (jax.ShapeDtypeStruct((WIDTH, FINAL), F32),),
        in_specs=[WHOLE] * 6,
        out_specs=(WHOLE,) * 5,
        compiler_params=params(),
        name="unpack",
    )(packed, residual, tags, gate, weight, bias)


def from_neighbour(values, by):
    total = GROUPS * HEADS
    pairs = [(i, i + by * HEADS) for i in range(total) if 0 <= i + by * HEADS < total]
    return lax.ppermute(values, ("g", "r"), pairs)


def shards(query, key, value, residual, token_clip, gate, weight, bias, out_grad):
    tags = (token_clip + 1).reshape(1, TOK)
    branch, chunk = pack(query, key, value, out_grad, tags, gate, weight)
    main = lax.all_to_all(chunk, "r", 0, 0, tiled=True)
    left = from_neighbour(main[HEADS - EDGE :, 0:SHARED], 1)
    right = from_neighbour(main[:EDGE, 0:SHARED], -1)
    left, right, branch = lax.optimization_barrier((left, right, branch))
    gathered = lax.all_gather(branch, "r", axis=0, tiled=False)
    own, back, ahead = attend(left, main, right)
    from_left = from_neighbour(ahead, 1)
    from_right = from_neighbour(back, -1)
    terms = lax.all_to_all(weight_term(own, gathered), "g", 0, 0, tiled=True)
    packed = lax.all_to_all(join(own, from_left, from_right, terms), "r", 0, 0, tiled=True)
    return unpack(packed, residual, tags, gate, weight, bias.reshape(1, WIDTH))


def solution(mesh):
    split = Mesh(mesh.devices.reshape(GROUPS, HEADS), ("g", "r"))
    both = ("g", "r")
    in_specs = (
        P(both, None), P(both, None), P(both, None), P(both, None), P(both), P(), P(), P(), P(both, None),
    )
    out_specs = (P(both, None),) * 4 + (P(None, both),)
    return jax.shard_map(shards, mesh=split, in_specs=in_specs, out_specs=out_specs, check_vma=False)
```

time: 202 us -> 168 us (0.83)
  starting transfers between devices: 55.9 us -> 26.2 us
  waiting for transfers between devices: 43.4 us -> 55.6 us
  blocking collectives: 32.7 us -> 25.1 us
  matrix products: 3.29 us -> 0 us
  local copies, waits for them, and re-layouts: 7.85 us -> 5.12 us
  Pallas kernels: 43.1 us -> 40.7 us
  other arithmetic: 3.4 us -> 1.23 us
    all_gather x1, waiting for transfers between devices: 0.02 us -> 19.8 us  [shards(): gathered = lax.all_gather(branch, 'r', axis=0, tiled=False)]
    ppermute x6 -> x4, starting transfers between devices: 28.8 us -> 13.4 us  [from_neighbour(): return lax.ppermute(values, ('g', 'r'), pairs)]
    all_to_all x3 -> x2, starting transfers between devices: 27.1 us -> 12.7 us  [the longest x1 6.61 us: shards(): terms = lax.all_to_all(weight_term(own, gathered), 'g', 0, 0, tiled=True)]
    ppermute x6 -> x4, waiting for transfers between devices: 18.2 us -> 10.5 us  [from_neighbour(): return lax.ppermute(values, ('g', 'r'), pairs)]
    all_to_all x1, blocking collectives: 32.7 us -> 25.1 us  [shards(): main = lax.all_to_all(chunk, 'r', 0, 0, tiled=True)]
    dot_general x1 -> x0, matrix products: 3.29 us -> none  [shards(): jnp.einsum('bct,btd->cd', mixed, gathered, preferred_element_type=F32)]
    pallas_call x3 -> x4, Pallas kernels: 38.5 us -> 36.1 us  [the longest x1 22.1 us: attend(): pl.pallas_call(attend_body, out_shape=(jax.ShapeDtypeStruct((HEADS, GRADS...]
    reshape x5 -> x1, local copies, waits for them, and re-layouts: 2.73 us -> 0.6 us  [shards(): return unpack(packed, residual, tags, gate, weight, bias.reshape(1, WIDTH))]
  transfers between devices with their start and end apart: 10 -> 7, of which waited for: 4 -> 4; matrix products, arithmetic and copies ran while one was open for 5% -> 0% of each run, Pallas kernels for 19% -> 17%
where the time goes in v2:
time: 168 us
  waiting for transfers between devices  55.6 us (33%)
  Pallas kernels  40.7 us (24%)
  starting transfers between devices  26.2 us (16%)
  blocking collectives  25.1 us (15%)
  between operations  14.1 us (8%)
  local copies, waits for them, and re-layouts  5.12 us (3%)
    all_to_all x1, blocking collectives, shards(): main = lax.all_to_all(chunk, 'r', 0, 0, tiled=True)  25.1 us
    pallas_call x1, Pallas kernels, attend(): pl.pallas_call(attend_body, out_shape=(jax.ShapeDtypeStruct((HEADS, GRADS...  22.1 us
    all_gather x1, waiting for transfers between devices, shards(): gathered = lax.all_gather(branch, 'r', axis=0, tiled=False)  19.8 us
    all_to_all x1, waiting for transfers between devices, shards(): lax.all_to_all(join(own, from_left, from_right, terms), 'r', 0, 0, tiled=...  17.4 us
    ppermute x4, starting transfers between devices, from_neighbour(): return lax.ppermute(values, ('g', 'r'), pairs)  13.4 us
    ppermute x4, waiting for transfers between devices, from_neighbour(): return lax.ppermute(values, ('g', 'r'), pairs)  10.5 us
    all_to_all x1, waiting for transfers between devices, shards(): terms = lax.all_to_all(weight_term(own, gathered), 'g', 0, 0, tiled=True)  7.95 us
    pallas_call x1, Pallas kernels, weight_term(): pl.pallas_call(weight_term_body, grid=(TILES,), out_shape=jax.ShapeDtypeS...  6.76 us
  transfers between devices with their start and end apart: 7, of which 4 were waited for; matrix products, arithmetic and copies ran while one was open for 0% of the time, Pallas kernels for 17%

profile of v2, /device:TPU:1, one launch (start us, length us, event | category | flops | bytes accessed | tf_op | source)
XLA Modules:
  0.0 168.0 jit_solution(16536032835696379967)
XLA Ops:
  7.2 0.0 all-gather.3.cloned.1.call-start
  7.2 1.2 add_bitcast_fusion.tags
  8.4 4.6 %pack.1 = (bf16[128,1152]{1,0:T(8,128)(2,1)}, bf16[16,304,128]{2,1,0:T(8,128)(2,1)}) custom-call(bf16[128,1152]{1,0:T(8,128)(2,1)} %query.1, bf16[128,1152]{1,0:T(8,128)(2,1)} %key.1, bf16[128,1152]{1,0:T(8,128)(2,1)} %value.1, bf16[128,1152]{1,0:T(8,128)(2,1)} %out_grad.1, s32[1,128]{1,0:T(1,128)} %add_bitcast_fusion.tags, f32[32,1152]{1,0:T(8,128)} %gate.3, ...), custom_call_target="tpu_custom_call" | custom-call | tf_op jit(solution)/shard_map/pack/pallas_call | solution.py:67
  13.1 25.1 %all_to_all.15.main = bf16[16,304,128]{2,1,0:T(8,128)(2,1)S(1)} all-to-all(bf16[16,304,128]{2,1,0:T(8,128)(2,1)} %get-tuple-element.13), channel_id=1, replica_groups=mesh['g'=8,'r'=16] {'r'}, dimensions={0} | all-to-all | bytes 2490368 | tf_op jit(solution)/shard_map/all_to_all | solution.py:321
  38.1 0.0 copy-start
  38.2 5.2 %collective-permute-start = (bf16[7,160,128]{2,1,0:T(8,128)(2,1)S(1)}, bf16[7,160,128]{2,1,0:T(8,128)(2,1)S(1)}, u32[]{:S(2)}, u32[]{:S(2)}) collective-permute-start(bf16[7,160,128]{2,1,0:T(8,128)(2,1)S(1)} %get-tuple-element.27), channel_id=1, source_target_pairs={{0,16},{1,17},{2,18},{3,19},{4,20},{5,21},{6,22},{7,23},{8,24},{9,... | collective-permute-start | bytes 860168 | tf_op jit(solution)/shard_map/ppermute | solution.py:315
  43.4 1.3 collective-permute-start.1
  44.7 10.5 %collective-permute-done.left = bf16[7,160,128]{2,1,0:T(8,128)(2,1)S(1)} collective-permute-done((bf16[7,160,128]{2,1,0:T(8,128)(2,1)S(1)}, bf16[7,160,128]{2,1,0:T(8,128)(2,1)S(1)}, u32[]{:S(2)}, u32[]{:S(2)}) %collective-permute-start) | collective-permute-done | bytes 286752 | tf_op jit(solution)/shard_map/ppermute | solution.py:315
  55.2 0.0 copy-start.3
  55.2 0.0 collective-permute-done.1.right
  55.2 0.0 copy-start.4
  55.2 0.0 all-gather.3.cloned.1.call-update
  55.2 0.0 copy-done
  55.2 0.7 copy-done.3
  55.9 0.1 copy-done.4
  56.0 22.1 %attend.1 = (bf16[16,288,128]{2,1,0:T(8,128)(2,1)}, bf16[7,144,128]{2,1,0:T(8,128)(2,1)}, bf16[7,144,128]{2,1,0:T(8,128)(2,1)}) custom-call(bf16[7,160,128]{2,1,0:T(8,128)(2,1)} %copy-done.3, bf16[16,304,128]{2,1,0:T(8,128)(2,1)} %copy-done, bf16[7,160,128]{2,1,0:T(8,128)(2,1)} %copy-done.4), custom_call_target="tpu_custom_call" | custom-call | tf_op jit(solution)/shard_map/attend/pallas_call | solution.py:208
  78.1 5.6 %collective-permute-start.2 = (bf16[7,144,128]{2,1,0:T(8,128)(2,1)}, bf16[7,144,128]{2,1,0:T(8,128)(2,1)S(1)}, u32[]{:S(2)}, u32[]{:S(2)}) collective-permute-start(bf16[7,144,128]{2,1,0:T(8,128)(2,1)} %get-tuple-element.18), channel_id=1, source_target_pairs={{0,16},{1,17},{2,18},{3,19},{4,20},{5,21},{6,22},{7,23},{8,24},{9,... | collective-permute-start | bytes 774152 | tf_op jit(solution)/shard_map/ppermute | solution.py:315
  83.7 1.3 collective-permute-start.3
  85.0 19.8 %all-gather.3.cloned.1.call-done = bf16[2048,1152]{1,0:T(8,128)(2,1)} async-done(((bf16[128,1152]{1,0:T(8,128)(2,1)}), bf16[2048,1152]{1,0:T(8,128)(2,1)}) %all-gather.3.cloned.1.call-update) | async-done | bytes 4718608 | tf_op jit(solution)/shard_map/all_gather | solution.py:325
  104.9 6.8 %weight_term.1 = bf16[8,144,128]{2,1,0:T(8,128)(2,1)} custom-call(bf16[16,288,128]{2,1,0:T(8,128)(2,1)} %get-tuple-element.17.own, bf16[16,128,1152]{2,1,0:T(8,128)(2,1)} %bitcast.3), custom_call_target="tpu_custom_call" | custom-call | tf_op jit(solution)/shard_map/weight_term/pallas_call | solution.py:245
  111.6 6.6 %all-to-all-start.1 = ((bf16[8,144,128]{2,1,0:T(8,128)(2,1)}), bf16[8,144,128]{2,1,0:T(8,128)(2,1)S(1)}, u32[]{:S(2)}, u32[]{:S(2)}) async-start(bf16[8,144,128]{2,1,0:T(8,128)(2,1)} %weight_term.1), calls=%async_computation.1 | async-start | bytes 589824 | tf_op jit(solution)/shard_map/all_to_all | solution.py:329
  118.2 0.0 collective-permute-done.2.from_left
  118.2 0.0 copy-start.5
  118.2 0.0 collective-permute-done.3.from_right
  118.3 0.0 copy-start.6
  118.3 8.0 %all-to-all-done.1.terms = bf16[8,144,128]{2,1,0:T(8,128)(2,1)S(1)} async-done(((bf16[8,144,128]{2,1,0:T(8,128)(2,1)}), bf16[8,144,128]{2,1,0:T(8,128)(2,1)S(1)}, u32[]{:S(2)}, u32[]{:S(2)}) %all-to-all-start.1) | async-done | bytes 294944 | tf_op jit(solution)/shard_map/all_to_all | solution.py:329
  126.2 0.0 copy-done.5
  126.2 0.0 copy-done.6
  126.2 0.0 copy-start.2
  126.2 0.7 copy-done.2
  126.9 2.8 %join.1 = bf16[16,304,128]{2,1,0:T(8,128)(2,1)} custom-call(bf16[16,288,128]{2,1,0:T(8,128)(2,1)} %get-tuple-element.17.own, bf16[7,144,128]{2,1,0:T(8,128)(2,1)} %copy-done.5, bf16[7,144,128]{2,1,0:T(8,128)(2,1)} %copy-done.6, bf16[8,144,128]{2,1,0:T(8,128)(2,1)} %copy-done.2), custom_call_target="tpu_custom_call" | custom-call | tf_op jit(solution)/shard_map/join/pallas_call | solution.py:274
  129.7 0.0 copy-start.7
  129.7 6.1 %all-to-all-start.2 = ((bf16[16,304,128]{2,1,0:T(8,128)(2,1)}), bf16[16,304,128]{2,1,0:T(8,128)(2,1)S(1)}, u32[]{:S(2)}, u32[]{:S(2)}) async-start(bf16[16,304,128]{2,1,0:T(8,128)(2,1)} %join.1), calls=%async_computation.2 | async-start | bytes 2490368 | tf_op jit(solution)/shard_map/all_to_all | solution.py:330
  135.9 0.0 copy-done.7
  135.9 0.6 reshape.17.bias
  136.5 17.4 %all-to-all-done.2.packed = bf16[16,304,128]{2,1,0:T(8,128)(2,1)S(1)} async-done(((bf16[16,304,128]{2,1,0:T(8,128)(2,1)}), bf16[16,304,128]{2,1,0:T(8,128)(2,1)S(1)}, u32[]{:S(2)}, u32[]{:S(2)}) %all-to-all-start.2) | async-done | bytes 1245216 | tf_op jit(solution)/shard_map/all_to_all | solution.py:330
  153.8 0.0 copy-start.1
  153.8 1.1 copy-done.1
  154.9 4.4 %unpack.1 = (bf16[128,1152]{1,0:T(8,128)(2,1)}, bf16[128,1152]{1,0:T(8,128)(2,1)}, bf16[128,1152]{1,0:T(8,128)(2,1)}, bf16[128,1152]{1,0:T(8,128)(2,1)}, f32[1152,9]{1,0:T(8,128)}) custom-call(bf16[16,304,128]{2,1,0:T(8,128)(2,1)} %copy-done.1, bf16[128,1152]{1,0:T(8,128)(2,1)} %residual.1, s32[1,128]{1,0:T(1,128)} %add_bitcast_fusion.tags, ...), custom_call_target="tpu_custom_call" | custom-call | tf_op jit(solution)/shard_map/unpack/pallas_call | solution.py:302
  159.3 1.9 %copy.14 = f32[1152,9]{0,1:T(8,128)} copy(f32[1152,9]{1,0:T(8,128)} %get-tuple-element.25) | data formatting | bytes 82944 | tf_op jit(solution)/shard_map/unpack/pallas_call | solution.py:302
  (1 shorter events, 0.0 us)
Async XLA Ops:
  7.2 97.7 %all-gather.3.cloned.1.call-start = ((), (), s32[]{:S(2)}) async-start(), calls=%async_computation.3 | async-start | bytes 5013504 | tf_op jit(solution)/shard_map/all_gather | solution.py:325
  38.1 17.1 %copy-start = (bf16[16,304,128]{2,1,0:T(8,128)(2,1)}, bf16[16,304,128]{2,1,0:T(8,128)(2,1)S(1)}, u32[]{:S(2)}) copy-start(bf16[16,304,128]{2,1,0:T(8,128)(2,1)S(1)} %all_to_all.15.main) | copy-start | bytes 3735556
  38.2 17.0 %collective-permute-start = (bf16[7,160,128]{2,1,0:T(8,128)(2,1)S(1)}, bf16[7,160,128]{2,1,0:T(8,128)(2,1)S(1)}, u32[]{:S(2)}, u32[]{:S(2)}) collective-permute-start(bf16[7,160,128]{2,1,0:T(8,128)(2,1)S(1)} %get-tuple-element.27), channel_id=1, source_target_pairs={{0,16},{1,17},{2,18},{3,19},{4,20},{5,21},{6,22},{7,23},{8,24},{9,... | collective-permute-start | bytes 860168 | tf_op jit(solution)/shard_map/ppermute | solution.py:315
  43.4 11.8 %collective-permute-start.1 = (bf16[7,160,128]{2,1,0:T(8,128)(2,1)S(1)}, bf16[7,160,128]{2,1,0:T(8,128)(2,1)S(1)}, u32[]{:S(2)}, u32[]{:S(2)}) collective-permute-start(bf16[7,160,128]{2,1,0:T(8,128)(2,1)S(1)} %get-tuple-element.26), channel_id=1, source_target_pairs={{16,0},{17,1},{18,2},{19,3},{20,4},{21,5},{22,6},{23,7},{24,8},{25... | collective-permute-start | bytes 860168 | tf_op jit(solution)/shard_map/ppermute | solution.py:315
  55.2 0.7 copy-start.3
  55.2 0.8 copy-start.4
  78.1 40.1 %collective-permute-start.2 = (bf16[7,144,128]{2,1,0:T(8,128)(2,1)}, bf16[7,144,128]{2,1,0:T(8,128)(2,1)S(1)}, u32[]{:S(2)}, u32[]{:S(2)}) collective-permute-start(bf16[7,144,128]{2,1,0:T(8,128)(2,1)} %get-tuple-element.18), channel_id=1, source_target_pairs={{0,16},{1,17},{2,18},{3,19},{4,20},{5,21},{6,22},{7,23},{8,24},{9,... | collective-permute-start | bytes 774152 | tf_op jit(solution)/shard_map/ppermute | solution.py:315
  83.7 34.5 %collective-permute-start.3 = (bf16[7,144,128]{2,1,0:T(8,128)(2,1)}, bf16[7,144,128]{2,1,0:T(8,128)(2,1)S(1)}, u32[]{:S(2)}, u32[]{:S(2)}) collective-permute-start(bf16[7,144,128]{2,1,0:T(8,128)(2,1)} %get-tuple-element.19), channel_id=1, source_target_pairs={{16,0},{17,1},{18,2},{19,3},{20,4},{21,5},{22,6},{23,7},{24,8},{25... | collective-permute-start | bytes 774152 | tf_op jit(solution)/shard_map/ppermute | solution.py:315
  111.6 14.6 %all-to-all-start.1 = ((bf16[8,144,128]{2,1,0:T(8,128)(2,1)}), bf16[8,144,128]{2,1,0:T(8,128)(2,1)S(1)}, u32[]{:S(2)}, u32[]{:S(2)}) async-start(bf16[8,144,128]{2,1,0:T(8,128)(2,1)} %weight_term.1), calls=%async_computation.1 | async-start | bytes 589824 | tf_op jit(solution)/shard_map/all_to_all | solution.py:329
  118.2 8.0 %copy-start.5 = (bf16[7,144,128]{2,1,0:T(8,128)(2,1)}, bf16[7,144,128]{2,1,0:T(8,128)(2,1)S(1)}, u32[]{:S(2)}) copy-start(bf16[7,144,128]{2,1,0:T(8,128)(2,1)S(1)} %collective-permute-done.2.from_left) | copy-start | bytes 774148
  118.3 8.0 %copy-start.6 = (bf16[7,144,128]{2,1,0:T(8,128)(2,1)}, bf16[7,144,128]{2,1,0:T(8,128)(2,1)S(1)}, u32[]{:S(2)}) copy-start(bf16[7,144,128]{2,1,0:T(8,128)(2,1)S(1)} %collective-permute-done.3.from_right) | copy-start | bytes 774148
  126.2 0.7 copy-start.2
  129.7 6.1 %copy-start.7 = (f32[1152]{0:T(1024)S(1)}, f32[1152]{0:T(1024)}, u32[]{:S(2)}) copy-start(f32[1152]{0:T(1024)} %param.16) | copy-start | bytes 13828
  129.7 24.1 %all-to-all-start.2 = ((bf16[16,304,128]{2,1,0:T(8,128)(2,1)}), bf16[16,304,128]{2,1,0:T(8,128)(2,1)S(1)}, u32[]{:S(2)}, u32[]{:S(2)}) async-start(bf16[16,304,128]{2,1,0:T(8,128)(2,1)} %join.1), calls=%async_computation.2 | async-start | bytes 2490368 | tf_op jit(solution)/shard_map/all_to_all | solution.py:330
  153.8 1.1 copy-start.1
Sparse Core Ops, SparseCore 0:
  55.3 49.5 all-gather.2

commit v3 on v2

--- a/solution.py
+++ b/solution.py
@@ -21,8 +21,7 @@
 ROOM = SPAN + STEP - 1
 CHUNKS = 5
 SHARED = 2 * HEAD_DIM + 16
-CHUNK = SHARED + 2 * HEAD_DIM
-GRADS = 4 * HEAD_DIM
+PAIR = 2 * HEAD_DIM
 SHARE = WIDTH // GROUPS
 FINAL = SHARE // HEADS
 CLIPS = 32
@@ -40,38 +39,64 @@
     return pltpu.CompilerParams(vmem_limit_bytes=VMEM_BYTES)
 
 
+def cost(micros):
+    return pl.CostEstimate(flops=int(micros * 4e8), bytes_accessed=int(micros * 2e6), transcendentals=0)
+
+
 def mm(left, right):
     return jnp.dot(left, right, preferred_element_type=F32)
 
 
-def pack_body(query, key, value, out_grad, tags, gate, weight, bg_ref, chunk_ref):
-    clip = tags[...]
-    onehot = (lax.broadcasted_iota(jnp.int32, (CLIPS, TOK), 0) + 1 == clip).astype(F32)
+def clip_onehot(tags):
+    ids = lax.broadcasted_iota(jnp.int32, (CLIPS, TOK), 0)
+    return (ids == tags[...].reshape(1, TOK)).astype(F32)
+
+
+def pack_keys_body(key, value, tags, out_ref):
+    key_t = key[...].astype(F32).T
+    value_t = value[...].astype(F32).T
+    tag_rows = jnp.broadcast_to(tags[...].reshape(1, TOK).astype(F32) + 1.0, (16, TOK))
+    for head in range(HEADS):
+        rows = slice(head * HEAD_DIM, (head + 1) * HEAD_DIM)
+        out_ref[head] = jnp.concatenate([key_t[rows], value_t[rows], tag_rows], 0).astype(BF)
+
+
+def pack_keys(key, value, tags):
+    return pl.pallas_call(
+        pack_keys_body,
+        out_shape=jax.ShapeDtypeStruct((HEADS, SHARED, TOK), BF),
+        in_specs=[WHOLE] * 3,
+        out_specs=WHOLE,
+        compiler_params=params(),
+        cost_estimate=cost(2),
+        name="pack_keys",
+    )(key, value, tags)
+
+
+def pack_queries_body(query, out_grad, tags, gate, weight, bg_ref, out_ref):
     gate_rows = lax.dot_general(
-        onehot, gate[...], (((0,), (0,)), ((), ())), precision=lax.Precision.HIGHEST, preferred_element_type=F32
+        clip_onehot(tags), gate[...], (((0,), (0,)), ((), ())),
+        precision=lax.Precision.HIGHEST, preferred_element_type=F32,
     )
     branch = (out_grad[...].astype(F32) * gate_rows).astype(BF)
     bg_ref[...] = branch
     grad_t = lax.dot_general(weight[...], branch, (((1,), (1,)), ((), ())), preferred_element_type=F32)
     query_t = query[...].astype(F32).T
-    key_t = key[...].astype(F32).T
-    value_t = value[...].astype(F32).T
-    tag_rows = jnp.broadcast_to(clip.astype(F32), (16, TOK))
     for head in range(HEADS):
         rows = slice(head * HEAD_DIM, (head + 1) * HEAD_DIM)
-        whole = jnp.concatenate([key_t[rows], value_t[rows], tag_rows, query_t[rows], grad_t[rows]], 0)
-        chunk_ref[head] = whole.astype(BF)
-
-
-def pack(query, key, value, out_grad, tags, gate, weight):
-    return pl.pallas_call(
-        pack_body,
-        out_shape=(jax.ShapeDtypeStruct((TOK, WIDTH), BF), jax.ShapeDtypeStruct((HEADS, CHUNK, TOK), BF)),
-        in_specs=[WHOLE] * 7,
+        out_ref[head] = jnp.concatenate([query_t[rows], grad_t[rows]], 0).astype(BF)
+
+
+def pack_queries(query, out_grad, tags, gate, weight):
+    return pl.pallas_call(
+        pack_queries_body,
+        out_shape=(jax.ShapeDtypeStruct((TOK, WIDTH), BF), jax.ShapeDtypeStruct((HEADS, PAIR, TOK), BF)),
+        in_specs=[WHOLE] * 5,
         out_specs=(WHOLE, WHOLE),
         compiler_params=params(),
-        name="pack",
-    )(query, key, value, out_grad, tags, gate, weight)
+        cost_estimate=cost(4),
+        name="pack_queries",
+    )(query, out_grad, tags, gate, weight)
 
 
 def filled(piece, extra):
@@ -82,11 +107,11 @@
     return jnp.concatenate(rows, 0)
 
 
-def lay_out_keys(block, left, main, right, key_n, key_t, value_n, value_t):
+def lay_out_keys(block, left, keys, right, key_n, key_t, value_n, value_t):
     if block < EDGE:
         whole = left[block]
     elif block < EDGE + HEADS:
-        whole = main[block - EDGE, 0:SHARED]
+        whole = keys[block - EDGE]
     else:
         whole = right[block - EDGE - HEADS]
     whole = whole.astype(F32)
@@ -102,8 +127,8 @@
     return clip
 
 
-def lay_out_queries(block, main, clip, query_t, query_n, grad_t, grad_n):
-    whole = main[block, SHARED:].astype(F32)
+def lay_out_queries(block, queries, clip, query_t, query_n, grad_t, grad_n):
+    whole = queries[block].astype(F32)
     ids = lax.broadcasted_iota(jnp.int32, (CLIPS, TOK), 0).astype(F32) + 1.0
     tile, cols = block // PART, slice((block % PART) * TOK, (block % PART + 1) * TOK)
     held = filled(whole[0:HEAD_DIM], [jnp.where(ids == clip, 1.0, 0.0)])
@@ -129,12 +154,12 @@
 
 
 def attend_body(
-    left, main, right, own_ref, back_ref, ahead_ref,
+    left, keys, right, queries, asked_ref, given_ref, back_ref, ahead_ref,
     key_n, key_t, value_n, value_t, query_t, query_n, grad_t, grad_n, held, dk, dv, first_ref, count_ref,
 ):
-    clips = [lay_out_keys(block, left, main, right, key_n, key_t, value_n, value_t) for block in range(SPAN)]
+    clips = [lay_out_keys(block, left, keys, right, key_n, key_t, value_n, value_t) for block in range(SPAN)]
     for block in range(HEADS):
-        lay_out_queries(block, main, clips[EDGE + block], query_t, query_n, grad_t, grad_n)
+        lay_out_queries(block, queries, clips[EDGE + block], query_t, query_n, grad_t, grad_n)
     rows = slice(SPAN * TOK, ROOM * TOK)
     lane = lax.broadcasted_iota(jnp.int32, ((ROOM - SPAN) * TOK, TOK), 1)
     key_n[rows, :] = jnp.where((lane >= HEAD_DIM) & (lane < HEAD_DIM + CLIPS), FAR, 0.0).astype(BF)
@@ -186,7 +211,7 @@
         total = lax.fori_loop(0, count, grad_step, jnp.zeros((80, TILE), F32))
         pair = jnp.concatenate([mixed.astype(F32), total[0:HEAD_DIM] * SCALE], 0).astype(BF)
         for part in range(PART):
-            own_ref[tile * PART + part, 0 : 2 * HEAD_DIM] = pair[:, part * TOK : (part + 1) * TOK]
+            asked_ref[tile * PART + part] = pair[:, part * TOK : (part + 1) * TOK]
         return carry
 
     lax.fori_loop(0, TILES, query_step, 0)
@@ -196,20 +221,22 @@
         if block < EDGE:
             back_ref[block] = pair
         elif block < EDGE + HEADS:
-            own_ref[block - EDGE, 2 * HEAD_DIM :] = pair
+            given_ref[block - EDGE] = pair
         else:
             ahead_ref[block - EDGE - HEADS] = pair
 
 
-def attend(left, main, right):
-    halo = jax.ShapeDtypeStruct((EDGE, 2 * HEAD_DIM, TOK), BF)
+def attend(left, keys, right, queries):
+    own = jax.ShapeDtypeStruct((HEADS, PAIR, TOK), BF)
+    halo = jax.ShapeDtypeStruct((EDGE, PAIR, TOK), BF)
     row_form = pltpu.VMEM((ROOM * TOK, TOK), BF)
     column_form = pltpu.VMEM((ROOM, 80, TOK), BF)
     return pl.pallas_call(
         attend_body,
-        out_shape=(jax.ShapeDtypeStruct((HEADS, GRADS, TOK), BF), halo, halo),
-        in_specs=[WHOLE] * 3,
-        out_specs=(WHOLE,) * 3,
+        out_shape=(own, own, halo, halo),
+        in_specs=[WHOLE] * 4,
+        out_specs=(WHOLE,) * 4,
+        cost_estimate=cost(20),
         scratch_shapes=[
             row_form, column_form, row_form, column_form,
             pltpu.VMEM((TILES, TOK, TILE), BF), pltpu.VMEM((TILES, TILE, TOK), BF),
@@ -222,12 +249,12 @@
         ],
         compiler_params=params(),
         name="attend",
-    )(left, main, right)
-
-
-def weight_term_body(own, branch, out_ref, total):
+    )(left, keys, right, queries)
+
+
+def weight_term_body(asked, branch, out_ref, total):
     step = pl.program_id(0)
-    mixed = jnp.concatenate([own[part, 0:80] for part in range(PART)], 1)
+    mixed = jnp.concatenate([asked[part, 0:80] for part in range(PART)], 1)
 
     @pl.when(step == 0)
     def _():
@@ -241,72 +268,93 @@
         out_ref[...] = whole.T.astype(BF).reshape(GROUPS, SHARE, TOK)
 
 
-def weight_term(own, branch):
+def weight_term(asked, branch):
     return pl.pallas_call(
         weight_term_body,
         grid=(TILES,),
         out_shape=jax.ShapeDtypeStruct((GROUPS, SHARE, TOK), BF),
         in_specs=[
-            pl.BlockSpec((PART, GRADS, TOK), lambda i: (i, 0, 0)),
+            pl.BlockSpec((PART, PAIR, TOK), lambda i: (i, 0, 0)),
             pl.BlockSpec((PART, TOK, WIDTH), lambda i: (i, 0, 0)),
         ],
         out_specs=pl.BlockSpec((GROUPS, SHARE, TOK), lambda i: (0, 0, 0)),
         scratch_shapes=[pltpu.VMEM((80, WIDTH), F32)],
         compiler_params=params(),
+        cost_estimate=cost(6),
         name="weight_term",
-    )(own, branch)
-
-
-def join_body(own, from_left, from_right, terms, out_ref, total):
+    )(asked, branch)
+
+
+def join_body(given, from_left, from_right, terms, out_ref, total):
     total[0:SHARE] = sum(terms[group].astype(F32) for group in range(GROUPS))
     total[SHARE:] = jnp.zeros((8, TOK), F32)
     for block in range(HEADS):
-        whole = own[block].astype(F32)
-        if block < EDGE or block >= HEADS - EDGE:
-            other = from_left[block] if block < EDGE else from_right[block - HEADS + EDGE]
-            pair = whole[2 * HEAD_DIM :] + other.astype(F32)
-            whole = jnp.concatenate([whole[0 : 2 * HEAD_DIM], pair], 0)
+        whole = given[block].astype(F32)
+        if block < EDGE:
+            whole += from_left[block].astype(F32)
+        if block >= HEADS - EDGE:
+            whole += from_right[block - HEADS + EDGE].astype(F32)
         tail = total[block * FINAL : block * FINAL + 16, :]
         out_ref[block] = jnp.concatenate([whole, tail], 0).astype(BF)
 
 
-def join(own, from_left, from_right, terms):
+def join(given, from_left, from_right, terms):
     return pl.pallas_call(
         join_body,
-        out_shape=jax.ShapeDtypeStruct((HEADS, GRADS + 16, TOK), BF),
+        out_shape=jax.ShapeDtypeStruct((HEADS, PAIR + 16, TOK), BF),
         in_specs=[WHOLE] * 4,
         out_specs=WHOLE,
         scratch_shapes=[pltpu.VMEM((SHARE + 8, TOK), F32)],
         compiler_params=params(),
+        cost_estimate=cost(2),
         name="join",
-    )(own, from_left, from_right, terms)
-
-
-def unpack_body(packed, residual, tags, gate, weight, bias, out_ref, dq_ref, dk_ref, dv_ref, dw_ref):
-    clip = tags[...]
-    onehot = (lax.broadcasted_iota(jnp.int32, (CLIPS, TOK), 0) + 1 == clip).astype(F32)
+    )(given, from_left, from_right, terms)
+
+
+def gathered_heads(packed, start):
+    rows = slice(start, start + HEAD_DIM)
+    return jnp.concatenate([packed[head].astype(F32)[rows] for head in range(HEADS)], 0).T.astype(BF)
+
+
+def finish_queries_body(packed, residual, tags, gate, weight, bias, out_ref, dq_ref):
     gate_rows = lax.dot_general(
-        onehot, gate[...], (((0,), (0,)), ((), ())), precision=lax.Precision.HIGHEST, preferred_element_type=F32
+        clip_onehot(tags), gate[...], (((0,), (0,)), ((), ())),
+        precision=lax.Precision.HIGHEST, preferred_element_type=F32,
     )
-    whole = [packed[head].astype(F32) for head in range(HEADS)]
-    mixed = jnp.concatenate([part[0:72] for part in whole], 0).T.astype(BF)
-    projected = mm(mixed, weight[...]) + bias[...]
+    projected = mm(gathered_heads(packed, 0), weight[...]) + bias[...].reshape(1, WIDTH)
     out_ref[...] = (residual[...].astype(F32) + gate_rows * projected).astype(BF)
-    for ref, start in ((dq_ref, 72), (dk_ref, 144), (dv_ref, 216)):
-        ref[...] = jnp.concatenate([part[start : start + 72] for part in whole], 0).T.astype(BF)
-    dw_ref[...] = jnp.concatenate([part[GRADS:].T[0:72] for part in whole], 0)[:, 0:FINAL]
-
-
-def unpack(packed, residual, tags, gate, weight, bias):
-    shape = jax.ShapeDtypeStruct((TOK, WIDTH), BF)
-    return pl.pallas_call(
-        unpack_body,
-        out_shape=(shape,) * 4 + (jax.ShapeDtypeStruct((WIDTH, FINAL), F32),),
+    dq_ref[...] = gathered_heads(packed, HEAD_DIM)
+
+
+def finish_queries(packed, residual, tags, gate, weight, bias):
+    return pl.pallas_call(
+        finish_queries_body,
+        out_shape=(jax.ShapeDtypeStruct((TOK, WIDTH), BF),) * 2,
         in_specs=[WHOLE] * 6,
-        out_specs=(WHOLE,) * 5,
-        compiler_params=params(),
-        name="unpack",
+        out_specs=(WHOLE,) * 2,
+        compiler_params=params(),
+        cost_estimate=cost(4),
+        name="finish_queries",
     )(packed, residual, tags, gate, weight, bias)
+
+
+def finish_keys_body(packed, dk_ref, dv_ref, dw_ref):
+    dk_ref[...] = gathered_heads(packed, 0)
+    dv_ref[...] = gathered_heads(packed, HEAD_DIM)
+    tails = [packed[head].astype(F32)[PAIR:, 0:HEAD_DIM] for head in range(HEADS)]
+    dw_ref[...] = jnp.concatenate(tails, 1)[0:FINAL]
+
+
+def finish_keys(packed):
+    return pl.pallas_call(
+        finish_keys_body,
+        out_shape=(jax.ShapeDtypeStruct((TOK, WIDTH), BF),) * 2 + (jax.ShapeDtypeStruct((FINAL, WIDTH), F32),),
+        in_specs=[WHOLE],
+        out_specs=(WHOLE,) * 3,
+        compiler_params=params(),
+        cost_estimate=cost(2),
+        name="finish_keys",
+    )(packed)
 
 
 def from_neighbour(values, by):
@@ -315,20 +363,28 @@
     return lax.ppermute(values, ("g", "r"), pairs)
 
 
-def shards(query, key, value, residual, token_clip, gate, weight, bias, out_grad):
-    tags = (token_clip + 1).reshape(1, TOK)
-    branch, chunk = pack(query, key, value, out_grad, tags, gate, weight)
-    main = lax.all_to_all(chunk, "r", 0, 0, tiled=True)
-    left = from_neighbour(main[HEADS - EDGE :, 0:SHARED], 1)
-    right = from_neighbour(main[:EDGE, 0:SHARED], -1)
-    left, right, branch = lax.optimization_barrier((left, right, branch))
+def traded(values, axis):
+    return lax.all_to_all(values, axis, 0, 0, tiled=True)
+
+
+def shards(query, key, value, residual, tags, gate, weight, bias, out_grad):
+    keys = pack_keys(key, value, tags)
+    keys, query = lax.optimization_barrier((keys, query))
+    keys = traded(keys, "r")
+    branch, asking = pack_queries(query, out_grad, tags, gate, weight)
     gathered = lax.all_gather(branch, "r", axis=0, tiled=False)
-    own, back, ahead = attend(left, main, right)
+    left = from_neighbour(keys[HEADS - EDGE :], 1)
+    right = from_neighbour(keys[:EDGE], -1)
+    queries = traded(asking, "r")
+    asked, given, back, ahead = attend(left, keys, right, queries)
     from_left = from_neighbour(ahead, 1)
     from_right = from_neighbour(back, -1)
-    terms = lax.all_to_all(weight_term(own, gathered), "g", 0, 0, tiled=True)
-    packed = lax.all_to_all(join(own, from_left, from_right, terms), "r", 0, 0, tiled=True)
-    return unpack(packed, residual, tags, gate, weight, bias.reshape(1, WIDTH))
+    asked_back = traded(asked, "r")
+    terms = traded(weight_term(asked, gathered), "g")
+    given_back = traded(join(given, from_left, from_right, terms), "r")
+    block_out, dq = finish_queries(asked_back, residual, tags, gate, weight, bias)
+    dk, dv, dw = finish_keys(given_back)
+    return block_out, dq, dk, dv, dw.T
 
 
 def solution(mesh):

time: 168 us -> 167 us (level)
  blocking collectives: 25.1 us -> 41.9 us
  waiting for transfers between devices: 55.6 us -> 41.3 us
  local copies, waits for them, and re-layouts: 5.12 us -> 3.09 us
    all_gather x1, waiting for transfers between devices: 19.8 us -> 0.01 us  [shards(): gathered = lax.all_gather(branch, 'r', axis=0, tiled=False)]
    all_to_all x1 -> x2, blocking collectives: 25.1 us -> 41.9 us  [traded(): return lax.all_to_all(values, axis, 0, 0, tiled=True)]
    ppermute x4, waiting for transfers between devices: 10.5 us -> 26 us  [from_neighbour(): return lax.ppermute(values, ('g', 'r'), pairs)]
    all_to_all x2 -> x3, waiting for transfers between devices: 25.3 us -> 15.2 us  [traded(): return lax.all_to_all(values, axis, 0, 0, tiled=True)]
    all_to_all x2 -> x3, starting transfers between devices: 12.7 us -> 15.4 us  [traded(): return lax.all_to_all(values, axis, 0, 0, tiled=True)]
    ppermute x4, starting transfers between devices: 13.4 us -> 11.5 us  [from_neighbour(): return lax.ppermute(values, ('g', 'r'), pairs)]
    pallas_call x1 -> x0, local copies, waits for them, and re-layouts: 1.92 us -> none  [unpack(): pl.pallas_call(unpack_body, out_shape=(shape,) * 4 + (jax.ShapeDtypeStruc...]
    pallas_call x4 -> x6, Pallas kernels: 33.9 us -> 32.6 us  [the longest x1 17.7 us: attend(): pl.pallas_call(attend_body, out_shape=(own, own, halo, halo), in_specs=[W...]
  transfers between devices with their start and end apart: 7 -> 8, of which waited for: 4 -> 4; matrix products, arithmetic and copies ran while one was open for 0% -> 0% of each run, Pallas kernels for 17% -> 14%
where the time goes in v3:
time: 167 us
  blocking collectives  41.9 us (25%)
  waiting for transfers between devices  41.3 us (25%)
  Pallas kernels  39.3 us (24%)
  starting transfers between devices  26.9 us (16%)
  between operations  14.1 us (8%)
  local copies, waits for them, and re-layouts  3.09 us (2%)
    all_to_all x2, blocking collectives, traded(): return lax.all_to_all(values, axis, 0, 0, tiled=True)  41.9 us
    ppermute x4, waiting for transfers between devices, from_neighbour(): return lax.ppermute(values, ('g', 'r'), pairs)  26 us
    pallas_call x1, Pallas kernels, attend(): pl.pallas_call(attend_body, out_shape=(own, own, halo, halo), in_specs=[W...  17.7 us
    all_to_all x3, starting transfers between devices, traded(): return lax.all_to_all(values, axis, 0, 0, tiled=True)  15.4 us
    all_to_all x3, waiting for transfers between devices, traded(): return lax.all_to_all(values, axis, 0, 0, tiled=True)  15.2 us
    ppermute x4, starting transfers between devices, from_neighbour(): return lax.ppermute(values, ('g', 'r'), pairs)  11.5 us
    pallas_call x1, Pallas kernels, weight_term(): pl.pallas_call(weight_term_body, grid=(TILES,), out_shape=jax.ShapeDtypeS...  6.69 us
    pallas_call x1, Pallas kernels, pack_queries(): pl.pallas_call(pack_queries_body, out_shape=(jax.ShapeDtypeStruct((TOK, W...  4.27 us
  transfers between devices with their start and end apart: 8, of which 4 were waited for; matrix products, arithmetic and copies ran while one was open for 0% of the time, Pallas kernels for 14%

profile of v3, /device:TPU:1, one launch (start us, length us, event | category | flops | bytes accessed | tf_op | source)
XLA Modules:
  0.0 166.6 jit_solution(9355093307620013291)
XLA Ops:
  7.2 0.0 all-gather.3.cloned.1.call-start
  7.2 2.1 %pack_keys.1 = bf16[16,160,128]{2,1,0:T(8,128)(2,1)} custom-call(bf16[128,1152]{1,0:T(8,128)(2,1)} %key.1, bf16[128,1152]{1,0:T(8,128)(2,1)} %value.1, s32[128]{0:T(128)} %tags.5), custom_call_target="tpu_custom_call" | custom-call | flops 800000000 | bytes 4000000 | tf_op jit(solution)/shard_map/pack_keys/pallas_call | solution.py:65
  9.4 0.0 copy-start.2
  9.4 4.3 %pack_queries.1 = (bf16[128,1152]{1,0:T(8,128)(2,1)}, bf16[16,144,128]{2,1,0:T(8,128)(2,1)}) custom-call(bf16[128,1152]{1,0:T(8,128)(2,1)} %query, bf16[128,1152]{1,0:T(8,128)(2,1)} %out_grad.1, s32[128]{0:T(128)} %tags.5, f32[32,1152]{1,0:T(8,128)} %gate.3, bf16[1152,1152]{1,0:T(8,128)(2,1)} %weight.3), custom_call_target="tpu_custom_call" | custom-call | flops 1600000000 | bytes 8000000 | tf_op jit(solution)/shard_map/pack_queries/pallas_call | solution.py:91
  13.6 0.0 all-gather.3.cloned.1.call-update
  13.7 0.0 copy-done.2
  13.7 20.6 %all_to_all.25.keys = bf16[16,160,128]{2,1,0:T(8,128)(2,1)S(1)} all-to-all(bf16[16,160,128]{2,1,0:T(8,128)(2,1)S(1)} %copy-done.2), channel_id=1, replica_groups=mesh['g'=8,'r'=16] {'r'}, dimensions={0} | all-to-all | bytes 1310720 | tf_op jit(solution)/shard_map/all_to_all | solution.py:367
  34.2 0.0 copy-start
  34.2 3.8 %all-to-all-start.1 = ((bf16[16,144,128]{2,1,0:T(8,128)(2,1)}), bf16[16,144,128]{2,1,0:T(8,128)(2,1)S(1)}, u32[]{:S(2)}, u32[]{:S(2)}) async-start(bf16[16,144,128]{2,1,0:T(8,128)(2,1)} %get-tuple-element.20), calls=%async_computation.1 | async-start | bytes 1179648 | tf_op jit(solution)/shard_map/all_to_all | solution.py:367
  38.0 5.9 %collective-permute-start = (bf16[7,160,128]{2,1,0:T(8,128)(2,1)S(1)}, bf16[7,160,128]{2,1,0:T(8,128)(2,1)S(1)}, u32[]{:S(2)}, u32[]{:S(2)}) collective-permute-start(bf16[7,160,128]{2,1,0:T(8,128)(2,1)S(1)} %get-tuple-element.32), channel_id=1, source_target_pairs={{0,16},{1,17},{2,18},{3,19},{4,20},{5,21},{6,22},{7,23},{8,24},{9,... | collective-permute-start | bytes 860168 | tf_op jit(solution)/shard_map/ppermute | solution.py:363
  44.0 1.3 collective-permute-start.1
  45.3 7.8 %all-to-all-done.1.queries = bf16[16,144,128]{2,1,0:T(8,128)(2,1)S(1)} async-done(((bf16[16,144,128]{2,1,0:T(8,128)(2,1)}), bf16[16,144,128]{2,1,0:T(8,128)(2,1)S(1)}, u32[]{:S(2)}, u32[]{:S(2)}) %all-to-all-start.1) | async-done | bytes 589856 | tf_op jit(solution)/shard_map/all_to_all | solution.py:367
  53.1 0.0 copy-start.4
  53.1 11.7 %collective-permute-done.left = bf16[7,160,128]{2,1,0:T(8,128)(2,1)S(1)} collective-permute-done((bf16[7,160,128]{2,1,0:T(8,128)(2,1)S(1)}, bf16[7,160,128]{2,1,0:T(8,128)(2,1)S(1)}, u32[]{:S(2)}, u32[]{:S(2)}) %collective-permute-start) | collective-permute-done | bytes 286752 | tf_op jit(solution)/shard_map/ppermute | solution.py:363
  64.8 0.0 copy-start.5
  64.8 0.0 collective-permute-done.1.right
  64.8 0.0 copy-done
  64.8 0.0 copy-done.4
  64.8 0.7 copy-done.5
  65.5 0.0 copy-start.6
  65.5 0.7 copy-done.6
  66.2 17.7 %attend.1 = (bf16[16,144,128]{2,1,0:T(8,128)(2,1)}, bf16[16,144,128]{2,1,0:T(8,128)(2,1)}, bf16[7,144,128]{2,1,0:T(8,128)(2,1)}, bf16[7,144,128]{2,1,0:T(8,128)(2,1)}) custom-call(bf16[7,160,128]{2,1,0:T(8,128)(2,1)} %copy-done.5, bf16[16,160,128]{2,1,0:T(8,128)(2,1)} %copy-done, bf16[7,160,128]{2,1,0:T(8,128)(2,1)} %copy-done.6, bf16[16,144,128]{2,1,0:T(8,128)(2,1)} %copy-done.4), custom_call_target="tpu_custom_call" | custom-call | flops 8000000000 | bytes 40000000 | tf_op jit(solution)/shard_map/attend/pallas_call | solution.py:234
  83.9 0.0 all-gather.3.cloned.1.call-done
  83.9 0.0 copy-start.8
  83.9 0.0 copy-start.7
  83.9 6.7 %weight_term.1 = bf16[8,144,128]{2,1,0:T(8,128)(2,1)} custom-call(bf16[16,144,128]{2,1,0:T(8,128)(2,1)} %get-tuple-element.21.asked, bf16[16,128,1152]{2,1,0:T(8,128)(2,1)} %bitcast.2), custom_call_target="tpu_custom_call" | custom-call | flops 2400000000 | bytes 12000000 | tf_op jit(solution)/shard_map/weight_term/pallas_call | solution.py:272
  90.6 21.3 %all_to_all.26.terms = bf16[8,144,128]{2,1,0:T(8,128)(2,1)} all-to-all(bf16[8,144,128]{2,1,0:T(8,128)(2,1)} %weight_term.1), channel_id=1, replica_groups=mesh['g'=8,'r'=16] {'g'}, dimensions={0} | all-to-all | bytes 589824 | tf_op jit(solution)/shard_map/all_to_all | solution.py:367
  112.0 6.4 %all-to-all-start.2 = ((bf16[16,144,128]{2,1,0:T(8,128)(2,1)}), bf16[16,144,128]{2,1,0:T(8,128)(2,1)S(1)}, u32[]{:S(2)}, u32[]{:S(2)}) async-start(bf16[16,144,128]{2,1,0:T(8,128)(2,1)} %get-tuple-element.21.asked), calls=%async_computation.2 | async-start | bytes 1179648 | tf_op jit(solution)/shard_map/all_to_all | solution.py:367
  118.4 0.0 copy-done.8
  118.4 3.0 %collective-permute-start.2 = (bf16[7,144,128]{2,1,0:T(8,128)(2,1)S(1)}, bf16[7,144,128]{2,1,0:T(8,128)(2,1)S(1)}, u32[]{:S(2)}, u32[]{:S(2)}) collective-permute-start(bf16[7,144,128]{2,1,0:T(8,128)(2,1)S(1)} %copy-done.8), channel_id=1, source_target_pairs={{0,16},{1,17},{2,18},{3,19},{4,20},{5,21},{6,22},{7,23},{8,24},{9,... | collective-permute-start | bytes 774152 | tf_op jit(solution)/shard_map/ppermute | solution.py:363
  121.4 0.0 copy-done.7
  121.4 1.3 collective-permute-start.3
  122.7 14.3 %collective-permute-done.2.from_left = bf16[7,144,128]{2,1,0:T(8,128)(2,1)S(1)} collective-permute-done((bf16[7,144,128]{2,1,0:T(8,128)(2,1)S(1)}, bf16[7,144,128]{2,1,0:T(8,128)(2,1)S(1)}, u32[]{:S(2)}, u32[]{:S(2)}) %collective-permute-start.2) | collective-permute-done | bytes 258080 | tf_op jit(solution)/shard_map/ppermute | solution.py:363
  137.0 0.0 copy-start.9
  137.0 0.0 collective-permute-done.3.from_right
  137.0 0.0 copy-start.10
  137.0 0.7 copy-done.9
  137.7 0.1 copy-done.10
  137.8 2.4 %join.1 = bf16[16,160,128]{2,1,0:T(8,128)(2,1)} custom-call(bf16[16,144,128]{2,1,0:T(8,128)(2,1)} %get-tuple-element.24.given, bf16[7,144,128]{2,1,0:T(8,128)(2,1)} %copy-done.9, bf16[7,144,128]{2,1,0:T(8,128)(2,1)} %copy-done.10, bf16[8,144,128]{2,1,0:T(8,128)(2,1)} %all_to_all.26.terms), custom_call_target="tpu_custom_call" | custom-call | flops 800000000 | bytes 4000000 | tf_op jit(solution)/shard_map/join/pallas_call | solution.py:302
  140.2 0.0 all-to-all-done.2.packed
  140.2 0.0 copy-start.3
  140.2 5.2 %all-to-all-start.4 = ((bf16[16,160,128]{2,1,0:T(8,128)(2,1)}), bf16[16,160,128]{2,1,0:T(8,128)(2,1)S(1)}, u32[]{:S(2)}, u32[]{:S(2)}) async-start(bf16[16,160,128]{2,1,0:T(8,128)(2,1)} %join.1), calls=%async_computation.4 | async-start | bytes 1310720 | tf_op jit(solution)/shard_map/all_to_all | solution.py:367
  145.4 0.0 copy-done.3
  145.4 4.0 %finish_queries.1 = (bf16[128,1152]{1,0:T(8,128)(2,1)}, bf16[128,1152]{1,0:T(8,128)(2,1)}) custom-call(bf16[16,144,128]{2,1,0:T(8,128)(2,1)} %copy-done.3, bf16[128,1152]{1,0:T(8,128)(2,1)} %residual.1, s32[128]{0:T(128)} %tags.5, f32[32,1152]{1,0:T(8,128)} %gate.3, bf16[1152,1152]{1,0:T(8,128)(2,1)} %weight.3, f32[1152]{0:T(1024)} %bias.1), custom_call_target="tpu_custom_call" | custom-call | flops 1600000000 | bytes 8000000 | tf_op jit(solution)/shard_map/finish_queries/pallas_call | solution.py:330
  149.4 7.4 %all-to-all-done.4.packed = bf16[16,160,128]{2,1,0:T(8,128)(2,1)S(1)} async-done(((bf16[16,160,128]{2,1,0:T(8,128)(2,1)}), bf16[16,160,128]{2,1,0:T(8,128)(2,1)S(1)}, u32[]{:S(2)}, u32[]{:S(2)}) %all-to-all-start.4) | async-done | bytes 655392 | tf_op jit(solution)/shard_map/all_to_all | solution.py:367
  156.8 0.0 copy-start.1
  156.8 0.8 copy-done.1
  157.6 2.1 %finish_keys.1 = (bf16[128,1152]{1,0:T(8,128)(2,1)}, bf16[128,1152]{1,0:T(8,128)(2,1)}, f32[9,1152]{1,0:T(8,128)}) custom-call(bf16[16,160,128]{2,1,0:T(8,128)(2,1)} %copy-done.1), custom_call_target="tpu_custom_call" | custom-call | flops 800000000 | bytes 4000000 | tf_op jit(solution)/shard_map/finish_keys/pallas_call | solution.py:349
  (1 shorter events, 0.0 us)
Async XLA Ops:
  7.2 76.8 %all-gather.3.cloned.1.call-start = ((), (), s32[]{:S(2)}) async-start(), calls=%async_computation.5 | async-start | bytes 5013504 | tf_op jit(solution)/shard_map/all_gather | solution.py:375
  9.4 4.3 %copy-start.2 = (bf16[16,160,128]{2,1,0:T(8,128)(2,1)S(1)}, bf16[16,160,128]{2,1,0:T(8,128)(2,1)}, u32[]{:S(2)}) copy-start(bf16[16,160,128]{2,1,0:T(8,128)(2,1)} %pack_keys.1) | copy-start | bytes 1966084
  34.2 30.6 %copy-start = (bf16[16,160,128]{2,1,0:T(8,128)(2,1)}, bf16[16,160,128]{2,1,0:T(8,128)(2,1)S(1)}, u32[]{:S(2)}) copy-start(bf16[16,160,128]{2,1,0:T(8,128)(2,1)S(1)} %all_to_all.25.keys) | copy-start | bytes 1966084
  34.2 18.9 %all-to-all-start.1 = ((bf16[16,144,128]{2,1,0:T(8,128)(2,1)}), bf16[16,144,128]{2,1,0:T(8,128)(2,1)S(1)}, u32[]{:S(2)}, u32[]{:S(2)}) async-start(bf16[16,144,128]{2,1,0:T(8,128)(2,1)} %get-tuple-element.20), calls=%async_computation.1 | async-start | bytes 1179648 | tf_op jit(solution)/shard_map/all_to_all | solution.py:367
  38.0 26.8 %collective-permute-start = (bf16[7,160,128]{2,1,0:T(8,128)(2,1)S(1)}, bf16[7,160,128]{2,1,0:T(8,128)(2,1)S(1)}, u32[]{:S(2)}, u32[]{:S(2)}) collective-permute-start(bf16[7,160,128]{2,1,0:T(8,128)(2,1)S(1)} %get-tuple-element.32), channel_id=1, source_target_pairs={{0,16},{1,17},{2,18},{3,19},{4,20},{5,21},{6,22},{7,23},{8,24},{9,... | collective-permute-start | bytes 860168 | tf_op jit(solution)/shard_map/ppermute | solution.py:363
  44.0 20.8 %collective-permute-start.1 = (bf16[7,160,128]{2,1,0:T(8,128)(2,1)S(1)}, bf16[7,160,128]{2,1,0:T(8,128)(2,1)S(1)}, u32[]{:S(2)}, u32[]{:S(2)}) collective-permute-start(bf16[7,160,128]{2,1,0:T(8,128)(2,1)S(1)} %get-tuple-element.31), channel_id=1, source_target_pairs={{16,0},{17,1},{18,2},{19,3},{20,4},{21,5},{22,6},{23,7},{24,8},{25... | collective-permute-start | bytes 860168 | tf_op jit(solution)/shard_map/ppermute | solution.py:363
  53.1 11.7 %copy-start.4 = (bf16[16,144,128]{2,1,0:T(8,128)(2,1)}, bf16[16,144,128]{2,1,0:T(8,128)(2,1)S(1)}, u32[]{:S(2)}) copy-start(bf16[16,144,128]{2,1,0:T(8,128)(2,1)S(1)} %all-to-all-done.1.queries) | copy-start | bytes 1769476
  64.8 0.7 copy-start.5
  65.5 0.7 copy-start.6
  83.9 34.5 %copy-start.8 = (bf16[7,144,128]{2,1,0:T(8,128)(2,1)S(1)}, bf16[7,144,128]{2,1,0:T(8,128)(2,1)}, u32[]{:S(2)}) copy-start(bf16[7,144,128]{2,1,0:T(8,128)(2,1)} %get-tuple-element.25) | copy-start | bytes 774148
  83.9 37.4 %copy-start.7 = (bf16[7,144,128]{2,1,0:T(8,128)(2,1)S(1)}, bf16[7,144,128]{2,1,0:T(8,128)(2,1)}, u32[]{:S(2)}) copy-start(bf16[7,144,128]{2,1,0:T(8,128)(2,1)} %get-tuple-element.26) | copy-start | bytes 774148
  112.0 28.2 %all-to-all-start.2 = ((bf16[16,144,128]{2,1,0:T(8,128)(2,1)}), bf16[16,144,128]{2,1,0:T(8,128)(2,1)S(1)}, u32[]{:S(2)}, u32[]{:S(2)}) async-start(bf16[16,144,128]{2,1,0:T(8,128)(2,1)} %get-tuple-element.21.asked), calls=%async_computation.2 | async-start | bytes 1179648 | tf_op jit(solution)/shard_map/all_to_all | solution.py:367
  118.4 18.6 %collective-permute-start.2 = (bf16[7,144,128]{2,1,0:T(8,128)(2,1)S(1)}, bf16[7,144,128]{2,1,0:T(8,128)(2,1)S(1)}, u32[]{:S(2)}, u32[]{:S(2)}) collective-permute-start(bf16[7,144,128]{2,1,0:T(8,128)(2,1)S(1)} %copy-done.8), channel_id=1, source_target_pairs={{0,16},{1,17},{2,18},{3,19},{4,20},{5,21},{6,22},{7,23},{8,24},{9,... | collective-permute-start | bytes 774152 | tf_op jit(solution)/shard_map/ppermute | solution.py:363
  121.4 15.7 %collective-permute-start.3 = (bf16[7,144,128]{2,1,0:T(8,128)(2,1)S(1)}, bf16[7,144,128]{2,1,0:T(8,128)(2,1)S(1)}, u32[]{:S(2)}, u32[]{:S(2)}) collective-permute-start(bf16[7,144,128]{2,1,0:T(8,128)(2,1)S(1)} %copy-done.7), channel_id=1, source_target_pairs={{16,0},{17,1},{18,2},{19,3},{20,4},{21,5},{22,6},{23,7},{24,8},{25... | collective-permute-start | bytes 774152 | tf_op jit(solution)/shard_map/ppermute | solution.py:363
  137.0 0.7 copy-start.9
  137.0 0.8 copy-start.10
  140.2 5.2 %copy-start.3 = (bf16[16,144,128]{2,1,0:T(8,128)(2,1)}, bf16[16,144,128]{2,1,0:T(8,128)(2,1)S(1)}, u32[]{:S(2)}) copy-start(bf16[16,144,128]{2,1,0:T(8,128)(2,1)S(1)} %all-to-all-done.2.packed) | copy-start | bytes 1769476
  140.2 16.6 %all-to-all-start.4 = ((bf16[16,160,128]{2,1,0:T(8,128)(2,1)}), bf16[16,160,128]{2,1,0:T(8,128)(2,1)S(1)}, u32[]{:S(2)}, u32[]{:S(2)}) async-start(bf16[16,160,128]{2,1,0:T(8,128)(2,1)} %join.1), calls=%async_computation.4 | async-start | bytes 1310720 | tf_op jit(solution)/shard_map/all_to_all | solution.py:367
  156.8 0.8 copy-start.1
Sparse Core Ops, SparseCore 0:
  13.8 60.4 all-gather.2

commit v4 on v3

v4 whole, which is shorter than its diff:
```python
import math

import jax
import jax.numpy as jnp
from jax import lax
from jax.experimental import pallas as pl
from jax.experimental.pallas import tpu as pltpu
from jax.sharding import Mesh, PartitionSpec as P

HEADS = 16
HEAD_DIM = 72
WIDTH = HEADS * HEAD_DIM
TOK = 128
GROUPS = 8
EDGE = 7
SPAN = HEADS + 2 * EDGE
TILE = 256
TILES = HEADS * TOK // TILE
PART = TILE // TOK
STEP = 4
ROOM = SPAN + STEP - 1
CHUNKS = 5
SHARED = 2 * HEAD_DIM + 16
PAIR = 2 * HEAD_DIM
SHARE = WIDTH // GROUPS
FINAL = SHARE // HEADS
CLIPS = 32
SCALE = 1.0 / math.sqrt(HEAD_DIM)
SCALE2 = SCALE / math.log(2.0)
FAR = -1e30
BF = jnp.bfloat16
F32 = jnp.float32
VMEM_BYTES = 56 * 1024 * 1024

WHOLE = pl.BlockSpec(memory_space=pltpu.VMEM)


def params():
    return pltpu.CompilerParams(vmem_limit_bytes=VMEM_BYTES)


def cost(micros):
    return pl.CostEstimate(flops=int(micros * 4e8), bytes_accessed=int(micros * 2e6), transcendentals=0)


def mm(left, right):
    return jnp.dot(left, right, preferred_element_type=F32)


def clip_onehot(tags):
    ids = lax.broadcasted_iota(jnp.int32, (CLIPS, TOK), 0)
    return (ids == tags[...].reshape(1, TOK)).astype(F32)


def pack_keys_body(key, value, tags, out_ref):
    key_t = key[...].astype(F32).T
    value_t = value[...].astype(F32).T
    tag_rows = jnp.broadcast_to(tags[...].reshape(1, TOK).astype(F32) + 1.0, (16, TOK))
    for head in range(HEADS):
        rows = slice(head * HEAD_DIM, (head + 1) * HEAD_DIM)
        out_ref[head] = jnp.concatenate([key_t[rows], value_t[rows], tag_rows], 0).astype(BF)


def pack_keys(key, value, tags):
    return pl.pallas_call(
        pack_keys_body,
        out_shape=jax.ShapeDtypeStruct((HEADS, SHARED, TOK), BF),
        in_specs=[WHOLE] * 3,
        out_specs=WHOLE,
        compiler_params=params(),
        cost_estimate=cost(2),
        name="pack_keys",
    )(key, value, tags)


def pack_queries_body(query, out_grad, tags, gate, weight, bg_ref, out_ref):
    gate_rows = lax.dot_general(
        clip_onehot(tags), gate[...], (((0,), (0,)), ((), ())),
        precision=lax.Precision.HIGHEST, preferred_element_type=F32,
    )
    branch = (out_grad[...].astype(F32) * gate_rows).astype(BF)
    bg_ref[...] = branch
    grad_t = lax.dot_general(weight[...], branch, (((1,), (1,)), ((), ())), preferred_element_type=F32)
    query_t = query[...].astype(F32).T
    for head in range(HEADS):
        rows = slice(head * HEAD_DIM, (head + 1) * HEAD_DIM)
        out_ref[head] = jnp.concatenate([query_t[rows], grad_t[rows]], 0).astype(BF)


def pack_queries(query, out_grad, tags, gate, weight):
    return pl.pallas_call(
        pack_queries_body,
        out_shape=(jax.ShapeDtypeStruct((TOK, WIDTH), BF), jax.ShapeDtypeStruct((HEADS, PAIR, TOK), BF)),
        in_specs=[WHOLE] * 5,
        out_specs=(WHOLE, WHOLE),
        compiler_params=params(),
        cost_estimate=cost(4),
        name="pack_queries",
    )(query, out_grad, tags, gate, weight)


def filled(piece, extra):
    rows = [piece] + extra
    have = sum(part.shape[0] for part in rows)
    if have < TOK:
        rows.append(jnp.zeros((TOK - have, TOK), F32))
    return jnp.concatenate(rows, 0)


def window_block(block, left, keys, right):
    if block < EDGE:
        return left[block].astype(F32)
    if block < EDGE + HEADS:
        return keys[block - EDGE].astype(F32)
    return right[block - EDGE - HEADS].astype(F32)


def same_clip(clip, same, other):
    ids = lax.broadcasted_iota(jnp.int32, (CLIPS, TOK), 0).astype(F32) + 1.0
    return jnp.where(ids == clip, same, other)


def lay_out_keys(block, whole, key_n, key_t):
    held = filled(whole[0:HEAD_DIM], [same_clip(whole[PAIR : PAIR + 1], 0.0, FAR)])
    key_n[block * TOK : (block + 1) * TOK, :] = held.T.astype(BF)
    if key_t is not None:
        key_t[block] = held[0:80].astype(BF)


def key_padding(key_n, key_t):
    rows = slice(SPAN * TOK, ROOM * TOK)
    lane = lax.broadcasted_iota(jnp.int32, ((ROOM - SPAN) * TOK, TOK), 1)
    key_n[rows, :] = jnp.where((lane >= HEAD_DIM) & (lane < HEAD_DIM + CLIPS), FAR, 0.0).astype(BF)
    if key_t is not None:
        for block in range(SPAN, ROOM):
            key_t[block] = jnp.zeros((80, TOK), BF)


def key_ranges(clips, first_ref, count_ref):
    clips = [jnp.where(row == 0.0, 100.0, row) if at >= EDGE + HEADS else row for at, row in enumerate(clips)]
    clips = jnp.concatenate(clips + [jnp.full((32 - SPAN, TOK), 100.0, F32)], 0)
    least = jnp.min(clips, axis=1, keepdims=True)
    most = jnp.max(clips, axis=1, keepdims=True)
    for tile in range(TILES):
        start = EDGE + tile * PART
        low, high = least[start : start + 1], most[start + PART - 1 : start + PART]
        first = jnp.sum(jnp.where(most < low, 1.0, 0.0)).astype(jnp.int32)
        end = jnp.sum(jnp.where(least <= high, 1.0, 0.0)).astype(jnp.int32)
        first_ref[tile] = first
        count_ref[tile] = (end - first + STEP - 1) // STEP


def side_by_side(ref, start):
    return jnp.concatenate([ref[start + at] for at in range(STEP)], 1)


def blocks(first, step):
    start = first + step * STEP
    return start, pl.ds(pl.multiple_of(start * TOK, TOK), STEP * TOK)


def forward_body(
    left, keys, right, queries, mixed_ref, stat_ref, key_n, value_t, query_t, held, first_ref, count_ref
):
    clips = []
    for block in range(SPAN):
        whole = window_block(block, left, keys, right)
        clips.append(whole[PAIR : PAIR + 1])
        lay_out_keys(block, whole, key_n, None)
        value_t[block] = filled(whole[HEAD_DIM:PAIR], [jnp.ones((8, TOK), F32)])[0:80].astype(BF)
    for block in range(SPAN, ROOM):
        value_t[block] = jnp.zeros((80, TOK), BF)
    key_padding(key_n, None)
    for block in range(HEADS):
        cols = slice((block % PART) * TOK, (block % PART + 1) * TOK)
        asked = filled(queries[block].astype(F32)[0:HEAD_DIM], [same_clip(clips[EDGE + block], 1.0, 0.0)])
        query_t[block // PART, :, cols] = asked.astype(BF)
    key_ranges(clips, first_ref, count_ref)

    def query_step(tile, carry):
        first, count = first_ref[tile], count_ref[tile]

        def score_step(step, top):
            scores = mm(key_n[blocks(first, step)[1], :], query_t[tile])
            held[step] = scores
            return jnp.maximum(top, jnp.max(scores, axis=0, keepdims=True))

        top = lax.fori_loop(0, count, score_step, jnp.full((1, TILE), 2.0 * FAR, F32))

        def value_step(step, total):
            weights = jnp.exp2((held[step] - top) * SCALE2).astype(BF)
            return total + mm(side_by_side(value_t, blocks(first, step)[0]), weights)

        total = lax.fori_loop(0, count, value_step, jnp.zeros((80, TILE), F32))
        sums = total[HEAD_DIM : HEAD_DIM + 1]
        mixed = (total[0:HEAD_DIM] / sums).astype(BF)
        stat_ref[tile] = jnp.broadcast_to(top * SCALE2 + jnp.log2(sums), (8, TILE))
        for part in range(PART):
            mixed_ref[tile * PART + part] = mixed[:, part * TOK : (part + 1) * TOK]
        return carry

    lax.fori_loop(0, TILES, query_step, 0)


def forward(left, keys, right, queries):
    return pl.pallas_call(
        forward_body,
        out_shape=(
            jax.ShapeDtypeStruct((HEADS, HEAD_DIM, TOK), BF),
            jax.ShapeDtypeStruct((TILES, 8, TILE), F32),
        ),
        in_specs=[WHOLE] * 4,
        out_specs=(WHOLE,) * 2,
        cost_estimate=cost(10),
        scratch_shapes=[
            pltpu.VMEM((ROOM * TOK, TOK), BF),
            pltpu.VMEM((ROOM, 80, TOK), BF),
            pltpu.VMEM((TILES, TOK, TILE), BF),
            pltpu.VMEM((CHUNKS, STEP * TOK, TILE), F32),
            pltpu.SMEM((TILES,), jnp.int32),
            pltpu.SMEM((TILES,), jnp.int32),
        ],
        compiler_params=params(),
        name="forward",
    )(left, keys, right, queries)


def backward_body(
    left, keys, right, queries, mixed, stat, dq_ref, given_ref, back_ref, ahead_ref,
    key_n, key_t, value_n, query_t, query_n, grad_t, grad_n, deltas, dk, dv, first_ref, count_ref,
):
    clips = []
    for block in range(SPAN):
        whole = window_block(block, left, keys, right)
        clips.append(whole[PAIR : PAIR + 1])
        lay_out_keys(block, whole, key_n, key_t)
        value_n[block * TOK : (block + 1) * TOK, :] = filled(whole[HEAD_DIM:PAIR], []).T.astype(BF)
    value_n[SPAN * TOK :, :] = jnp.zeros(((ROOM - SPAN) * TOK, TOK), BF)
    key_padding(key_n, key_t)
    for block in range(HEADS):
        tile, cols = block // PART, slice((block % PART) * TOK, (block % PART + 1) * TOK)
        whole = queries[block].astype(F32)
        asked = filled(whole[0:HEAD_DIM], [same_clip(clips[EDGE + block], 1.0, 0.0)])
        query_t[tile, :, cols] = asked.astype(BF)
        query_n[tile, cols, :] = asked.T.astype(BF)
        grad = filled(whole[HEAD_DIM:], [])
        grad_t[tile, :, cols] = grad.astype(BF)
        grad_n[tile, cols, :] = grad.T.astype(BF)
        delta = jnp.sum(whole[HEAD_DIM:] * mixed[block].astype(F32), axis=0, keepdims=True)
        deltas[tile, :, cols] = jnp.broadcast_to(delta, (8, TOK))
    key_ranges(clips, first_ref, count_ref)
    dk[...] = jnp.zeros_like(dk)
    dv[...] = jnp.zeros_like(dv)

    def query_step(tile, carry):
        first, count = first_ref[tile], count_ref[tile]
        log_sum = stat[tile, 0:1]
        delta = deltas[tile, 0:1]

        def grad_step(step, total):
            start, rows = blocks(first, step)
            scores = mm(key_n[rows, :], query_t[tile])
            prob = jnp.exp2(scores * SCALE2 - log_sum)
            pull = mm(value_n[rows, :], grad_t[tile])
            dv[rows, :] += mm(prob.astype(BF), grad_n[tile])
            score_grad = (prob * (pull - delta)).astype(BF)
            dk[rows, :] += mm(score_grad, query_n[tile])
            return total + mm(side_by_side(key_t, start), score_grad)

        total = lax.fori_loop(0, count, grad_step, jnp.zeros((80, TILE), F32))
        grad = (total[0:HEAD_DIM] * SCALE).astype(BF)
        for part in range(PART):
            dq_ref[tile * PART + part] = grad[:, part * TOK : (part + 1) * TOK]
        return carry

    lax.fori_loop(0, TILES, query_step, 0)
    for block in range(SPAN):
        rows = slice(block * TOK, (block + 1) * TOK)
        pair = jnp.concatenate([dk[rows, :].T[0:HEAD_DIM] * SCALE, dv[rows, :].T[0:HEAD_DIM]], 0).astype(BF)
        if block < EDGE:
            back_ref[block] = pair
        elif block < EDGE + HEADS:
            given_ref[block - EDGE] = pair
        else:
            ahead_ref[block - EDGE - HEADS] = pair


def backward(left, keys, right, queries, mixed, stat):
    halo = jax.ShapeDtypeStruct((EDGE, PAIR, TOK), BF)
    row_form = pltpu.VMEM((ROOM * TOK, TOK), BF)
    return pl.pallas_call(
        backward_body,
        out_shape=(
            jax.ShapeDtypeStruct((HEADS, HEAD_DIM, TOK), BF),
            jax.ShapeDtypeStruct((HEADS, PAIR, TOK), BF),
            halo,
            halo,
        ),
        in_specs=[WHOLE] * 6,
        out_specs=(WHOLE,) * 4,
        cost_estimate=cost(14),
        scratch_shapes=[
            row_form, pltpu.VMEM((ROOM, 80, TOK), BF), row_form,
            pltpu.VMEM((TILES, TOK, TILE), BF), pltpu.VMEM((TILES, TILE, TOK), BF),
            pltpu.VMEM((TILES, TOK, TILE), BF), pltpu.VMEM((TILES, TILE, TOK), BF),
            pltpu.VMEM((TILES, 8, TILE), F32),
            pltpu.VMEM((ROOM * TOK, TOK), F32),
            pltpu.VMEM((ROOM * TOK, TOK), F32),
            pltpu.SMEM((TILES,), jnp.int32),
            pltpu.SMEM((TILES,), jnp.int32),
        ],
        compiler_params=params(),
        name="backward",
    )(left, keys, right, queries, mixed, stat)


def weight_term_body(mixed_ref, branch, out_ref, total):
    step = pl.program_id(0)
    mixed = jnp.concatenate([mixed_ref[part].astype(F32) for part in range(PART)], 1).astype(BF)

    @pl.when(step == 0)
    def _():
        total[...] = jnp.zeros_like(total)

    total[...] += mm(mixed, branch[...].reshape(TILE, WIDTH))

    @pl.when(step == TILES - 1)
    def _():
        whole = jnp.concatenate([total[...], jnp.zeros((TOK - HEAD_DIM, WIDTH), F32)], 0)
        out_ref[...] = whole.T.astype(BF).reshape(GROUPS, SHARE, TOK)


def weight_term(mixed, branch):
    return pl.pallas_call(
        weight_term_body,
        grid=(TILES,),
        out_shape=jax.ShapeDtypeStruct((GROUPS, SHARE, TOK), BF),
        in_specs=[
            pl.BlockSpec((PART, HEAD_DIM, TOK), lambda i: (i, 0, 0)),
            pl.BlockSpec((PART, TOK, WIDTH), lambda i: (i, 0, 0)),
        ],
        out_specs=pl.BlockSpec((GROUPS, SHARE, TOK), lambda i: (0, 0, 0)),
        scratch_shapes=[pltpu.VMEM((HEAD_DIM, WIDTH), F32)],
        compiler_params=params(),
        cost_estimate=cost(6),
        name="weight_term",
    )(mixed, branch)


def join_body(mixed, dq, given, from_left, from_right, terms, out_ref, total):
    total[0:SHARE] = sum(terms[group].astype(F32) for group in range(GROUPS))
    total[SHARE:] = jnp.zeros((8, TOK), F32)
    for block in range(HEADS):
        pair = given[block].astype(F32)
        if block < EDGE:
            pair += from_left[block].astype(F32)
        if block >= HEADS - EDGE:
            pair += from_right[block - HEADS + EDGE].astype(F32)
        tail = total[block * FINAL : block * FINAL + 16, :]
        whole = [mixed[block].astype(F32), dq[block].astype(F32), pair, tail]
        out_ref[block] = jnp.concatenate(whole, 0).astype(BF)


def join(mixed, dq, given, from_left, from_right, terms):
    return pl.pallas_call(
        join_body,
        out_shape=jax.ShapeDtypeStruct((HEADS, 2 * PAIR + 16, TOK), BF),
        in_specs=[WHOLE] * 6,
        out_specs=WHOLE,
        scratch_shapes=[pltpu.VMEM((SHARE + 8, TOK), F32)],
        compiler_params=params(),
        cost_estimate=cost(2),
        name="join",
    )(mixed, dq, given, from_left, from_right, terms)


def finish_body(packed, residual, tags, gate, weight, bias, out_ref, dq_ref, dk_ref, dv_ref, dw_ref):
    whole = [packed[head].astype(F32) for head in range(HEADS)]

    def rows(at):
        part = slice(at * HEAD_DIM, (at + 1) * HEAD_DIM)
        return jnp.concatenate([one[part] for one in whole], 0).T.astype(BF)

    gate_rows = lax.dot_general(
        clip_onehot(tags), gate[...], (((0,), (0,)), ((), ())),
        precision=lax.Precision.HIGHEST, preferred_element_type=F32,
    )
    projected = mm(rows(0), weight[...]) + bias[...].reshape(1, WIDTH)
    out_ref[...] = (residual[...].astype(F32) + gate_rows * projected).astype(BF)
    dq_ref[...] = rows(1)
    dk_ref[...] = rows(2)
    dv_ref[...] = rows(3)
    dw_ref[...] = jnp.concatenate([one[2 * PAIR :, 0:HEAD_DIM] for one in whole], 1)[0:FINAL]


def finish(packed, residual, tags, gate, weight, bias):
    return pl.pallas_call(
        finish_body,
        out_shape=(jax.ShapeDtypeStruct((TOK, WIDTH), BF),) * 4 + (jax.ShapeDtypeStruct((FINAL, WIDTH), F32),),
        in_specs=[WHOLE] * 6,
        out_specs=(WHOLE,) * 5,
        compiler_params=params(),
        cost_estimate=cost(4),
        name="finish",
    )(packed, residual, tags, gate, weight, bias)


def from_neighbour(values, by):
    total = GROUPS * HEADS
    pairs = [(i, i + by * HEADS) for i in range(total) if 0 <= i + by * HEADS < total]
    return lax.ppermute(values, ("g", "r"), pairs)


def traded(values, axis):
    return lax.all_to_all(values, axis, 0, 0, tiled=True)


def shards(query, key, value, residual, tags, gate, weight, bias, out_grad):
    keys = pack_keys(key, value, tags)
    keys, query = lax.optimization_barrier((keys, query))
    keys = traded(keys, "r")
    branch, asking = pack_queries(query, out_grad, tags, gate, weight)
    gathered = lax.all_gather(branch, "r", axis=0, tiled=False)
    left = from_neighbour(keys[HEADS - EDGE :], 1)
    right = from_neighbour(keys[:EDGE], -1)
    queries = traded(asking, "r")
    mixed, stat = forward(left, keys, right, queries)
    term = weight_term(mixed, gathered)
    term, stat = lax.optimization_barrier((term, stat))
    terms = traded(term, "g")
    dq, given, back, ahead = backward(left, keys, right, queries, mixed, stat)
    from_left = from_neighbour(ahead, 1)
    from_right = from_neighbour(back, -1)
    packed = traded(join(mixed, dq, given, from_left, from_right, terms), "r")
    block_out, dq, dk, dv, dw = finish(packed, residual, tags, gate, weight, bias)
    return block_out, dq, dk, dv, dw.T


def solution(mesh):
    split = Mesh(mesh.devices.reshape(GROUPS, HEADS), ("g", "r"))
    both = ("g", "r")
    in_specs = (
        P(both, None), P(both, None), P(both, None), P(both, None), P(both), P(), P(), P(), P(both, None),
    )
    out_specs = (P(both, None),) * 4 + (P(None, both),)
    return jax.shard_map(shards, mesh=split, in_specs=in_specs, out_specs=out_specs, check_vma=False)
```

time: 167 us -> 163 us (0.976); the launches traced: 167 us -> 160 us
  waiting for transfers between devices: 41.3 us -> 28.2 us
  blocking collectives: 41.9 us -> 45.6 us
  Pallas kernels: 39.3 us -> 42.9 us
    all_to_all x3 -> x2, waiting for transfers between devices: 15.2 us -> 7.2 us  [traded(): return lax.all_to_all(values, axis, 0, 0, tiled=True)]
    ppermute x4, waiting for transfers between devices: 26 us -> 21 us  [from_neighbour(): return lax.ppermute(values, ('g', 'r'), pairs)]
    pallas_call x4, Pallas kernels: 26.1 us -> 29.9 us  [the longest x1 12.3 us: backward(): pl.pallas_call(backward_body, out_shape=(jax.ShapeDtypeStruct((HEADS, HEA...]
    all_to_all x2, blocking collectives: 41.9 us -> 45.6 us  [traded(): return lax.all_to_all(values, axis, 0, 0, tiled=True)]
    ppermute x4, starting transfers between devices: 11.5 us -> 14 us  [from_neighbour(): return lax.ppermute(values, ('g', 'r'), pairs)]
    all_to_all x3 -> x2, starting transfers between devices: 15.4 us -> 14 us  [traded(): return lax.all_to_all(values, axis, 0, 0, tiled=True)]
  transfers between devices with their start and end apart: 8 -> 7, of which waited for: 4 -> 5; matrix products, arithmetic and copies ran while one was open for 0% -> 0% of each run, Pallas kernels for 14% -> 14%
where the time goes in v4:
time: 163 us; the launch traced here: 160 us
  blocking collectives  45.6 us (28%)
  Pallas kernels  42.9 us (26%)
  waiting for transfers between devices  28.2 us (17%)
  starting transfers between devices  28.1 us (17%)
  between operations  14.1 us (9%)
    all_to_all x2, blocking collectives, traded(): return lax.all_to_all(values, axis, 0, 0, tiled=True)  45.6 us
    ppermute x4, waiting for transfers between devices, from_neighbour(): return lax.ppermute(values, ('g', 'r'), pairs)  21 us
    all_to_all x2, starting transfers between devices, traded(): return lax.all_to_all(values, axis, 0, 0, tiled=True)  14 us
    ppermute x4, starting transfers between devices, from_neighbour(): return lax.ppermute(values, ('g', 'r'), pairs)  14 us
    pallas_call x1, Pallas kernels, backward(): pl.pallas_call(backward_body, out_shape=(jax.ShapeDtypeStruct((HEADS, HEA...  12.3 us
    pallas_call x1, Pallas kernels, forward(): pl.pallas_call(forward_body, out_shape=(jax.ShapeDtypeStruct((HEADS, HEAD...  10.6 us
    all_to_all x2, waiting for transfers between devices, traded(): return lax.all_to_all(values, axis, 0, 0, tiled=True)  7.2 us
    pallas_call x1, Pallas kernels, weight_term(): pl.pallas_call(weight_term_body, grid=(TILES,), out_shape=jax.ShapeDtypeS...  6.58 us
  transfers between devices with their start and end apart: 7, of which 5 were waited for; matrix products, arithmetic and copies ran while one was open for 0% of the time, Pallas kernels for 14%

profile of v4, /device:TPU:1, one launch (start us, length us, event | category | flops | bytes accessed | tf_op | source)
XLA Modules:
  0.0 160.4 jit_solution(11001376066945445236)
XLA Ops:
  7.2 0.0 all-gather.3.cloned.1.call-start
  7.2 2.1 %pack_keys.1 = bf16[16,160,128]{2,1,0:T(8,128)(2,1)} custom-call(bf16[128,1152]{1,0:T(8,128)(2,1)} %key.1, bf16[128,1152]{1,0:T(8,128)(2,1)} %value.1, s32[128]{0:T(128)} %tags.5), custom_call_target="tpu_custom_call" | custom-call | flops 800000000 | bytes 4000000 | tf_op jit(solution)/shard_map/pack_keys/pallas_call | solution.py:65
  9.4 0.0 copy-start.2
  9.4 4.3 %pack_queries.1 = (bf16[128,1152]{1,0:T(8,128)(2,1)}, bf16[16,144,128]{2,1,0:T(8,128)(2,1)}) custom-call(bf16[128,1152]{1,0:T(8,128)(2,1)} %query, bf16[128,1152]{1,0:T(8,128)(2,1)} %out_grad.1, s32[128]{0:T(128)} %tags.5, f32[32,1152]{1,0:T(8,128)} %gate.3, bf16[1152,1152]{1,0:T(8,128)(2,1)} %weight.3), custom_call_target="tpu_custom_call" | custom-call | flops 1600000000 | bytes 8000000 | tf_op jit(solution)/shard_map/pack_queries/pallas_call | solution.py:91
  13.6 0.0 all-gather.3.cloned.1.call-update
  13.7 0.0 copy-done.2
  13.7 20.6 %all_to_all.20.keys = bf16[16,160,128]{2,1,0:T(8,128)(2,1)S(1)} all-to-all(bf16[16,160,128]{2,1,0:T(8,128)(2,1)S(1)} %copy-done.2), channel_id=1, replica_groups=mesh['g'=8,'r'=16] {'r'}, dimensions={0} | all-to-all | bytes 1310720 | tf_op jit(solution)/shard_map/all_to_all | solution.py:415
  34.2 0.0 copy-start
  34.2 3.8 %all-to-all-start.1 = ((bf16[16,144,128]{2,1,0:T(8,128)(2,1)}), bf16[16,144,128]{2,1,0:T(8,128)(2,1)S(1)}, u32[]{:S(2)}, u32[]{:S(2)}) async-start(bf16[16,144,128]{2,1,0:T(8,128)(2,1)} %get-tuple-element.24), calls=%async_computation.1 | async-start | bytes 1179648 | tf_op jit(solution)/shard_map/all_to_all | solution.py:415
  38.0 1.3 collective-permute-start.1
  39.3 6.6 %collective-permute-start = (bf16[7,160,128]{2,1,0:T(8,128)(2,1)S(1)}, bf16[7,160,128]{2,1,0:T(8,128)(2,1)S(1)}, u32[]{:S(2)}, u32[]{:S(2)}) collective-permute-start(bf16[7,160,128]{2,1,0:T(8,128)(2,1)S(1)} %get-tuple-element.40), channel_id=1, source_target_pairs={{0,16},{1,17},{2,18},{3,19},{4,20},{5,21},{6,22},{7,23},{8,24},{9,... | collective-permute-start | bytes 860168 | tf_op jit(solution)/shard_map/ppermute | solution.py:411
  45.9 7.2 %all-to-all-done.1.queries = bf16[16,144,128]{2,1,0:T(8,128)(2,1)S(1)} async-done(((bf16[16,144,128]{2,1,0:T(8,128)(2,1)}), bf16[16,144,128]{2,1,0:T(8,128)(2,1)S(1)}, u32[]{:S(2)}, u32[]{:S(2)}) %all-to-all-start.1) | async-done | bytes 589856 | tf_op jit(solution)/shard_map/all_to_all | solution.py:415
  53.1 0.0 copy-start.3
  53.1 10.4 %collective-permute-done.1.right = bf16[7,160,128]{2,1,0:T(8,128)(2,1)S(1)} collective-permute-done((bf16[7,160,128]{2,1,0:T(8,128)(2,1)S(1)}, bf16[7,160,128]{2,1,0:T(8,128)(2,1)S(1)}, u32[]{:S(2)}, u32[]{:S(2)}) %collective-permute-start.1) | collective-permute-done | bytes 286752 | tf_op jit(solution)/shard_map/ppermute | solution.py:411
  63.5 0.0 copy-start.6
  63.5 2.0 %collective-permute-done.left = bf16[7,160,128]{2,1,0:T(8,128)(2,1)S(1)} collective-permute-done((bf16[7,160,128]{2,1,0:T(8,128)(2,1)S(1)}, bf16[7,160,128]{2,1,0:T(8,128)(2,1)S(1)}, u32[]{:S(2)}, u32[]{:S(2)}) %collective-permute-start) | collective-permute-done | bytes 286752 | tf_op jit(solution)/shard_map/ppermute | solution.py:411
  65.5 0.0 copy-done
  65.5 0.0 copy-done.3
  65.5 0.0 copy-done.6
  65.5 0.0 copy-start.7
  65.5 0.7 copy-done.7
  66.2 10.6 %forward.1 = (bf16[16,72,128]{2,1,0:T(8,128)(2,1)}, f32[8,8,256]{2,1,0:T(8,128)}) custom-call(bf16[7,160,128]{2,1,0:T(8,128)(2,1)} %copy-done.7, bf16[16,160,128]{2,1,0:T(8,128)(2,1)} %copy-done, bf16[7,160,128]{2,1,0:T(8,128)(2,1)} %copy-done.6, bf16[16,144,128]{2,1,0:T(8,128)(2,1)} %copy-done.3), custom_call_target="tpu_custom_call" | custom-call | flops 4000000000 | bytes 20000000 | tf_op jit(solution)/shard_map/forward/pallas_call | solution.py:206
  76.8 0.0 all-gather.3.cloned.1.call-done
  76.8 6.6 %weight_term.1 = bf16[8,144,128]{2,1,0:T(8,128)(2,1)} custom-call(bf16[16,72,128]{2,1,0:T(8,128)(2,1)} %get-tuple-element.25.mixed_ref.mixed, bf16[16,128,1152]{2,1,0:T(8,128)(2,1)} %bitcast.2), custom_call_target="tpu_custom_call" | custom-call | flops 2400000000 | bytes 12000000 | tf_op jit(solution)/shard_map/weight_term/pallas_call | solution.py:334
  83.4 10.3 %all-to-all-start.2 = ((bf16[8,144,128]{2,1,0:T(8,128)(2,1)}), bf16[8,144,128]{2,1,0:T(8,128)(2,1)S(1)}, u32[]{:S(2)}, u32[]{:S(2)}) async-start(bf16[8,144,128]{2,1,0:T(8,128)(2,1)} %weight_term.1), calls=%async_computation.2 | async-start | bytes 589824 | tf_op jit(solution)/shard_map/all_to_all | solution.py:415
  93.6 12.3 %backward.1 = (bf16[16,72,128]{2,1,0:T(8,128)(2,1)}, bf16[16,144,128]{2,1,0:T(8,128)(2,1)}, bf16[7,144,128]{2,1,0:T(8,128)(2,1)}, bf16[7,144,128]{2,1,0:T(8,128)(2,1)}) custom-call(bf16[7,160,128]{2,1,0:T(8,128)(2,1)} %copy-done.7, bf16[16,160,128]{2,1,0:T(8,128)(2,1)} %copy-done, bf16[7,160,128]{2,1,0:T(8,128)(2,1)} %copy-done.6, ...), custom_call_target="tpu_custom_call" | custom-call | flops 5600000000 | bytes 28000000 | tf_op jit(solution)/shard_map/backward/pallas_call | solution.py:291
  105.9 4.9 %collective-permute-start.2 = (bf16[7,144,128]{2,1,0:T(8,128)(2,1)}, bf16[7,144,128]{2,1,0:T(8,128)(2,1)S(1)}, u32[]{:S(2)}, u32[]{:S(2)}) collective-permute-start(bf16[7,144,128]{2,1,0:T(8,128)(2,1)} %get-tuple-element.31), channel_id=1, source_target_pairs={{0,16},{1,17},{2,18},{3,19},{4,20},{5,21},{6,22},{7,23},{8,24},{9,... | collective-permute-start | bytes 774152 | tf_op jit(solution)/shard_map/ppermute | solution.py:411
  110.8 1.3 collective-permute-start.3
  112.1 0.0 all-to-all-done.2.terms
  112.1 0.0 copy-start.1
  112.1 3.4 %collective-permute-done.2.from_left = bf16[7,144,128]{2,1,0:T(8,128)(2,1)S(1)} collective-permute-done((bf16[7,144,128]{2,1,0:T(8,128)(2,1)}, bf16[7,144,128]{2,1,0:T(8,128)(2,1)S(1)}, u32[]{:S(2)}, u32[]{:S(2)}) %collective-permute-start.2) | collective-permute-done | bytes 258080 | tf_op jit(solution)/shard_map/ppermute | solution.py:411
  115.5 0.0 copy-start.4
  115.5 5.2 %collective-permute-done.3.from_right = bf16[7,144,128]{2,1,0:T(8,128)(2,1)S(1)} collective-permute-done((bf16[7,144,128]{2,1,0:T(8,128)(2,1)}, bf16[7,144,128]{2,1,0:T(8,128)(2,1)S(1)}, u32[]{:S(2)}, u32[]{:S(2)}) %collective-permute-start.3) | collective-permute-done | bytes 258080 | tf_op jit(solution)/shard_map/ppermute | solution.py:411
  120.8 0.0 copy-start.5
  120.8 0.0 copy-done.1
  120.8 0.0 copy-done.4
  120.8 0.7 copy-done.5
  121.5 2.8 %join.1 = bf16[16,304,128]{2,1,0:T(8,128)(2,1)} custom-call(bf16[16,72,128]{2,1,0:T(8,128)(2,1)} %get-tuple-element.25.mixed_ref.mixed, bf16[16,72,128]{2,1,0:T(8,128)(2,1)} %get-tuple-element.29.dq, bf16[16,144,128]{2,1,0:T(8,128)(2,1)} %get-tuple-element.30.given, bf16[7,144,128]{2,1,0:T(8,128)(2,1)} %copy-done.4, bf16[7,144,128]{2,1,0:T(8,128)(2,1)} %copy-done.5, ...), custom_call_target="tpu_custom_call" | custom-call | flops 800000000 | bytes 4000000 | tf_op jit(solution)/shard_map/join/pallas_call | solution.py:365
  124.2 25.1 %all_to_all.21.packed = bf16[16,304,128]{2,1,0:T(8,128)(2,1)} all-to-all(bf16[16,304,128]{2,1,0:T(8,128)(2,1)} %join.1), channel_id=1, replica_groups=mesh['g'=8,'r'=16] {'r'}, dimensions={0} | all-to-all | bytes 2490368 | tf_op jit(solution)/shard_map/all_to_all | solution.py:415
  149.3 4.3 %finish.1 = (bf16[128,1152]{1,0:T(8,128)(2,1)}, bf16[128,1152]{1,0:T(8,128)(2,1)}, bf16[128,1152]{1,0:T(8,128)(2,1)}, bf16[128,1152]{1,0:T(8,128)(2,1)}, f32[9,1152]{1,0:T(8,128)}) custom-call(bf16[16,304,128]{2,1,0:T(8,128)(2,1)} %all_to_all.21.packed, bf16[128,1152]{1,0:T(8,128)(2,1)} %residual.1, s32[128]{0:T(128)} %tags.5, f32[32,1152]{1,0:T(8,128)} %gate.3, ...), custom_call_target="tpu_custom_call" | custom-call | flops 1600000000 | bytes 8000000 | tf_op jit(solution)/shard_map/finish/pallas_call | solution.py:397
  (1 shorter events, 0.0 us)
Async XLA Ops:
  7.2 69.6 %all-gather.3.cloned.1.call-start = ((), (), s32[]{:S(2)}) async-start(), calls=%async_computation.4 | async-start | bytes 5013504 | tf_op jit(solution)/shard_map/all_gather | solution.py:423
  9.4 4.3 %copy-start.2 = (bf16[16,160,128]{2,1,0:T(8,128)(2,1)S(1)}, bf16[16,160,128]{2,1,0:T(8,128)(2,1)}, u32[]{:S(2)}) copy-start(bf16[16,160,128]{2,1,0:T(8,128)(2,1)} %pack_keys.1) | copy-start | bytes 1966084
  34.2 31.2 %copy-start = (bf16[16,160,128]{2,1,0:T(8,128)(2,1)}, bf16[16,160,128]{2,1,0:T(8,128)(2,1)S(1)}, u32[]{:S(2)}) copy-start(bf16[16,160,128]{2,1,0:T(8,128)(2,1)S(1)} %all_to_all.20.keys) | copy-start | bytes 1966084
  34.2 18.9 %all-to-all-start.1 = ((bf16[16,144,128]{2,1,0:T(8,128)(2,1)}), bf16[16,144,128]{2,1,0:T(8,128)(2,1)S(1)}, u32[]{:S(2)}, u32[]{:S(2)}) async-start(bf16[16,144,128]{2,1,0:T(8,128)(2,1)} %get-tuple-element.24), calls=%async_computation.1 | async-start | bytes 1179648 | tf_op jit(solution)/shard_map/all_to_all | solution.py:415
  38.0 25.4 %collective-permute-start.1 = (bf16[7,160,128]{2,1,0:T(8,128)(2,1)S(1)}, bf16[7,160,128]{2,1,0:T(8,128)(2,1)S(1)}, u32[]{:S(2)}, u32[]{:S(2)}) collective-permute-start(bf16[7,160,128]{2,1,0:T(8,128)(2,1)S(1)} %get-tuple-element.39), channel_id=1, source_target_pairs={{16,0},{17,1},{18,2},{19,3},{20,4},{21,5},{22,6},{23,7},{24,8},{25... | collective-permute-start | bytes 860168 | tf_op jit(solution)/shard_map/ppermute | solution.py:411
  39.3 26.1 %collective-permute-start = (bf16[7,160,128]{2,1,0:T(8,128)(2,1)S(1)}, bf16[7,160,128]{2,1,0:T(8,128)(2,1)S(1)}, u32[]{:S(2)}, u32[]{:S(2)}) collective-permute-start(bf16[7,160,128]{2,1,0:T(8,128)(2,1)S(1)} %get-tuple-element.40), channel_id=1, source_target_pairs={{0,16},{1,17},{2,18},{3,19},{4,20},{5,21},{6,22},{7,23},{8,24},{9,... | collective-permute-start | bytes 860168 | tf_op jit(solution)/shard_map/ppermute | solution.py:411
  53.1 12.4 %copy-start.3 = (bf16[16,144,128]{2,1,0:T(8,128)(2,1)}, bf16[16,144,128]{2,1,0:T(8,128)(2,1)S(1)}, u32[]{:S(2)}) copy-start(bf16[16,144,128]{2,1,0:T(8,128)(2,1)S(1)} %all-to-all-done.1.queries) | copy-start | bytes 1769476
  63.5 2.0 %copy-start.6 = (bf16[7,160,128]{2,1,0:T(8,128)(2,1)}, bf16[7,160,128]{2,1,0:T(8,128)(2,1)S(1)}, u32[]{:S(2)}) copy-start(bf16[7,160,128]{2,1,0:T(8,128)(2,1)S(1)} %collective-permute-done.1.right) | copy-start | bytes 860164
  65.5 0.7 copy-start.7
  83.4 28.7 %all-to-all-start.2 = ((bf16[8,144,128]{2,1,0:T(8,128)(2,1)}), bf16[8,144,128]{2,1,0:T(8,128)(2,1)S(1)}, u32[]{:S(2)}, u32[]{:S(2)}) async-start(bf16[8,144,128]{2,1,0:T(8,128)(2,1)} %weight_term.1), calls=%async_computation.2 | async-start | bytes 589824 | tf_op jit(solution)/shard_map/all_to_all | solution.py:415
  105.9 9.6 %collective-permute-start.2 = (bf16[7,144,128]{2,1,0:T(8,128)(2,1)}, bf16[7,144,128]{2,1,0:T(8,128)(2,1)S(1)}, u32[]{:S(2)}, u32[]{:S(2)}) collective-permute-start(bf16[7,144,128]{2,1,0:T(8,128)(2,1)} %get-tuple-element.31), channel_id=1, source_target_pairs={{0,16},{1,17},{2,18},{3,19},{4,20},{5,21},{6,22},{7,23},{8,24},{9,... | collective-permute-start | bytes 774152 | tf_op jit(solution)/shard_map/ppermute | solution.py:411
  110.8 10.0 %collective-permute-start.3 = (bf16[7,144,128]{2,1,0:T(8,128)(2,1)}, bf16[7,144,128]{2,1,0:T(8,128)(2,1)S(1)}, u32[]{:S(2)}, u32[]{:S(2)}) collective-permute-start(bf16[7,144,128]{2,1,0:T(8,128)(2,1)} %get-tuple-element.32), channel_id=1, source_target_pairs={{16,0},{17,1},{18,2},{19,3},{20,4},{21,5},{22,6},{23,7},{24,8},{25... | collective-permute-start | bytes 774152 | tf_op jit(solution)/shard_map/ppermute | solution.py:411
  112.1 8.7 %copy-start.1 = (bf16[8,144,128]{2,1,0:T(8,128)(2,1)}, bf16[8,144,128]{2,1,0:T(8,128)(2,1)S(1)}, u32[]{:S(2)}) copy-start(bf16[8,144,128]{2,1,0:T(8,128)(2,1)S(1)} %all-to-all-done.2.terms) | copy-start | bytes 884740
  115.5 5.3 %copy-start.4 = (bf16[7,144,128]{2,1,0:T(8,128)(2,1)}, bf16[7,144,128]{2,1,0:T(8,128)(2,1)S(1)}, u32[]{:S(2)}) copy-start(bf16[7,144,128]{2,1,0:T(8,128)(2,1)S(1)} %collective-permute-done.2.from_left) | copy-start | bytes 774148
  120.8 0.7 copy-start.5
Sparse Core Ops, SparseCore 0:
  13.8 60.3 all-gather.2

commit v5 on v4

v5 whole, which is shorter than its diff:
```python
import math

import jax
import jax.numpy as jnp
from jax import lax
from jax.experimental import pallas as pl
from jax.experimental.pallas import tpu as pltpu
from jax.sharding import PartitionSpec as P

HEADS = 16
HEAD_DIM = 72
WIDTH = HEADS * HEAD_DIM
TOK = 128
DEVICES = 128
PLANES = 4
PLANE = 32
SIDE = 16
EDGE = 7
SPAN = SIDE + 2 * EDGE
NEAR = SIDE + EDGE
TILE = 256
TILES = SIDE * TOK // TILE
PART = TILE // TOK
STEP = 4
ROOM = SPAN + STEP - 1
CHUNKS = 5
HALF = 40
FULL = 2 * HALF
FINAL = WIDTH // DEVICES
SHARE = WIDTH // PLANES // 2
CLIPS = 32
SCALE = 1.0 / math.sqrt(HEAD_DIM)
SCALE2 = SCALE / math.log(2.0)
FAR = -1e30
BF = jnp.bfloat16
F32 = jnp.float32
VMEM_BYTES = 56 * 1024 * 1024

WHOLE = pl.BlockSpec(memory_space=pltpu.VMEM)


def params():
    return pltpu.CompilerParams(vmem_limit_bytes=VMEM_BYTES)


def cost(micros):
    return pl.CostEstimate(flops=int(micros * 4e8), bytes_accessed=int(micros * 2e6), transcendentals=0)


def mm(left, right):
    return jnp.dot(left, right, preferred_element_type=F32)


def clip_onehot(tags):
    ids = lax.broadcasted_iota(jnp.int32, (CLIPS, TOK), 0)
    return (ids == tags[...].reshape(1, TOK)).astype(F32)


def core():
    return lax.axis_index("dp") % 2


def pick(flag, first, second):
    return jnp.where(jnp.full(first.shape, flag, jnp.int32) == 0, first, second)


def pack_body(query, key, value, out_grad, tags, gate, weight, chunk_ref, mine_ref, theirs_ref):
    gate_t = lax.dot_general(
        gate[...], clip_onehot(tags), (((0,), (0,)), ((), ())),
        precision=lax.Precision.HIGHEST, preferred_element_type=F32,
    )
    branch_t = (out_grad[...].astype(F32).T * gate_t).astype(BF)
    grad_t = mm(weight[...], branch_t)
    wide = branch_t.astype(F32)
    halves = []
    for side in range(2):
        starts = [(2 * plane + side) * SHARE for plane in range(PLANES)]
        halves.append(jnp.concatenate([wide[start : start + SHARE] for start in starts], 0))
    side = core()
    mine_ref[...] = pick(side, halves[0], halves[1]).astype(BF)
    theirs_ref[...] = pick(side, halves[1], halves[0]).astype(BF)
    key_t = key[...].astype(F32).T
    value_t = value[...].astype(F32).T
    query_t = query[...].astype(F32).T
    tag_rows = jnp.broadcast_to(tags[...].reshape(1, TOK).astype(F32) + 1.0, (8, TOK))
    blank = jnp.zeros((8, TOK), F32)
    for head in range(HEADS):
        start = head * HEAD_DIM
        low, high = slice(start, start + HALF), slice(start + HALF, start + HEAD_DIM)
        whole = [key_t[low], value_t[low], query_t[low], grad_t[low]]
        chunk_ref[2 * head] = jnp.concatenate(whole, 0).astype(BF)
        whole = [key_t[high], tag_rows, value_t[high], blank, query_t[high], blank, grad_t[high], blank]
        chunk_ref[2 * head + 1] = jnp.concatenate(whole, 0).astype(BF)


def pack(query, key, value, out_grad, tags, gate, weight):
    half = jax.ShapeDtypeStruct((WIDTH // 2, TOK), BF)
    return pl.pallas_call(
        pack_body,
        out_shape=(jax.ShapeDtypeStruct((PLANE, 2 * FULL, TOK), BF), half, half),
        in_specs=[WHOLE] * 7,
        out_specs=(WHOLE,) * 3,
        compiler_params=params(),
        cost_estimate=cost(5),
        name="pack",
    )(query, key, value, out_grad, tags, gate, weight)


def filled(piece, extra):
    rows = [piece] + extra
    have = sum(part.shape[0] for part in rows)
    if have < TOK:
        rows.append(jnp.zeros((TOK - have, TOK), F32))
    return jnp.concatenate(rows, 0)


def natural(side, own, other):
    own, other = own.astype(F32), other.astype(F32)
    low, high = pick(side, own, other), pick(side, other, own)
    return [jnp.concatenate([low[rows], high[rows]], 0) for rows in (slice(0, HALF), slice(HALF, FULL))]


def window(side, own, near, far_own, far_other):
    for block in range(NEAR):
        at = block + EDGE * (1 - side)
        yield (at,) + tuple(natural(side, own[block + (SIDE - EDGE) * side, 0:FULL], near[block]))
    for block in range(EDGE):
        yield (block + NEAR * side,) + tuple(natural(side, far_own[block], far_other[block]))


def token_rows(block):
    return pl.ds(pl.multiple_of(block * TOK, TOK), TOK)


def same_clip(clip, same, other):
    ids = lax.broadcasted_iota(jnp.int32, (CLIPS, TOK), 0).astype(F32) + 1.0
    return jnp.where(ids == clip, same, other)


def lay_out_keys(block, key, key_n, key_t, clips):
    clip = key[HEAD_DIM : HEAD_DIM + 1]
    clips[block] = key[HEAD_DIM:]
    held = filled(key[0:HEAD_DIM], [same_clip(clip, 0.0, FAR)])
    key_n[token_rows(block), :] = held.T.astype(BF)
    if key_t is not None:
        key_t[block] = jnp.concatenate([key[0:HEAD_DIM], jnp.zeros((8, TOK), F32)], 0).astype(BF)


def key_padding(key_n, key_t):
    rows = slice(SPAN * TOK, ROOM * TOK)
    lane = lax.broadcasted_iota(jnp.int32, ((ROOM - SPAN) * TOK, TOK), 1)
    key_n[rows, :] = jnp.where((lane >= HEAD_DIM) & (lane < HEAD_DIM + CLIPS), FAR, 0.0).astype(BF)
    if key_t is not None:
        for block in range(SPAN, ROOM):
            key_t[block] = jnp.zeros((80, TOK), BF)


def key_ranges(clips, first_ref, count_ref):
    rows = [clips[block][0:1] for block in range(SPAN)]
    rows = [jnp.where(row == 0.0, 100.0, row) if at >= NEAR else row for at, row in enumerate(rows)]
    rows = jnp.concatenate(rows + [jnp.full((32 - SPAN, TOK), 100.0, F32)], 0)
    least = jnp.min(rows, axis=1, keepdims=True)
    most = jnp.max(rows, axis=1, keepdims=True)
    for tile in range(TILES):
        start = EDGE + tile * PART
        low, high = least[start : start + 1], most[start + PART - 1 : start + PART]
        first = jnp.sum(jnp.where(most < low, 1.0, 0.0)).astype(jnp.int32)
        end = jnp.sum(jnp.where(least <= high, 1.0, 0.0)).astype(jnp.int32)
        first_ref[tile] = first
        count_ref[tile] = (end - first + STEP - 1) // STEP


def side_by_side(ref, start):
    return jnp.concatenate([ref[start + at] for at in range(STEP)], 1)


def blocks(first, step):
    start = first + step * STEP
    return start, pl.ds(pl.multiple_of(start * TOK, TOK), STEP * TOK)


def forward_body(
    own, near, asked, far_own, far_other, mixed_ref, stat_ref,
    key_n, value_t, query_t, held, clips, first_ref, count_ref,
):
    side = core()
    for at, key, value in window(side, own, near, far_own, far_other):
        lay_out_keys(at, key, key_n, None, clips)
        value_t[at] = jnp.concatenate([value[0:HEAD_DIM], jnp.ones((8, TOK), F32)], 0).astype(BF)
    for block in range(SPAN, ROOM):
        value_t[block] = jnp.zeros((80, TOK), BF)
    key_padding(key_n, None)
    for block in range(SIDE):
        cols = slice((block % PART) * TOK, (block % PART + 1) * TOK)
        query = natural(side, own[SIDE * side + block, FULL:], asked[block])[0][0:HEAD_DIM]
        query = filled(query, [same_clip(clips[EDGE + block][0:1], 1.0, 0.0)])
        query_t[block // PART, :, cols] = query.astype(BF)
    key_ranges(clips, first_ref, count_ref)

    def query_step(tile, carry):
        first, count = first_ref[tile], count_ref[tile]

        def score_step(step, top):
            scores = mm(key_n[blocks(first, step)[1], :], query_t[tile])
            held[step] = scores
            return jnp.maximum(top, jnp.max(scores, axis=0, keepdims=True))

        top = lax.fori_loop(0, count, score_step, jnp.full((1, TILE), 2.0 * FAR, F32))

        def value_step(step, total):
            weights = jnp.exp2((held[step] - top) * SCALE2).astype(BF)
            return total + mm(side_by_side(value_t, blocks(first, step)[0]), weights)

        total = lax.fori_loop(0, count, value_step, jnp.zeros((80, TILE), F32))
        sums = total[HEAD_DIM : HEAD_DIM + 1]
        mixed = jnp.concatenate([total[0:HEAD_DIM] / sums, jnp.zeros((8, TILE), F32)], 0).astype(BF)
        stat_ref[tile] = jnp.broadcast_to(top * SCALE2 + jnp.log2(sums), (8, TILE))
        for part in range(PART):
            mixed_ref[tile * PART + part] = mixed[:, part * TOK : (part + 1) * TOK]
        return carry

    lax.fori_loop(0, TILES, query_step, 0)


def forward(own, near, asked, far_own, far_other):
    return pl.pallas_call(
        forward_body,
        out_shape=(
            jax.ShapeDtypeStruct((SIDE, FULL, TOK), BF),
            jax.ShapeDtypeStruct((TILES, 8, TILE), F32),
        ),
        in_specs=[WHOLE] * 5,
        out_specs=(WHOLE,) * 2,
        cost_estimate=cost(10),
        scratch_shapes=[
            pltpu.VMEM((ROOM * TOK, TOK), BF),
            pltpu.VMEM((ROOM, 80, TOK), BF),
            pltpu.VMEM((TILES, TOK, TILE), BF),
            pltpu.VMEM((CHUNKS, STEP * TOK, TILE), F32),
            pltpu.VMEM((SPAN, 8, TOK), F32),
            pltpu.SMEM((TILES,), jnp.int32),
            pltpu.SMEM((TILES,), jnp.int32),
        ],
        compiler_params=params(),
        name="forward",
    )(own, near, asked, far_own, far_other)


def backward_body(
    own, near, asked, far_own, far_other, mixed, stat,
    keep_ref, give_ref, keep_near_ref, give_near_ref, keep_far_ref, give_far_ref,
    key_n, key_t, value_n, query_t, query_n, grad_t, grad_n, deltas, dq, dk, dv, clips, first_ref, count_ref,
):
    side = core()
    for at, key, value in window(side, own, near, far_own, far_other):
        lay_out_keys(at, key, key_n, key_t, clips)
        value_n[token_rows(at), :] = filled(value[0:HEAD_DIM], []).T.astype(BF)
    value_n[SPAN * TOK :, :] = jnp.zeros(((ROOM - SPAN) * TOK, TOK), BF)
    key_padding(key_n, key_t)
    for block in range(SIDE):
        tile, cols = block // PART, slice((block % PART) * TOK, (block % PART + 1) * TOK)
        query, grad = natural(side, own[SIDE * side + block, FULL:], asked[block])
        query = filled(query[0:HEAD_DIM], [same_clip(clips[EDGE + block][0:1], 1.0, 0.0)])
        query_t[tile, :, cols] = query.astype(BF)
        query_n[tile, cols, :] = query.T.astype(BF)
        delta = jnp.sum(grad * mixed[block].astype(F32), axis=0, keepdims=True)
        deltas[tile, :, cols] = jnp.broadcast_to(delta, (8, TOK))
        grad = filled(grad, [])
        grad_t[tile, :, cols] = grad.astype(BF)
        grad_n[tile, cols, :] = grad.T.astype(BF)
    key_ranges(clips, first_ref, count_ref)
    dk[...] = jnp.zeros_like(dk)
    dv[...] = jnp.zeros_like(dv)

    def query_step(tile, carry):
        first, count = first_ref[tile], count_ref[tile]
        log_sum = stat[tile, 0:1]
        delta = deltas[tile, 0:1]

        def grad_step(step, total):
            start, rows = blocks(first, step)
            scores = mm(key_n[rows, :], query_t[tile])
            prob = jnp.exp2(scores * SCALE2 - log_sum)
            pull = mm(value_n[rows, :], grad_t[tile])
            dv[rows, :] += mm(prob.astype(BF), grad_n[tile])
            score_grad = (prob * (pull - delta)).astype(BF)
            dk[rows, :] += mm(score_grad, query_n[tile])
            return total + mm(side_by_side(key_t, start), score_grad)

        total = lax.fori_loop(0, count, grad_step, jnp.zeros((80, TILE), F32))
        for part in range(PART):
            dq[tile * PART + part] = total[:, part * TOK : (part + 1) * TOK] * SCALE
        return carry

    lax.fori_loop(0, TILES, query_step, 0)

    def halves(wholes):
        low = jnp.concatenate([whole[0:HALF] for whole in wholes], 0)
        high = jnp.concatenate([whole[HALF:] for whole in wholes], 0)
        return pick(side, low, high).astype(BF), pick(side, high, low).astype(BF)

    def key_grads(at):
        rows = token_rows(at)
        return [dk[rows, :].T[0:FULL] * SCALE, dv[rows, :].T[0:FULL]]

    for block in range(SIDE):
        wholes = [mixed[block].astype(F32), dq[block]] + key_grads(EDGE + block)
        keep_ref[block], give_ref[block] = halves(wholes)
    for block in range(EDGE):
        keep_near_ref[block], give_near_ref[block] = halves(key_grads(block + NEAR * (1 - side)))
        keep_far_ref[block], give_far_ref[block] = halves(key_grads(block + NEAR * side))


def backward(own, near, asked, far_own, far_other, mixed, stat):
    whole = jax.ShapeDtypeStruct((SIDE, 2 * FULL, TOK), BF)
    edge = jax.ShapeDtypeStruct((EDGE, FULL, TOK), BF)
    row_form = pltpu.VMEM((ROOM * TOK, TOK), BF)
    return pl.pallas_call(
        backward_body,
        out_shape=(whole, whole, edge, edge, edge, edge),
        in_specs=[WHOLE] * 7,
        out_specs=(WHOLE,) * 6,
        cost_estimate=cost(14),
        scratch_shapes=[
            row_form, pltpu.VMEM((ROOM, 80, TOK), BF), row_form,
            pltpu.VMEM((TILES, TOK, TILE), BF), pltpu.VMEM((TILES, TILE, TOK), BF),
            pltpu.VMEM((TILES, TOK, TILE), BF), pltpu.VMEM((TILES, TILE, TOK), BF),
            pltpu.VMEM((TILES, 8, TILE), F32),
            pltpu.VMEM((SIDE, FULL, TOK), F32),
            pltpu.VMEM((ROOM * TOK, TOK), F32),
            pltpu.VMEM((ROOM * TOK, TOK), F32),
            pltpu.VMEM((SPAN, 8, TOK), F32),
            pltpu.SMEM((TILES,), jnp.int32),
            pltpu.SMEM((TILES,), jnp.int32),
        ],
        compiler_params=params(),
        name="backward",
    )(own, near, asked, far_own, far_other, mixed, stat)


def weight_term_body(mixed, other, branch, out_ref, total):
    step = pl.program_id(0)
    side = core()
    blocks_here = []
    for at in range(2):
        block = 2 * step + (side if at == 0 else 1 - side)
        place = lax.rem(block, SIDE)
        foreign = jnp.where(block // SIDE == side, 0, 1)
        blocks_here.append(pick(foreign, mixed[place].astype(F32), other[place].astype(F32)))
    right = jnp.concatenate(blocks_here, 1).astype(BF)
    left = jnp.concatenate([branch[0, 0], branch[0, 1]], 1)
    term = lax.dot_general(left, right, (((1,), (1,)), ((), ())), preferred_element_type=F32)

    @pl.when(step == 0)
    def _():
        total[...] = term

    @pl.when(step > 0)
    def _():
        total[...] += term

    @pl.when(step == HEADS - 1)
    def _():
        whole = jnp.concatenate([total[...], jnp.zeros((WIDTH // 2, TOK - FULL), F32)], 1)
        out_ref[...] = whole.astype(BF).reshape(PLANES, SHARE, TOK)


def weight_term(mixed, other, branch):
    return pl.pallas_call(
        weight_term_body,
        grid=(HEADS,),
        out_shape=jax.ShapeDtypeStruct((PLANES, SHARE, TOK), BF),
        in_specs=[
            pl.BlockSpec((SIDE, FULL, TOK), lambda i: (0, 0, 0)),
            pl.BlockSpec((SIDE, FULL, TOK), lambda i: (0, 0, 0)),
            pl.BlockSpec((1, 2, WIDTH // 2, TOK), lambda i: (i, 0, 0, 0)),
        ],
        out_specs=pl.BlockSpec((PLANES, SHARE, TOK), lambda i: (0, 0, 0)),
        scratch_shapes=[pltpu.VMEM((WIDTH // 2, FULL), F32)],
        compiler_params=params(),
        cost_estimate=cost(6),
        name="weight_term",
    )(mixed, other, branch)


def join_body(
    keep, got, keep_near, got_near, got_same, got_cross, term, term1, term2, term3, out_ref, total, pairs
):
    side = core()
    plane = lax.axis_index("dp") // PLANE
    total[0:SHARE] = sum(one.astype(F32) for one in (term[plane], term1[...], term2[...], term3[...]))
    total[SHARE:] = jnp.zeros((8, TOK), F32)
    mine, others = SIDE * side, SIDE * (1 - side)
    for block in range(SIDE):
        pairs[mine + block] = keep[block, FULL:].astype(F32)
        pairs[others + block] = got[block, FULL:].astype(F32)
    late, early = (SIDE - EDGE) * side, (SIDE - EDGE) * (1 - side)
    for block in range(EDGE):
        pairs[others + late + block] += keep_near[block].astype(F32)
        pairs[mine + early + block] += got_near[block].astype(F32)
    for block in range(EDGE):
        pairs[others + early + block] += got_same[block].astype(F32)
        pairs[mine + late + block] += got_cross[block].astype(F32)
    for block in range(SIDE):
        tail = total[block * FINAL : block * FINAL + 16, :]
        for start, asked in ((mine, keep), (others, got)):
            whole = [asked[block, 0:FULL].astype(F32), pairs[start + block], tail]
            out_ref[start + block] = jnp.concatenate(whole, 0).astype(BF)


def join(*values):
    return pl.pallas_call(
        join_body,
        out_shape=jax.ShapeDtypeStruct((PLANE, 2 * FULL + 16, TOK), BF),
        in_specs=[WHOLE] * 10,
        out_specs=WHOLE,
        scratch_shapes=[pltpu.VMEM((SHARE + 8, TOK), F32), pltpu.VMEM((PLANE, FULL, TOK), F32)],
        compiler_params=params(),
        cost_estimate=cost(3),
        name="join",
    )(*values)


def finish_body(packed, residual, tags, gate, weight, bias, out_ref, dq_ref, dk_ref, dv_ref, dw_ref):
    def rows(at):
        low = slice(at * HALF, (at + 1) * HALF)
        high = slice(at * HALF, at * HALF + HEAD_DIM - HALF)
        parts = []
        for head in range(HEADS):
            parts += [packed[2 * head].astype(F32)[low], packed[2 * head + 1].astype(F32)[high]]
        return jnp.concatenate(parts, 0).T.astype(BF)

    gate_rows = lax.dot_general(
        clip_onehot(tags), gate[...], (((0,), (0,)), ((), ())),
        precision=lax.Precision.HIGHEST, preferred_element_type=F32,
    )
    projected = mm(rows(0), weight[...]) + bias[...].reshape(1, WIDTH)
    out_ref[...] = (residual[...].astype(F32) + gate_rows * projected).astype(BF)
    dq_ref[...] = rows(1)
    dk_ref[...] = rows(2)
    dv_ref[...] = rows(3)
    source = lax.rem(lax.axis_index("dp"), PLANE) // SIDE
    tails = [packed[2 * head + source, 2 * FULL :].astype(F32)[:, 0:HEAD_DIM] for head in range(HEADS)]
    dw_ref[...] = jnp.concatenate(tails, 1)[0:FINAL]


def finish(packed, residual, tags, gate, weight, bias):
    return pl.pallas_call(
        finish_body,
        out_shape=(jax.ShapeDtypeStruct((TOK, WIDTH), BF),) * 4 + (jax.ShapeDtypeStruct((FINAL, WIDTH), F32),),
        in_specs=[WHOLE] * 6,
        out_specs=(WHOLE,) * 5,
        compiler_params=params(),
        cost_estimate=cost(4),
        name="finish",
    )(packed, residual, tags, gate, weight, bias)


def sent(values, target):
    pairs = [(i, target(i)) for i in range(DEVICES)]
    return lax.ppermute(values, "dp", [(i, j) for i, j in pairs if 0 <= j < DEVICES])


def other_core(device):
    return device ^ 1


def same_out(device):
    return device + PLANE if device % 2 == 0 else device - PLANE


def same_back(device):
    return device - PLANE if device % 2 == 0 else device + PLANE


def cross(device):
    return device - PLANE + 1 if device % 2 == 0 else device + PLANE - 1


def planes_on(count):
    return lambda device: (device + count * PLANE) % DEVICES


def traded(values):
    groups = [[plane * PLANE + i for i in range(PLANE)] for plane in range(PLANES)]
    return lax.all_to_all(values, "dp", 0, 0, axis_index_groups=groups, tiled=True)


def some_blocks(values, start, rows, count):
    return lax.dynamic_slice(values, (start, rows, 0), (count, FULL, TOK))


def shards(query, key, value, residual, tags, gate, weight, bias, out_grad):
    me = lax.axis_index("dp")
    side, plane = me % 2, me // PLANE
    chunk, branch, branch_away = pack(query, key, value, out_grad, tags, gate, weight)
    branch = jnp.stack([branch, sent(branch_away, other_core)])
    cores = [[plane * PLANE + 2 * chip + at for chip in range(HEADS)] for plane in range(PLANES) for at in range(2)]
    gathered = lax.all_gather(branch, "dp", axis=0, axis_index_groups=cores, tiled=False)
    own = traded(chunk)
    near = sent(some_blocks(own, (SIDE - EDGE) * (1 - side), 0, NEAR), other_core)
    asked = sent(some_blocks(own, SIDE * (1 - side), FULL, SIDE), other_core)
    last = PLANE - EDGE
    far_own = sent(some_blocks(own, last * (1 - side), 0, EDGE), same_out)
    far_other = sent(some_blocks(own, last * side, 0, EDGE), cross)
    mixed, stat = forward(own, near, asked, far_own, far_other)
    mixed_other = sent(mixed, other_core)
    keep, give, keep_near, give_near, keep_far, give_far = backward(
        own, near, asked, far_own, far_other, mixed, stat
    )
    got = sent(give, other_core)
    got_near = sent(give_near, other_core)
    got_same = sent(keep_far, same_back)
    got_cross = sent(give_far, cross)
    term = weight_term(mixed, mixed_other, gathered)
    terms = [sent(lax.dynamic_index_in_dim(term, (plane + k) % PLANES, 0, False), planes_on(k)) for k in (1, 2, 3)]
    packed = traded(join(keep, got, keep_near, got_near, got_same, got_cross, term, *terms))
    block_out, dq, dk, dv, dw = finish(packed, residual, tags, gate, weight, bias)
    return block_out, dq, dk, dv, dw.T


def solution(mesh):
    rows = P("dp", None)
    in_specs = (rows, rows, rows, rows, P("dp"), P(), P(), P(), rows)
    out_specs = (rows,) * 4 + (P(None, "dp"),)
    return jax.shard_map(shards, mesh=mesh, in_specs=in_specs, out_specs=out_specs, check_vma=False)
```

time: 163 us -> 156 us (0.957); the launches traced: 160 us -> 156 us
  blocking collectives: 45.6 us -> 27.3 us
  Pallas kernels: 42.9 us -> 50 us
  local copies, waits for them, and re-layouts: 1.46 us -> 3.75 us
  other arithmetic: 0 us -> 1.65 us
    all_to_all x2 -> x1, blocking collectives: 45.6 us -> 27.3 us  [traded(): lax.all_to_all(values, 'dp', 0, 0, axis_index_groups=groups, tiled=True)]
    all_to_all x2 -> x1, waiting for transfers between devices: 7.2 us -> 24 us  [traded(): lax.all_to_all(values, 'dp', 0, 0, axis_index_groups=groups, tiled=True)]
    ppermute x4 -> x13, waiting for transfers between devices: 21 us -> 5.48 us  [sent(): lax.ppermute(values, 'dp', [(i, j) for i, j in pairs if 0 <= j < DEVICES])]
    pallas_call x6 -> x5, Pallas kernels: 38.6 us -> 45.7 us  [the longest x1 14.1 us: backward(): pl.pallas_call(backward_body, out_shape=(whole, whole, edge, edge, edge,...]
    ppermute x4 -> x13, starting transfers between devices: 14 us -> 20.9 us  [sent(): lax.ppermute(values, 'dp', [(i, j) for i, j in pairs if 0 <= j < DEVICES])]
    all_to_all x2 -> x1, starting transfers between devices: 14 us -> 8.39 us  [traded(): lax.all_to_all(values, 'dp', 0, 0, axis_index_groups=groups, tiled=True)]
    another operation x0 -> x1, other arithmetic: none -> 1.65 us  [shards(): branch = jnp.stack([branch, sent(branch_away, other_core)])]
  transfers between devices with their start and end apart: 7 -> 15, of which waited for: 5 -> 5; matrix products, arithmetic and copies ran while one was open for 0% -> 1% of each run, Pallas kernels for 14% -> 24%
where the time goes in v5:
time: 156 us
  Pallas kernels  50 us (32%)
  waiting for transfers between devices  29.5 us (19%)
  starting transfers between devices  29.4 us (19%)
  blocking collectives  27.3 us (18%)
  between operations  14.3 us (9%)
  local copies, waits for them, and re-layouts  3.75 us (2%)
  other arithmetic  1.65 us (1%)
    all_to_all x1, blocking collectives, traded(): lax.all_to_all(values, 'dp', 0, 0, axis_index_groups=groups, tiled=True)  27.3 us
    all_to_all x1, waiting for transfers between devices, traded(): lax.all_to_all(values, 'dp', 0, 0, axis_index_groups=groups, tiled=True)  24 us
    ppermute x13, starting transfers between devices, sent(): lax.ppermute(values, 'dp', [(i, j) for i, j in pairs if 0 <= j < DEVICES])  20.9 us
    pallas_call x1, Pallas kernels, backward(): pl.pallas_call(backward_body, out_shape=(whole, whole, edge, edge, edge,...  14.1 us
    pallas_call x1, Pallas kernels, forward(): pl.pallas_call(forward_body, out_shape=(jax.ShapeDtypeStruct((SIDE, FULL,...  11.8 us
    pallas_call x1, Pallas kernels, weight_term(): pl.pallas_call(weight_term_body, grid=(HEADS,), out_shape=jax.ShapeDtypeS...  11.2 us
    all_to_all x1, starting transfers between devices, traded(): lax.all_to_all(values, 'dp', 0, 0, axis_index_groups=groups, tiled=True)  8.39 us
    pallas_call x1, Pallas kernels, pack(): pl.pallas_call(pack_body, out_shape=(jax.ShapeDtypeStruct((PLANE, 2 * FUL...  5.55 us
  transfers between devices with their start and end apart: 15, of which 5 were waited for; matrix products, arithmetic and copies ran while one was open for 1% of the time, Pallas kernels for 24%

profile of v5, /device:TPU:1, one launch (start us, length us, event | category | flops | bytes accessed | tf_op | source)
XLA Modules:
  0.0 155.9 jit_solution(18339004672975120206)
XLA Ops:
  7.2 0.0 all-gather.3.cloned.1.call-start
  7.2 5.5 %pack.1 = (bf16[32,160,128]{2,1,0:T(8,128)(2,1)}, bf16[576,128]{1,0:T(8,128)(2,1)}, bf16[576,128]{1,0:T(8,128)(2,1)}) custom-call(bf16[128,1152]{1,0:T(8,128)(2,1)} %query.1, bf16[128,1152]{1,0:T(8,128)(2,1)} %key.1, bf16[128,1152]{1,0:T(8,128)(2,1)} %value.1, bf16[128,1152]{1,0:T(8,128)(2,1)} %out_grad.1, s32[128]{0:T(128)} %tags.3, f32[32,1152]{1,0:T(8,128)} %gate.3, ...), custom_call_target="tpu_custom_call" | custom-call | flops 2000000000 | bytes 10000000 | tf_op jit(solution)/shard_map/pack/pallas_call | solution.py:98
  12.8 1.4 collective-permute-start.9
  14.2 1.2 collective-permute-done.9
  15.4 1.7 %pad_maximum_fusion = bf16[2,576,128]{2,1,0:T(8,128)(2,1)} fusion(bf16[1,576,128]{2,1,0:T(8,128)(2,1)S(1)} %bitcast.11, bf16[1,576,128]{2,1,0:T(8,128)(2,1)} %bitcast.10), kind=kLoop, calls=%fused_computation | loop fusion | flops 147456 | bytes 589824 | tf_op jit(solution)/shard_map/stack | solution.py:497
  17.1 0.0 all-gather.3.cloned.1.call-update
  17.1 8.4 %all-to-all-start = ((bf16[32,160,128]{2,1,0:T(8,128)(2,1)}), bf16[32,160,128]{2,1,0:T(8,128)(2,1)S(1)}, u32[]{:S(2)}, u32[]{:S(2)}) async-start(bf16[32,160,128]{2,1,0:T(8,128)(2,1)} %get-tuple-element.21), calls=%async_computation | async-start | bytes 2621440 | tf_op jit(solution)/shard_map/all_to_all | solution.py:486
  25.5 24.0 %all-to-all-done.own = bf16[32,160,128]{2,1,0:T(8,128)(2,1)S(1)} async-done(((bf16[32,160,128]{2,1,0:T(8,128)(2,1)}), bf16[32,160,128]{2,1,0:T(8,128)(2,1)S(1)}, u32[]{:S(2)}, u32[]{:S(2)}) %all-to-all-start) | async-done | bytes 1310752 | tf_op jit(solution)/shard_map/all_to_all | solution.py:486
  49.5 0.5 collective-permute-start
  50.1 0.1 collective-permute-start.1
  50.2 1.3 collective-permute-start.2
  51.5 6.1 %collective-permute-start.3 = (bf16[7,80,128]{2,1,0:T(8,128)(2,1)S(1)}, bf16[7,80,128]{2,1,0:T(8,128)(2,1)S(1)}, u32[]{:S(2)}, u32[]{:S(2)}) collective-permute-start(bf16[7,80,128]{2,1,0:T(8,128)(2,1)S(1)} %get-tuple-element.37), channel_id=1, source_target_pairs={{1,32},{3,34},{5,36},{7,38},{9,40},{11,42},{13,44},{15,46},{17,48}... | collective-permute-start | bytes 430088 | tf_op jit(solution)/shard_map/ppermute | solution.py:461
  57.6 0.0 collective-permute-done.2.far_own
  57.6 0.0 copy-start.8
  57.6 3.1 %collective-permute-done.3.far_other = bf16[7,80,128]{2,1,0:T(8,128)(2,1)S(1)} collective-permute-done((bf16[7,80,128]{2,1,0:T(8,128)(2,1)S(1)}, bf16[7,80,128]{2,1,0:T(8,128)(2,1)S(1)}, u32[]{:S(2)}, u32[]{:S(2)}) %collective-permute-start.3) | collective-permute-done | bytes 143392 | tf_op jit(solution)/shard_map/ppermute | solution.py:461
  60.8 0.0 collective-permute-done.1.asked
  60.8 0.0 collective-permute-done.near
  60.8 0.0 copy-done
  60.8 0.6 copy-done.9
  61.5 0.1 copy-done.4
  61.6 0.8 copy-done.2
  62.4 11.8 %forward.1 = (bf16[16,80,128]{2,1,0:T(8,128)(2,1)}, f32[8,8,256]{2,1,0:T(8,128)}) custom-call(bf16[32,160,128]{2,1,0:T(8,128)(2,1)} %copy-done, bf16[23,80,128]{2,1,0:T(8,128)(2,1)} %copy-done.2, bf16[16,80,128]{2,1,0:T(8,128)(2,1)} %copy-done.4, bf16[7,80,128]{2,1,0:T(8,128)(2,1)} %copy-done.8, bf16[7,80,128]{2,1,0:T(8,128)(2,1)} %copy-done.9), custom_call_target="tpu_custom_call" | custom-call | flops 4000000000 | bytes 20000000 | tf_op jit(solution)/shard_map/forward/pallas_call | solution.py:226
  74.2 0.0 collective-permute-start.8
  74.2 14.1 %backward.1 = (bf16[16,160,128]{2,1,0:T(8,128)(2,1)}, bf16[16,160,128]{2,1,0:T(8,128)(2,1)}, bf16[7,80,128]{2,1,0:T(8,128)(2,1)}, bf16[7,80,128]{2,1,0:T(8,128)(...) custom-call(bf16[32,160,128]{2,1,0:T(8,128)(2,1)} %copy-done, bf16[23,80,128]{2,1,0:T(8,128)(2,1)} %copy-done.2, ...), custom_call_target="tpu_custom_call" | custom-call | flops 5600000000 | bytes 28000000 | tf_op jit(solution)/shard_map/backward/pallas_call | solution.py:318
  88.3 0.0 collective-permute-start.4
  88.4 0.4 collective-permute-start.5
  88.8 3.4 %collective-permute-start.6 = (bf16[7,80,128]{2,1,0:T(8,128)(2,1)}, bf16[7,80,128]{2,1,0:T(8,128)(2,1)S(1)}, u32[]{:S(2)}, u32[]{:S(2)}) collective-permute-start(bf16[7,80,128]{2,1,0:T(8,128)(2,1)} %get-tuple-element.28), channel_id=1, source_target_pairs={{1,33},{3,35},{5,37},{7,39},{9,41},{11,43},{13,45},{15,47},{17,49}... | collective-permute-start | bytes 430088 | tf_op jit(solution)/shard_map/ppermute | solution.py:461
  92.2 2.2 %collective-permute-start.7 = (bf16[7,80,128]{2,1,0:T(8,128)(2,1)}, bf16[7,80,128]{2,1,0:T(8,128)(2,1)S(1)}, u32[]{:S(2)}, u32[]{:S(2)}) collective-permute-start(bf16[7,80,128]{2,1,0:T(8,128)(2,1)} %get-tuple-element.29), channel_id=1, source_target_pairs={{1,32},{3,34},{5,36},{7,38},{9,40},{11,42},{13,44},{15,46},{17,48}... | collective-permute-start | bytes 430088 | tf_op jit(solution)/shard_map/ppermute | solution.py:461
  94.5 0.0 collective-permute-done.8.other
  94.5 0.0 all-gather.3.cloned.1.call-done
  94.5 0.7 copy-done.3
  95.2 11.2 %weight_term.1.term = bf16[4,144,128]{2,1,0:T(8,128)(2,1)} custom-call(bf16[16,80,128]{2,1,0:T(8,128)(2,1)} %get-tuple-element.22.mixed, bf16[16,80,128]{2,1,0:T(8,128)(2,1)} %copy-done.3, bf16[16,2,576,128]{3,2,1,0:T(8,128)(2,1)} %bitcast.12), custom_call_target="tpu_custom_call" | custom-call | flops 2400000000 | bytes 12000000 | tf_op jit(solution)/shard_map/weight_term/pallas_call | solution.py:369
  106.4 0.8 dynamic-slice_bitcast_fusion
  107.2 1.5 collective-permute-start.10
  108.7 0.0 collective-permute-done.5.got_near
  108.7 2.0 %collective-permute-start.11 = (bf16[144,128]{1,0:T(8,128)(2,1)S(1)}, bf16[144,128]{1,0:T(8,128)(2,1)S(1)}, u32[]{:S(2)}, u32[]{:S(2)}) collective-permute-start(bf16[144,128]{1,0:T(8,128)(2,1)S(1)} %get-tuple-element.40), channel_id=1, source_target_pairs={{0,64},{1,65},{2,66},{3,67},{4,68},{5,69},{6,70},{7,71},{8,72},{9,... | collective-permute-start | bytes 110600 | tf_op jit(solution)/shard_map/ppermute | solution.py:461
  110.7 0.0 collective-permute-done.6.got_same
  110.7 2.0 %collective-permute-start.12 = (bf16[144,128]{1,0:T(8,128)(2,1)S(1)}, bf16[144,128]{1,0:T(8,128)(2,1)S(1)}, u32[]{:S(2)}, u32[]{:S(2)}) collective-permute-start(bf16[144,128]{1,0:T(8,128)(2,1)S(1)} %get-tuple-element.39), channel_id=1, source_target_pairs={{0,96},{1,97},{2,98},{3,99},{4,100},{5,101},{6,102},{7,103},{8,104... | collective-permute-start | bytes 110600 | tf_op jit(solution)/shard_map/ppermute | solution.py:461
  112.6 0.0 collective-permute-done.7.got_cross
  112.7 0.0 collective-permute-done.4.got
  112.7 0.0 collective-permute-done.10.term1
  112.7 0.0 copy-start.10
  112.7 0.3 collective-permute-done.11.term2
  113.0 0.8 collective-permute-done.12.term3
  113.8 0.6 copy-done.12
  114.4 3.0 %join.1 = bf16[32,176,128]{2,1,0:T(8,128)(2,1)} custom-call(bf16[16,160,128]{2,1,0:T(8,128)(2,1)} %get-tuple-element.24.keep, bf16[16,160,128]{2,1,0:T(8,128)(2,1)} %copy-done.1, bf16[7,80,128]{2,1,0:T(8,128)(2,1)} %get-tuple-element.26.keep_near, bf16[7,80,128]{2,1,0:T(8,128)(2,1)} %copy-done.5, bf16[7,80,128]{2,1,0:T(8,128)(2,1)} %copy-done.6, ...), custom_call_target="tpu_custom_call" | custom-call | flops 1200000000 | bytes 6000000 | tf_op jit(solution)/shard_map/join/pallas_call | solution.py:412
  117.4 27.3 %all_to_all.10.packed = bf16[32,176,128]{2,1,0:T(8,128)(2,1)} all-to-all(bf16[32,176,128]{2,1,0:T(8,128)(2,1)} %join.1), channel_id=1, replica_groups={{0,1,2,3,4,5,6,7,8,9,10,11,12,13,14,15,16,17,18,19,20,21,22,23,24,25,26..., dimensions={0} | all-to-all | bytes 2883584 | tf_op jit(solution)/shard_map/all_to_all | solution.py:486
  144.8 4.3 %finish.1 = (bf16[128,1152]{1,0:T(8,128)(2,1)}, bf16[128,1152]{1,0:T(8,128)(2,1)}, bf16[128,1152]{1,0:T(8,128)(2,1)}, bf16[128,1152]{1,0:T(8,128)(2,1)}, f32[9,1152]{1,0:T(8,128)}) custom-call(bf16[32,176,128]{2,1,0:T(8,128)(2,1)} %all_to_all.10.packed, bf16[128,1152]{1,0:T(8,128)(2,1)} %residual.1, s32[128]{0:T(128)} %tags.3, f32[32,1152]{1,0:T(8,128)} %gate.3, ...), custom_call_target="tpu_custom_call" | custom-call | flops 1600000000 | bytes 8000000 | tf_op jit(solution)/shard_map/finish/pallas_call | solution.py:448
  (21 shorter events, 0.1 us)
Async XLA Ops:
  7.2 87.3 %all-gather.3.cloned.1.call-start = ((), (), s32[]{:S(2)}) async-start(), calls=%async_computation.2 | async-start | bytes 5013504 | tf_op jit(solution)/shard_map/all_gather | solution.py:499
  12.8 2.6 %collective-permute-start.9 = (bf16[576,128]{1,0:T(8,128)(2,1)}, bf16[576,128]{1,0:T(8,128)(2,1)S(1)}, u32[]{:S(2)}, u32[]{:S(2)}) collective-permute-start(bf16[576,128]{1,0:T(8,128)(2,1)} %get-tuple-element.31), channel_id=1, source_target_pairs={{0,1},{1,0},{2,3},{3,2},{4,5},{5,4},{6,7},{7,6},{8,9},{9,8},{10,11... | collective-permute-start | bytes 442376 | tf_op jit(solution)/shard_map/ppermute | solution.py:461
  17.1 32.4 %all-to-all-start = ((bf16[32,160,128]{2,1,0:T(8,128)(2,1)}), bf16[32,160,128]{2,1,0:T(8,128)(2,1)S(1)}, u32[]{:S(2)}, u32[]{:S(2)}) async-start(bf16[32,160,128]{2,1,0:T(8,128)(2,1)} %get-tuple-element.21), calls=%async_computation | async-start | bytes 2621440 | tf_op jit(solution)/shard_map/all_to_all | solution.py:486
  49.5 11.3 %copy-start = (bf16[32,160,128]{2,1,0:T(8,128)(2,1)}, bf16[32,160,128]{2,1,0:T(8,128)(2,1)S(1)}, u32[]{:S(2)}) copy-start(bf16[32,160,128]{2,1,0:T(8,128)(2,1)S(1)} %all-to-all-done.own) | copy-start | bytes 3932164
  49.5 11.3 %collective-permute-start = (bf16[23,80,128]{2,1,0:T(8,128)(2,1)S(1)}, bf16[23,80,128]{2,1,0:T(8,128)(2,1)S(1)}, u32[]{:S(2)}, u32[]{:S(2)}) collective-permute-start(bf16[23,80,128]{2,1,0:T(8,128)(2,1)S(1)} %constant_dynamic-slice_fusion.3), channel_id=1, source_target_pairs={{0,1},{1,0},{2,3},{3,2},{4,5},{5,4},{6,7},{7,6},{8,9},{9,8},{10,11... | collective-permute-start | bytes 1413128 | tf_op jit(solution)/shard_map/ppermute | solution.py:461
  50.1 10.7 %collective-permute-start.1 = (bf16[16,80,128]{2,1,0:T(8,128)(2,1)S(1)}, bf16[16,80,128]{2,1,0:T(8,128)(2,1)S(1)}, u32[]{:S(2)}, u32[]{:S(2)}) collective-permute-start(bf16[16,80,128]{2,1,0:T(8,128)(2,1)S(1)} %constant_dynamic-slice_fusion.2), channel_id=1, source_target_pairs={{0,1},{1,0},{2,3},{3,2},{4,5},{5,4},{6,7},{7,6},{8,9},{9,8},{10,11... | collective-permute-start | bytes 983048 | tf_op jit(solution)/shard_map/ppermute | solution.py:461
  50.2 7.4 %collective-permute-start.2 = (bf16[7,80,128]{2,1,0:T(8,128)(2,1)S(1)}, bf16[7,80,128]{2,1,0:T(8,128)(2,1)S(1)}, u32[]{:S(2)}, u32[]{:S(2)}) collective-permute-start(bf16[7,80,128]{2,1,0:T(8,128)(2,1)S(1)} %get-tuple-element.38), channel_id=1, source_target_pairs={{0,32},{2,34},{4,36},{6,38},{8,40},{10,42},{12,44},{14,46},{16,48}... | collective-permute-start | bytes 430088 | tf_op jit(solution)/shard_map/ppermute | solution.py:461
  51.5 9.3 %collective-permute-start.3 = (bf16[7,80,128]{2,1,0:T(8,128)(2,1)S(1)}, bf16[7,80,128]{2,1,0:T(8,128)(2,1)S(1)}, u32[]{:S(2)}, u32[]{:S(2)}) collective-permute-start(bf16[7,80,128]{2,1,0:T(8,128)(2,1)S(1)} %get-tuple-element.37), channel_id=1, source_target_pairs={{1,32},{3,34},{5,36},{7,38},{9,40},{11,42},{13,44},{15,46},{17,48}... | collective-permute-start | bytes 430088 | tf_op jit(solution)/shard_map/ppermute | solution.py:461
  57.6 3.2 %copy-start.8 = (bf16[7,80,128]{2,1,0:T(8,128)(2,1)}, bf16[7,80,128]{2,1,0:T(8,128)(2,1)S(1)}, u32[]{:S(2)}) copy-start(bf16[7,80,128]{2,1,0:T(8,128)(2,1)S(1)} %collective-permute-done.2.far_own) | copy-start | bytes 430084
  60.8 0.7 copy-start.9
  60.8 0.8 copy-start.4
  61.6 0.8 copy-start.2
  74.2 20.3 %collective-permute-start.8 = (bf16[16,80,128]{2,1,0:T(8,128)(2,1)}, bf16[16,80,128]{2,1,0:T(8,128)(2,1)S(1)}, u32[]{:S(2)}, u32[]{:S(2)}) collective-permute-start(bf16[16,80,128]{2,1,0:T(8,128)(2,1)} %get-tuple-element.22.mixed), channel_id=1, source_target_pairs={{0,1},{1,0},{2,3},{3,2},{4,5},{5,4},{6,7},{7,6},{8,9},{9,8},{10,11... | collective-permute-start | bytes 983048 | tf_op jit(solution)/shard_map/ppermute | solution.py:461
  88.3 24.3 %collective-permute-start.4 = (bf16[16,160,128]{2,1,0:T(8,128)(2,1)}, bf16[16,160,128]{2,1,0:T(8,128)(2,1)S(1)}, u32[]{:S(2)}, u32[]{:S(2)}) collective-permute-start(bf16[16,160,128]{2,1,0:T(8,128)(2,1)} %get-tuple-element.25), channel_id=1, source_target_pairs={{0,1},{1,0},{2,3},{3,2},{4,5},{5,4},{6,7},{7,6},{8,9},{9,8},{10,11... | collective-permute-start | bytes 1966088 | tf_op jit(solution)/shard_map/ppermute | solution.py:461
  88.4 20.3 %collective-permute-start.5 = (bf16[7,80,128]{2,1,0:T(8,128)(2,1)}, bf16[7,80,128]{2,1,0:T(8,128)(2,1)S(1)}, u32[]{:S(2)}, u32[]{:S(2)}) collective-permute-start(bf16[7,80,128]{2,1,0:T(8,128)(2,1)} %get-tuple-element.27), channel_id=1, source_target_pairs={{0,1},{1,0},{2,3},{3,2},{4,5},{5,4},{6,7},{7,6},{8,9},{9,8},{10,11... | collective-permute-start | bytes 430088 | tf_op jit(solution)/shard_map/ppermute | solution.py:461
  88.8 21.8 %collective-permute-start.6 = (bf16[7,80,128]{2,1,0:T(8,128)(2,1)}, bf16[7,80,128]{2,1,0:T(8,128)(2,1)S(1)}, u32[]{:S(2)}, u32[]{:S(2)}) collective-permute-start(bf16[7,80,128]{2,1,0:T(8,128)(2,1)} %get-tuple-element.28), channel_id=1, source_target_pairs={{1,33},{3,35},{5,37},{7,39},{9,41},{11,43},{13,45},{15,47},{17,49}... | collective-permute-start | bytes 430088 | tf_op jit(solution)/shard_map/ppermute | solution.py:461
  92.2 20.4 %collective-permute-start.7 = (bf16[7,80,128]{2,1,0:T(8,128)(2,1)}, bf16[7,80,128]{2,1,0:T(8,128)(2,1)S(1)}, u32[]{:S(2)}, u32[]{:S(2)}) collective-permute-start(bf16[7,80,128]{2,1,0:T(8,128)(2,1)} %get-tuple-element.29), channel_id=1, source_target_pairs={{1,32},{3,34},{5,36},{7,38},{9,40},{11,42},{13,44},{15,46},{17,48}... | collective-permute-start | bytes 430088 | tf_op jit(solution)/shard_map/ppermute | solution.py:461
  94.5 0.7 copy-start.3
  107.2 5.5 %collective-permute-start.10 = (bf16[144,128]{1,0:T(8,128)(2,1)S(1)}, bf16[144,128]{1,0:T(8,128)(2,1)S(1)}, u32[]{:S(2)}, u32[]{:S(2)}) collective-permute-start(bf16[144,128]{1,0:T(8,128)(2,1)S(1)} %get-tuple-element.41), channel_id=1, source_target_pairs={{0,32},{1,33},{2,34},{3,35},{4,36},{5,37},{6,38},{7,39},{8,40},{9,... | collective-permute-start | bytes 110600 | tf_op jit(solution)/shard_map/ppermute | solution.py:461
  108.7 5.1 %copy-start.5 = (bf16[7,80,128]{2,1,0:T(8,128)(2,1)}, bf16[7,80,128]{2,1,0:T(8,128)(2,1)S(1)}, u32[]{:S(2)}) copy-start(bf16[7,80,128]{2,1,0:T(8,128)(2,1)S(1)} %collective-permute-done.5.got_near) | copy-start | bytes 430084
  108.7 4.3 %collective-permute-start.11 = (bf16[144,128]{1,0:T(8,128)(2,1)S(1)}, bf16[144,128]{1,0:T(8,128)(2,1)S(1)}, u32[]{:S(2)}, u32[]{:S(2)}) collective-permute-start(bf16[144,128]{1,0:T(8,128)(2,1)S(1)} %get-tuple-element.40), channel_id=1, source_target_pairs={{0,64},{1,65},{2,66},{3,67},{4,68},{5,69},{6,70},{7,71},{8,72},{9,... | collective-permute-start | bytes 110600 | tf_op jit(solution)/shard_map/ppermute | solution.py:461
  110.7 3.1 %copy-start.6 = (bf16[7,80,128]{2,1,0:T(8,128)(2,1)}, bf16[7,80,128]{2,1,0:T(8,128)(2,1)S(1)}, u32[]{:S(2)}) copy-start(bf16[7,80,128]{2,1,0:T(8,128)(2,1)S(1)} %collective-permute-done.6.got_same) | copy-start | bytes 430084
  110.7 3.1 %collective-permute-start.12 = (bf16[144,128]{1,0:T(8,128)(2,1)S(1)}, bf16[144,128]{1,0:T(8,128)(2,1)S(1)}, u32[]{:S(2)}, u32[]{:S(2)}) collective-permute-start(bf16[144,128]{1,0:T(8,128)(2,1)S(1)} %get-tuple-element.39), channel_id=1, source_target_pairs={{0,96},{1,97},{2,98},{3,99},{4,100},{5,101},{6,102},{7,103},{8,104... | collective-permute-start | bytes 110600 | tf_op jit(solution)/shard_map/ppermute | solution.py:461
  112.6 1.1 copy-start.7
  112.7 1.1 copy-start.1
  112.7 1.1 copy-start.10
  113.0 0.8 copy-start.11
  113.8 0.6 copy-start.12
Sparse Core Ops, SparseCore 0:
  17.2 63.5 all-gather.2

commit v6 on v5

--- a/solution.py
+++ b/solution.py
@@ -27,6 +27,7 @@
 HALF = 40
 FULL = 2 * HALF
 FINAL = WIDTH // DEVICES
+CHIPS = 4
 SHARE = WIDTH // PLANES // 2
 CLIPS = 32
 SCALE = 1.0 / math.sqrt(HEAD_DIM)
@@ -34,13 +35,12 @@
 FAR = -1e30
 BF = jnp.bfloat16
 F32 = jnp.float32
-VMEM_BYTES = 56 * 1024 * 1024
 
 WHOLE = pl.BlockSpec(memory_space=pltpu.VMEM)
 
 
-def params():
-    return pltpu.CompilerParams(vmem_limit_bytes=VMEM_BYTES)
+def params(mebibytes):
+    return pltpu.CompilerParams(vmem_limit_bytes=mebibytes * 1024 * 1024)
 
 
 def cost(micros):
@@ -77,7 +77,8 @@
         starts = [(2 * plane + side) * SHARE for plane in range(PLANES)]
         halves.append(jnp.concatenate([wide[start : start + SHARE] for start in starts], 0))
     side = core()
-    mine_ref[...] = pick(side, halves[0], halves[1]).astype(BF)
+    mine_ref[0] = pick(side, halves[0], halves[1]).astype(BF)
+    mine_ref[1] = jnp.zeros((WIDTH // 2, TOK), BF)
     theirs_ref[...] = pick(side, halves[1], halves[0]).astype(BF)
     key_t = key[...].astype(F32).T
     value_t = value[...].astype(F32).T
@@ -95,12 +96,13 @@
 
 def pack(query, key, value, out_grad, tags, gate, weight):
     half = jax.ShapeDtypeStruct((WIDTH // 2, TOK), BF)
+    room = jax.ShapeDtypeStruct((2, WIDTH // 2, TOK), BF)
     return pl.pallas_call(
         pack_body,
-        out_shape=(jax.ShapeDtypeStruct((PLANE, 2 * FULL, TOK), BF), half, half),
+        out_shape=(jax.ShapeDtypeStruct((PLANE, 2 * FULL, TOK), BF), room, half),
         in_specs=[WHOLE] * 7,
         out_specs=(WHOLE,) * 3,
-        compiler_params=params(),
+        compiler_params=params(24),
         cost_estimate=cost(5),
         name="pack",
     )(query, key, value, out_grad, tags, gate, weight)
@@ -179,83 +181,21 @@
     return start, pl.ds(pl.multiple_of(start * TOK, TOK), STEP * TOK)
 
 
-def forward_body(
-    own, near, asked, far_own, far_other, mixed_ref, stat_ref,
-    key_n, value_t, query_t, held, clips, first_ref, count_ref,
-):
-    side = core()
-    for at, key, value in window(side, own, near, far_own, far_other):
-        lay_out_keys(at, key, key_n, None, clips)
-        value_t[at] = jnp.concatenate([value[0:HEAD_DIM], jnp.ones((8, TOK), F32)], 0).astype(BF)
-    for block in range(SPAN, ROOM):
-        value_t[block] = jnp.zeros((80, TOK), BF)
-    key_padding(key_n, None)
-    for block in range(SIDE):
-        cols = slice((block % PART) * TOK, (block % PART + 1) * TOK)
-        query = natural(side, own[SIDE * side + block, FULL:], asked[block])[0][0:HEAD_DIM]
-        query = filled(query, [same_clip(clips[EDGE + block][0:1], 1.0, 0.0)])
-        query_t[block // PART, :, cols] = query.astype(BF)
-    key_ranges(clips, first_ref, count_ref)
-
-    def query_step(tile, carry):
-        first, count = first_ref[tile], count_ref[tile]
-
-        def score_step(step, top):
-            scores = mm(key_n[blocks(first, step)[1], :], query_t[tile])
-            held[step] = scores
-            return jnp.maximum(top, jnp.max(scores, axis=0, keepdims=True))
-
-        top = lax.fori_loop(0, count, score_step, jnp.full((1, TILE), 2.0 * FAR, F32))
-
-        def value_step(step, total):
-            weights = jnp.exp2((held[step] - top) * SCALE2).astype(BF)
-            return total + mm(side_by_side(value_t, blocks(first, step)[0]), weights)
-
-        total = lax.fori_loop(0, count, value_step, jnp.zeros((80, TILE), F32))
-        sums = total[HEAD_DIM : HEAD_DIM + 1]
-        mixed = jnp.concatenate([total[0:HEAD_DIM] / sums, jnp.zeros((8, TILE), F32)], 0).astype(BF)
-        stat_ref[tile] = jnp.broadcast_to(top * SCALE2 + jnp.log2(sums), (8, TILE))
-        for part in range(PART):
-            mixed_ref[tile * PART + part] = mixed[:, part * TOK : (part + 1) * TOK]
-        return carry
-
-    lax.fori_loop(0, TILES, query_step, 0)
-
-
-def forward(own, near, asked, far_own, far_other):
-    return pl.pallas_call(
-        forward_body,
-        out_shape=(
-            jax.ShapeDtypeStruct((SIDE, FULL, TOK), BF),
-            jax.ShapeDtypeStruct((TILES, 8, TILE), F32),
-        ),
-        in_specs=[WHOLE] * 5,
-        out_specs=(WHOLE,) * 2,
-        cost_estimate=cost(10),
-        scratch_shapes=[
-            pltpu.VMEM((ROOM * TOK, TOK), BF),
-            pltpu.VMEM((ROOM, 80, TOK), BF),
-            pltpu.VMEM((TILES, TOK, TILE), BF),
-            pltpu.VMEM((CHUNKS, STEP * TOK, TILE), F32),
-            pltpu.VMEM((SPAN, 8, TOK), F32),
-            pltpu.SMEM((TILES,), jnp.int32),
-            pltpu.SMEM((TILES,), jnp.int32),
-        ],
-        compiler_params=params(),
-        name="forward",
-    )(own, near, asked, far_own, far_other)
-
-
-def backward_body(
-    own, near, asked, far_own, far_other, mixed, stat,
-    keep_ref, give_ref, keep_near_ref, give_near_ref, keep_far_ref, give_far_ref,
-    key_n, key_t, value_n, query_t, query_n, grad_t, grad_n, deltas, dq, dk, dv, clips, first_ref, count_ref,
+def attend_body(
+    own, near, asked, far_own, far_other,
+    mixed_ref, keep_ref, give_ref, keep_near_ref, give_near_ref, keep_far_ref, give_far_ref,
+    key_n, key_t, value_n, value_t, query_t, query_n, grad_t, grad_n, held, mixed_t, dq, dk, dv,
+    clips, first_ref, count_ref,
 ):
     side = core()
     for at, key, value in window(side, own, near, far_own, far_other):
         lay_out_keys(at, key, key_n, key_t, clips)
-        value_n[token_rows(at), :] = filled(value[0:HEAD_DIM], []).T.astype(BF)
+        value = filled(value[0:HEAD_DIM], [jnp.ones((8, TOK), F32)])
+        value_n[token_rows(at), :] = value.T.astype(BF)
+        value_t[at] = value[0:80].astype(BF)
     value_n[SPAN * TOK :, :] = jnp.zeros(((ROOM - SPAN) * TOK, TOK), BF)
+    for block in range(SPAN, ROOM):
+        value_t[block] = jnp.zeros((80, TOK), BF)
     key_padding(key_n, key_t)
     for block in range(SIDE):
         tile, cols = block // PART, slice((block % PART) * TOK, (block % PART + 1) * TOK)
@@ -263,8 +203,6 @@
         query = filled(query[0:HEAD_DIM], [same_clip(clips[EDGE + block][0:1], 1.0, 0.0)])
         query_t[tile, :, cols] = query.astype(BF)
         query_n[tile, cols, :] = query.T.astype(BF)
-        delta = jnp.sum(grad * mixed[block].astype(F32), axis=0, keepdims=True)
-        deltas[tile, :, cols] = jnp.broadcast_to(delta, (8, TOK))
         grad = filled(grad, [])
         grad_t[tile, :, cols] = grad.astype(BF)
         grad_n[tile, cols, :] = grad.T.astype(BF)
@@ -274,22 +212,36 @@
 
     def query_step(tile, carry):
         first, count = first_ref[tile], count_ref[tile]
-        log_sum = stat[tile, 0:1]
-        delta = deltas[tile, 0:1]
+
+        def score_step(step, top):
+            scores = mm(key_n[blocks(first, step)[1], :], query_t[tile])
+            held[step] = scores
+            return jnp.maximum(top, jnp.max(scores, axis=0, keepdims=True))
+
+        top = lax.fori_loop(0, count, score_step, jnp.full((1, TILE), 2.0 * FAR, F32))
+
+        def value_step(step, total):
+            weights = jnp.exp2((held[step] - top) * SCALE2)
+            held[step] = weights
+            return total + mm(side_by_side(value_t, blocks(first, step)[0]), weights.astype(BF))
+
+        total = lax.fori_loop(0, count, value_step, jnp.zeros((80, TILE), F32))
+        inverse = 1.0 / total[HEAD_DIM : HEAD_DIM + 1]
+        mixed = jnp.concatenate([total[0:HEAD_DIM] * inverse, jnp.zeros((8, TILE), F32)], 0).astype(BF)
+        grad = grad_t[tile]
+        delta = jnp.sum(mixed.astype(F32) * grad[0:FULL].astype(F32), axis=0, keepdims=True)
+        mixed_t[tile] = mixed
 
         def grad_step(step, total):
             start, rows = blocks(first, step)
-            scores = mm(key_n[rows, :], query_t[tile])
-            prob = jnp.exp2(scores * SCALE2 - log_sum)
-            pull = mm(value_n[rows, :], grad_t[tile])
+            prob = held[step] * inverse
+            pull = mm(value_n[rows, :], grad)
             dv[rows, :] += mm(prob.astype(BF), grad_n[tile])
             score_grad = (prob * (pull - delta)).astype(BF)
             dk[rows, :] += mm(score_grad, query_n[tile])
             return total + mm(side_by_side(key_t, start), score_grad)
 
-        total = lax.fori_loop(0, count, grad_step, jnp.zeros((80, TILE), F32))
-        for part in range(PART):
-            dq[tile * PART + part] = total[:, part * TOK : (part + 1) * TOK] * SCALE
+        dq[tile] = lax.fori_loop(0, count, grad_step, jnp.zeros((80, TILE), F32)) * SCALE
         return carry
 
     lax.fori_loop(0, TILES, query_step, 0)
@@ -304,81 +256,91 @@
         return [dk[rows, :].T[0:FULL] * SCALE, dv[rows, :].T[0:FULL]]
 
     for block in range(SIDE):
-        wholes = [mixed[block].astype(F32), dq[block]] + key_grads(EDGE + block)
+        tile, cols = block // PART, slice((block % PART) * TOK, (block % PART + 1) * TOK)
+        mixed = mixed_t[tile, :, cols]
+        mixed_ref[block] = mixed
+        wholes = [mixed.astype(F32), dq[tile, :, cols]] + key_grads(EDGE + block)
         keep_ref[block], give_ref[block] = halves(wholes)
     for block in range(EDGE):
         keep_near_ref[block], give_near_ref[block] = halves(key_grads(block + NEAR * (1 - side)))
         keep_far_ref[block], give_far_ref[block] = halves(key_grads(block + NEAR * side))
 
 
-def backward(own, near, asked, far_own, far_other, mixed, stat):
+def attend(own, near, asked, far_own, far_other):
     whole = jax.ShapeDtypeStruct((SIDE, 2 * FULL, TOK), BF)
     edge = jax.ShapeDtypeStruct((EDGE, FULL, TOK), BF)
     row_form = pltpu.VMEM((ROOM * TOK, TOK), BF)
+    column_form = pltpu.VMEM((ROOM, 80, TOK), BF)
     return pl.pallas_call(
-        backward_body,
-        out_shape=(whole, whole, edge, edge, edge, edge),
-        in_specs=[WHOLE] * 7,
-        out_specs=(WHOLE,) * 6,
-        cost_estimate=cost(14),
+        attend_body,
+        out_shape=(jax.ShapeDtypeStruct((SIDE, FULL, TOK), BF), whole, whole, edge, edge, edge, edge),
+        in_specs=[WHOLE] * 5,
+        out_specs=(WHOLE,) * 7,
+        cost_estimate=cost(20),
         scratch_shapes=[
-            row_form, pltpu.VMEM((ROOM, 80, TOK), BF), row_form,
+            row_form, column_form, row_form, column_form,
             pltpu.VMEM((TILES, TOK, TILE), BF), pltpu.VMEM((TILES, TILE, TOK), BF),
             pltpu.VMEM((TILES, TOK, TILE), BF), pltpu.VMEM((TILES, TILE, TOK), BF),
-            pltpu.VMEM((TILES, 8, TILE), F32),
-            pltpu.VMEM((SIDE, FULL, TOK), F32),
+            pltpu.VMEM((CHUNKS, STEP * TOK, TILE), F32),
+            pltpu.VMEM((TILES, FULL, TILE), BF),
+            pltpu.VMEM((TILES, FULL, TILE), F32),
             pltpu.VMEM((ROOM * TOK, TOK), F32),
             pltpu.VMEM((ROOM * TOK, TOK), F32),
             pltpu.VMEM((SPAN, 8, TOK), F32),
             pltpu.SMEM((TILES,), jnp.int32),
             pltpu.SMEM((TILES,), jnp.int32),
         ],
-        compiler_params=params(),
-        name="backward",
-    )(own, near, asked, far_own, far_other, mixed, stat)
-
-
-def weight_term_body(mixed, other, branch, out_ref, total):
+        compiler_params=params(32),
+        name="attend",
+    )(own, near, asked, far_own, far_other)
+
+
+def weight_term_body(mixed, other, branch, *refs):
+    out_refs, total = refs[:PLANES], refs[PLANES]
     step = pl.program_id(0)
     side = core()
-    blocks_here = []
-    for at in range(2):
-        block = 2 * step + (side if at == 0 else 1 - side)
-        place = lax.rem(block, SIDE)
-        foreign = jnp.where(block // SIDE == side, 0, 1)
-        blocks_here.append(pick(foreign, mixed[place].astype(F32), other[place].astype(F32)))
-    right = jnp.concatenate(blocks_here, 1).astype(BF)
-    left = jnp.concatenate([branch[0, 0], branch[0, 1]], 1)
-    term = lax.dot_general(left, right, (((1,), (1,)), ((), ())), preferred_element_type=F32)
+    left, right = [], []
+    for chip in range(CHIPS):
+        for at in range(2):
+            block = 2 * (CHIPS * step + chip) + (side if at == 0 else 1 - side)
+            place = lax.rem(block, SIDE)
+            foreign = jnp.where(block // SIDE == side, 0, 1)
+            right.append(pick(foreign, mixed[place].astype(F32), other[place].astype(F32)))
+            left.append(branch[chip, at])
+    term = lax.dot_general(
+        jnp.concatenate(left, 1), jnp.concatenate(right, 1).astype(BF), (((1,), (1,)), ((), ())),
+        preferred_element_type=F32,
+    )
 
     @pl.when(step == 0)
     def _():
-        total[...] = term
+        total[:, 0:FULL] = term
+        total[:, FULL:] = jnp.zeros((WIDTH // 2, TOK - FULL), F32)
 
     @pl.when(step > 0)
     def _():
-        total[...] += term
-
-    @pl.when(step == HEADS - 1)
+        total[:, 0:FULL] += term
+
+    @pl.when(step == HEADS // CHIPS - 1)
     def _():
-        whole = jnp.concatenate([total[...], jnp.zeros((WIDTH // 2, TOK - FULL), F32)], 1)
-        out_ref[...] = whole.astype(BF).reshape(PLANES, SHARE, TOK)
+        plane = lax.axis_index("dp") // PLANE
+        for away in range(PLANES):
+            start = pl.multiple_of(lax.rem(plane + away, PLANES) * SHARE, 8)
+            out_refs[away][...] = total[pl.ds(start, SHARE), :].astype(BF)
 
 
 def weight_term(mixed, other, branch):
+    share = pl.BlockSpec((SHARE, TOK), lambda i: (0, 0))
+    held = pl.BlockSpec((SIDE, FULL, TOK), lambda i: (0, 0, 0))
     return pl.pallas_call(
         weight_term_body,
-        grid=(HEADS,),
-        out_shape=jax.ShapeDtypeStruct((PLANES, SHARE, TOK), BF),
-        in_specs=[
-            pl.BlockSpec((SIDE, FULL, TOK), lambda i: (0, 0, 0)),
-            pl.BlockSpec((SIDE, FULL, TOK), lambda i: (0, 0, 0)),
-            pl.BlockSpec((1, 2, WIDTH // 2, TOK), lambda i: (i, 0, 0, 0)),
-        ],
-        out_specs=pl.BlockSpec((PLANES, SHARE, TOK), lambda i: (0, 0, 0)),
-        scratch_shapes=[pltpu.VMEM((WIDTH // 2, FULL), F32)],
-        compiler_params=params(),
-        cost_estimate=cost(6),
+        grid=(HEADS // CHIPS,),
+        out_shape=(jax.ShapeDtypeStruct((SHARE, TOK), BF),) * PLANES,
+        in_specs=[held, held, pl.BlockSpec((CHIPS, 2, WIDTH // 2, TOK), lambda i: (i, 0, 0, 0))],
+        out_specs=(share,) * PLANES,
+        scratch_shapes=[pltpu.VMEM((WIDTH // 2, TOK), F32)],
+        compiler_params=params(24),
+        cost_estimate=cost(5),
         name="weight_term",
     )(mixed, other, branch)
 
@@ -387,8 +349,7 @@
     keep, got, keep_near, got_near, got_same, got_cross, term, term1, term2, term3, out_ref, total, pairs
 ):
     side = core()
-    plane = lax.axis_index("dp") // PLANE
-    total[0:SHARE] = sum(one.astype(F32) for one in (term[plane], term1[...], term2[...], term3[...]))
+    total[0:SHARE] = sum(one[...].astype(F32) for one in (term, term1, term2, term3))
     total[SHARE:] = jnp.zeros((8, TOK), F32)
     mine, others = SIDE * side, SIDE * (1 - side)
     for block in range(SIDE):
@@ -415,7 +376,7 @@
         in_specs=[WHOLE] * 10,
         out_specs=WHOLE,
         scratch_shapes=[pltpu.VMEM((SHARE + 8, TOK), F32), pltpu.VMEM((PLANE, FULL, TOK), F32)],
-        compiler_params=params(),
+        compiler_params=params(24),
         cost_estimate=cost(3),
         name="join",
     )(*values)
@@ -450,7 +411,7 @@
         out_shape=(jax.ShapeDtypeStruct((TOK, WIDTH), BF),) * 4 + (jax.ShapeDtypeStruct((FINAL, WIDTH), F32),),
         in_specs=[WHOLE] * 6,
         out_specs=(WHOLE,) * 5,
-        compiler_params=params(),
+        compiler_params=params(24),
         cost_estimate=cost(4),
         name="finish",
     )(packed, residual, tags, gate, weight, bias)
@@ -492,9 +453,9 @@
 
 def shards(query, key, value, residual, tags, gate, weight, bias, out_grad):
     me = lax.axis_index("dp")
-    side, plane = me % 2, me // PLANE
+    side = me % 2
     chunk, branch, branch_away = pack(query, key, value, out_grad, tags, gate, weight)
-    branch = jnp.stack([branch, sent(branch_away, other_core)])
+    branch = lax.dynamic_update_slice(branch, sent(branch_away, other_core)[None], (1, 0, 0))
     cores = [[plane * PLANE + 2 * chip + at for chip in range(HEADS)] for plane in range(PLANES) for at in range(2)]
     gathered = lax.all_gather(branch, "dp", axis=0, axis_index_groups=cores, tiled=False)
     own = traded(chunk)
@@ -503,17 +464,14 @@
     last = PLANE - EDGE
     far_own = sent(some_blocks(own, last * (1 - side), 0, EDGE), same_out)
     far_other = sent(some_blocks(own, last * side, 0, EDGE), cross)
-    mixed, stat = forward(own, near, asked, far_own, far_other)
+    mixed, keep, give, keep_near, give_near, keep_far, give_far = attend(own, near, asked, far_own, far_other)
     mixed_other = sent(mixed, other_core)
-    keep, give, keep_near, give_near, keep_far, give_far = backward(
-        own, near, asked, far_own, far_other, mixed, stat
-    )
     got = sent(give, other_core)
     got_near = sent(give_near, other_core)
     got_same = sent(keep_far, same_back)
     got_cross = sent(give_far, cross)
-    term = weight_term(mixed, mixed_other, gathered)
-    terms = [sent(lax.dynamic_index_in_dim(term, (plane + k) % PLANES, 0, False), planes_on(k)) for k in (1, 2, 3)]
+    term, *terms = weight_term(mixed, mixed_other, gathered)
+    terms = [sent(one, planes_on(away + 1)) for away, one in enumerate(terms)]
     packed = traded(join(keep, got, keep_near, got_near, got_same, got_cross, term, *terms))
     block_out, dq, dk, dv, dw = finish(packed, residual, tags, gate, weight, bias)
     return block_out, dq, dk, dv, dw.T

time: 156 us -> 140 us (0.90)
  Pallas kernels: 50 us -> 27.1 us
  local copies, waits for them, and re-layouts: 3.75 us -> 11.9 us
  other arithmetic: 1.65 us -> 0 us
    pallas_call x3 -> x2, Pallas kernels: 37.1 us -> 21.3 us  [the longest x1 19.1 us: attend(): pl.pallas_call(attend_body, out_shape=(jax.ShapeDtypeStruct((SIDE, FULL,...]
    unnamed x26 -> x36, local copies, waits for them, and re-layouts: 2.85 us -> 11.7 us
    pallas_call x1, Pallas kernels: 3.03 us -> 0.4 us  [join(): pl.pallas_call(join_body, out_shape=jax.ShapeDtypeStruct((PLANE, 2 * FULL...]
    pallas_call x1, Pallas kernels: 4.31 us -> 1.99 us  [finish(): pl.pallas_call(finish_body, out_shape=(jax.ShapeDtypeStruct((TOK, WIDTH),...]
    pallas_call x1, Pallas kernels: 5.55 us -> 3.36 us  [pack(): pl.pallas_call(pack_body, out_shape=(jax.ShapeDtypeStruct((PLANE, 2 * FUL...]
    another operation x1 -> x0, other arithmetic: 1.65 us -> none  [shards(): branch = jnp.stack([branch, sent(branch_away, other_core)])]
  transfers between devices with their start and end apart: 15 -> 15, of which waited for: 5 -> 4; matrix products, arithmetic and copies ran while one was open for 1% -> 0% of each run, Pallas kernels for 24% -> 15%
where the time goes in v6:
time: 140 us
  starting transfers between devices  30 us (21%)
  waiting for transfers between devices  29.6 us (21%)
  Pallas kernels  27.1 us (19%)
  blocking collectives  26.8 us (19%)
  between operations  14.3 us (10%)
  local copies, waits for them, and re-layouts  11.9 us (8%)
    all_to_all x1, blocking collectives, traded(): lax.all_to_all(values, 'dp', 0, 0, axis_index_groups=groups, tiled=True)  26.8 us
    all_to_all x1, waiting for transfers between devices, traded(): lax.all_to_all(values, 'dp', 0, 0, axis_index_groups=groups, tiled=True)  24 us
    ppermute x13, starting transfers between devices, sent(): lax.ppermute(values, 'dp', [(i, j) for i, j in pairs if 0 <= j < DEVICES])  21.5 us
    pallas_call x1, Pallas kernels, attend(): pl.pallas_call(attend_body, out_shape=(jax.ShapeDtypeStruct((SIDE, FULL,...  19.1 us
    unnamed x36, local copies, waits for them, and re-layouts  11.7 us
    all_to_all x1, starting transfers between devices, traded(): lax.all_to_all(values, 'dp', 0, 0, axis_index_groups=groups, tiled=True)  8.39 us
    ppermute x13, waiting for transfers between devices, sent(): lax.ppermute(values, 'dp', [(i, j) for i, j in pairs if 0 <= j < DEVICES])  5.6 us
    pallas_call x1, Pallas kernels, pack(): pl.pallas_call(pack_body, out_shape=(jax.ShapeDtypeStruct((PLANE, 2 * FUL...  3.36 us
  transfers between devices with their start and end apart: 15, of which 4 were waited for; matrix products, arithmetic and copies ran while one was open for 0% of the time, Pallas kernels for 15%

profile of v6, /device:TPU:1, one launch (start us, length us, event | category | flops | bytes accessed | tf_op | source)
XLA Modules:
  0.0 139.5 jit_solution(10195375974152132216)
XLA Ops:
  7.2 0.0 all-gather.2.cloned.1.call-start
  7.2 0.0 copy-start.2
  7.2 1.7 %copy-done.2 = bf16[1152,1152]{1,0:T(8,128)(2,1)S(1)} copy-done((bf16[1152,1152]{1,0:T(8,128)(2,1)S(1)}, bf16[1152,1152]{1,0:T(8,128)(2,1)}, u32[]{:S(2)}) %copy-start.2) | copy-done | bytes 2654232
  9.0 1.0 copy-done.4
  9.9 1.0 copy-done.5
  10.9 1.0 copy-done.6
  11.9 1.0 copy-done.7
  12.8 0.9 copy-done.9
  13.7 0.7 copy-done.12
  14.4 3.4 %pack.1 = (bf16[32,160,128]{2,1,0:T(8,128)(2,1)}, bf16[2,576,128]{2,1,0:T(8,128)(2,1)S(1)}, bf16[576,128]{1,0:T(8,128)(2,1)S(1)}) custom-call(bf16[128,1152]{1,0:T(8,128)(2,1)S(1)} %copy-done.4, bf16[128,1152]{1,0:T(8,128)(2,1)S(1)} %copy-done.5, bf16[128,1152]{1,0:T(8,128)(2,1)S(1)} %copy-done.6, bf16[128,1152]{1,0:T(8,128)(2,1)S(1)} %copy-done.7, ...), custom_call_target="tpu_custom_call" | custom-call | flops 2000000000 | bytes 10000000 | tf_op jit(solution)/shard_map/pack/pallas_call | solution.py:100
  17.7 1.4 %collective-permute-start.9 = (bf16[576,128]{1,0:T(8,128)(2,1)S(1)}, bf16[576,128]{1,0:T(8,128)(2,1)S(1)}, u32[]{:S(2)}, u32[]{:S(2)}) collective-permute-start(bf16[576,128]{1,0:T(8,128)(2,1)S(1)} %get-tuple-element.33), channel_id=1, source_target_pairs={{0,1},{1,0},{2,3},{3,2},{4,5},{5,4},{6,7},{7,6},{8,9},{9,8},{10,11... | collective-permute-start | bytes 442376 | tf_op jit(solution)/shard_map/ppermute | solution.py:422
  19.2 1.0 collective-permute-done.9
  20.2 0.0 copy-start
  20.2 0.7 copy-done
  20.9 0.0 all-gather.2.cloned.1.call-update
  20.9 8.4 %all-to-all-start = ((bf16[32,160,128]{2,1,0:T(8,128)(2,1)}), bf16[32,160,128]{2,1,0:T(8,128)(2,1)S(1)}, u32[]{:S(2)}, u32[]{:S(2)}) async-start(bf16[32,160,128]{2,1,0:T(8,128)(2,1)} %get-tuple-element.24), calls=%async_computation | async-start | bytes 2621440 | tf_op jit(solution)/shard_map/all_to_all | solution.py:447
  29.4 24.0 %all-to-all-done.own = bf16[32,160,128]{2,1,0:T(8,128)(2,1)S(1)} async-done(((bf16[32,160,128]{2,1,0:T(8,128)(2,1)}), bf16[32,160,128]{2,1,0:T(8,128)(2,1)S(1)}, u32[]{:S(2)}, u32[]{:S(2)}) %all-to-all-start) | async-done | bytes 1310752 | tf_op jit(solution)/shard_map/all_to_all | solution.py:447
  53.4 0.5 collective-permute-start
  53.9 0.1 collective-permute-start.1
  54.1 1.3 collective-permute-start.2
  55.4 6.1 %collective-permute-start.3 = (bf16[7,80,128]{2,1,0:T(8,128)(2,1)S(1)}, bf16[7,80,128]{2,1,0:T(8,128)(2,1)S(1)}, u32[]{:S(2)}, u32[]{:S(2)}) collective-permute-start(bf16[7,80,128]{2,1,0:T(8,128)(2,1)S(1)} %get-tuple-element.43), channel_id=1, source_target_pairs={{1,32},{3,34},{5,36},{7,38},{9,40},{11,42},{13,44},{15,46},{17,48}... | collective-permute-start | bytes 430088 | tf_op jit(solution)/shard_map/ppermute | solution.py:422
  61.5 0.0 collective-permute-done.2.far_own
  61.5 2.8 %collective-permute-done.3.far_other = bf16[7,80,128]{2,1,0:T(8,128)(2,1)S(1)} collective-permute-done((bf16[7,80,128]{2,1,0:T(8,128)(2,1)S(1)}, bf16[7,80,128]{2,1,0:T(8,128)(2,1)S(1)}, u32[]{:S(2)}, u32[]{:S(2)}) %collective-permute-start.3) | collective-permute-done | bytes 143392 | tf_op jit(solution)/shard_map/ppermute | solution.py:422
  64.3 0.0 collective-permute-done.1.asked
  64.3 19.1 %attend.1 = (bf16[16,80,128]{2,1,0:T(8,128)(2,1)S(1)}, bf16[16,160,128]{2,1,0:T(8,128)(2,1)S(1)}, bf16[16,160,128]{2,1,0:T(8,128)(2,1)S(1)}, bf16[7,80,128]{2,1,...) custom-call(bf16[32,160,128]{2,1,0:T(8,128)(2,1)S(1)} %all-to-all-do, ...), custom_call_target="tpu_custom_call" | custom-call | flops 8000000000 | bytes 40000000 | tf_op jit(solution)/shard_map/attend/pallas_call | solution.py:274
  83.4 0.9 copy-done.14
  84.3 0.7 copy-done.16
  84.9 0.5 collective-permute-start.8
  85.4 0.0 collective-permute-start.5
  85.4 5.5 %collective-permute-start.6 = (bf16[7,80,128]{2,1,0:T(8,128)(2,1)S(1)}, bf16[7,80,128]{2,1,0:T(8,128)(2,1)S(1)}, u32[]{:S(2)}, u32[]{:S(2)}) collective-permute-start(bf16[7,80,128]{2,1,0:T(8,128)(2,1)S(1)} %get-tuple-element.29), channel_id=1, source_target_pairs={{1,33},{3,35},{5,37},{7,39},{9,41},{11,43},{13,45},{15,47},{17,49}... | collective-permute-start | bytes 430088 | tf_op jit(solution)/shard_map/ppermute | solution.py:422
  90.9 1.9 %collective-permute-start.7 = (bf16[7,80,128]{2,1,0:T(8,128)(2,1)S(1)}, bf16[7,80,128]{2,1,0:T(8,128)(2,1)S(1)}, u32[]{:S(2)}, u32[]{:S(2)}) collective-permute-start(bf16[7,80,128]{2,1,0:T(8,128)(2,1)S(1)} %get-tuple-element.30), channel_id=1, source_target_pairs={{1,32},{3,34},{5,36},{7,38},{9,40},{11,42},{13,44},{15,46},{17,48}... | collective-permute-start | bytes 430088 | tf_op jit(solution)/shard_map/ppermute | solution.py:422
  92.8 0.0 all-gather.2.cloned.1.call-done.branch
  92.9 2.3 %copy-done.1 = bf16[16,2,576,128]{3,2,1,0:T(8,128)(2,1)S(1)} copy-done((bf16[16,2,576,128]{3,2,1,0:T(8,128)(2,1)S(1)}, bf16[16,2,576,128]{3,2,1,0:T(8,128)(2,1)}, u32[]{:S(2)}) %copy-start.1) | copy-done | bytes 4718616
  95.2 2.2 %weight_term.1 = (bf16[144,128]{1,0:T(8,128)(2,1)S(1)}, bf16[144,128]{1,0:T(8,128)(2,1)S(1)}, bf16[144,128]{1,0:T(8,128)(2,1)S(1)}, bf16[144,128]{1,0:T(8,128)(2,1)S(1)}) custom-call(bf16[16,80,128]{2,1,0:T(8,128)(2,1)S(1)} %get-tuple-element.31.mixed, bf16[16,80,128]{2,1,0:T(8,128)(2,1)S(1)} %collective-permute-done.8.other, ...), custom_call_target="tpu_custom_call" | custom-call | flops 2000000000 | bytes 10000000 | tf_op jit(solution)/shard_map/weight_term/pallas_call | solution.py:335
  97.4 1.7 %collective-permute-start.10 = (bf16[144,128]{1,0:T(8,128)(2,1)S(1)}, bf16[144,128]{1,0:T(8,128)(2,1)S(1)}, u32[]{:S(2)}, u32[]{:S(2)}) collective-permute-start(bf16[144,128]{1,0:T(8,128)(2,1)S(1)} %get-tuple-element.35), channel_id=1, source_target_pairs={{0,32},{1,33},{2,34},{3,35},{4,36},{5,37},{6,38},{7,39},{8,40},{9,... | collective-permute-start | bytes 110600 | tf_op jit(solution)/shard_map/ppermute | solution.py:422
  99.1 0.0 collective-permute-done.5.got_near
  99.1 0.0 collective-permute-start.11
  99.1 0.0 collective-permute-done.6.got_same
  99.1 2.5 %collective-permute-start.12 = (bf16[144,128]{1,0:T(8,128)(2,1)S(1)}, bf16[144,128]{1,0:T(8,128)(2,1)S(1)}, u32[]{:S(2)}, u32[]{:S(2)}) collective-permute-start(bf16[144,128]{1,0:T(8,128)(2,1)S(1)} %get-tuple-element.37), channel_id=1, source_target_pairs={{0,96},{1,97},{2,98},{3,99},{4,100},{5,101},{6,102},{7,103},{8,104... | collective-permute-start | bytes 110600 | tf_op jit(solution)/shard_map/ppermute | solution.py:422
  101.6 1.8 %collective-permute-done.11.term2 = bf16[144,128]{1,0:T(8,128)(2,1)S(1)} collective-permute-done((bf16[144,128]{1,0:T(8,128)(2,1)S(1)}, bf16[144,128]{1,0:T(8,128)(2,1)S(1)}, u32[]{:S(2)}, u32[]{:S(2)}) %collective-permute-start.11) | collective-permute-done | bytes 36896 | tf_op jit(solution)/shard_map/ppermute | solution.py:422
  103.4 0.0 copy-start.8
  103.4 0.4 join.1
  103.8 0.0 copy-start.3
  103.8 0.0 copy-start.10
  103.9 0.0 copy-start.11
  103.9 0.0 copy-start.13
  103.9 26.8 %all_to_all.10.packed = bf16[32,176,128]{2,1,0:T(8,128)(2,1)S(1)} all-to-all(bf16[32,176,128]{2,1,0:T(8,128)(2,1)S(1)} %join.1), channel_id=1, replica_groups={{0,1,2,3,4,5,6,7,8,9,10,11,12,13,14,15,16,17,18,19,20,21,22,23,24,25,26..., dimensions={0} | all-to-all | bytes 2883584 | tf_op jit(solution)/shard_map/all_to_all | solution.py:447
  130.7 2.0 %finish.1 = (bf16[128,1152]{1,0:T(8,128)(2,1)}, bf16[128,1152]{1,0:T(8,128)(2,1)}, bf16[128,1152]{1,0:T(8,128)(2,1)}, bf16[128,1152]{1,0:T(8,128)(2,1)}, f32[9,1152]{1,0:T(8,128)}) custom-call(bf16[32,176,128]{2,1,0:T(8,128)(2,1)S(1)} %all_to_all.10.packed, bf16[128,1152]{1,0:T(8,128)(2,1)S(1)} %copy-done.8, s32[128]{0:T(128)S(1)} %copy-done.13, ...), custom_call_target="tpu_custom_call" | custom-call | flops 1600000000 | bytes 8000000 | tf_op jit(solution)/shard_map/finish/pallas_call | solution.py:409
  (29 shorter events, 0.2 us)
Async XLA Ops:
  7.2 85.7 %all-gather.2.cloned.1.call-start = ((), (), s32[]{:S(2)}) async-start(), calls=%async_computation.2 | async-start | bytes 5013504 | tf_op jit(solution)/shard_map/all_gather | solution.py:460
  7.2 1.8 %copy-start.2 = (bf16[1152,1152]{1,0:T(8,128)(2,1)S(1)}, bf16[1152,1152]{1,0:T(8,128)(2,1)}, u32[]{:S(2)}) copy-start(bf16[1152,1152]{1,0:T(8,128)(2,1)} %weight.3) | copy-start | bytes 7962628
  9.0 1.0 copy-start.4
  9.9 1.0 copy-start.5
  10.9 1.0 copy-start.6
  11.9 1.0 copy-start.7
  12.8 0.9 copy-start.9
  13.7 0.7 copy-start.12
  17.7 2.4 %collective-permute-start.9 = (bf16[576,128]{1,0:T(8,128)(2,1)S(1)}, bf16[576,128]{1,0:T(8,128)(2,1)S(1)}, u32[]{:S(2)}, u32[]{:S(2)}) collective-permute-start(bf16[576,128]{1,0:T(8,128)(2,1)S(1)} %get-tuple-element.33), channel_id=1, source_target_pairs={{0,1},{1,0},{2,3},{3,2},{4,5},{5,4},{6,7},{7,6},{8,9},{9,8},{10,11... | collective-permute-start | bytes 442376 | tf_op jit(solution)/shard_map/ppermute | solution.py:422
  20.2 0.7 copy-start
  20.9 32.4 %all-to-all-start = ((bf16[32,160,128]{2,1,0:T(8,128)(2,1)}), bf16[32,160,128]{2,1,0:T(8,128)(2,1)S(1)}, u32[]{:S(2)}, u32[]{:S(2)}) async-start(bf16[32,160,128]{2,1,0:T(8,128)(2,1)} %get-tuple-element.24), calls=%async_computation | async-start | bytes 2621440 | tf_op jit(solution)/shard_map/all_to_all | solution.py:447
  53.4 10.9 %collective-permute-start = (bf16[23,80,128]{2,1,0:T(8,128)(2,1)S(1)}, bf16[23,80,128]{2,1,0:T(8,128)(2,1)S(1)}, u32[]{:S(2)}, u32[]{:S(2)}) collective-permute-start(bf16[23,80,128]{2,1,0:T(8,128)(2,1)S(1)} %constant_dynamic-slice_fusion.3), channel_id=1, source_target_pairs={{0,1},{1,0},{2,3},{3,2},{4,5},{5,4},{6,7},{7,6},{8,9},{9,8},{10,11... | collective-permute-start | bytes 1413128 | tf_op jit(solution)/shard_map/ppermute | solution.py:422
  53.9 10.3 %collective-permute-start.1 = (bf16[16,80,128]{2,1,0:T(8,128)(2,1)S(1)}, bf16[16,80,128]{2,1,0:T(8,128)(2,1)S(1)}, u32[]{:S(2)}, u32[]{:S(2)}) collective-permute-start(bf16[16,80,128]{2,1,0:T(8,128)(2,1)S(1)} %constant_dynamic-slice_fusion.2), channel_id=1, source_target_pairs={{0,1},{1,0},{2,3},{3,2},{4,5},{5,4},{6,7},{7,6},{8,9},{9,8},{10,11... | collective-permute-start | bytes 983048 | tf_op jit(solution)/shard_map/ppermute | solution.py:422
  54.1 7.4 %collective-permute-start.2 = (bf16[7,80,128]{2,1,0:T(8,128)(2,1)S(1)}, bf16[7,80,128]{2,1,0:T(8,128)(2,1)S(1)}, u32[]{:S(2)}, u32[]{:S(2)}) collective-permute-start(bf16[7,80,128]{2,1,0:T(8,128)(2,1)S(1)} %get-tuple-element.44), channel_id=1, source_target_pairs={{0,32},{2,34},{4,36},{6,38},{8,40},{10,42},{12,44},{14,46},{16,48}... | collective-permute-start | bytes 430088 | tf_op jit(solution)/shard_map/ppermute | solution.py:422
  55.4 8.9 %collective-permute-start.3 = (bf16[7,80,128]{2,1,0:T(8,128)(2,1)S(1)}, bf16[7,80,128]{2,1,0:T(8,128)(2,1)S(1)}, u32[]{:S(2)}, u32[]{:S(2)}) collective-permute-start(bf16[7,80,128]{2,1,0:T(8,128)(2,1)S(1)} %get-tuple-element.43), channel_id=1, source_target_pairs={{1,32},{3,34},{5,36},{7,38},{9,40},{11,42},{13,44},{15,46},{17,48}... | collective-permute-start | bytes 430088 | tf_op jit(solution)/shard_map/ppermute | solution.py:422
  83.4 0.9 copy-start.14
  84.3 0.7 copy-start.16
  84.9 16.7 %collective-permute-start.4 = (bf16[16,160,128]{2,1,0:T(8,128)(2,1)S(1)}, bf16[16,160,128]{2,1,0:T(8,128)(2,1)S(1)}, u32[]{:S(2)}, u32[]{:S(2)}) collective-permute-start(bf16[16,160,128]{2,1,0:T(8,128)(2,1)S(1)} %get-tuple-element.26), channel_id=1, source_target_pairs={{0,1},{1,0},{2,3},{3,2},{4,5},{5,4},{6,7},{7,6},{8,9},{9,8},{10,11... | collective-permute-start | bytes 1966088 | tf_op jit(solution)/shard_map/ppermute | solution.py:422
  84.9 7.9 %collective-permute-start.8 = (bf16[16,80,128]{2,1,0:T(8,128)(2,1)S(1)}, bf16[16,80,128]{2,1,0:T(8,128)(2,1)S(1)}, u32[]{:S(2)}, u32[]{:S(2)}) collective-permute-start(bf16[16,80,128]{2,1,0:T(8,128)(2,1)S(1)} %get-tuple-element.31.mixed), channel_id=1, source_target_pairs={{0,1},{1,0},{2,3},{3,2},{4,5},{5,4},{6,7},{7,6},{8,9},{9,8},{10,11... | collective-permute-start | bytes 983048 | tf_op jit(solution)/shard_map/ppermute | solution.py:422
  85.4 13.6 %collective-permute-start.5 = (bf16[7,80,128]{2,1,0:T(8,128)(2,1)S(1)}, bf16[7,80,128]{2,1,0:T(8,128)(2,1)S(1)}, u32[]{:S(2)}, u32[]{:S(2)}) collective-permute-start(bf16[7,80,128]{2,1,0:T(8,128)(2,1)S(1)} %get-tuple-element.28), channel_id=1, source_target_pairs={{0,1},{1,0},{2,3},{3,2},{4,5},{5,4},{6,7},{7,6},{8,9},{9,8},{10,11... | collective-permute-start | bytes 430088 | tf_op jit(solution)/shard_map/ppermute | solution.py:422
  85.4 13.7 %collective-permute-start.6 = (bf16[7,80,128]{2,1,0:T(8,128)(2,1)S(1)}, bf16[7,80,128]{2,1,0:T(8,128)(2,1)S(1)}, u32[]{:S(2)}, u32[]{:S(2)}) collective-permute-start(bf16[7,80,128]{2,1,0:T(8,128)(2,1)S(1)} %get-tuple-element.29), channel_id=1, source_target_pairs={{1,33},{3,35},{5,37},{7,39},{9,41},{11,43},{13,45},{15,47},{17,49}... | collective-permute-start | bytes 430088 | tf_op jit(solution)/shard_map/ppermute | solution.py:422
  90.9 10.7 %collective-permute-start.7 = (bf16[7,80,128]{2,1,0:T(8,128)(2,1)S(1)}, bf16[7,80,128]{2,1,0:T(8,128)(2,1)S(1)}, u32[]{:S(2)}, u32[]{:S(2)}) collective-permute-start(bf16[7,80,128]{2,1,0:T(8,128)(2,1)S(1)} %get-tuple-element.30), channel_id=1, source_target_pairs={{1,32},{3,34},{5,36},{7,38},{9,40},{11,42},{13,44},{15,46},{17,48}... | collective-permute-start | bytes 430088 | tf_op jit(solution)/shard_map/ppermute | solution.py:422
  92.9 2.3 %copy-start.1 = (bf16[16,2,576,128]{3,2,1,0:T(8,128)(2,1)S(1)}, bf16[16,2,576,128]{3,2,1,0:T(8,128)(2,1)}, u32[]{:S(2)}) copy-start(bf16[16,2,576,128]{3,2,1,0:T(8,128)(2,1)} %all-gather.2.cloned.1.call-done.branch) | copy-start | bytes 14155780
  95.2 8.2 %copy-start.15 = (bf16[16,160,128]{2,1,0:T(8,128)(2,1)S(1)}, bf16[16,160,128]{2,1,0:T(8,128)(2,1)}, u32[]{:S(2)}) copy-start(bf16[16,160,128]{2,1,0:T(8,128)(2,1)} %copy-done.14) | copy-start | bytes 1966084
  95.2 8.2 %copy-start.17 = (bf16[7,80,128]{2,1,0:T(8,128)(2,1)S(1)}, bf16[7,80,128]{2,1,0:T(8,128)(2,1)}, u32[]{:S(2)}) copy-start(bf16[7,80,128]{2,1,0:T(8,128)(2,1)} %copy-done.16) | copy-start | bytes 430084
  97.4 4.2 %collective-permute-start.10 = (bf16[144,128]{1,0:T(8,128)(2,1)S(1)}, bf16[144,128]{1,0:T(8,128)(2,1)S(1)}, u32[]{:S(2)}, u32[]{:S(2)}) collective-permute-start(bf16[144,128]{1,0:T(8,128)(2,1)S(1)} %get-tuple-element.35), channel_id=1, source_target_pairs={{0,32},{1,33},{2,34},{3,35},{4,36},{5,37},{6,38},{7,39},{8,40},{9,... | collective-permute-start | bytes 110600 | tf_op jit(solution)/shard_map/ppermute | solution.py:422
  99.1 4.3 %collective-permute-start.11 = (bf16[144,128]{1,0:T(8,128)(2,1)S(1)}, bf16[144,128]{1,0:T(8,128)(2,1)S(1)}, u32[]{:S(2)}, u32[]{:S(2)}) collective-permute-start(bf16[144,128]{1,0:T(8,128)(2,1)S(1)} %get-tuple-element.36), channel_id=1, source_target_pairs={{0,64},{1,65},{2,66},{3,67},{4,68},{5,69},{6,70},{7,71},{8,72},{9,... | collective-permute-start | bytes 110600 | tf_op jit(solution)/shard_map/ppermute | solution.py:422
  99.1 4.3 %collective-permute-start.12 = (bf16[144,128]{1,0:T(8,128)(2,1)S(1)}, bf16[144,128]{1,0:T(8,128)(2,1)S(1)}, u32[]{:S(2)}, u32[]{:S(2)}) collective-permute-start(bf16[144,128]{1,0:T(8,128)(2,1)S(1)} %get-tuple-element.37), channel_id=1, source_target_pairs={{0,96},{1,97},{2,98},{3,99},{4,100},{5,101},{6,102},{7,103},{8,104... | collective-permute-start | bytes 110600 | tf_op jit(solution)/shard_map/ppermute | solution.py:422
  103.4 27.2 %copy-start.8 = (bf16[128,1152]{1,0:T(8,128)(2,1)S(1)}, bf16[128,1152]{1,0:T(8,128)(2,1)}, u32[]{:S(2)}) copy-start(bf16[128,1152]{1,0:T(8,128)(2,1)} %residual.1) | copy-start | bytes 884740
  103.8 26.8 %copy-start.3 = (bf16[1152,1152]{1,0:T(8,128)(2,1)S(1)}, bf16[1152,1152]{1,0:T(8,128)(2,1)}, u32[]{:S(2)}) copy-start(bf16[1152,1152]{1,0:T(8,128)(2,1)} %weight.3) | copy-start | bytes 7962628
  103.8 26.8 %copy-start.10 = (f32[32,1152]{1,0:T(8,128)S(1)}, f32[32,1152]{1,0:T(8,128)}, u32[]{:S(2)}) copy-start(f32[32,1152]{1,0:T(8,128)} %gate.3) | copy-start | bytes 442372
  103.9 26.8 %copy-start.11 = (f32[1152]{0:T(1024)S(1)}, f32[1152]{0:T(1024)}, u32[]{:S(2)}) copy-start(f32[1152]{0:T(1024)} %bias.1) | copy-start | bytes 13828
  103.9 26.8 %copy-start.13 = (s32[128]{0:T(128)S(1)}, s32[128]{0:T(128)}, u32[]{:S(2)}) copy-start(s32[128]{0:T(128)} %tags.3) | copy-start | bytes 1540
Sparse Core Ops, SparseCore 0:
  21.1 63.5 all-gather.1

commit v7 on v6

--- a/solution.py
+++ b/solution.py
@@ -37,6 +37,7 @@
 F32 = jnp.float32
 
 WHOLE = pl.BlockSpec(memory_space=pltpu.VMEM)
+FAR_AWAY = pl.BlockSpec(memory_space=pltpu.HBM)
 
 
 def params(mebibytes):
@@ -64,13 +65,13 @@
     return jnp.where(jnp.full(first.shape, flag, jnp.int32) == 0, first, second)
 
 
-def pack_body(query, key, value, out_grad, tags, gate, weight, chunk_ref, mine_ref, theirs_ref):
+def branch_body(out_grad, tags, gate, branch_ref, mine_ref, theirs_ref):
     gate_t = lax.dot_general(
         gate[...], clip_onehot(tags), (((0,), (0,)), ((), ())),
         precision=lax.Precision.HIGHEST, preferred_element_type=F32,
     )
     branch_t = (out_grad[...].astype(F32).T * gate_t).astype(BF)
-    grad_t = mm(weight[...], branch_t)
+    branch_ref[...] = branch_t
     wide = branch_t.astype(F32)
     halves = []
     for side in range(2):
@@ -80,11 +81,34 @@
     mine_ref[0] = pick(side, halves[0], halves[1]).astype(BF)
     mine_ref[1] = jnp.zeros((WIDTH // 2, TOK), BF)
     theirs_ref[...] = pick(side, halves[1], halves[0]).astype(BF)
+
+
+def branch_columns(out_grad, tags, gate):
+    return pl.pallas_call(
+        branch_body,
+        out_shape=(
+            jax.ShapeDtypeStruct((WIDTH, TOK), BF),
+            jax.ShapeDtypeStruct((2, WIDTH // 2, TOK), BF),
+            jax.ShapeDtypeStruct((WIDTH // 2, TOK), BF),
+        ),
+        in_specs=[WHOLE] * 3,
+        out_specs=(WHOLE,) * 3,
+        compiler_params=params(56),
+        cost_estimate=cost(2),
+        name="branch_columns",
+    )(out_grad, tags, gate)
+
+
+def pack_body(query, key, value, tags, branch, weight, chunk_ref, weight_here, weight_sem):
+    load = pltpu.make_async_copy(weight, weight_here, weight_sem)
+    load.start()
     key_t = key[...].astype(F32).T
     value_t = value[...].astype(F32).T
     query_t = query[...].astype(F32).T
     tag_rows = jnp.broadcast_to(tags[...].reshape(1, TOK).astype(F32) + 1.0, (8, TOK))
     blank = jnp.zeros((8, TOK), F32)
+    load.wait()
+    grad_t = mm(weight_here[...], branch[...])
     for head in range(HEADS):
         start = head * HEAD_DIM
         low, high = slice(start, start + HALF), slice(start + HALF, start + HEAD_DIM)
@@ -94,18 +118,17 @@
         chunk_ref[2 * head + 1] = jnp.concatenate(whole, 0).astype(BF)
 
 
-def pack(query, key, value, out_grad, tags, gate, weight):
-    half = jax.ShapeDtypeStruct((WIDTH // 2, TOK), BF)
-    room = jax.ShapeDtypeStruct((2, WIDTH // 2, TOK), BF)
+def pack(query, key, value, tags, branch, weight):
     return pl.pallas_call(
         pack_body,
-        out_shape=(jax.ShapeDtypeStruct((PLANE, 2 * FULL, TOK), BF), room, half),
-        in_specs=[WHOLE] * 7,
-        out_specs=(WHOLE,) * 3,
-        compiler_params=params(24),
-        cost_estimate=cost(5),
+        out_shape=jax.ShapeDtypeStruct((PLANE, 2 * FULL, TOK), BF),
+        in_specs=[WHOLE] * 5 + [FAR_AWAY],
+        out_specs=WHOLE,
+        scratch_shapes=[pltpu.VMEM((WIDTH, WIDTH), BF), pltpu.SemaphoreType.DMA],
+        compiler_params=params(52),
+        cost_estimate=cost(4),
         name="pack",
-    )(query, key, value, out_grad, tags, gate, weight)
+    )(query, key, value, tags, branch, weight)
 
 
 def filled(piece, extra):
@@ -290,57 +313,54 @@
             pltpu.SMEM((TILES,), jnp.int32),
             pltpu.SMEM((TILES,), jnp.int32),
         ],
-        compiler_params=params(32),
+        compiler_params=params(24),
         name="attend",
     )(own, near, asked, far_own, far_other)
 
 
 def weight_term_body(mixed, other, branch, *refs):
-    out_refs, total = refs[:PLANES], refs[PLANES]
-    step = pl.program_id(0)
+    out_refs, (columns, sems) = refs[:PLANES], refs[PLANES:]
+    loads = []
+    for step in range(HEADS // CHIPS):
+        chips = pl.ds(step * CHIPS, CHIPS)
+        loads.append(pltpu.make_async_copy(branch.at[chips], columns.at[chips], sems.at[step]))
+        loads[-1].start()
     side = core()
-    left, right = [], []
-    for chip in range(CHIPS):
-        for at in range(2):
-            block = 2 * (CHIPS * step + chip) + (side if at == 0 else 1 - side)
-            place = lax.rem(block, SIDE)
-            foreign = jnp.where(block // SIDE == side, 0, 1)
-            right.append(pick(foreign, mixed[place].astype(F32), other[place].astype(F32)))
-            left.append(branch[chip, at])
-    term = lax.dot_general(
-        jnp.concatenate(left, 1), jnp.concatenate(right, 1).astype(BF), (((1,), (1,)), ((), ())),
-        preferred_element_type=F32,
-    )
-
-    @pl.when(step == 0)
-    def _():
-        total[:, 0:FULL] = term
-        total[:, FULL:] = jnp.zeros((WIDTH // 2, TOK - FULL), F32)
-
-    @pl.when(step > 0)
-    def _():
-        total[:, 0:FULL] += term
-
-    @pl.when(step == HEADS // CHIPS - 1)
-    def _():
-        plane = lax.axis_index("dp") // PLANE
-        for away in range(PLANES):
-            start = pl.multiple_of(lax.rem(plane + away, PLANES) * SHARE, 8)
-            out_refs[away][...] = total[pl.ds(start, SHARE), :].astype(BF)
+    right = []
+    for block in range(2 * HEADS):
+        place = lax.rem(2 * (block // 2) + (side if block % 2 == 0 else 1 - side), SIDE)
+        foreign = jnp.where(side == block // SIDE, 0, 1)
+        right.append(pick(foreign, mixed[place].astype(F32), other[place].astype(F32)).astype(BF))
+    total = jnp.zeros((WIDTH // 2, FULL), F32)
+    for step, load in enumerate(loads):
+        load.wait()
+        left = [columns[chip, at] for chip in range(step * CHIPS, (step + 1) * CHIPS) for at in range(2)]
+        total += lax.dot_general(
+            jnp.concatenate(left, 1), jnp.concatenate(right[2 * step * CHIPS : 2 * (step + 1) * CHIPS], 1),
+            (((1,), (1,)), ((), ())), preferred_element_type=F32,
+        )
+    plane = lax.axis_index("dp") // PLANE
+    for away in range(PLANES):
+        share = total[0:SHARE]
+        for at in range(1, PLANES):
+            here = jnp.where(lax.rem(plane + away, PLANES) == at, 1, 0)
+            share = pick(here, share, total[at * SHARE : (at + 1) * SHARE])
+        out_refs[away][:, 0:FULL] = share.astype(BF)
+        out_refs[away][:, FULL:] = jnp.zeros((SHARE, TOK - FULL), BF)
 
 
 def weight_term(mixed, other, branch):
-    share = pl.BlockSpec((SHARE, TOK), lambda i: (0, 0))
-    held = pl.BlockSpec((SIDE, FULL, TOK), lambda i: (0, 0, 0))
     return pl.pallas_call(
         weight_term_body,
-        grid=(HEADS // CHIPS,),
         out_shape=(jax.ShapeDtypeStruct((SHARE, TOK), BF),) * PLANES,
-        in_specs=[held, held, pl.BlockSpec((CHIPS, 2, WIDTH // 2, TOK), lambda i: (i, 0, 0, 0))],
-        out_specs=(share,) * PLANES,
-        scratch_shapes=[pltpu.VMEM((WIDTH // 2, TOK), F32)],
-        compiler_params=params(24),
-        cost_estimate=cost(5),
+        in_specs=[WHOLE, WHOLE, FAR_AWAY],
+        out_specs=(WHOLE,) * PLANES,
+        scratch_shapes=[
+            pltpu.VMEM((HEADS, 2, WIDTH // 2, TOK), BF),
+            pltpu.SemaphoreType.DMA((HEADS // CHIPS,)),
+        ],
+        compiler_params=params(60),
+        cost_estimate=cost(4),
         name="weight_term",
     )(mixed, other, branch)
 
@@ -376,7 +396,7 @@
         in_specs=[WHOLE] * 10,
         out_specs=WHOLE,
         scratch_shapes=[pltpu.VMEM((SHARE + 8, TOK), F32), pltpu.VMEM((PLANE, FULL, TOK), F32)],
-        compiler_params=params(24),
+        compiler_params=params(12),
         cost_estimate=cost(3),
         name="join",
     )(*values)
@@ -411,7 +431,7 @@
         out_shape=(jax.ShapeDtypeStruct((TOK, WIDTH), BF),) * 4 + (jax.ShapeDtypeStruct((FINAL, WIDTH), F32),),
         in_specs=[WHOLE] * 6,
         out_specs=(WHOLE,) * 5,
-        compiler_params=params(24),
+        compiler_params=params(16),
         cost_estimate=cost(4),
         name="finish",
     )(packed, residual, tags, gate, weight, bias)
@@ -454,11 +474,11 @@
 def shards(query, key, value, residual, tags, gate, weight, bias, out_grad):
     me = lax.axis_index("dp")
     side = me % 2
-    chunk, branch, branch_away = pack(query, key, value, out_grad, tags, gate, weight)
+    whole_branch, branch, branch_away = branch_columns(out_grad, tags, gate)
     branch = lax.dynamic_update_slice(branch, sent(branch_away, other_core)[None], (1, 0, 0))
     cores = [[plane * PLANE + 2 * chip + at for chip in range(HEADS)] for plane in range(PLANES) for at in range(2)]
     gathered = lax.all_gather(branch, "dp", axis=0, axis_index_groups=cores, tiled=False)
-    own = traded(chunk)
+    own = traded(pack(query, key, value, tags, whole_branch, weight))
     near = sent(some_blocks(own, (SIDE - EDGE) * (1 - side), 0, NEAR), other_core)
     asked = sent(some_blocks(own, SIDE * (1 - side), FULL, SIDE), other_core)
     last = PLANE - EDGE

time: 140 us -> 139 us (level)
  local copies, waits for them, and re-layouts: 11.9 us -> 4.06 us
  Pallas kernels: 27.1 us -> 34.1 us
    unnamed x36 -> x30, local copies, waits for them, and re-layouts: 11.7 us -> 3.3 us
    pallas_call x2 -> x3, Pallas kernels: 5.52 us -> 12.6 us  [the longest x1 6.17 us: weight_term(): pl.pallas_call(weight_term_body, out_shape=(jax.ShapeDtypeStruct((SHARE,...]
  transfers between devices with their start and end apart: 15 -> 15, of which waited for: 4 -> 5; matrix products, arithmetic and copies ran while one was open for 0% -> 0% of each run, Pallas kernels for 15% -> 21%
where the time goes in v7:
time: 139 us; the launch traced here: 140 us
  Pallas kernels  34.1 us (25%)
  waiting for transfers between devices  30.7 us (22%)
  starting transfers between devices  30.4 us (22%)
  blocking collectives  26.1 us (19%)
  between operations  14.3 us (10%)
  local copies, waits for them, and re-layouts  4.06 us (3%)
    all_to_all x1, blocking collectives, traded(): lax.all_to_all(values, 'dp', 0, 0, axis_index_groups=groups, tiled=True)  26.1 us
    all_to_all x1, waiting for transfers between devices, traded(): lax.all_to_all(values, 'dp', 0, 0, axis_index_groups=groups, tiled=True)  24.2 us
    ppermute x13, starting transfers between devices, sent(): lax.ppermute(values, 'dp', [(i, j) for i, j in pairs if 0 <= j < DEVICES])  22 us
    pallas_call x1, Pallas kernels, attend(): pl.pallas_call(attend_body, out_shape=(jax.ShapeDtypeStruct((SIDE, FULL,...  19.1 us
    all_to_all x1, starting transfers between devices, traded(): lax.all_to_all(values, 'dp', 0, 0, axis_index_groups=groups, tiled=True)  8.38 us
    ppermute x13, waiting for transfers between devices, sent(): lax.ppermute(values, 'dp', [(i, j) for i, j in pairs if 0 <= j < DEVICES])  6.42 us
    pallas_call x1, Pallas kernels, weight_term(): pl.pallas_call(weight_term_body, out_shape=(jax.ShapeDtypeStruct((SHARE,...  6.17 us
    pallas_call x1, Pallas kernels, pack(): pl.pallas_call(pack_body, out_shape=jax.ShapeDtypeStruct((PLANE, 2 * FULL...  3.83 us
  transfers between devices with their start and end apart: 15, of which 5 were waited for; matrix products, arithmetic and copies ran while one was open for 0% of the time, Pallas kernels for 21%

profile of v7, /device:TPU:1, one launch (start us, length us, event | category | flops | bytes accessed | tf_op | source)
XLA Modules:
  0.0 139.8 jit_solution(4430487950705617590)
XLA Ops:
  7.2 0.0 all-gather.2.cloned.1.call-start
  7.3 2.6 %branch_columns.1 = (bf16[1152,128]{1,0:T(8,128)(2,1)}, bf16[2,576,128]{2,1,0:T(8,128)(2,1)}, bf16[576,128]{1,0:T(8,128)(2,1)}) custom-call(bf16[128,1152]{1,0:T(8,128)(2,1)} %out_grad.1, s32[128]{0:T(128)} %tags.5, f32[32,1152]{1,0:T(8,128)} %gate.3), custom_call_target="tpu_custom_call" | custom-call | flops 800000000 | bytes 4000000 | tf_op jit(solution)/shard_map/branch_columns/pallas_call | solution.py:87
  9.9 1.4 %collective-permute-start.9 = (bf16[576,128]{1,0:T(8,128)(2,1)}, bf16[576,128]{1,0:T(8,128)(2,1)S(1)}, u32[]{:S(2)}, u32[]{:S(2)}) collective-permute-start(bf16[576,128]{1,0:T(8,128)(2,1)} %get-tuple-element.33), channel_id=1, source_target_pairs={{0,1},{1,0},{2,3},{3,2},{4,5},{5,4},{6,7},{7,6},{8,9},{9,8},{10,11... | collective-permute-start | bytes 442376 | tf_op jit(solution)/shard_map/ppermute | solution.py:442
  11.3 1.2 collective-permute-done.9
  12.5 0.7 bitcast_dynamic-update-slice_fusion
  13.2 0.0 all-gather.2.cloned.1.call-update
  13.2 0.0 copy-start.11
  13.3 1.0 copy-done.11
  14.2 3.8 %pack.1 = bf16[32,160,128]{2,1,0:T(8,128)(2,1)} custom-call(bf16[128,1152]{1,0:T(8,128)(2,1)S(1)} %copy-done.2, bf16[128,1152]{1,0:T(8,128)(2,1)S(1)} %copy-done.3, bf16[128,1152]{1,0:T(8,128)(2,1)S(1)} %copy-done.4, s32[128]{0:T(128)S(1)} %copy-done.8, bf16[1152,128]{1,0:T(8,128)(2,1)S(1)} %copy-done.11, bf16[1152,1152]{1,0:T(8,128)(2,1)} %weight.3), custom_call_target="tpu_custom_call" | custom-call | flops 1600000000 | bytes 8000000 | tf_op jit(solution)/shard_map/pack/pallas_call | solution.py:122
  18.1 8.4 %all-to-all-start = ((bf16[32,160,128]{2,1,0:T(8,128)(2,1)}), bf16[32,160,128]{2,1,0:T(8,128)(2,1)S(1)}, u32[]{:S(2)}, u32[]{:S(2)}) async-start(bf16[32,160,128]{2,1,0:T(8,128)(2,1)} %pack.1), calls=%async_computation | async-start | bytes 2621440 | tf_op jit(solution)/shard_map/all_to_all | solution.py:467
  26.5 24.2 %all-to-all-done.own = bf16[32,160,128]{2,1,0:T(8,128)(2,1)S(1)} async-done(((bf16[32,160,128]{2,1,0:T(8,128)(2,1)}), bf16[32,160,128]{2,1,0:T(8,128)(2,1)S(1)}, u32[]{:S(2)}, u32[]{:S(2)}) %all-to-all-start) | async-done | bytes 1310752 | tf_op jit(solution)/shard_map/all_to_all | solution.py:467
  50.7 0.8 collective-permute-start
  51.5 0.1 collective-permute-start.1
  51.7 1.3 collective-permute-start.2
  53.0 5.8 %collective-permute-start.3 = (bf16[7,80,128]{2,1,0:T(8,128)(2,1)S(1)}, bf16[7,80,128]{2,1,0:T(8,128)(2,1)S(1)}, u32[]{:S(2)}, u32[]{:S(2)}) collective-permute-start(bf16[7,80,128]{2,1,0:T(8,128)(2,1)S(1)} %get-tuple-element.43), channel_id=1, source_target_pairs={{1,32},{3,34},{5,36},{7,38},{9,40},{11,42},{13,44},{15,46},{17,48}... | collective-permute-start | bytes 430088 | tf_op jit(solution)/shard_map/ppermute | solution.py:442
  58.8 3.2 %collective-permute-done.3.far_other = bf16[7,80,128]{2,1,0:T(8,128)(2,1)S(1)} collective-permute-done((bf16[7,80,128]{2,1,0:T(8,128)(2,1)S(1)}, bf16[7,80,128]{2,1,0:T(8,128)(2,1)S(1)}, u32[]{:S(2)}, u32[]{:S(2)}) %collective-permute-start.3) | collective-permute-done | bytes 143392 | tf_op jit(solution)/shard_map/ppermute | solution.py:442
  61.9 0.0 collective-permute-done.1.asked
  61.9 0.0 collective-permute-done.near
  61.9 19.1 %attend.1 = (bf16[16,80,128]{2,1,0:T(8,128)(2,1)S(1)}, bf16[16,160,128]{2,1,0:T(8,128)(2,1)S(1)}, bf16[16,160,128]{2,1,0:T(8,128)(2,1)S(1)}, bf16[7,80,128]{2,1,...) custom-call(bf16[32,160,128]{2,1,0:T(8,128)(2,1)S(1)} %all-to-all-do, ...), custom_call_target="tpu_custom_call" | custom-call | flops 8000000000 | bytes 40000000 | tf_op jit(solution)/shard_map/attend/pallas_call | solution.py:297
  81.1 0.9 copy-done.9
  81.9 0.7 copy-done.12
  82.6 0.0 collective-permute-start.4
  82.6 0.5 collective-permute-start.8
  83.1 0.0 collective-permute-start.5
  83.1 5.9 %collective-permute-start.6 = (bf16[7,80,128]{2,1,0:T(8,128)(2,1)S(1)}, bf16[7,80,128]{2,1,0:T(8,128)(2,1)S(1)}, u32[]{:S(2)}, u32[]{:S(2)}) collective-permute-start(bf16[7,80,128]{2,1,0:T(8,128)(2,1)S(1)} %get-tuple-element.29), channel_id=1, source_target_pairs={{1,33},{3,35},{5,37},{7,39},{9,41},{11,43},{13,45},{15,47},{17,49}... | collective-permute-start | bytes 430088 | tf_op jit(solution)/shard_map/ppermute | solution.py:442
  89.1 0.0 copy-start.13
  89.1 2.1 %collective-permute-start.7 = (bf16[7,80,128]{2,1,0:T(8,128)(2,1)S(1)}, bf16[7,80,128]{2,1,0:T(8,128)(2,1)S(1)}, u32[]{:S(2)}, u32[]{:S(2)}) collective-permute-start(bf16[7,80,128]{2,1,0:T(8,128)(2,1)S(1)} %get-tuple-element.30), channel_id=1, source_target_pairs={{1,32},{3,34},{5,36},{7,38},{9,40},{11,42},{13,44},{15,46},{17,48}... | collective-permute-start | bytes 430088 | tf_op jit(solution)/shard_map/ppermute | solution.py:442
  91.1 0.0 collective-permute-done.8.other
  91.1 0.0 all-gather.2.cloned.1.call-done.branch
  91.2 6.2 %weight_term.1 = (bf16[144,128]{1,0:T(8,128)(2,1)}, bf16[144,128]{1,0:T(8,128)(2,1)}, bf16[144,128]{1,0:T(8,128)(2,1)}, bf16[144,128]{1,0:T(8,128)(2,1)}) custom-call(bf16[16,80,128]{2,1,0:T(8,128)(2,1)} %copy-done.1, bf16[16,80,128]{2,1,0:T(8,128)(2,1)} %collective-permute-done.8.other, bf16[16,2,576,128]{3,2,1,0:T(8,128)(2,1)} %all-gather.2.cloned.1.call-done.branch), custom_call_target="tpu_custom_call" | custom-call | flops 1600000000 | bytes 8000000 | tf_op jit(solution)/shard_map/weight_term/pallas_call | solution.py:353
  97.4 1.7 %collective-permute-start.10 = (bf16[144,128]{1,0:T(8,128)(2,1)}, bf16[144,128]{1,0:T(8,128)(2,1)S(1)}, u32[]{:S(2)}, u32[]{:S(2)}) collective-permute-start(bf16[144,128]{1,0:T(8,128)(2,1)} %get-tuple-element.35), channel_id=1, source_target_pairs={{0,32},{1,33},{2,34},{3,35},{4,36},{5,37},{6,38},{7,39},{8,40},{9,... | collective-permute-start | bytes 110600 | tf_op jit(solution)/shard_map/ppermute | solution.py:442
  99.1 0.0 collective-permute-done.5.got_near
  99.1 0.0 collective-permute-start.11
  99.1 0.0 collective-permute-done.6.got_same
  99.1 2.5 %collective-permute-start.12 = (bf16[144,128]{1,0:T(8,128)(2,1)}, bf16[144,128]{1,0:T(8,128)(2,1)S(1)}, u32[]{:S(2)}, u32[]{:S(2)}) collective-permute-start(bf16[144,128]{1,0:T(8,128)(2,1)} %get-tuple-element.37), channel_id=1, source_target_pairs={{0,96},{1,97},{2,98},{3,99},{4,100},{5,101},{6,102},{7,103},{8,104... | collective-permute-start | bytes 110600 | tf_op jit(solution)/shard_map/ppermute | solution.py:442
  101.6 0.0 collective-permute-done.7.got_cross
  101.6 0.0 collective-permute-done.4.got
  101.6 0.1 collective-permute-done.10.term1
  101.7 1.9 %collective-permute-done.11.term2 = bf16[144,128]{1,0:T(8,128)(2,1)S(1)} collective-permute-done((bf16[144,128]{1,0:T(8,128)(2,1)}, bf16[144,128]{1,0:T(8,128)(2,1)S(1)}, u32[]{:S(2)}, u32[]{:S(2)}) %collective-permute-start.11) | collective-permute-done | bytes 36896 | tf_op jit(solution)/shard_map/ppermute | solution.py:442
  103.6 0.0 collective-permute-done.12.term3
  103.6 0.0 copy-start.14
  103.6 0.8 copy-done.14
  104.4 0.4 join.1
  104.8 0.0 copy-start
  104.8 0.0 copy-start.6
  104.8 0.0 copy-start.7
  104.8 26.1 %all_to_all.10.packed = bf16[32,176,128]{2,1,0:T(8,128)(2,1)S(1)} all-to-all(bf16[32,176,128]{2,1,0:T(8,128)(2,1)S(1)} %join.1), channel_id=1, replica_groups={{0,1,2,3,4,5,6,7,8,9,10,11,12,13,14,15,16,17,18,19,20,21,22,23,24,25,26..., dimensions={0} | all-to-all | bytes 2883584 | tf_op jit(solution)/shard_map/all_to_all | solution.py:467
  131.0 2.0 %finish.1 = (bf16[128,1152]{1,0:T(8,128)(2,1)}, bf16[128,1152]{1,0:T(8,128)(2,1)}, bf16[128,1152]{1,0:T(8,128)(2,1)}, bf16[128,1152]{1,0:T(8,128)(2,1)}, f32[9,1152]{1,0:T(8,128)}) custom-call(bf16[32,176,128]{2,1,0:T(8,128)(2,1)S(1)} %all_to_all.10.packed, bf16[128,1152]{1,0:T(8,128)(2,1)S(1)} %copy-done.5, s32[128]{0:T(128)S(1)} %copy-done.8, ...), custom_call_target="tpu_custom_call" | custom-call | flops 1600000000 | bytes 8000000 | tf_op jit(solution)/shard_map/finish/pallas_call | solution.py:429
  (24 shorter events, 0.1 us)
Async XLA Ops:
  7.2 6.0 %copy-start.8 = (s32[128]{0:T(128)S(1)}, s32[128]{0:T(128)}, u32[]{:S(2)}) copy-start(s32[128]{0:T(128)} %tags.5) | copy-start | bytes 1540
  7.2 6.0 %copy-start.2 = (bf16[128,1152]{1,0:T(8,128)(2,1)S(1)}, bf16[128,1152]{1,0:T(8,128)(2,1)}, u32[]{:S(2)}) copy-start(bf16[128,1152]{1,0:T(8,128)(2,1)} %query.1) | copy-start | bytes 884740
  7.2 6.0 %copy-start.3 = (bf16[128,1152]{1,0:T(8,128)(2,1)S(1)}, bf16[128,1152]{1,0:T(8,128)(2,1)}, u32[]{:S(2)}) copy-start(bf16[128,1152]{1,0:T(8,128)(2,1)} %key.1) | copy-start | bytes 884740
  7.2 6.0 %copy-start.4 = (bf16[128,1152]{1,0:T(8,128)(2,1)S(1)}, bf16[128,1152]{1,0:T(8,128)(2,1)}, u32[]{:S(2)}) copy-start(bf16[128,1152]{1,0:T(8,128)(2,1)} %value.1) | copy-start | bytes 884740
  7.2 84.0 %all-gather.2.cloned.1.call-start = ((), (), s32[]{:S(2)}) async-start(), calls=%async_computation.2 | async-start | bytes 5013504 | tf_op jit(solution)/shard_map/all_gather | solution.py:480
  9.9 2.6 %collective-permute-start.9 = (bf16[576,128]{1,0:T(8,128)(2,1)}, bf16[576,128]{1,0:T(8,128)(2,1)S(1)}, u32[]{:S(2)}, u32[]{:S(2)}) collective-permute-start(bf16[576,128]{1,0:T(8,128)(2,1)} %get-tuple-element.33), channel_id=1, source_target_pairs={{0,1},{1,0},{2,3},{3,2},{4,5},{5,4},{6,7},{7,6},{8,9},{9,8},{10,11... | collective-permute-start | bytes 442376 | tf_op jit(solution)/shard_map/ppermute | solution.py:442
  13.2 1.0 copy-start.11
  18.1 32.6 %all-to-all-start = ((bf16[32,160,128]{2,1,0:T(8,128)(2,1)}), bf16[32,160,128]{2,1,0:T(8,128)(2,1)S(1)}, u32[]{:S(2)}, u32[]{:S(2)}) async-start(bf16[32,160,128]{2,1,0:T(8,128)(2,1)} %pack.1), calls=%async_computation | async-start | bytes 2621440 | tf_op jit(solution)/shard_map/all_to_all | solution.py:467
  50.7 11.2 %collective-permute-start = (bf16[23,80,128]{2,1,0:T(8,128)(2,1)S(1)}, bf16[23,80,128]{2,1,0:T(8,128)(2,1)S(1)}, u32[]{:S(2)}, u32[]{:S(2)}) collective-permute-start(bf16[23,80,128]{2,1,0:T(8,128)(2,1)S(1)} %constant_dynamic-slice_fusion.3), channel_id=1, source_target_pairs={{0,1},{1,0},{2,3},{3,2},{4,5},{5,4},{6,7},{7,6},{8,9},{9,8},{10,11... | collective-permute-start | bytes 1413128 | tf_op jit(solution)/shard_map/ppermute | solution.py:442
  51.5 10.4 %collective-permute-start.1 = (bf16[16,80,128]{2,1,0:T(8,128)(2,1)S(1)}, bf16[16,80,128]{2,1,0:T(8,128)(2,1)S(1)}, u32[]{:S(2)}, u32[]{:S(2)}) collective-permute-start(bf16[16,80,128]{2,1,0:T(8,128)(2,1)S(1)} %constant_dynamic-slice_fusion.2), channel_id=1, source_target_pairs={{0,1},{1,0},{2,3},{3,2},{4,5},{5,4},{6,7},{7,6},{8,9},{9,8},{10,11... | collective-permute-start | bytes 983048 | tf_op jit(solution)/shard_map/ppermute | solution.py:442
  51.7 7.1 %collective-permute-start.2 = (bf16[7,80,128]{2,1,0:T(8,128)(2,1)S(1)}, bf16[7,80,128]{2,1,0:T(8,128)(2,1)S(1)}, u32[]{:S(2)}, u32[]{:S(2)}) collective-permute-start(bf16[7,80,128]{2,1,0:T(8,128)(2,1)S(1)} %get-tuple-element.44), channel_id=1, source_target_pairs={{0,32},{2,34},{4,36},{6,38},{8,40},{10,42},{12,44},{14,46},{16,48}... | collective-permute-start | bytes 430088 | tf_op jit(solution)/shard_map/ppermute | solution.py:442
  53.0 8.9 %collective-permute-start.3 = (bf16[7,80,128]{2,1,0:T(8,128)(2,1)S(1)}, bf16[7,80,128]{2,1,0:T(8,128)(2,1)S(1)}, u32[]{:S(2)}, u32[]{:S(2)}) collective-permute-start(bf16[7,80,128]{2,1,0:T(8,128)(2,1)S(1)} %get-tuple-element.43), channel_id=1, source_target_pairs={{1,32},{3,34},{5,36},{7,38},{9,40},{11,42},{13,44},{15,46},{17,48}... | collective-permute-start | bytes 430088 | tf_op jit(solution)/shard_map/ppermute | solution.py:442
  81.1 0.9 copy-start.9
  81.9 0.7 copy-start.12
  82.6 8.6 %copy-start.1 = (bf16[16,80,128]{2,1,0:T(8,128)(2,1)}, bf16[16,80,128]{2,1,0:T(8,128)(2,1)S(1)}, u32[]{:S(2)}) copy-start(bf16[16,80,128]{2,1,0:T(8,128)(2,1)S(1)} %get-tuple-element.31.mixed) | copy-start | bytes 983044
  82.6 19.0 %collective-permute-start.4 = (bf16[16,160,128]{2,1,0:T(8,128)(2,1)S(1)}, bf16[16,160,128]{2,1,0:T(8,128)(2,1)S(1)}, u32[]{:S(2)}, u32[]{:S(2)}) collective-permute-start(bf16[16,160,128]{2,1,0:T(8,128)(2,1)S(1)} %get-tuple-element.26), channel_id=1, source_target_pairs={{0,1},{1,0},{2,3},{3,2},{4,5},{5,4},{6,7},{7,6},{8,9},{9,8},{10,11... | collective-permute-start | bytes 1966088 | tf_op jit(solution)/shard_map/ppermute | solution.py:442
  82.6 8.5 %collective-permute-start.8 = (bf16[16,80,128]{2,1,0:T(8,128)(2,1)S(1)}, bf16[16,80,128]{2,1,0:T(8,128)(2,1)}, u32[]{:S(2)}, u32[]{:S(2)}) collective-permute-start(bf16[16,80,128]{2,1,0:T(8,128)(2,1)S(1)} %get-tuple-element.31.mixed), channel_id=1, source_target_pairs={{0,1},{1,0},{2,3},{3,2},{4,5},{5,4},{6,7},{7,6},{8,9},{9,8},{10,11... | collective-permute-start | bytes 983048 | tf_op jit(solution)/shard_map/ppermute | solution.py:442
  83.1 15.9 %collective-permute-start.5 = (bf16[7,80,128]{2,1,0:T(8,128)(2,1)S(1)}, bf16[7,80,128]{2,1,0:T(8,128)(2,1)S(1)}, u32[]{:S(2)}, u32[]{:S(2)}) collective-permute-start(bf16[7,80,128]{2,1,0:T(8,128)(2,1)S(1)} %get-tuple-element.28), channel_id=1, source_target_pairs={{0,1},{1,0},{2,3},{3,2},{4,5},{5,4},{6,7},{7,6},{8,9},{9,8},{10,11... | collective-permute-start | bytes 430088 | tf_op jit(solution)/shard_map/ppermute | solution.py:442
  83.1 15.9 %collective-permute-start.6 = (bf16[7,80,128]{2,1,0:T(8,128)(2,1)S(1)}, bf16[7,80,128]{2,1,0:T(8,128)(2,1)S(1)}, u32[]{:S(2)}, u32[]{:S(2)}) collective-permute-start(bf16[7,80,128]{2,1,0:T(8,128)(2,1)S(1)} %get-tuple-element.29), channel_id=1, source_target_pairs={{1,33},{3,35},{5,37},{7,39},{9,41},{11,43},{13,45},{15,47},{17,49}... | collective-permute-start | bytes 430088 | tf_op jit(solution)/shard_map/ppermute | solution.py:442
  89.1 14.5 %copy-start.10 = (bf16[16,160,128]{2,1,0:T(8,128)(2,1)S(1)}, bf16[16,160,128]{2,1,0:T(8,128)(2,1)}, u32[]{:S(2)}) copy-start(bf16[16,160,128]{2,1,0:T(8,128)(2,1)} %copy-done.9) | copy-start | bytes 1966084
  89.1 14.5 %copy-start.13 = (bf16[7,80,128]{2,1,0:T(8,128)(2,1)S(1)}, bf16[7,80,128]{2,1,0:T(8,128)(2,1)}, u32[]{:S(2)}) copy-start(bf16[7,80,128]{2,1,0:T(8,128)(2,1)} %copy-done.12) | copy-start | bytes 430084
  89.1 12.5 %collective-permute-start.7 = (bf16[7,80,128]{2,1,0:T(8,128)(2,1)S(1)}, bf16[7,80,128]{2,1,0:T(8,128)(2,1)S(1)}, u32[]{:S(2)}, u32[]{:S(2)}) collective-permute-start(bf16[7,80,128]{2,1,0:T(8,128)(2,1)S(1)} %get-tuple-element.30), channel_id=1, source_target_pairs={{1,32},{3,34},{5,36},{7,38},{9,40},{11,42},{13,44},{15,46},{17,48}... | collective-permute-start | bytes 430088 | tf_op jit(solution)/shard_map/ppermute | solution.py:442
  97.4 4.3 %collective-permute-start.10 = (bf16[144,128]{1,0:T(8,128)(2,1)}, bf16[144,128]{1,0:T(8,128)(2,1)S(1)}, u32[]{:S(2)}, u32[]{:S(2)}) collective-permute-start(bf16[144,128]{1,0:T(8,128)(2,1)} %get-tuple-element.35), channel_id=1, source_target_pairs={{0,32},{1,33},{2,34},{3,35},{4,36},{5,37},{6,38},{7,39},{8,40},{9,... | collective-permute-start | bytes 110600 | tf_op jit(solution)/shard_map/ppermute | solution.py:442
  99.1 4.5 %collective-permute-start.11 = (bf16[144,128]{1,0:T(8,128)(2,1)}, bf16[144,128]{1,0:T(8,128)(2,1)S(1)}, u32[]{:S(2)}, u32[]{:S(2)}) collective-permute-start(bf16[144,128]{1,0:T(8,128)(2,1)} %get-tuple-element.36), channel_id=1, source_target_pairs={{0,64},{1,65},{2,66},{3,67},{4,68},{5,69},{6,70},{7,71},{8,72},{9,... | collective-permute-start | bytes 110600 | tf_op jit(solution)/shard_map/ppermute | solution.py:442
  99.1 4.5 %collective-permute-start.12 = (bf16[144,128]{1,0:T(8,128)(2,1)}, bf16[144,128]{1,0:T(8,128)(2,1)S(1)}, u32[]{:S(2)}, u32[]{:S(2)}) collective-permute-start(bf16[144,128]{1,0:T(8,128)(2,1)} %get-tuple-element.37), channel_id=1, source_target_pairs={{0,96},{1,97},{2,98},{3,99},{4,100},{5,101},{6,102},{7,103},{8,104... | collective-permute-start | bytes 110600 | tf_op jit(solution)/shard_map/ppermute | solution.py:442
  103.6 0.8 copy-start.14
  104.4 26.6 %copy-start.5 = (bf16[128,1152]{1,0:T(8,128)(2,1)S(1)}, bf16[128,1152]{1,0:T(8,128)(2,1)}, u32[]{:S(2)}) copy-start(bf16[128,1152]{1,0:T(8,128)(2,1)} %residual.1) | copy-start | bytes 884740
  104.8 26.2 %copy-start = (bf16[1152,1152]{1,0:T(8,128)(2,1)S(1)}, bf16[1152,1152]{1,0:T(8,128)(2,1)}, u32[]{:S(2)}) copy-start(bf16[1152,1152]{1,0:T(8,128)(2,1)} %weight.3) | copy-start | bytes 7962628
  104.8 26.2 %copy-start.6 = (f32[32,1152]{1,0:T(8,128)S(1)}, f32[32,1152]{1,0:T(8,128)}, u32[]{:S(2)}) copy-start(f32[32,1152]{1,0:T(8,128)} %gate.3) | copy-start | bytes 442372
  104.8 26.2 %copy-start.7 = (f32[1152]{0:T(1024)S(1)}, f32[1152]{0:T(1024)}, u32[]{:S(2)}) copy-start(f32[1152]{0:T(1024)} %bias.1) | copy-start | bytes 13828
Sparse Core Ops, SparseCore 0:
  13.3 66.2 all-gather.1

commit v8 on v6

--- a/solution.py
+++ b/solution.py
@@ -37,6 +37,7 @@
 F32 = jnp.float32
 
 WHOLE = pl.BlockSpec(memory_space=pltpu.VMEM)
+FAR_AWAY = pl.BlockSpec(memory_space=pltpu.HBM)
 
 
 def params(mebibytes):
@@ -64,13 +65,13 @@
     return jnp.where(jnp.full(first.shape, flag, jnp.int32) == 0, first, second)
 
 
-def pack_body(query, key, value, out_grad, tags, gate, weight, chunk_ref, mine_ref, theirs_ref):
+def branch_body(out_grad, tags, gate, branch_ref, mine_ref, theirs_ref):
     gate_t = lax.dot_general(
         gate[...], clip_onehot(tags), (((0,), (0,)), ((), ())),
         precision=lax.Precision.HIGHEST, preferred_element_type=F32,
     )
     branch_t = (out_grad[...].astype(F32).T * gate_t).astype(BF)
-    grad_t = mm(weight[...], branch_t)
+    branch_ref[...] = branch_t
     wide = branch_t.astype(F32)
     halves = []
     for side in range(2):
@@ -80,11 +81,54 @@
     mine_ref[0] = pick(side, halves[0], halves[1]).astype(BF)
     mine_ref[1] = jnp.zeros((WIDTH // 2, TOK), BF)
     theirs_ref[...] = pick(side, halves[1], halves[0]).astype(BF)
+
+
+def branch_columns(out_grad, tags, gate):
+    return pl.pallas_call(
+        branch_body,
+        out_shape=(
+            jax.ShapeDtypeStruct((WIDTH, TOK), BF),
+            jax.ShapeDtypeStruct((2, WIDTH // 2, TOK), BF),
+            jax.ShapeDtypeStruct((WIDTH // 2, TOK), BF),
+        ),
+        in_specs=[WHOLE] * 3,
+        out_specs=(WHOLE,) * 3,
+        compiler_params=params(56),
+        cost_estimate=cost(2),
+        name="branch_columns",
+    )(out_grad, tags, gate)
+
+
+def fill_body(_, got, out_ref, sem):
+    load = pltpu.make_async_copy(got, out_ref.at[1], sem)
+    load.start()
+    load.wait()
+
+
+def fill(branch, got):
+    return pl.pallas_call(
+        fill_body,
+        out_shape=jax.ShapeDtypeStruct(branch.shape, BF),
+        in_specs=[FAR_AWAY] * 2,
+        out_specs=FAR_AWAY,
+        input_output_aliases={0: 0},
+        scratch_shapes=[pltpu.SemaphoreType.DMA],
+        compiler_params=params(16),
+        cost_estimate=cost(1),
+        name="fill",
+    )(branch, got)
+
+
+def pack_body(query, key, value, tags, branch, weight, chunk_ref, weight_here, weight_sem):
+    load = pltpu.make_async_copy(weight, weight_here, weight_sem)
+    load.start()
     key_t = key[...].astype(F32).T
     value_t = value[...].astype(F32).T
     query_t = query[...].astype(F32).T
     tag_rows = jnp.broadcast_to(tags[...].reshape(1, TOK).astype(F32) + 1.0, (8, TOK))
     blank = jnp.zeros((8, TOK), F32)
+    load.wait()
+    grad_t = mm(weight_here[...], branch[...])
     for head in range(HEADS):
         start = head * HEAD_DIM
         low, high = slice(start, start + HALF), slice(start + HALF, start + HEAD_DIM)
@@ -94,18 +138,17 @@
         chunk_ref[2 * head + 1] = jnp.concatenate(whole, 0).astype(BF)
 
 
-def pack(query, key, value, out_grad, tags, gate, weight):
-    half = jax.ShapeDtypeStruct((WIDTH // 2, TOK), BF)
-    room = jax.ShapeDtypeStruct((2, WIDTH // 2, TOK), BF)
+def pack(query, key, value, tags, branch, weight):
     return pl.pallas_call(
         pack_body,
-        out_shape=(jax.ShapeDtypeStruct((PLANE, 2 * FULL, TOK), BF), room, half),
-        in_specs=[WHOLE] * 7,
-        out_specs=(WHOLE,) * 3,
-        compiler_params=params(24),
-        cost_estimate=cost(5),
+        out_shape=jax.ShapeDtypeStruct((PLANE, 2 * FULL, TOK), BF),
+        in_specs=[WHOLE] * 5 + [FAR_AWAY],
+        out_specs=WHOLE,
+        scratch_shapes=[pltpu.VMEM((WIDTH, WIDTH), BF), pltpu.SemaphoreType.DMA],
+        compiler_params=params(61),
+        cost_estimate=cost(4),
         name="pack",
-    )(query, key, value, out_grad, tags, gate, weight)
+    )(query, key, value, tags, branch, weight)
 
 
 def filled(piece, extra):
@@ -183,7 +226,7 @@
 
 def attend_body(
     own, near, asked, far_own, far_other,
-    mixed_ref, keep_ref, give_ref, keep_near_ref, give_near_ref, keep_far_ref, give_far_ref,
+    mixed_ref, keep_asked_ref, give_asked_ref, keep_ref, give_ref, keep_far_ref, give_far_ref,
     key_n, key_t, value_n, value_t, query_t, query_n, grad_t, grad_n, held, mixed_t, dq, dk, dv,
     clips, first_ref, count_ref,
 ):
@@ -259,21 +302,22 @@
         tile, cols = block // PART, slice((block % PART) * TOK, (block % PART + 1) * TOK)
         mixed = mixed_t[tile, :, cols]
         mixed_ref[block] = mixed
-        wholes = [mixed.astype(F32), dq[tile, :, cols]] + key_grads(EDGE + block)
-        keep_ref[block], give_ref[block] = halves(wholes)
+        keep_asked_ref[block], give_asked_ref[block] = halves([mixed.astype(F32), dq[tile, :, cols]])
+        keep_ref[block], give_ref[block] = halves(key_grads(EDGE + block))
     for block in range(EDGE):
-        keep_near_ref[block], give_near_ref[block] = halves(key_grads(block + NEAR * (1 - side)))
+        keep_ref[SIDE + block], give_ref[SIDE + block] = halves(key_grads(block + NEAR * (1 - side)))
         keep_far_ref[block], give_far_ref[block] = halves(key_grads(block + NEAR * side))
 
 
 def attend(own, near, asked, far_own, far_other):
-    whole = jax.ShapeDtypeStruct((SIDE, 2 * FULL, TOK), BF)
+    whole = jax.ShapeDtypeStruct((SIDE, FULL, TOK), BF)
+    keys = jax.ShapeDtypeStruct((NEAR, FULL, TOK), BF)
     edge = jax.ShapeDtypeStruct((EDGE, FULL, TOK), BF)
     row_form = pltpu.VMEM((ROOM * TOK, TOK), BF)
     column_form = pltpu.VMEM((ROOM, 80, TOK), BF)
     return pl.pallas_call(
         attend_body,
-        out_shape=(jax.ShapeDtypeStruct((SIDE, FULL, TOK), BF), whole, whole, edge, edge, edge, edge),
+        out_shape=(whole, whole, whole, keys, keys, edge, edge),
         in_specs=[WHOLE] * 5,
         out_specs=(WHOLE,) * 7,
         cost_estimate=cost(20),
@@ -290,7 +334,7 @@
             pltpu.SMEM((TILES,), jnp.int32),
             pltpu.SMEM((TILES,), jnp.int32),
         ],
-        compiler_params=params(32),
+        compiler_params=params(24),
         name="attend",
     )(own, near, asked, far_own, far_other)
 
@@ -339,82 +383,113 @@
         in_specs=[held, held, pl.BlockSpec((CHIPS, 2, WIDTH // 2, TOK), lambda i: (i, 0, 0, 0))],
         out_specs=(share,) * PLANES,
         scratch_shapes=[pltpu.VMEM((WIDTH // 2, TOK), F32)],
-        compiler_params=params(24),
-        cost_estimate=cost(5),
+        compiler_params=params(16),
+        cost_estimate=cost(4),
         name="weight_term",
     )(mixed, other, branch)
 
 
-def join_body(
-    keep, got, keep_near, got_near, got_same, got_cross, term, term1, term2, term3, out_ref, total, pairs
-):
+def join_asked_body(keep, got, out_ref):
+    side = core()
+    for block in range(SIDE):
+        out_ref[SIDE * side + block] = keep[block]
+        out_ref[SIDE * (1 - side) + block] = got[block]
+
+
+def join_asked(keep, got):
+    return pl.pallas_call(
+        join_asked_body,
+        out_shape=jax.ShapeDtypeStruct((PLANE, FULL, TOK), BF),
+        in_specs=[WHOLE] * 2,
+        out_specs=WHOLE,
+        compiler_params=params(8),
+        cost_estimate=cost(1),
+        name="join_asked",
+    )(keep, got)
+
+
+def join_body(keep, got, got_same, got_cross, term, term1, term2, term3, out_ref, total, pairs):
     side = core()
     total[0:SHARE] = sum(one[...].astype(F32) for one in (term, term1, term2, term3))
     total[SHARE:] = jnp.zeros((8, TOK), F32)
     mine, others = SIDE * side, SIDE * (1 - side)
     for block in range(SIDE):
-        pairs[mine + block] = keep[block, FULL:].astype(F32)
-        pairs[others + block] = got[block, FULL:].astype(F32)
+        pairs[mine + block] = keep[block].astype(F32)
+        pairs[others + block] = got[block].astype(F32)
     late, early = (SIDE - EDGE) * side, (SIDE - EDGE) * (1 - side)
     for block in range(EDGE):
-        pairs[others + late + block] += keep_near[block].astype(F32)
-        pairs[mine + early + block] += got_near[block].astype(F32)
+        pairs[others + late + block] += keep[SIDE + block].astype(F32)
+        pairs[mine + early + block] += got[SIDE + block].astype(F32)
     for block in range(EDGE):
         pairs[others + early + block] += got_same[block].astype(F32)
         pairs[mine + late + block] += got_cross[block].astype(F32)
-    for block in range(SIDE):
-        tail = total[block * FINAL : block * FINAL + 16, :]
-        for start, asked in ((mine, keep), (others, got)):
-            whole = [asked[block, 0:FULL].astype(F32), pairs[start + block], tail]
-            out_ref[start + block] = jnp.concatenate(whole, 0).astype(BF)
+    for block in range(PLANE):
+        start = (block % SIDE) * FINAL
+        out_ref[block] = jnp.concatenate([pairs[block], total[start : start + 16, :]], 0).astype(BF)
 
 
 def join(*values):
     return pl.pallas_call(
         join_body,
-        out_shape=jax.ShapeDtypeStruct((PLANE, 2 * FULL + 16, TOK), BF),
-        in_specs=[WHOLE] * 10,
+        out_shape=jax.ShapeDtypeStruct((PLANE, FULL + 16, TOK), BF),
+        in_specs=[WHOLE] * 8,
         out_specs=WHOLE,
         scratch_shapes=[pltpu.VMEM((SHARE + 8, TOK), F32), pltpu.VMEM((PLANE, FULL, TOK), F32)],
-        compiler_params=params(24),
-        cost_estimate=cost(3),
+        compiler_params=params(12),
+        cost_estimate=cost(1),
         name="join",
     )(*values)
 
 
-def finish_body(packed, residual, tags, gate, weight, bias, out_ref, dq_ref, dk_ref, dv_ref, dw_ref):
-    def rows(at):
-        low = slice(at * HALF, (at + 1) * HALF)
-        high = slice(at * HALF, at * HALF + HEAD_DIM - HALF)
-        parts = []
-        for head in range(HEADS):
-            parts += [packed[2 * head].astype(F32)[low], packed[2 * head + 1].astype(F32)[high]]
-        return jnp.concatenate(parts, 0).T.astype(BF)
-
+def all_heads(packed, at):
+    low = slice(at * HALF, (at + 1) * HALF)
+    high = slice(at * HALF, at * HALF + HEAD_DIM - HALF)
+    parts = []
+    for head in range(HEADS):
+        parts += [packed[2 * head].astype(F32)[low], packed[2 * head + 1].astype(F32)[high]]
+    return jnp.concatenate(parts, 0).T.astype(BF)
+
+
+def finish_asked_body(packed, residual, tags, gate, weight, bias, out_ref, dq_ref):
     gate_rows = lax.dot_general(
         clip_onehot(tags), gate[...], (((0,), (0,)), ((), ())),
         precision=lax.Precision.HIGHEST, preferred_element_type=F32,
     )
-    projected = mm(rows(0), weight[...]) + bias[...].reshape(1, WIDTH)
+    projected = mm(all_heads(packed, 0), weight[...]) + bias[...].reshape(1, WIDTH)
     out_ref[...] = (residual[...].astype(F32) + gate_rows * projected).astype(BF)
-    dq_ref[...] = rows(1)
-    dk_ref[...] = rows(2)
-    dv_ref[...] = rows(3)
+    dq_ref[...] = all_heads(packed, 1)
+
+
+def finish_asked(packed, residual, tags, gate, weight, bias):
+    return pl.pallas_call(
+        finish_asked_body,
+        out_shape=(jax.ShapeDtypeStruct((TOK, WIDTH), BF),) * 2,
+        in_specs=[WHOLE] * 6,
+        out_specs=(WHOLE,) * 2,
+        compiler_params=params(16),
+        cost_estimate=cost(2),
+        name="finish_asked",
+    )(packed, residual, tags, gate, weight, bias)
+
+
+def finish_body(packed, dk_ref, dv_ref, dw_ref):
+    dk_ref[...] = all_heads(packed, 0)
+    dv_ref[...] = all_heads(packed, 1)
     source = lax.rem(lax.axis_index("dp"), PLANE) // SIDE
-    tails = [packed[2 * head + source, 2 * FULL :].astype(F32)[:, 0:HEAD_DIM] for head in range(HEADS)]
+    tails = [packed[2 * head + source, FULL:].astype(F32)[:, 0:HEAD_DIM] for head in range(HEADS)]
     dw_ref[...] = jnp.concatenate(tails, 1)[0:FINAL]
 
 
-def finish(packed, residual, tags, gate, weight, bias):
+def finish(packed):
     return pl.pallas_call(
         finish_body,
-        out_shape=(jax.ShapeDtypeStruct((TOK, WIDTH), BF),) * 4 + (jax.ShapeDtypeStruct((FINAL, WIDTH), F32),),
-        in_specs=[WHOLE] * 6,
-        out_specs=(WHOLE,) * 5,
-        compiler_params=params(24),
-        cost_estimate=cost(4),
+        out_shape=(jax.ShapeDtypeStruct((TOK, WIDTH), BF),) * 2 + (jax.ShapeDtypeStruct((FINAL, WIDTH), F32),),
+        in_specs=[WHOLE],
+        out_specs=(WHOLE,) * 3,
+        compiler_params=params(16),
+        cost_estimate=cost(1),
         name="finish",
-    )(packed, residual, tags, gate, weight, bias)
+    )(packed)
 
 
 def sent(values, target):
@@ -454,8 +529,10 @@
 def shards(query, key, value, residual, tags, gate, weight, bias, out_grad):
     me = lax.axis_index("dp")
     side = me % 2
-    chunk, branch, branch_away = pack(query, key, value, out_grad, tags, gate, weight)
-    branch = lax.dynamic_update_slice(branch, sent(branch_away, other_core)[None], (1, 0, 0))
+    whole_branch, branch, branch_away = branch_columns(out_grad, tags, gate)
+    chunk = pack(query, key, value, tags, whole_branch, weight)
+    branch_got, chunk = lax.optimization_barrier((sent(branch_away, other_core), chunk))
+    branch = fill(branch, branch_got)
     cores = [[plane * PLANE + 2 * chip + at for chip in range(HEADS)] for plane in range(PLANES) for at in range(2)]
     gathered = lax.all_gather(branch, "dp", axis=0, axis_index_groups=cores, tiled=False)
     own = traded(chunk)
@@ -464,16 +541,19 @@
     last = PLANE - EDGE
     far_own = sent(some_blocks(own, last * (1 - side), 0, EDGE), same_out)
     far_other = sent(some_blocks(own, last * side, 0, EDGE), cross)
-    mixed, keep, give, keep_near, give_near, keep_far, give_far = attend(own, near, asked, far_own, far_other)
+    mixed, keep_asked, give_asked, keep, give, keep_far, give_far = attend(own, near, asked, far_own, far_other)
+    joined = join_asked(keep_asked, sent(give_asked, other_core))
+    joined, mixed, give, keep_far, give_far = lax.optimization_barrier((joined, mixed, give, keep_far, give_far))
+    asked_back = traded(joined)
     mixed_other = sent(mixed, other_core)
     got = sent(give, other_core)
-    got_near = sent(give_near, other_core)
     got_same = sent(keep_far, same_back)
     got_cross = sent(give_far, cross)
     term, *terms = weight_term(mixed, mixed_other, gathered)
     terms = [sent(one, planes_on(away + 1)) for away, one in enumerate(terms)]
-    packed = traded(join(keep, got, keep_near, got_near, got_same, got_cross, term, *terms))
-    block_out, dq, dk, dv, dw = finish(packed, residual, tags, gate, weight, bias)
+    keys_back = traded(join(keep, got, got_same, got_cross, term, *terms))
+    block_out, dq = finish_asked(asked_back, residual, tags, gate, weight, bias)
+    dk, dv, dw = finish(keys_back)
     return block_out, dq, dk, dv, dw.T
 
 

time: 140 us -> 142 us (1.014); the launches traced: 140 us -> 140 us
  blocking collectives: 26.8 us -> 0 us
  starting transfers between devices: 30 us -> 42.6 us
  waiting for transfers between devices: 29.6 us -> 40.1 us
  Pallas kernels: 27.1 us -> 34.8 us
  local copies, waits for them, and re-layouts: 11.9 us -> 8.28 us
    all_to_all x1 -> x0, blocking collectives: 26.8 us -> none  [traded(): lax.all_to_all(values, 'dp', 0, 0, axis_index_groups=groups, tiled=True)]
    all_to_all x1 -> x3, starting transfers between devices: 8.39 us -> 20.7 us  [traded(): lax.all_to_all(values, 'dp', 0, 0, axis_index_groups=groups, tiled=True)]
    all_to_all x1 -> x3, waiting for transfers between devices: 24 us -> 35.4 us  [traded(): lax.all_to_all(values, 'dp', 0, 0, axis_index_groups=groups, tiled=True)]
    pallas_call x3 -> x7, Pallas kernels: 22.9 us -> 30.5 us  [the longest x1 18.3 us: attend(): pl.pallas_call(attend_body, out_shape=(whole, whole, whole, keys, keys, e...]
    unnamed x36, local copies, waits for them, and re-layouts: 11.7 us -> 8.19 us
  transfers between devices with their start and end apart: 15 -> 17, of which waited for: 4 -> 5; matrix products, arithmetic and copies ran while one was open for 0% -> 0% of each run, Pallas kernels for 15% -> 21%
where the time goes in v8:
time: 142 us; the launch traced here: 140 us
  starting transfers between devices  42.6 us (30%)
  waiting for transfers between devices  40.1 us (28%)
  Pallas kernels  34.8 us (25%)
  between operations  14.3 us (10%)
  local copies, waits for them, and re-layouts  8.28 us (6%)
    all_to_all x3, waiting for transfers between devices, traded(): lax.all_to_all(values, 'dp', 0, 0, axis_index_groups=groups, tiled=True)  35.4 us
    ppermute x13, starting transfers between devices, sent(): lax.ppermute(values, 'dp', [(i, j) for i, j in pairs if 0 <= j < DEVICES])  21.9 us
    all_to_all x3, starting transfers between devices, traded(): lax.all_to_all(values, 'dp', 0, 0, axis_index_groups=groups, tiled=True)  20.7 us
    pallas_call x1, Pallas kernels, attend(): pl.pallas_call(attend_body, out_shape=(whole, whole, whole, keys, keys, e...  18.3 us
    unnamed x36, local copies, waits for them, and re-layouts  8.19 us
    pallas_call x1, Pallas kernels, pack(): pl.pallas_call(pack_body, out_shape=jax.ShapeDtypeStruct((PLANE, 2 * FULL...  5 us
    ppermute x13, waiting for transfers between devices, sent(): lax.ppermute(values, 'dp', [(i, j) for i, j in pairs if 0 <= j < DEVICES])  4.63 us
  transfers between devices with their start and end apart: 17, of which 5 were waited for; matrix products, arithmetic and copies ran while one was open for 0% of the time, Pallas kernels for 21%

profile of v8, /device:TPU:1, one launch (start us, length us, event | category | flops | bytes accessed | tf_op | source)
XLA Modules:
  0.0 140.0 jit_solution(4093404528041514118)
XLA Ops:
  7.2 0.0 all-gather.3.cloned.1.call-start
  7.2 2.5 %branch_columns.1 = (bf16[1152,128]{1,0:T(8,128)(2,1)}, bf16[2,576,128]{2,1,0:T(8,128)(2,1)}, bf16[576,128]{1,0:T(8,128)(2,1)}) custom-call(bf16[128,1152]{1,0:T(8,128)(2,1)} %out_grad.1, s32[128]{0:T(128)} %tags.5, f32[32,1152]{1,0:T(8,128)} %gate.3), custom_call_target="tpu_custom_call" | custom-call | flops 800000000 | bytes 4000000 | tf_op jit(solution)/shard_map/branch_columns/pallas_call | solution.py:87
  9.8 1.4 %collective-permute-start = (bf16[576,128]{1,0:T(8,128)(2,1)}, bf16[576,128]{1,0:T(8,128)(2,1)S(1)}, u32[]{:S(2)}, u32[]{:S(2)}) collective-permute-start(bf16[576,128]{1,0:T(8,128)(2,1)} %get-tuple-element.31), channel_id=1, source_target_pairs={{0,1},{1,0},{2,3},{3,2},{4,5},{5,4},{6,7},{7,6},{8,9},{9,8},{10,11... | collective-permute-start | bytes 442376 | tf_op jit(solution)/shard_map/ppermute | solution.py:497
  11.2 5.0 %pack.1 = bf16[32,160,128]{2,1,0:T(8,128)(2,1)} custom-call(bf16[128,1152]{1,0:T(8,128)(2,1)} %query.1, bf16[128,1152]{1,0:T(8,128)(2,1)} %key.1, bf16[128,1152]{1,0:T(8,128)(2,1)} %value.1, s32[128]{0:T(128)} %tags.5, bf16[1152,128]{1,0:T(8,128)(2,1)} %get-tuple-element.32.branch, bf16[1152,1152]{1,0:T(8,128)(2,1)} %weight.3), custom_call_target="tpu_custom_call" | custom-call | flops 1600000000 | bytes 8000000 | tf_op jit(solution)/shard_map/pack/pallas_call | solution.py:142
  16.2 0.0 collective-permute-done.got
  16.2 0.7 fill.1
  16.9 0.0 all-gather.3.cloned.1.call-update
  16.9 8.1 %all-to-all-start = ((bf16[32,160,128]{2,1,0:T(8,128)(2,1)}), bf16[32,160,128]{2,1,0:T(8,128)(2,1)S(1)}, u32[]{:S(2)}, u32[]{:S(2)}) async-start(bf16[32,160,128]{2,1,0:T(8,128)(2,1)} %pack.1), calls=%async_computation | async-start | bytes 2621440 | tf_op jit(solution)/shard_map/all_to_all | solution.py:522
  25.1 24.0 %all-to-all-done.own = bf16[32,160,128]{2,1,0:T(8,128)(2,1)S(1)} async-done(((bf16[32,160,128]{2,1,0:T(8,128)(2,1)}), bf16[32,160,128]{2,1,0:T(8,128)(2,1)S(1)}, u32[]{:S(2)}, u32[]{:S(2)}) %all-to-all-start) | async-done | bytes 1310752 | tf_op jit(solution)/shard_map/all_to_all | solution.py:522
  49.1 0.5 collective-permute-start.1
  49.7 0.1 collective-permute-start.2
  49.8 1.3 collective-permute-start.3
  51.1 6.0 %collective-permute-start.4 = (bf16[7,80,128]{2,1,0:T(8,128)(2,1)S(1)}, bf16[7,80,128]{2,1,0:T(8,128)(2,1)S(1)}, u32[]{:S(2)}, u32[]{:S(2)}) collective-permute-start(bf16[7,80,128]{2,1,0:T(8,128)(2,1)S(1)} %get-tuple-element.57), channel_id=1, source_target_pairs={{1,32},{3,34},{5,36},{7,38},{9,40},{11,42},{13,44},{15,46},{17,48}... | collective-permute-start | bytes 430088 | tf_op jit(solution)/shard_map/ppermute | solution.py:497
  57.2 0.0 collective-permute-done.3.far_own
  57.2 2.8 %collective-permute-done.4.far_other = bf16[7,80,128]{2,1,0:T(8,128)(2,1)S(1)} collective-permute-done((bf16[7,80,128]{2,1,0:T(8,128)(2,1)S(1)}, bf16[7,80,128]{2,1,0:T(8,128)(2,1)S(1)}, u32[]{:S(2)}, u32[]{:S(2)}) %collective-permute-start.4) | collective-permute-done | bytes 143392 | tf_op jit(solution)/shard_map/ppermute | solution.py:497
  59.9 18.3 %attend.1 = (bf16[16,80,128]{2,1,0:T(8,128)(2,1)S(1)}, bf16[16,80,128]{2,1,0:T(8,128)(2,1)S(1)}, bf16[16,80,128]{2,1,0:T(8,128)(2,1)S(1)}, bf16[23,80,128]{2,1,0...) custom-call(bf16[32,160,128]{2,1,0:T(8,128)(2,1)S(1)} %all-to-all-do, ...), custom_call_target="tpu_custom_call" | custom-call | flops 8000000000 | bytes 40000000 | tf_op jit(solution)/shard_map/attend/pallas_call | solution.py:318
  78.2 0.8 copy-done.1
  79.0 0.7 copy-done.12
  79.8 1.6 %collective-permute-done.5.got = bf16[16,80,128]{2,1,0:T(8,128)(2,1)S(1)} collective-permute-done((bf16[16,80,128]{2,1,0:T(8,128)(2,1)S(1)}, bf16[16,80,128]{2,1,0:T(8,128)(2,1)S(1)}, u32[]{:S(2)}, u32[]{:S(2)}) %collective-permute-start.5) | collective-permute-done | bytes 327712 | tf_op jit(solution)/shard_map/ppermute | solution.py:497
  81.4 0.9 join_asked.1
  82.4 3.9 %all-to-all-start.1 = ((bf16[32,80,128]{2,1,0:T(8,128)(2,1)}), bf16[32,80,128]{2,1,0:T(8,128)(2,1)S(1)}, u32[]{:S(2)}, u32[]{:S(2)}) async-start(bf16[32,80,128]{2,1,0:T(8,128)(2,1)} %join_asked.1), calls=%async_computation.1 | async-start | bytes 1310720 | tf_op jit(solution)/shard_map/all_to_all | solution.py:522
  86.3 0.4 collective-permute-start.9
  86.6 0.2 collective-permute-start.6
  86.9 5.3 %collective-permute-start.7 = (bf16[7,80,128]{2,1,0:T(8,128)(2,1)S(1)}, bf16[7,80,128]{2,1,0:T(8,128)(2,1)S(1)}, u32[]{:S(2)}, u32[]{:S(2)}) collective-permute-start(bf16[7,80,128]{2,1,0:T(8,128)(2,1)S(1)} %copy-done.17), channel_id=1, source_target_pairs={{1,33},{3,35},{5,37},{7,39},{9,41},{11,43},{13,45},{15,47},{17,49}... | collective-permute-start | bytes 430088 | tf_op jit(solution)/shard_map/ppermute | solution.py:497
  92.2 2.1 %collective-permute-start.8 = (bf16[7,80,128]{2,1,0:T(8,128)(2,1)S(1)}, bf16[7,80,128]{2,1,0:T(8,128)(2,1)S(1)}, u32[]{:S(2)}, u32[]{:S(2)}) collective-permute-start(bf16[7,80,128]{2,1,0:T(8,128)(2,1)S(1)} %copy-done.15), channel_id=1, source_target_pairs={{1,32},{3,34},{5,36},{7,38},{9,40},{11,42},{13,44},{15,46},{17,48}... | collective-permute-start | bytes 430088 | tf_op jit(solution)/shard_map/ppermute | solution.py:497
  94.3 0.0 collective-permute-done.9.other
  94.3 0.0 all-gather.3.cloned.1.call-done
  94.3 2.3 %copy-done.11 = bf16[32,576,128]{2,1,0:T(8,128)(2,1)S(1)} copy-done((bf16[32,576,128]{2,1,0:T(8,128)(2,1)S(1)}, bf16[32,576,128]{2,1,0:T(8,128)(2,1)}, u32[]{:S(2)}) %copy-start.11) | copy-done | bytes 4718616
  96.7 2.1 %weight_term.1 = (bf16[144,128]{1,0:T(8,128)(2,1)S(1)}, bf16[144,128]{1,0:T(8,128)(2,1)S(1)}, bf16[144,128]{1,0:T(8,128)(2,1)S(1)}, bf16[144,128]{1,0:T(8,128)(2,1)S(1)}) custom-call(bf16[16,80,128]{2,1,0:T(8,128)(2,1)S(1)} %copy-done.13, bf16[16,80,128]{2,1,0:T(8,128)(2,1)S(1)} %collective-permute-done.9.other, bf16[16,2,576,128]{3,2,1,0:T(8,128)(2,1)S(1)} %bitcast.2), custom_call_target="tpu_custom_call" | custom-call | flops 1600000000 | bytes 8000000 | tf_op jit(solution)/shard_map/weight_term/pallas_call | solution.py:379
  98.8 1.8 %collective-permute-start.10 = (bf16[144,128]{1,0:T(8,128)(2,1)S(1)}, bf16[144,128]{1,0:T(8,128)(2,1)S(1)}, u32[]{:S(2)}, u32[]{:S(2)}) collective-permute-start(bf16[144,128]{1,0:T(8,128)(2,1)S(1)} %get-tuple-element.51), channel_id=1, source_target_pairs={{0,32},{1,33},{2,34},{3,35},{4,36},{5,37},{6,38},{7,39},{8,40},{9,... | collective-permute-start | bytes 110600 | tf_op jit(solution)/shard_map/ppermute | solution.py:497
  100.6 0.7 collective-permute-start.11
  101.3 0.0 collective-permute-done.7.got_same
  101.3 2.0 %collective-permute-start.12 = (bf16[144,128]{1,0:T(8,128)(2,1)S(1)}, bf16[144,128]{1,0:T(8,128)(2,1)S(1)}, u32[]{:S(2)}, u32[]{:S(2)}) collective-permute-start(bf16[144,128]{1,0:T(8,128)(2,1)S(1)} %get-tuple-element.53), channel_id=1, source_target_pairs={{0,96},{1,97},{2,98},{3,99},{4,100},{5,101},{6,102},{7,103},{8,104... | collective-permute-start | bytes 110600 | tf_op jit(solution)/shard_map/ppermute | solution.py:497
  103.3 0.7 copy-done.7
  104.0 0.8 copy-done.3
  104.7 0.0 collective-permute-done.10.term1
  104.7 0.2 collective-permute-done.11.term2
  104.9 0.0 collective-permute-done.12.term3
  104.9 1.0 copy-done.4
  106.0 0.9 copy-done.8
  106.9 1.2 join.1
  108.1 0.0 all-to-all-done.1.packed
  108.1 8.7 %all-to-all-start.2 = ((bf16[32,96,128]{2,1,0:T(8,128)(2,1)}), bf16[32,96,128]{2,1,0:T(8,128)(2,1)}, u32[]{:S(2)}, u32[]{:S(2)}) async-start(bf16[32,96,128]{2,1,0:T(8,128)(2,1)} %join.1), calls=%async_computation.2 | async-start | bytes 1572864 | tf_op jit(solution)/shard_map/all_to_all | solution.py:522
  116.8 0.0 copy-start.5
  116.8 1.0 copy-done.5
  117.8 1.9 %finish_asked.1 = (bf16[128,1152]{1,0:T(8,128)(2,1)}, bf16[128,1152]{1,0:T(8,128)(2,1)}) custom-call(bf16[32,80,128]{2,1,0:T(8,128)(2,1)S(1)} %all-to-all-done.1.packed, bf16[128,1152]{1,0:T(8,128)(2,1)S(1)} %copy-done.5, s32[128]{0:T(128)S(1)} %copy-done.10, f32[32,1152]{1,0:T(8,128)S(1)} %copy-done.6, bf16[1152,1152]{1,0:T(8,128)(2,1)S(1)} %copy-done, ...), custom_call_target="tpu_custom_call" | custom-call | flops 800000000 | bytes 4000000 | tf_op jit(solution)/shard_map/finish_asked/pallas_call | solution.py:464
  119.6 11.4 %all-to-all-done.2.packed = bf16[32,96,128]{2,1,0:T(8,128)(2,1)} async-done(((bf16[32,96,128]{2,1,0:T(8,128)(2,1)}), bf16[32,96,128]{2,1,0:T(8,128)(2,1)}, u32[]{:S(2)}, u32[]{:S(2)}) %all-to-all-start.2) | async-done | bytes 786464 | tf_op jit(solution)/shard_map/all_to_all | solution.py:522
  131.0 2.1 %finish.1 = (bf16[128,1152]{1,0:T(8,128)(2,1)}, bf16[128,1152]{1,0:T(8,128)(2,1)}, f32[9,1152]{1,0:T(8,128)}) custom-call(bf16[32,96,128]{2,1,0:T(8,128)(2,1)} %all-to-all-done.2.packed), custom_call_target="tpu_custom_call" | custom-call | flops 400000000 | bytes 2000000 | tf_op jit(solution)/shard_map/finish/pallas_call | solution.py:484
  (35 shorter events, 0.1 us)
Async XLA Ops:
  7.2 87.2 %all-gather.3.cloned.1.call-start = ((), (), s32[]{:S(2)}) async-start(), calls=%async_computation.3 | async-start | bytes 5013504 | tf_op jit(solution)/shard_map/all_gather | solution.py:537
  9.8 6.4 %collective-permute-start = (bf16[576,128]{1,0:T(8,128)(2,1)}, bf16[576,128]{1,0:T(8,128)(2,1)S(1)}, u32[]{:S(2)}, u32[]{:S(2)}) collective-permute-start(bf16[576,128]{1,0:T(8,128)(2,1)} %get-tuple-element.31), channel_id=1, source_target_pairs={{0,1},{1,0},{2,3},{3,2},{4,5},{5,4},{6,7},{7,6},{8,9},{9,8},{10,11... | collective-permute-start | bytes 442376 | tf_op jit(solution)/shard_map/ppermute | solution.py:497
  16.9 32.2 %all-to-all-start = ((bf16[32,160,128]{2,1,0:T(8,128)(2,1)}), bf16[32,160,128]{2,1,0:T(8,128)(2,1)S(1)}, u32[]{:S(2)}, u32[]{:S(2)}) async-start(bf16[32,160,128]{2,1,0:T(8,128)(2,1)} %pack.1), calls=%async_computation | async-start | bytes 2621440 | tf_op jit(solution)/shard_map/all_to_all | solution.py:522
  49.1 10.8 %collective-permute-start.1 = (bf16[23,80,128]{2,1,0:T(8,128)(2,1)S(1)}, bf16[23,80,128]{2,1,0:T(8,128)(2,1)S(1)}, u32[]{:S(2)}, u32[]{:S(2)}) collective-permute-start(bf16[23,80,128]{2,1,0:T(8,128)(2,1)S(1)} %constant_dynamic-slice_fusion.3), channel_id=1, source_target_pairs={{0,1},{1,0},{2,3},{3,2},{4,5},{5,4},{6,7},{7,6},{8,9},{9,8},{10,11... | collective-permute-start | bytes 1413128 | tf_op jit(solution)/shard_map/ppermute | solution.py:497
  49.7 10.3 %collective-permute-start.2 = (bf16[16,80,128]{2,1,0:T(8,128)(2,1)S(1)}, bf16[16,80,128]{2,1,0:T(8,128)(2,1)S(1)}, u32[]{:S(2)}, u32[]{:S(2)}) collective-permute-start(bf16[16,80,128]{2,1,0:T(8,128)(2,1)S(1)} %constant_dynamic-slice_fusion.2), channel_id=1, source_target_pairs={{0,1},{1,0},{2,3},{3,2},{4,5},{5,4},{6,7},{7,6},{8,9},{9,8},{10,11... | collective-permute-start | bytes 983048 | tf_op jit(solution)/shard_map/ppermute | solution.py:497
  49.8 7.3 %collective-permute-start.3 = (bf16[7,80,128]{2,1,0:T(8,128)(2,1)S(1)}, bf16[7,80,128]{2,1,0:T(8,128)(2,1)S(1)}, u32[]{:S(2)}, u32[]{:S(2)}) collective-permute-start(bf16[7,80,128]{2,1,0:T(8,128)(2,1)S(1)} %get-tuple-element.58), channel_id=1, source_target_pairs={{0,32},{2,34},{4,36},{6,38},{8,40},{10,42},{12,44},{14,46},{16,48}... | collective-permute-start | bytes 430088 | tf_op jit(solution)/shard_map/ppermute | solution.py:497
  51.1 8.8 %collective-permute-start.4 = (bf16[7,80,128]{2,1,0:T(8,128)(2,1)S(1)}, bf16[7,80,128]{2,1,0:T(8,128)(2,1)S(1)}, u32[]{:S(2)}, u32[]{:S(2)}) collective-permute-start(bf16[7,80,128]{2,1,0:T(8,128)(2,1)S(1)} %get-tuple-element.57), channel_id=1, source_target_pairs={{1,32},{3,34},{5,36},{7,38},{9,40},{11,42},{13,44},{15,46},{17,48}... | collective-permute-start | bytes 430088 | tf_op jit(solution)/shard_map/ppermute | solution.py:497
  78.2 0.8 copy-start.1
  79.0 0.7 copy-start.12
  79.8 2.6 %copy-start.14 = (bf16[7,80,128]{2,1,0:T(8,128)(2,1)}, bf16[7,80,128]{2,1,0:T(8,128)(2,1)S(1)}, u32[]{:S(2)}) copy-start(bf16[7,80,128]{2,1,0:T(8,128)(2,1)S(1)} %get-tuple-element.46) | copy-start | bytes 430084
  79.8 2.6 %copy-start.16 = (bf16[7,80,128]{2,1,0:T(8,128)(2,1)}, bf16[7,80,128]{2,1,0:T(8,128)(2,1)S(1)}, u32[]{:S(2)}) copy-start(bf16[7,80,128]{2,1,0:T(8,128)(2,1)S(1)} %get-tuple-element.45) | copy-start | bytes 430084
  79.8 1.6 %collective-permute-start.5 = (bf16[16,80,128]{2,1,0:T(8,128)(2,1)S(1)}, bf16[16,80,128]{2,1,0:T(8,128)(2,1)S(1)}, u32[]{:S(2)}, u32[]{:S(2)}) collective-permute-start(bf16[16,80,128]{2,1,0:T(8,128)(2,1)S(1)} %get-tuple-element.35), channel_id=1, source_target_pairs={{0,1},{1,0},{2,3},{3,2},{4,5},{5,4},{6,7},{7,6},{8,9},{9,8},{10,11... | collective-permute-start | bytes 983048 | tf_op jit(solution)/shard_map/ppermute | solution.py:497
  81.4 4.9 %copy-start.13 = (bf16[16,80,128]{2,1,0:T(8,128)(2,1)S(1)}, bf16[16,80,128]{2,1,0:T(8,128)(2,1)}, u32[]{:S(2)}) copy-start(bf16[16,80,128]{2,1,0:T(8,128)(2,1)} %copy-done.12) | copy-start | bytes 983044
  82.3 9.8 %copy-start.15 = (bf16[7,80,128]{2,1,0:T(8,128)(2,1)S(1)}, bf16[7,80,128]{2,1,0:T(8,128)(2,1)}, u32[]{:S(2)}) copy-start(bf16[7,80,128]{2,1,0:T(8,128)(2,1)} %copy-done.14) | copy-start | bytes 430084
  82.3 4.5 %copy-start.17 = (bf16[7,80,128]{2,1,0:T(8,128)(2,1)S(1)}, bf16[7,80,128]{2,1,0:T(8,128)(2,1)}, u32[]{:S(2)}) copy-start(bf16[7,80,128]{2,1,0:T(8,128)(2,1)} %copy-done.16) | copy-start | bytes 430084
  82.4 25.7 %all-to-all-start.1 = ((bf16[32,80,128]{2,1,0:T(8,128)(2,1)}), bf16[32,80,128]{2,1,0:T(8,128)(2,1)S(1)}, u32[]{:S(2)}, u32[]{:S(2)}) async-start(bf16[32,80,128]{2,1,0:T(8,128)(2,1)} %join_asked.1), calls=%async_computation.1 | async-start | bytes 1310720 | tf_op jit(solution)/shard_map/all_to_all | solution.py:522
  86.3 8.0 %collective-permute-start.9 = (bf16[16,80,128]{2,1,0:T(8,128)(2,1)S(1)}, bf16[16,80,128]{2,1,0:T(8,128)(2,1)S(1)}, u32[]{:S(2)}, u32[]{:S(2)}) collective-permute-start(bf16[16,80,128]{2,1,0:T(8,128)(2,1)S(1)} %copy-done.13), channel_id=1, source_target_pairs={{0,1},{1,0},{2,3},{3,2},{4,5},{5,4},{6,7},{7,6},{8,9},{9,8},{10,11... | collective-permute-start | bytes 983048 | tf_op jit(solution)/shard_map/ppermute | solution.py:497
  86.6 17.3 %collective-permute-start.6 = (bf16[23,80,128]{2,1,0:T(8,128)(2,1)S(1)}, bf16[23,80,128]{2,1,0:T(8,128)(2,1)S(1)}, u32[]{:S(2)}, u32[]{:S(2)}) collective-permute-start(bf16[23,80,128]{2,1,0:T(8,128)(2,1)S(1)} %get-tuple-element.44), channel_id=1, source_target_pairs={{0,1},{1,0},{2,3},{3,2},{4,5},{5,4},{6,7},{7,6},{8,9},{9,8},{10,11... | collective-permute-start | bytes 1413128 | tf_op jit(solution)/shard_map/ppermute | solution.py:497
  86.9 14.4 %collective-permute-start.7 = (bf16[7,80,128]{2,1,0:T(8,128)(2,1)S(1)}, bf16[7,80,128]{2,1,0:T(8,128)(2,1)S(1)}, u32[]{:S(2)}, u32[]{:S(2)}) collective-permute-start(bf16[7,80,128]{2,1,0:T(8,128)(2,1)S(1)} %copy-done.17), channel_id=1, source_target_pairs={{1,33},{3,35},{5,37},{7,39},{9,41},{11,43},{13,45},{15,47},{17,49}... | collective-permute-start | bytes 430088 | tf_op jit(solution)/shard_map/ppermute | solution.py:497
  92.2 11.1 %collective-permute-start.8 = (bf16[7,80,128]{2,1,0:T(8,128)(2,1)S(1)}, bf16[7,80,128]{2,1,0:T(8,128)(2,1)S(1)}, u32[]{:S(2)}, u32[]{:S(2)}) collective-permute-start(bf16[7,80,128]{2,1,0:T(8,128)(2,1)S(1)} %copy-done.15), channel_id=1, source_target_pairs={{1,32},{3,34},{5,36},{7,38},{9,40},{11,42},{13,44},{15,46},{17,48}... | collective-permute-start | bytes 430088 | tf_op jit(solution)/shard_map/ppermute | solution.py:497
  94.3 2.3 %copy-start.11 = (bf16[32,576,128]{2,1,0:T(8,128)(2,1)S(1)}, bf16[32,576,128]{2,1,0:T(8,128)(2,1)}, u32[]{:S(2)}) copy-start(bf16[32,576,128]{2,1,0:T(8,128)(2,1)} %all-gather.3.cloned.1.call-done) | copy-start | bytes 14155780
  96.7 8.3 %copy-start.2 = (bf16[23,80,128]{2,1,0:T(8,128)(2,1)S(1)}, bf16[23,80,128]{2,1,0:T(8,128)(2,1)}, u32[]{:S(2)}) copy-start(bf16[23,80,128]{2,1,0:T(8,128)(2,1)} %copy-done.1) | copy-start | bytes 1413124
  98.8 5.9 %collective-permute-start.10 = (bf16[144,128]{1,0:T(8,128)(2,1)S(1)}, bf16[144,128]{1,0:T(8,128)(2,1)S(1)}, u32[]{:S(2)}, u32[]{:S(2)}) collective-permute-start(bf16[144,128]{1,0:T(8,128)(2,1)S(1)} %get-tuple-element.51), channel_id=1, source_target_pairs={{0,32},{1,33},{2,34},{3,35},{4,36},{5,37},{6,38},{7,39},{8,40},{9,... | collective-permute-start | bytes 110600 | tf_op jit(solution)/shard_map/ppermute | solution.py:497
  100.6 4.3 %collective-permute-start.11 = (bf16[144,128]{1,0:T(8,128)(2,1)S(1)}, bf16[144,128]{1,0:T(8,128)(2,1)S(1)}, u32[]{:S(2)}, u32[]{:S(2)}) collective-permute-start(bf16[144,128]{1,0:T(8,128)(2,1)S(1)} %get-tuple-element.52), channel_id=1, source_target_pairs={{0,64},{1,65},{2,66},{3,67},{4,68},{5,69},{6,70},{7,71},{8,72},{9,... | collective-permute-start | bytes 110600 | tf_op jit(solution)/shard_map/ppermute | solution.py:497
  101.3 3.6 %collective-permute-start.12 = (bf16[144,128]{1,0:T(8,128)(2,1)S(1)}, bf16[144,128]{1,0:T(8,128)(2,1)S(1)}, u32[]{:S(2)}, u32[]{:S(2)}) collective-permute-start(bf16[144,128]{1,0:T(8,128)(2,1)S(1)} %get-tuple-element.53), channel_id=1, source_target_pairs={{0,96},{1,97},{2,98},{3,99},{4,100},{5,101},{6,102},{7,103},{8,104... | collective-permute-start | bytes 110600 | tf_op jit(solution)/shard_map/ppermute | solution.py:497
  103.3 0.7 copy-start.7
  103.9 0.8 copy-start.3
  104.9 1.0 copy-start.4
  106.0 0.9 copy-start.8
  106.9 9.9 %copy-start = (bf16[1152,1152]{1,0:T(8,128)(2,1)S(1)}, bf16[1152,1152]{1,0:T(8,128)(2,1)}, u32[]{:S(2)}) copy-start(bf16[1152,1152]{1,0:T(8,128)(2,1)} %weight.3) | copy-start | bytes 7962628
  108.1 8.7 %copy-start.6 = (f32[32,1152]{1,0:T(8,128)S(1)}, f32[32,1152]{1,0:T(8,128)}, u32[]{:S(2)}) copy-start(f32[32,1152]{1,0:T(8,128)} %gate.3) | copy-start | bytes 442372
  108.1 8.7 %copy-start.9 = (f32[1152]{0:T(1024)S(1)}, f32[1152]{0:T(1024)}, u32[]{:S(2)}) copy-start(f32[1152]{0:T(1024)} %bias.1) | copy-start | bytes 13828
  108.1 8.7 %copy-start.10 = (s32[128]{0:T(128)S(1)}, s32[128]{0:T(128)}, u32[]{:S(2)}) copy-start(s32[128]{0:T(128)} %tags.5) | copy-start | bytes 1540
  108.1 22.9 %all-to-all-start.2 = ((bf16[32,96,128]{2,1,0:T(8,128)(2,1)}), bf16[32,96,128]{2,1,0:T(8,128)(2,1)}, u32[]{:S(2)}, u32[]{:S(2)}) async-start(bf16[32,96,128]{2,1,0:T(8,128)(2,1)} %join.1), calls=%async_computation.2 | async-start | bytes 1572864 | tf_op jit(solution)/shard_map/all_to_all | solution.py:522
  116.8 1.0 copy-start.5
Sparse Core Ops, SparseCore 0:
  17.0 63.3 all-gather.2

commit v9 on v8

--- a/solution.py
+++ b/solution.py
@@ -23,7 +23,7 @@
 PART = TILE // TOK
 STEP = 4
 ROOM = SPAN + STEP - 1
-CHUNKS = 5
+CHUNKS = 4
 HALF = 40
 FULL = 2 * HALF
 FINAL = WIDTH // DEVICES
@@ -165,6 +165,12 @@
     return [jnp.concatenate([low[rows], high[rows]], 0) for rows in (slice(0, HALF), slice(HALF, FULL))]
 
 
+def halves(side, wholes):
+    low = jnp.concatenate([whole[0:HALF] for whole in wholes], 0)
+    high = jnp.concatenate([whole[HALF:] for whole in wholes], 0)
+    return pick(side, low, high), pick(side, high, low)
+
+
 def window(side, own, near, far_own, far_other):
     for block in range(NEAR):
         at = block + EDGE * (1 - side)
@@ -226,8 +232,8 @@
 
 def attend_body(
     own, near, asked, far_own, far_other,
-    mixed_ref, keep_asked_ref, give_asked_ref, keep_ref, give_ref, keep_far_ref, give_far_ref,
-    key_n, key_t, value_n, value_t, query_t, query_n, grad_t, grad_n, held, mixed_t, dq, dk, dv,
+    mixed_ref, keep_asked_ref, give_asked_ref, keep_ref, give_ref, far_ref,
+    key_n, key_t, value_n, value_t, query_t, query_n, grad_t, grad_n, held, pulls, mixed_t, dq, dk, dv,
     clips, first_ref, count_ref,
 ):
     side = core()
@@ -253,78 +259,83 @@
     dk[...] = jnp.zeros_like(dk)
     dv[...] = jnp.zeros_like(dv)
 
-    def query_step(tile, carry):
-        first, count = first_ref[tile], count_ref[tile]
-
-        def score_step(step, top):
+    def whole_tile(tile, first, count):
+        tops = []
+        grad = grad_t[tile]
+        for step in range(count):
             scores = mm(key_n[blocks(first, step)[1], :], query_t[tile])
             held[step] = scores
-            return jnp.maximum(top, jnp.max(scores, axis=0, keepdims=True))
-
-        top = lax.fori_loop(0, count, score_step, jnp.full((1, TILE), 2.0 * FAR, F32))
-
-        def value_step(step, total):
+            tops.append(jnp.max(scores, axis=0, keepdims=True))
+            pulls[step] = mm(value_n[blocks(first, step)[1], :], grad)
+        top = tops[0]
+        for other in tops[1:]:
+            top = jnp.maximum(top, other)
+        total = None
+        for step in range(count):
             weights = jnp.exp2((held[step] - top) * SCALE2)
             held[step] = weights
-            return total + mm(side_by_side(value_t, blocks(first, step)[0]), weights.astype(BF))
-
-        total = lax.fori_loop(0, count, value_step, jnp.zeros((80, TILE), F32))
+            term = mm(side_by_side(value_t, blocks(first, step)[0]), weights.astype(BF))
+            total = term if total is None else total + term
         inverse = 1.0 / total[HEAD_DIM : HEAD_DIM + 1]
         mixed = jnp.concatenate([total[0:HEAD_DIM] * inverse, jnp.zeros((8, TILE), F32)], 0).astype(BF)
-        grad = grad_t[tile]
         delta = jnp.sum(mixed.astype(F32) * grad[0:FULL].astype(F32), axis=0, keepdims=True)
         mixed_t[tile] = mixed
-
-        def grad_step(step, total):
+        total = None
+        for step in range(count):
             start, rows = blocks(first, step)
             prob = held[step] * inverse
-            pull = mm(value_n[rows, :], grad)
+            pull = pulls[step]
             dv[rows, :] += mm(prob.astype(BF), grad_n[tile])
             score_grad = (prob * (pull - delta)).astype(BF)
             dk[rows, :] += mm(score_grad, query_n[tile])
-            return total + mm(side_by_side(key_t, start), score_grad)
-
-        dq[tile] = lax.fori_loop(0, count, grad_step, jnp.zeros((80, TILE), F32)) * SCALE
+            term = mm(side_by_side(key_t, start), score_grad)
+            total = term if total is None else total + term
+        dq[tile] = total * SCALE
+
+    def query_step(tile, carry):
+        first, count = first_ref[tile], count_ref[tile]
+        for steps in range(1, CHUNKS + 1):
+            pl.when(count == steps)(lambda steps=steps: whole_tile(tile, first, steps))
         return carry
 
     lax.fori_loop(0, TILES, query_step, 0)
-
-    def halves(wholes):
-        low = jnp.concatenate([whole[0:HALF] for whole in wholes], 0)
-        high = jnp.concatenate([whole[HALF:] for whole in wholes], 0)
-        return pick(side, low, high).astype(BF), pick(side, high, low).astype(BF)
 
     def key_grads(at):
         rows = token_rows(at)
         return [dk[rows, :].T[0:FULL] * SCALE, dv[rows, :].T[0:FULL]]
+
+    def hand_out(keep, give, block, wholes):
+        first, second = halves(side, wholes)
+        keep[block], give[block] = first.astype(BF), second.astype(BF)
 
     for block in range(SIDE):
         tile, cols = block // PART, slice((block % PART) * TOK, (block % PART + 1) * TOK)
         mixed = mixed_t[tile, :, cols]
         mixed_ref[block] = mixed
-        keep_asked_ref[block], give_asked_ref[block] = halves([mixed.astype(F32), dq[tile, :, cols]])
-        keep_ref[block], give_ref[block] = halves(key_grads(EDGE + block))
+        hand_out(keep_asked_ref, give_asked_ref, block, [mixed.astype(F32), dq[tile, :, cols]])
+        hand_out(keep_ref, give_ref, block, key_grads(EDGE + block))
     for block in range(EDGE):
-        keep_ref[SIDE + block], give_ref[SIDE + block] = halves(key_grads(block + NEAR * (1 - side)))
-        keep_far_ref[block], give_far_ref[block] = halves(key_grads(block + NEAR * side))
+        hand_out(keep_ref, give_ref, SIDE + block, key_grads(block + NEAR * (1 - side)))
+        far_ref[block] = jnp.concatenate(key_grads(block + NEAR * side), 0).astype(BF)
 
 
 def attend(own, near, asked, far_own, far_other):
     whole = jax.ShapeDtypeStruct((SIDE, FULL, TOK), BF)
     keys = jax.ShapeDtypeStruct((NEAR, FULL, TOK), BF)
-    edge = jax.ShapeDtypeStruct((EDGE, FULL, TOK), BF)
+    edge = jax.ShapeDtypeStruct((EDGE, 2 * FULL, TOK), BF)
     row_form = pltpu.VMEM((ROOM * TOK, TOK), BF)
     column_form = pltpu.VMEM((ROOM, 80, TOK), BF)
     return pl.pallas_call(
         attend_body,
-        out_shape=(whole, whole, whole, keys, keys, edge, edge),
+        out_shape=(whole, whole, whole, keys, keys, edge),
         in_specs=[WHOLE] * 5,
-        out_specs=(WHOLE,) * 7,
+        out_specs=(WHOLE,) * 6,
         cost_estimate=cost(20),
         scratch_shapes=[
             row_form, column_form, row_form, column_form,
             pltpu.VMEM((TILES, TOK, TILE), BF), pltpu.VMEM((TILES, TILE, TOK), BF),
             pltpu.VMEM((TILES, TOK, TILE), BF), pltpu.VMEM((TILES, TILE, TOK), BF),
+            pltpu.VMEM((CHUNKS, STEP * TOK, TILE), F32),
             pltpu.VMEM((CHUNKS, STEP * TOK, TILE), F32),
             pltpu.VMEM((TILES, FULL, TILE), BF),
             pltpu.VMEM((TILES, FULL, TILE), F32),
@@ -389,26 +400,32 @@
     )(mixed, other, branch)
 
 
-def join_asked_body(keep, got, out_ref):
+def fold_body(keep, give, far, keep_ref, give_ref):
     side = core()
-    for block in range(SIDE):
-        out_ref[SIDE * side + block] = keep[block]
-        out_ref[SIDE * (1 - side) + block] = got[block]
-
-
-def join_asked(keep, got):
-    return pl.pallas_call(
-        join_asked_body,
-        out_shape=jax.ShapeDtypeStruct((PLANE, FULL, TOK), BF),
-        in_specs=[WHOLE] * 2,
-        out_specs=WHOLE,
+    keep_ref[...] = keep[...]
+    give_ref[...] = give[...]
+    for block in range(EDGE):
+        place = block + (SIDE - EDGE) * side
+        whole = far[block].astype(F32)
+        first, second = halves(side, [whole[0:FULL], whole[FULL:]])
+        keep_ref[place] = (keep[place].astype(F32) + first).astype(BF)
+        give_ref[place] = (give[place].astype(F32) + second).astype(BF)
+
+
+def fold(keep, give, far):
+    keys = jax.ShapeDtypeStruct((NEAR, FULL, TOK), BF)
+    return pl.pallas_call(
+        fold_body,
+        out_shape=(keys, keys),
+        in_specs=[WHOLE] * 3,
+        out_specs=(WHOLE,) * 2,
         compiler_params=params(8),
         cost_estimate=cost(1),
-        name="join_asked",
-    )(keep, got)
-
-
-def join_body(keep, got, got_same, got_cross, term, term1, term2, term3, out_ref, total, pairs):
+        name="fold",
+    )(keep, give, far)
+
+
+def join_body(keep_asked, got_asked, keep, got, term, term1, term2, term3, out_ref, total, pairs):
     side = core()
     total[0:SHARE] = sum(one[...].astype(F32) for one in (term, term1, term2, term3))
     total[SHARE:] = jnp.zeros((8, TOK), F32)
@@ -416,22 +433,20 @@
     for block in range(SIDE):
         pairs[mine + block] = keep[block].astype(F32)
         pairs[others + block] = got[block].astype(F32)
-    late, early = (SIDE - EDGE) * side, (SIDE - EDGE) * (1 - side)
     for block in range(EDGE):
-        pairs[others + late + block] += keep[SIDE + block].astype(F32)
-        pairs[mine + early + block] += got[SIDE + block].astype(F32)
-    for block in range(EDGE):
-        pairs[others + early + block] += got_same[block].astype(F32)
-        pairs[mine + late + block] += got_cross[block].astype(F32)
-    for block in range(PLANE):
-        start = (block % SIDE) * FINAL
-        out_ref[block] = jnp.concatenate([pairs[block], total[start : start + 16, :]], 0).astype(BF)
+        pairs[others + (SIDE - EDGE) * side + block] += keep[SIDE + block].astype(F32)
+        pairs[mine + (SIDE - EDGE) * (1 - side) + block] += got[SIDE + block].astype(F32)
+    for block in range(SIDE):
+        tail = total[block * FINAL : block * FINAL + 16, :]
+        for start, asked in ((mine, keep_asked), (others, got_asked)):
+            whole = [asked[block].astype(F32), pairs[start + block], tail]
+            out_ref[start + block] = jnp.concatenate(whole, 0).astype(BF)
 
 
 def join(*values):
     return pl.pallas_call(
         join_body,
-        out_shape=jax.ShapeDtypeStruct((PLANE, FULL + 16, TOK), BF),
+        out_shape=jax.ShapeDtypeStruct((PLANE, 2 * FULL + 16, TOK), BF),
         in_specs=[WHOLE] * 8,
         out_specs=WHOLE,
         scratch_shapes=[pltpu.VMEM((SHARE + 8, TOK), F32), pltpu.VMEM((PLANE, FULL, TOK), F32)],
@@ -441,55 +456,39 @@
     )(*values)
 
 
-def all_heads(packed, at):
-    low = slice(at * HALF, (at + 1) * HALF)
-    high = slice(at * HALF, at * HALF + HEAD_DIM - HALF)
-    parts = []
-    for head in range(HEADS):
-        parts += [packed[2 * head].astype(F32)[low], packed[2 * head + 1].astype(F32)[high]]
-    return jnp.concatenate(parts, 0).T.astype(BF)
-
-
-def finish_asked_body(packed, residual, tags, gate, weight, bias, out_ref, dq_ref):
+def finish_body(packed, residual, tags, gate, weight, bias, out_ref, dq_ref, dk_ref, dv_ref, dw_ref):
+    def rows(at):
+        low = slice(at * HALF, (at + 1) * HALF)
+        high = slice(at * HALF, at * HALF + HEAD_DIM - HALF)
+        parts = []
+        for head in range(HEADS):
+            parts += [packed[2 * head].astype(F32)[low], packed[2 * head + 1].astype(F32)[high]]
+        return jnp.concatenate(parts, 0).T.astype(BF)
+
     gate_rows = lax.dot_general(
         clip_onehot(tags), gate[...], (((0,), (0,)), ((), ())),
         precision=lax.Precision.HIGHEST, preferred_element_type=F32,
     )
-    projected = mm(all_heads(packed, 0), weight[...]) + bias[...].reshape(1, WIDTH)
+    projected = mm(rows(0), weight[...]) + bias[...].reshape(1, WIDTH)
     out_ref[...] = (residual[...].astype(F32) + gate_rows * projected).astype(BF)
-    dq_ref[...] = all_heads(packed, 1)
-
-
-def finish_asked(packed, residual, tags, gate, weight, bias):
-    return pl.pallas_call(
-        finish_asked_body,
-        out_shape=(jax.ShapeDtypeStruct((TOK, WIDTH), BF),) * 2,
+    dq_ref[...] = rows(1)
+    dk_ref[...] = rows(2)
+    dv_ref[...] = rows(3)
+    source = lax.rem(lax.axis_index("dp"), PLANE) // SIDE
+    tails = [packed[2 * head + source, 2 * FULL :].astype(F32)[:, 0:HEAD_DIM] for head in range(HEADS)]
+    dw_ref[...] = jnp.concatenate(tails, 1)[0:FINAL]
+
+
+def finish(packed, residual, tags, gate, weight, bias):
+    return pl.pallas_call(
+        finish_body,
+        out_shape=(jax.ShapeDtypeStruct((TOK, WIDTH), BF),) * 4 + (jax.ShapeDtypeStruct((FINAL, WIDTH), F32),),
         in_specs=[WHOLE] * 6,
-        out_specs=(WHOLE,) * 2,
+        out_specs=(WHOLE,) * 5,
         compiler_params=params(16),
-        cost_estimate=cost(2),
-        name="finish_asked",
+        cost_estimate=cost(3),
+        name="finish",
     )(packed, residual, tags, gate, weight, bias)
-
-
-def finish_body(packed, dk_ref, dv_ref, dw_ref):
-    dk_ref[...] = all_heads(packed, 0)
-    dv_ref[...] = all_heads(packed, 1)
-    source = lax.rem(lax.axis_index("dp"), PLANE) // SIDE
-    tails = [packed[2 * head + source, FULL:].astype(F32)[:, 0:HEAD_DIM] for head in range(HEADS)]
-    dw_ref[...] = jnp.concatenate(tails, 1)[0:FINAL]
-
-
-def finish(packed):
-    return pl.pallas_call(
-        finish_body,
-        out_shape=(jax.ShapeDtypeStruct((TOK, WIDTH), BF),) * 2 + (jax.ShapeDtypeStruct((FINAL, WIDTH), F32),),
-        in_specs=[WHOLE],
-        out_specs=(WHOLE,) * 3,
-        compiler_params=params(16),
-        cost_estimate=cost(1),
-        name="finish",
-    )(packed)
 
 
 def sent(values, target):
@@ -499,14 +498,6 @@
 
 def other_core(device):
     return device ^ 1
-
-
-def same_out(device):
-    return device + PLANE if device % 2 == 0 else device - PLANE
-
-
-def same_back(device):
-    return device - PLANE if device % 2 == 0 else device + PLANE
 
 
 def cross(device):
@@ -538,22 +529,18 @@
     own = traded(chunk)
     near = sent(some_blocks(own, (SIDE - EDGE) * (1 - side), 0, NEAR), other_core)
     asked = sent(some_blocks(own, SIDE * (1 - side), FULL, SIDE), other_core)
-    last = PLANE - EDGE
-    far_own = sent(some_blocks(own, last * (1 - side), 0, EDGE), same_out)
-    far_other = sent(some_blocks(own, last * side, 0, EDGE), cross)
-    mixed, keep_asked, give_asked, keep, give, keep_far, give_far = attend(own, near, asked, far_own, far_other)
-    joined = join_asked(keep_asked, sent(give_asked, other_core))
-    joined, mixed, give, keep_far, give_far = lax.optimization_barrier((joined, mixed, give, keep_far, give_far))
-    asked_back = traded(joined)
+    far_other = sent(some_blocks(own, (PLANE - EDGE) * side, 0, EDGE), cross)
+    far_own = sent(some_blocks(near, SIDE * side, 0, EDGE), cross)
+    mixed, keep_asked, give_asked, keep, give, far = attend(own, near, asked, far_own, far_other)
+    far = sent(far, cross)
     mixed_other = sent(mixed, other_core)
-    got = sent(give, other_core)
-    got_same = sent(keep_far, same_back)
-    got_cross = sent(give_far, cross)
+    got_asked = sent(give_asked, other_core)
     term, *terms = weight_term(mixed, mixed_other, gathered)
     terms = [sent(one, planes_on(away + 1)) for away, one in enumerate(terms)]
-    keys_back = traded(join(keep, got, got_same, got_cross, term, *terms))
-    block_out, dq = finish_asked(asked_back, residual, tags, gate, weight, bias)
-    dk, dv, dw = finish(keys_back)
+    keep, give = fold(keep, give, far)
+    got = sent(give, other_core)
+    packed = traded(join(keep_asked, got_asked, keep, got, term, *terms))
+    block_out, dq, dk, dv, dw = finish(packed, residual, tags, gate, weight, bias)
     return block_out, dq, dk, dv, dw.T
 
 

time: 142 us -> 132 us (0.930)
  blocking collectives: 0 us -> 27 us
  starting transfers between devices: 42.6 us -> 24 us
  Pallas kernels: 34.8 us -> 28 us
  local copies, waits for them, and re-layouts: 8.28 us -> 2.45 us
  waiting for transfers between devices: 40.1 us -> 35.4 us
    all_to_all x0 -> x1, blocking collectives: none -> 27 us  [traded(): lax.all_to_all(values, 'dp', 0, 0, axis_index_groups=groups, tiled=True)]
    all_to_all x3 -> x1, starting transfers between devices: 20.7 us -> 8.16 us  [traded(): lax.all_to_all(values, 'dp', 0, 0, axis_index_groups=groups, tiled=True)]
    all_to_all x3 -> x1, waiting for transfers between devices: 35.4 us -> 24 us  [traded(): lax.all_to_all(values, 'dp', 0, 0, axis_index_groups=groups, tiled=True)]
    ppermute x13 -> x12, waiting for transfers between devices: 4.63 us -> 11.4 us  [sent(): lax.ppermute(values, 'dp', [(i, j) for i, j in pairs if 0 <= j < DEVICES])]
    ppermute x13 -> x12, starting transfers between devices: 21.9 us -> 15.8 us  [sent(): lax.ppermute(values, 'dp', [(i, j) for i, j in pairs if 0 <= j < DEVICES])]
    unnamed x36 -> x12, local copies, waits for them, and re-layouts: 8.19 us -> 2.37 us
    pallas_call x3 -> x2, Pallas kernels: 4 us -> 0.49 us  [the longest x1 0.34 us: join(): pl.pallas_call(join_body, out_shape=jax.ShapeDtypeStruct((PLANE, 2 * FULL...]
    pallas_call x1, Pallas kernels: 18.3 us -> 15.2 us  [attend(): pl.pallas_call(attend_body, out_shape=(whole, whole, whole, keys, keys, e...]
  transfers between devices with their start and end apart: 17 -> 14, of which waited for: 5 -> 6; matrix products, arithmetic and copies ran while one was open for 0% -> 0% of each run, Pallas kernels for 21% -> 17%
where the time goes in v9:
time: 132 us; the launch traced here: 131 us
  waiting for transfers between devices  35.4 us (27%)
  Pallas kernels  28 us (21%)
  blocking collectives  27 us (20%)
  starting transfers between devices  24 us (18%)
  between operations  14.2 us (11%)
  local copies, waits for them, and re-layouts  2.45 us (2%)
    all_to_all x1, blocking collectives, traded(): lax.all_to_all(values, 'dp', 0, 0, axis_index_groups=groups, tiled=True)  27 us
    all_to_all x1, waiting for transfers between devices, traded(): lax.all_to_all(values, 'dp', 0, 0, axis_index_groups=groups, tiled=True)  24 us
    ppermute x12, starting transfers between devices, sent(): lax.ppermute(values, 'dp', [(i, j) for i, j in pairs if 0 <= j < DEVICES])  15.8 us
    pallas_call x1, Pallas kernels, attend(): pl.pallas_call(attend_body, out_shape=(whole, whole, whole, keys, keys, e...  15.2 us
    ppermute x12, waiting for transfers between devices, sent(): lax.ppermute(values, 'dp', [(i, j) for i, j in pairs if 0 <= j < DEVICES])  11.4 us
    all_to_all x1, starting transfers between devices, traded(): lax.all_to_all(values, 'dp', 0, 0, axis_index_groups=groups, tiled=True)  8.16 us
    pallas_call x1, Pallas kernels, pack(): pl.pallas_call(pack_body, out_shape=jax.ShapeDtypeStruct((PLANE, 2 * FULL...  4.99 us
  transfers between devices with their start and end apart: 14, of which 6 were waited for; matrix products, arithmetic and copies ran while one was open for 0% of the time, Pallas kernels for 17%

profile of v9, /device:TPU:1, one launch (start us, length us, event | category | flops | bytes accessed | tf_op | source)
XLA Modules:
  0.0 131.1 jit_solution(1265720896744228166)
XLA Ops:
  7.2 0.0 all-gather.3.cloned.1.call-start
  7.2 2.5 %branch_columns.1 = (bf16[1152,128]{1,0:T(8,128)(2,1)}, bf16[2,576,128]{2,1,0:T(8,128)(2,1)}, bf16[576,128]{1,0:T(8,128)(2,1)}) custom-call(bf16[128,1152]{1,0:T(8,128)(2,1)} %out_grad.1, s32[128]{0:T(128)} %tags.5, f32[32,1152]{1,0:T(8,128)} %gate.3), custom_call_target="tpu_custom_call" | custom-call | flops 800000000 | bytes 4000000 | tf_op jit(solution)/shard_map/branch_columns/pallas_call | solution.py:87
  9.8 1.4 %collective-permute-start = (bf16[576,128]{1,0:T(8,128)(2,1)}, bf16[576,128]{1,0:T(8,128)(2,1)S(1)}, u32[]{:S(2)}, u32[]{:S(2)}) collective-permute-start(bf16[576,128]{1,0:T(8,128)(2,1)} %get-tuple-element.27), channel_id=1, source_target_pairs={{0,1},{1,0},{2,3},{3,2},{4,5},{5,4},{6,7},{7,6},{8,9},{9,8},{10,11... | collective-permute-start | bytes 442376 | tf_op jit(solution)/shard_map/ppermute | solution.py:496
  11.2 5.0 %pack.1 = bf16[32,160,128]{2,1,0:T(8,128)(2,1)} custom-call(bf16[128,1152]{1,0:T(8,128)(2,1)} %query.1, bf16[128,1152]{1,0:T(8,128)(2,1)} %key.1, bf16[128,1152]{1,0:T(8,128)(2,1)} %value.1, s32[128]{0:T(128)} %tags.5, bf16[1152,128]{1,0:T(8,128)(2,1)} %get-tuple-element.28.branch, bf16[1152,1152]{1,0:T(8,128)(2,1)} %weight.3), custom_call_target="tpu_custom_call" | custom-call | flops 1600000000 | bytes 8000000 | tf_op jit(solution)/shard_map/pack/pallas_call | solution.py:142
  16.2 0.0 collective-permute-done.got
  16.2 0.7 fill.1
  16.9 0.0 all-gather.3.cloned.1.call-update
  16.9 8.2 %all-to-all-start = ((bf16[32,160,128]{2,1,0:T(8,128)(2,1)}), bf16[32,160,128]{2,1,0:T(8,128)(2,1)S(1)}, u32[]{:S(2)}, u32[]{:S(2)}) async-start(bf16[32,160,128]{2,1,0:T(8,128)(2,1)} %pack.1), calls=%async_computation | async-start | bytes 2621440 | tf_op jit(solution)/shard_map/all_to_all | solution.py:513
  25.1 24.0 %all-to-all-done.own = bf16[32,160,128]{2,1,0:T(8,128)(2,1)S(1)} async-done(((bf16[32,160,128]{2,1,0:T(8,128)(2,1)}), bf16[32,160,128]{2,1,0:T(8,128)(2,1)S(1)}, u32[]{:S(2)}, u32[]{:S(2)}) %all-to-all-start) | async-done | bytes 1310752 | tf_op jit(solution)/shard_map/all_to_all | solution.py:513
  49.1 0.6 collective-permute-start.1
  49.7 0.1 collective-permute-start.2
  49.8 3.5 %collective-permute-start.4 = (bf16[7,80,128]{2,1,0:T(8,128)(2,1)S(1)}, bf16[7,80,128]{2,1,0:T(8,128)(2,1)S(1)}, u32[]{:S(2)}, u32[]{:S(2)}) collective-permute-start(bf16[7,80,128]{2,1,0:T(8,128)(2,1)S(1)} %constant_dynamic-slice_fusion), channel_id=1, source_target_pairs={{1,32},{3,34},{5,36},{7,38},{9,40},{11,42},{13,44},{15,46},{17,48}... | collective-permute-start | bytes 430088 | tf_op jit(solution)/shard_map/ppermute | solution.py:496
  53.3 0.0 collective-permute-done.1.near
  53.4 2.0 %collective-permute-start.3 = (bf16[7,80,128]{2,1,0:T(8,128)(2,1)S(1)}, bf16[7,80,128]{2,1,0:T(8,128)(2,1)S(1)}, u32[]{:S(2)}, u32[]{:S(2)}) collective-permute-start(bf16[7,80,128]{2,1,0:T(8,128)(2,1)S(1)} %constant_dynamic-slice_fusion.1), channel_id=1, source_target_pairs={{1,32},{3,34},{5,36},{7,38},{9,40},{11,42},{13,44},{15,46},{17,48}... | collective-permute-start | bytes 430088 | tf_op jit(solution)/shard_map/ppermute | solution.py:496
  55.4 0.8 collective-permute-done.4.far_other
  56.2 0.0 collective-permute-done.2.asked
  56.2 3.6 %collective-permute-done.3.far_own = bf16[7,80,128]{2,1,0:T(8,128)(2,1)S(1)} collective-permute-done((bf16[7,80,128]{2,1,0:T(8,128)(2,1)S(1)}, bf16[7,80,128]{2,1,0:T(8,128)(2,1)S(1)}, u32[]{:S(2)}, u32[]{:S(2)}) %collective-permute-start.3) | collective-permute-done | bytes 143392 | tf_op jit(solution)/shard_map/ppermute | solution.py:496
  59.8 15.2 %attend.1 = (bf16[16,80,128]{2,1,0:T(8,128)(2,1)S(1)}, bf16[16,80,128]{2,1,0:T(8,128)(2,1)S(1)}, bf16[16,80,128]{2,1,0:T(8,128)(2,1)S(1)}, bf16[23,80,128]{2,1,0...) custom-call(bf16[32,160,128]{2,1,0:T(8,128)(2,1)S(1)} %all-to-all-done.own, ...), custom_call_target="tpu_custom_call" | custom-call | flops 8000000000 | bytes 40000000 | tf_op jit(solution)/shard_map/attend/pallas_call | solution.py:328
  75.0 1.9 %collective-permute-start.6 = (bf16[7,160,128]{2,1,0:T(8,128)(2,1)S(1)}, bf16[7,160,128]{2,1,0:T(8,128)(2,1)S(1)}, u32[]{:S(2)}, u32[]{:S(2)}) collective-permute-start(bf16[7,160,128]{2,1,0:T(8,128)(2,1)S(1)} %get-tuple-element.34), channel_id=1, source_target_pairs={{1,32},{3,34},{5,36},{7,38},{9,40},{11,42},{13,44},{15,46},{17,48}... | collective-permute-start | bytes 860168 | tf_op jit(solution)/shard_map/ppermute | solution.py:496
  76.9 0.1 collective-permute-start.8
  77.0 5.9 %collective-permute-done.6.far = bf16[7,160,128]{2,1,0:T(8,128)(2,1)S(1)} collective-permute-done((bf16[7,160,128]{2,1,0:T(8,128)(2,1)S(1)}, bf16[7,160,128]{2,1,0:T(8,128)(2,1)S(1)}, u32[]{:S(2)}, u32[]{:S(2)}) %collective-permute-start.6) | collective-permute-done | bytes 286752 | tf_op jit(solution)/shard_map/ppermute | solution.py:496
  82.9 0.1 fold.1
  83.1 0.1 collective-permute-start.7
  83.2 0.5 collective-permute-start.5
  83.7 0.0 collective-permute-done.8.other
  83.7 0.0 all-gather.3.cloned.1.call-done
  83.7 2.3 %copy-done.5 = bf16[32,576,128]{2,1,0:T(8,128)(2,1)S(1)} copy-done((bf16[32,576,128]{2,1,0:T(8,128)(2,1)S(1)}, bf16[32,576,128]{2,1,0:T(8,128)(2,1)}, u32[]{:S(2)}) %copy-start.5) | copy-done | bytes 4718616
  86.0 2.2 %weight_term.1 = (bf16[144,128]{1,0:T(8,128)(2,1)S(1)}, bf16[144,128]{1,0:T(8,128)(2,1)S(1)}, bf16[144,128]{1,0:T(8,128)(2,1)S(1)}, bf16[144,128]{1,0:T(8,128)(2,1)S(1)}) custom-call(bf16[16,80,128]{2,1,0:T(8,128)(2,1)S(1)} %get-tuple-element.37.mixed, bf16[16,80,128]{2,1,0:T(8,128)(2,1)S(1)} %collective-permute-done.8.other, ...), custom_call_target="tpu_custom_call" | custom-call | flops 1600000000 | bytes 8000000 | tf_op jit(solution)/shard_map/weight_term/pallas_call | solution.py:390
  88.2 1.2 collective-permute-start.9
  89.4 2.3 %collective-permute-start.10 = (bf16[144,128]{1,0:T(8,128)(2,1)S(1)}, bf16[144,128]{1,0:T(8,128)(2,1)S(1)}, u32[]{:S(2)}, u32[]{:S(2)}) collective-permute-start(bf16[144,128]{1,0:T(8,128)(2,1)S(1)} %get-tuple-element.42), channel_id=1, source_target_pairs={{0,64},{1,65},{2,66},{3,67},{4,68},{5,69},{6,70},{7,71},{8,72},{9,... | collective-permute-start | bytes 110600 | tf_op jit(solution)/shard_map/ppermute | solution.py:496
  91.7 2.0 %collective-permute-start.11 = (bf16[144,128]{1,0:T(8,128)(2,1)S(1)}, bf16[144,128]{1,0:T(8,128)(2,1)S(1)}, u32[]{:S(2)}, u32[]{:S(2)}) collective-permute-start(bf16[144,128]{1,0:T(8,128)(2,1)S(1)} %get-tuple-element.43), channel_id=1, source_target_pairs={{0,96},{1,97},{2,98},{3,99},{4,100},{5,101},{6,102},{7,103},{8,104... | collective-permute-start | bytes 110600 | tf_op jit(solution)/shard_map/ppermute | solution.py:496
  93.7 0.0 collective-permute-done.5.got_asked
  93.7 0.0 collective-permute-done.7.got
  93.7 0.0 collective-permute-done.9.term1
  93.7 0.2 collective-permute-done.10.term2
  93.9 0.9 collective-permute-done.11.term3
  94.8 0.3 join.1
  95.2 0.0 copy-start
  95.2 0.0 copy-start.2
  95.2 0.0 copy-start.3
  95.2 0.0 copy-start.4
  95.2 27.0 %all_to_all.10.packed = bf16[32,176,128]{2,1,0:T(8,128)(2,1)S(1)} all-to-all(bf16[32,176,128]{2,1,0:T(8,128)(2,1)S(1)} %join.1), channel_id=1, replica_groups={{0,1,2,3,4,5,6,7,8,9,10,11,12,13,14,15,16,17,18,19,20,21,22,23,24,25,26..., dimensions={0} | all-to-all | bytes 2883584 | tf_op jit(solution)/shard_map/all_to_all | solution.py:513
  122.2 0.0 copy-done.1
  122.2 0.0 copy-done
  122.2 0.0 copy-done.2
  122.2 0.0 copy-done.3
  122.2 0.0 copy-done.4
  122.2 2.0 %finish.1 = (bf16[128,1152]{1,0:T(8,128)(2,1)}, bf16[128,1152]{1,0:T(8,128)(2,1)}, bf16[128,1152]{1,0:T(8,128)(2,1)}, bf16[128,1152]{1,0:T(8,128)(2,1)}, f32[9,1152]{1,0:T(8,128)}) custom-call(bf16[32,176,128]{2,1,0:T(8,128)(2,1)S(1)} %all_to_all.10.packed, bf16[128,1152]{1,0:T(8,128)(2,1)S(1)} %copy-done.1, s32[128]{0:T(128)S(1)} %copy-done.4, ...), custom_call_target="tpu_custom_call" | custom-call | flops 1200000000 | bytes 6000000 | tf_op jit(solution)/shard_map/finish/pallas_call | solution.py:483
  (6 shorter events, 0.1 us)
Async XLA Ops:
  7.2 76.5 %all-gather.3.cloned.1.call-start = ((), (), s32[]{:S(2)}) async-start(), calls=%async_computation.2 | async-start | bytes 5013504 | tf_op jit(solution)/shard_map/all_gather | solution.py:528
  9.8 6.4 %collective-permute-start = (bf16[576,128]{1,0:T(8,128)(2,1)}, bf16[576,128]{1,0:T(8,128)(2,1)S(1)}, u32[]{:S(2)}, u32[]{:S(2)}) collective-permute-start(bf16[576,128]{1,0:T(8,128)(2,1)} %get-tuple-element.27), channel_id=1, source_target_pairs={{0,1},{1,0},{2,3},{3,2},{4,5},{5,4},{6,7},{7,6},{8,9},{9,8},{10,11... | collective-permute-start | bytes 442376 | tf_op jit(solution)/shard_map/ppermute | solution.py:496
  16.9 32.2 %all-to-all-start = ((bf16[32,160,128]{2,1,0:T(8,128)(2,1)}), bf16[32,160,128]{2,1,0:T(8,128)(2,1)S(1)}, u32[]{:S(2)}, u32[]{:S(2)}) async-start(bf16[32,160,128]{2,1,0:T(8,128)(2,1)} %pack.1), calls=%async_computation | async-start | bytes 2621440 | tf_op jit(solution)/shard_map/all_to_all | solution.py:513
  49.1 4.3 %collective-permute-start.1 = (bf16[23,80,128]{2,1,0:T(8,128)(2,1)S(1)}, bf16[23,80,128]{2,1,0:T(8,128)(2,1)S(1)}, u32[]{:S(2)}, u32[]{:S(2)}) collective-permute-start(bf16[23,80,128]{2,1,0:T(8,128)(2,1)S(1)} %constant_dynamic-slice_fusion.3), channel_id=1, source_target_pairs={{0,1},{1,0},{2,3},{3,2},{4,5},{5,4},{6,7},{7,6},{8,9},{9,8},{10,11... | collective-permute-start | bytes 1413128 | tf_op jit(solution)/shard_map/ppermute | solution.py:496
  49.7 6.6 %collective-permute-start.2 = (bf16[16,80,128]{2,1,0:T(8,128)(2,1)S(1)}, bf16[16,80,128]{2,1,0:T(8,128)(2,1)S(1)}, u32[]{:S(2)}, u32[]{:S(2)}) collective-permute-start(bf16[16,80,128]{2,1,0:T(8,128)(2,1)S(1)} %constant_dynamic-slice_fusion.2), channel_id=1, source_target_pairs={{0,1},{1,0},{2,3},{3,2},{4,5},{5,4},{6,7},{7,6},{8,9},{9,8},{10,11... | collective-permute-start | bytes 983048 | tf_op jit(solution)/shard_map/ppermute | solution.py:496
  49.8 6.4 %collective-permute-start.4 = (bf16[7,80,128]{2,1,0:T(8,128)(2,1)S(1)}, bf16[7,80,128]{2,1,0:T(8,128)(2,1)S(1)}, u32[]{:S(2)}, u32[]{:S(2)}) collective-permute-start(bf16[7,80,128]{2,1,0:T(8,128)(2,1)S(1)} %constant_dynamic-slice_fusion), channel_id=1, source_target_pairs={{1,32},{3,34},{5,36},{7,38},{9,40},{11,42},{13,44},{15,46},{17,48}... | collective-permute-start | bytes 430088 | tf_op jit(solution)/shard_map/ppermute | solution.py:496
  53.4 6.4 %collective-permute-start.3 = (bf16[7,80,128]{2,1,0:T(8,128)(2,1)S(1)}, bf16[7,80,128]{2,1,0:T(8,128)(2,1)S(1)}, u32[]{:S(2)}, u32[]{:S(2)}) collective-permute-start(bf16[7,80,128]{2,1,0:T(8,128)(2,1)S(1)} %constant_dynamic-slice_fusion.1), channel_id=1, source_target_pairs={{1,32},{3,34},{5,36},{7,38},{9,40},{11,42},{13,44},{15,46},{17,48}... | collective-permute-start | bytes 430088 | tf_op jit(solution)/shard_map/ppermute | solution.py:496
  75.0 8.0 %collective-permute-start.6 = (bf16[7,160,128]{2,1,0:T(8,128)(2,1)S(1)}, bf16[7,160,128]{2,1,0:T(8,128)(2,1)S(1)}, u32[]{:S(2)}, u32[]{:S(2)}) collective-permute-start(bf16[7,160,128]{2,1,0:T(8,128)(2,1)S(1)} %get-tuple-element.34), channel_id=1, source_target_pairs={{1,32},{3,34},{5,36},{7,38},{9,40},{11,42},{13,44},{15,46},{17,48}... | collective-permute-start | bytes 860168 | tf_op jit(solution)/shard_map/ppermute | solution.py:496
  76.9 6.8 %collective-permute-start.8 = (bf16[16,80,128]{2,1,0:T(8,128)(2,1)S(1)}, bf16[16,80,128]{2,1,0:T(8,128)(2,1)S(1)}, u32[]{:S(2)}, u32[]{:S(2)}) collective-permute-start(bf16[16,80,128]{2,1,0:T(8,128)(2,1)S(1)} %get-tuple-element.37.mixed), channel_id=1, source_target_pairs={{0,1},{1,0},{2,3},{3,2},{4,5},{5,4},{6,7},{7,6},{8,9},{9,8},{10,11... | collective-permute-start | bytes 983048 | tf_op jit(solution)/shard_map/ppermute | solution.py:496
  83.1 10.6 %collective-permute-start.7 = (bf16[23,80,128]{2,1,0:T(8,128)(2,1)S(1)}, bf16[23,80,128]{2,1,0:T(8,128)(2,1)S(1)}, u32[]{:S(2)}, u32[]{:S(2)}) collective-permute-start(bf16[23,80,128]{2,1,0:T(8,128)(2,1)S(1)} %get-tuple-element.36), channel_id=1, source_target_pairs={{0,1},{1,0},{2,3},{3,2},{4,5},{5,4},{6,7},{7,6},{8,9},{9,8},{10,11... | collective-permute-start | bytes 1413128 | tf_op jit(solution)/shard_map/ppermute | solution.py:496
  83.2 10.5 %collective-permute-start.5 = (bf16[16,80,128]{2,1,0:T(8,128)(2,1)S(1)}, bf16[16,80,128]{2,1,0:T(8,128)(2,1)S(1)}, u32[]{:S(2)}, u32[]{:S(2)}) collective-permute-start(bf16[16,80,128]{2,1,0:T(8,128)(2,1)S(1)} %get-tuple-element.31), channel_id=1, source_target_pairs={{0,1},{1,0},{2,3},{3,2},{4,5},{5,4},{6,7},{7,6},{8,9},{9,8},{10,11... | collective-permute-start | bytes 983048 | tf_op jit(solution)/shard_map/ppermute | solution.py:496
  83.7 2.3 %copy-start.5 = (bf16[32,576,128]{2,1,0:T(8,128)(2,1)S(1)}, bf16[32,576,128]{2,1,0:T(8,128)(2,1)}, u32[]{:S(2)}) copy-start(bf16[32,576,128]{2,1,0:T(8,128)(2,1)} %all-gather.3.cloned.1.call-done) | copy-start | bytes 14155780
  88.2 5.5 %collective-permute-start.9 = (bf16[144,128]{1,0:T(8,128)(2,1)S(1)}, bf16[144,128]{1,0:T(8,128)(2,1)S(1)}, u32[]{:S(2)}, u32[]{:S(2)}) collective-permute-start(bf16[144,128]{1,0:T(8,128)(2,1)S(1)} %get-tuple-element.41), channel_id=1, source_target_pairs={{0,32},{1,33},{2,34},{3,35},{4,36},{5,37},{6,38},{7,39},{8,40},{9,... | collective-permute-start | bytes 110600 | tf_op jit(solution)/shard_map/ppermute | solution.py:496
  89.4 4.6 %collective-permute-start.10 = (bf16[144,128]{1,0:T(8,128)(2,1)S(1)}, bf16[144,128]{1,0:T(8,128)(2,1)S(1)}, u32[]{:S(2)}, u32[]{:S(2)}) collective-permute-start(bf16[144,128]{1,0:T(8,128)(2,1)S(1)} %get-tuple-element.42), channel_id=1, source_target_pairs={{0,64},{1,65},{2,66},{3,67},{4,68},{5,69},{6,70},{7,71},{8,72},{9,... | collective-permute-start | bytes 110600 | tf_op jit(solution)/shard_map/ppermute | solution.py:496
  91.7 3.1 %collective-permute-start.11 = (bf16[144,128]{1,0:T(8,128)(2,1)S(1)}, bf16[144,128]{1,0:T(8,128)(2,1)S(1)}, u32[]{:S(2)}, u32[]{:S(2)}) collective-permute-start(bf16[144,128]{1,0:T(8,128)(2,1)S(1)} %get-tuple-element.43), channel_id=1, source_target_pairs={{0,96},{1,97},{2,98},{3,99},{4,100},{5,101},{6,102},{7,103},{8,104... | collective-permute-start | bytes 110600 | tf_op jit(solution)/shard_map/ppermute | solution.py:496
  94.8 27.4 %copy-start.1 = (bf16[128,1152]{1,0:T(8,128)(2,1)S(1)}, bf16[128,1152]{1,0:T(8,128)(2,1)}, u32[]{:S(2)}) copy-start(bf16[128,1152]{1,0:T(8,128)(2,1)} %residual.1) | copy-start | bytes 884740
  95.2 27.0 %copy-start = (bf16[1152,1152]{1,0:T(8,128)(2,1)S(1)}, bf16[1152,1152]{1,0:T(8,128)(2,1)}, u32[]{:S(2)}) copy-start(bf16[1152,1152]{1,0:T(8,128)(2,1)} %weight.3) | copy-start | bytes 7962628
  95.2 27.0 %copy-start.2 = (f32[32,1152]{1,0:T(8,128)S(1)}, f32[32,1152]{1,0:T(8,128)}, u32[]{:S(2)}) copy-start(f32[32,1152]{1,0:T(8,128)} %gate.3) | copy-start | bytes 442372
  95.2 27.0 %copy-start.3 = (f32[1152]{0:T(1024)S(1)}, f32[1152]{0:T(1024)}, u32[]{:S(2)}) copy-start(f32[1152]{0:T(1024)} %bias.1) | copy-start | bytes 13828
  95.2 27.0 %copy-start.4 = (s32[128]{0:T(128)S(1)}, s32[128]{0:T(128)}, u32[]{:S(2)}) copy-start(s32[128]{0:T(128)} %tags.5) | copy-start | bytes 1540
Sparse Core Ops, SparseCore 0:
  17.0 63.3 all-gather.2

commit v10 on v9

--- a/solution.py
+++ b/solution.py
@@ -119,15 +119,22 @@
     )(branch, got)
 
 
-def pack_body(query, key, value, tags, branch, weight, chunk_ref, weight_here, weight_sem):
-    load = pltpu.make_async_copy(weight, weight_here, weight_sem)
-    load.start()
-    key_t = key[...].astype(F32).T
-    value_t = value[...].astype(F32).T
-    query_t = query[...].astype(F32).T
+def pack_body(query, key, value, weight, tags, branch, chunk_ref, query_here, key_here, value_here, weight_here, sems):
+    loads = []
+    for at, (source, here) in enumerate(
+        ((key, key_here), (value, value_here), (query, query_here), (weight, weight_here))
+    ):
+        loads.append(pltpu.make_async_copy(source, here, sems.at[at]))
+        loads[-1].start()
     tag_rows = jnp.broadcast_to(tags[...].reshape(1, TOK).astype(F32) + 1.0, (8, TOK))
     blank = jnp.zeros((8, TOK), F32)
-    load.wait()
+    loads[0].wait()
+    key_t = key_here[...].astype(F32).T
+    loads[1].wait()
+    value_t = value_here[...].astype(F32).T
+    loads[2].wait()
+    query_t = query_here[...].astype(F32).T
+    loads[3].wait()
     grad_t = mm(weight_here[...], branch[...])
     for head in range(HEADS):
         start = head * HEAD_DIM
@@ -139,16 +146,17 @@
 
 
 def pack(query, key, value, tags, branch, weight):
+    rows = pltpu.VMEM((TOK, WIDTH), BF)
     return pl.pallas_call(
         pack_body,
         out_shape=jax.ShapeDtypeStruct((PLANE, 2 * FULL, TOK), BF),
-        in_specs=[WHOLE] * 5 + [FAR_AWAY],
+        in_specs=[FAR_AWAY] * 4 + [WHOLE] * 2,
         out_specs=WHOLE,
-        scratch_shapes=[pltpu.VMEM((WIDTH, WIDTH), BF), pltpu.SemaphoreType.DMA],
+        scratch_shapes=[rows, rows, rows, pltpu.VMEM((WIDTH, WIDTH), BF), pltpu.SemaphoreType.DMA((4,))],
         compiler_params=params(61),
         cost_estimate=cost(4),
         name="pack",
-    )(query, key, value, tags, branch, weight)
+    )(query, key, value, weight, tags, branch)
 
 
 def filled(piece, extra):
@@ -537,6 +545,7 @@
     got_asked = sent(give_asked, other_core)
     term, *terms = weight_term(mixed, mixed_other, gathered)
     terms = [sent(one, planes_on(away + 1)) for away, one in enumerate(terms)]
+    far, _ = lax.optimization_barrier((far, term))
     keep, give = fold(keep, give, far)
     got = sent(give, other_core)
     packed = traded(join(keep_asked, got_asked, keep, got, term, *terms))

time: 132 us -> 131 us (level)
  waiting for transfers between devices: 35.4 us -> 29.9 us
  starting transfers between devices: 24 us -> 26 us
  blocking collectives: 27 us -> 28.6 us
    ppermute x12, waiting for transfers between devices: 11.4 us -> 5.89 us  [sent(): lax.ppermute(values, 'dp', [(i, j) for i, j in pairs if 0 <= j < DEVICES])]
    ppermute x12, starting transfers between devices: 15.8 us -> 17.8 us  [sent(): lax.ppermute(values, 'dp', [(i, j) for i, j in pairs if 0 <= j < DEVICES])]
    all_to_all x1, blocking collectives: 27 us -> 28.6 us  [traded(): lax.all_to_all(values, 'dp', 0, 0, axis_index_groups=groups, tiled=True)]
    unnamed x12 -> x16, local copies, waits for them, and re-layouts: 2.37 us -> 3.14 us
  transfers between devices with their start and end apart: 14 -> 14, of which waited for: 6 -> 5; matrix products, arithmetic and copies ran while one was open for 0% -> 0% of each run, Pallas kernels for 17% -> 18%
where the time goes in v10:
time: 131 us
  waiting for transfers between devices  29.9 us (23%)
  Pallas kernels  28.6 us (22%)
  blocking collectives  28.6 us (22%)
  starting transfers between devices  26 us (20%)
  between operations  14.2 us (11%)
  local copies, waits for them, and re-layouts  3.23 us (2%)
    all_to_all x1, blocking collectives, traded(): lax.all_to_all(values, 'dp', 0, 0, axis_index_groups=groups, tiled=True)  28.6 us
    all_to_all x1, waiting for transfers between devices, traded(): lax.all_to_all(values, 'dp', 0, 0, axis_index_groups=groups, tiled=True)  24 us
    ppermute x12, starting transfers between devices, sent(): lax.ppermute(values, 'dp', [(i, j) for i, j in pairs if 0 <= j < DEVICES])  17.8 us
    pallas_call x1, Pallas kernels, attend(): pl.pallas_call(attend_body, out_shape=(whole, whole, whole, keys, keys, e...  15.7 us
    all_to_all x1, starting transfers between devices, traded(): lax.all_to_all(values, 'dp', 0, 0, axis_index_groups=groups, tiled=True)  8.16 us
    ppermute x12, waiting for transfers between devices, sent(): lax.ppermute(values, 'dp', [(i, j) for i, j in pairs if 0 <= j < DEVICES])  5.89 us
    pallas_call x1, Pallas kernels, pack(): pl.pallas_call(pack_body, out_shape=jax.ShapeDtypeStruct((PLANE, 2 * FULL...  5.04 us
    unnamed x16, local copies, waits for them, and re-layouts  3.14 us
  transfers between devices with their start and end apart: 14, of which 5 were waited for; matrix products, arithmetic and copies ran while one was open for 0% of the time, Pallas kernels for 18%

profile of v10, /device:TPU:1, one launch (start us, length us, event | category | flops | bytes accessed | tf_op | source)
XLA Modules:
  0.0 130.6 jit_solution(7299701442492174281)
XLA Ops:
  7.2 0.0 all-gather.3.cloned.1.call-start
  7.2 2.5 %branch_columns.1 = (bf16[1152,128]{1,0:T(8,128)(2,1)}, bf16[2,576,128]{2,1,0:T(8,128)(2,1)}, bf16[576,128]{1,0:T(8,128)(2,1)}) custom-call(bf16[128,1152]{1,0:T(8,128)(2,1)} %out_grad.1, s32[128]{0:T(128)} %tags.5, f32[32,1152]{1,0:T(8,128)} %gate.3), custom_call_target="tpu_custom_call" | custom-call | flops 800000000 | bytes 4000000 | tf_op jit(solution)/shard_map/branch_columns/pallas_call | solution.py:87
  9.8 1.4 %collective-permute-start = (bf16[576,128]{1,0:T(8,128)(2,1)}, bf16[576,128]{1,0:T(8,128)(2,1)S(1)}, u32[]{:S(2)}, u32[]{:S(2)}) collective-permute-start(bf16[576,128]{1,0:T(8,128)(2,1)} %get-tuple-element.28), channel_id=1, source_target_pairs={{0,1},{1,0},{2,3},{3,2},{4,5},{5,4},{6,7},{7,6},{8,9},{9,8},{10,11... | collective-permute-start | bytes 442376 | tf_op jit(solution)/shard_map/ppermute | solution.py:504
  11.2 5.0 %pack.1 = bf16[32,160,128]{2,1,0:T(8,128)(2,1)} custom-call(bf16[128,1152]{1,0:T(8,128)(2,1)} %query.1, bf16[128,1152]{1,0:T(8,128)(2,1)} %key.1, bf16[128,1152]{1,0:T(8,128)(2,1)} %value.1, bf16[1152,1152]{1,0:T(8,128)(2,1)} %weight.3, s32[128]{0:T(128)} %tags.5, bf16[1152,128]{1,0:T(8,128)(2,1)} %get-tuple-element.29.branch), custom_call_target="tpu_custom_call" | custom-call | flops 1600000000 | bytes 8000000 | tf_op jit(solution)/shard_map/pack/pallas_call | solution.py:150
  16.2 0.0 collective-permute-done.got
  16.2 0.7 fill.1
  16.9 0.0 all-gather.3.cloned.1.call-update
  16.9 8.2 %all-to-all-start = ((bf16[32,160,128]{2,1,0:T(8,128)(2,1)}), bf16[32,160,128]{2,1,0:T(8,128)(2,1)S(1)}, u32[]{:S(2)}, u32[]{:S(2)}) async-start(bf16[32,160,128]{2,1,0:T(8,128)(2,1)} %pack.1), calls=%async_computation | async-start | bytes 2621440 | tf_op jit(solution)/shard_map/all_to_all | solution.py:521
  25.1 24.0 %all-to-all-done.own = bf16[32,160,128]{2,1,0:T(8,128)(2,1)S(1)} async-done(((bf16[32,160,128]{2,1,0:T(8,128)(2,1)}), bf16[32,160,128]{2,1,0:T(8,128)(2,1)S(1)}, u32[]{:S(2)}, u32[]{:S(2)}) %all-to-all-start) | async-done | bytes 1310752 | tf_op jit(solution)/shard_map/all_to_all | solution.py:521
  49.1 0.6 collective-permute-start.1
  49.7 0.1 collective-permute-start.2
  49.9 3.5 %collective-permute-start.4 = (bf16[7,80,128]{2,1,0:T(8,128)(2,1)S(1)}, bf16[7,80,128]{2,1,0:T(8,128)(2,1)S(1)}, u32[]{:S(2)}, u32[]{:S(2)}) collective-permute-start(bf16[7,80,128]{2,1,0:T(8,128)(2,1)S(1)} %constant_dynamic-slice_fusion), channel_id=1, source_target_pairs={{1,32},{3,34},{5,36},{7,38},{9,40},{11,42},{13,44},{15,46},{17,48}... | collective-permute-start | bytes 430088 | tf_op jit(solution)/shard_map/ppermute | solution.py:504
  53.4 0.0 collective-permute-done.1.near
  53.4 2.0 %collective-permute-start.3 = (bf16[7,80,128]{2,1,0:T(8,128)(2,1)S(1)}, bf16[7,80,128]{2,1,0:T(8,128)(2,1)S(1)}, u32[]{:S(2)}, u32[]{:S(2)}) collective-permute-start(bf16[7,80,128]{2,1,0:T(8,128)(2,1)S(1)} %constant_dynamic-slice_fusion.1), channel_id=1, source_target_pairs={{1,32},{3,34},{5,36},{7,38},{9,40},{11,42},{13,44},{15,46},{17,48}... | collective-permute-start | bytes 430088 | tf_op jit(solution)/shard_map/ppermute | solution.py:504
  55.5 0.8 collective-permute-done.4.far_other
  56.3 0.0 collective-permute-done.2.asked
  56.3 3.6 %collective-permute-done.3.far_own = bf16[7,80,128]{2,1,0:T(8,128)(2,1)S(1)} collective-permute-done((bf16[7,80,128]{2,1,0:T(8,128)(2,1)S(1)}, bf16[7,80,128]{2,1,0:T(8,128)(2,1)S(1)}, u32[]{:S(2)}, u32[]{:S(2)}) %collective-permute-start.3) | collective-permute-done | bytes 143392 | tf_op jit(solution)/shard_map/ppermute | solution.py:504
  59.9 15.7 %attend.1 = (bf16[16,80,128]{2,1,0:T(8,128)(2,1)S(1)}, bf16[16,80,128]{2,1,0:T(8,128)(2,1)S(1)}, bf16[16,80,128]{2,1,0:T(8,128)(2,1)S(1)}, bf16[23,80,128]{2,1,0...) custom-call(bf16[32,160,128]{2,1,0:T(8,128)(2,1)S(1)} %all-to-all-done.own, ...), custom_call_target="tpu_custom_call" | custom-call | flops 8000000000 | bytes 40000000 | tf_op jit(solution)/shard_map/attend/pallas_call | solution.py:336
  75.5 0.0 copy-start.6
  75.6 0.8 copy-done.6
  76.3 0.0 collective-permute-start.7
  76.3 4.0 %collective-permute-start.6 = (bf16[7,160,128]{2,1,0:T(8,128)(2,1)S(1)}, bf16[7,160,128]{2,1,0:T(8,128)(2,1)S(1)}, u32[]{:S(2)}, u32[]{:S(2)}) collective-permute-start(bf16[7,160,128]{2,1,0:T(8,128)(2,1)S(1)} %get-tuple-element.35), channel_id=1, source_target_pairs={{1,32},{3,34},{5,36},{7,38},{9,40},{11,42},{13,44},{15,46},{17,48}... | collective-permute-start | bytes 860168 | tf_op jit(solution)/shard_map/ppermute | solution.py:504
  80.4 0.0 collective-permute-done.7.other
  80.4 0.1 all-gather.3.cloned.1.call-done
  80.4 2.3 %copy-done.5 = bf16[32,576,128]{2,1,0:T(8,128)(2,1)S(1)} copy-done((bf16[32,576,128]{2,1,0:T(8,128)(2,1)S(1)}, bf16[32,576,128]{2,1,0:T(8,128)(2,1)}, u32[]{:S(2)}) %copy-start.5) | copy-done | bytes 4718616
  82.8 2.2 %weight_term.1 = (bf16[144,128]{1,0:T(8,128)(2,1)S(1)}, bf16[144,128]{1,0:T(8,128)(2,1)S(1)}, bf16[144,128]{1,0:T(8,128)(2,1)S(1)}, bf16[144,128]{1,0:T(8,128)(2,1)S(1)}) custom-call(bf16[16,80,128]{2,1,0:T(8,128)(2,1)S(1)} %get-tuple-element.36.mixed, bf16[16,80,128]{2,1,0:T(8,128)(2,1)S(1)} %collective-permute-done.7.other, ...), custom_call_target="tpu_custom_call" | custom-call | flops 1600000000 | bytes 8000000 | tf_op jit(solution)/shard_map/weight_term/pallas_call | solution.py:398
  84.9 0.0 collective-permute-done.6.far
  84.9 0.0 copy-done.7
  85.0 0.2 fold.1
  85.1 0.7 collective-permute-start.8
  85.9 0.1 collective-permute-start.5
  86.0 1.9 %collective-permute-start.9 = (bf16[144,128]{1,0:T(8,128)(2,1)S(1)}, bf16[144,128]{1,0:T(8,128)(2,1)S(1)}, u32[]{:S(2)}, u32[]{:S(2)}) collective-permute-start(bf16[144,128]{1,0:T(8,128)(2,1)S(1)} %get-tuple-element.43), channel_id=1, source_target_pairs={{0,32},{1,33},{2,34},{3,35},{4,36},{5,37},{6,38},{7,39},{8,40},{9,... | collective-permute-start | bytes 110600 | tf_op jit(solution)/shard_map/ppermute | solution.py:504
  87.8 1.8 %collective-permute-start.10 = (bf16[144,128]{1,0:T(8,128)(2,1)S(1)}, bf16[144,128]{1,0:T(8,128)(2,1)S(1)}, u32[]{:S(2)}, u32[]{:S(2)}) collective-permute-start(bf16[144,128]{1,0:T(8,128)(2,1)S(1)} %get-tuple-element.44), channel_id=1, source_target_pairs={{0,64},{1,65},{2,66},{3,67},{4,68},{5,69},{6,70},{7,71},{8,72},{9,... | collective-permute-start | bytes 110600 | tf_op jit(solution)/shard_map/ppermute | solution.py:504
  89.6 1.6 %collective-permute-start.11 = (bf16[144,128]{1,0:T(8,128)(2,1)S(1)}, bf16[144,128]{1,0:T(8,128)(2,1)S(1)}, u32[]{:S(2)}, u32[]{:S(2)}) collective-permute-start(bf16[144,128]{1,0:T(8,128)(2,1)S(1)} %get-tuple-element.45), channel_id=1, source_target_pairs={{0,96},{1,97},{2,98},{3,99},{4,100},{5,101},{6,102},{7,103},{8,104... | collective-permute-start | bytes 110600 | tf_op jit(solution)/shard_map/ppermute | solution.py:504
  91.2 0.0 collective-permute-done.5.got_asked
  91.2 0.0 collective-permute-done.9.term1
  91.2 1.0 collective-permute-done.10.term2
  92.2 0.5 collective-permute-done.11.term3
  92.7 0.0 collective-permute-done.8.got
  92.7 0.3 join.1
  93.1 0.0 copy-start
  93.1 0.0 copy-start.2
  93.1 0.0 copy-start.3
  93.1 0.0 copy-start.4
  93.1 28.6 %all_to_all.10.packed = bf16[32,176,128]{2,1,0:T(8,128)(2,1)S(1)} all-to-all(bf16[32,176,128]{2,1,0:T(8,128)(2,1)S(1)} %join.1), channel_id=1, replica_groups={{0,1,2,3,4,5,6,7,8,9,10,11,12,13,14,15,16,17,18,19,20,21,22,23,24,25,26..., dimensions={0} | all-to-all | bytes 2883584 | tf_op jit(solution)/shard_map/all_to_all | solution.py:521
  121.8 0.0 copy-done.3
  121.8 0.0 copy-done.4
  121.8 2.0 %finish.1 = (bf16[128,1152]{1,0:T(8,128)(2,1)}, bf16[128,1152]{1,0:T(8,128)(2,1)}, bf16[128,1152]{1,0:T(8,128)(2,1)}, bf16[128,1152]{1,0:T(8,128)(2,1)}, f32[9,1152]{1,0:T(8,128)}) custom-call(bf16[32,176,128]{2,1,0:T(8,128)(2,1)S(1)} %all_to_all.10.packed, bf16[128,1152]{1,0:T(8,128)(2,1)S(1)} %copy-done.1, s32[128]{0:T(128)S(1)} %copy-done.4, ...), custom_call_target="tpu_custom_call" | custom-call | flops 1200000000 | bytes 6000000 | tf_op jit(solution)/shard_map/finish/pallas_call | solution.py:491
  (10 shorter events, 0.1 us)
Async XLA Ops:
  7.2 73.3 %all-gather.3.cloned.1.call-start = ((), (), s32[]{:S(2)}) async-start(), calls=%async_computation.2 | async-start | bytes 5013504 | tf_op jit(solution)/shard_map/all_gather | solution.py:536
  9.8 6.5 %collective-permute-start = (bf16[576,128]{1,0:T(8,128)(2,1)}, bf16[576,128]{1,0:T(8,128)(2,1)S(1)}, u32[]{:S(2)}, u32[]{:S(2)}) collective-permute-start(bf16[576,128]{1,0:T(8,128)(2,1)} %get-tuple-element.28), channel_id=1, source_target_pairs={{0,1},{1,0},{2,3},{3,2},{4,5},{5,4},{6,7},{7,6},{8,9},{9,8},{10,11... | collective-permute-start | bytes 442376 | tf_op jit(solution)/shard_map/ppermute | solution.py:504
  16.9 32.2 %all-to-all-start = ((bf16[32,160,128]{2,1,0:T(8,128)(2,1)}), bf16[32,160,128]{2,1,0:T(8,128)(2,1)S(1)}, u32[]{:S(2)}, u32[]{:S(2)}) async-start(bf16[32,160,128]{2,1,0:T(8,128)(2,1)} %pack.1), calls=%async_computation | async-start | bytes 2621440 | tf_op jit(solution)/shard_map/all_to_all | solution.py:521
  49.1 4.3 %collective-permute-start.1 = (bf16[23,80,128]{2,1,0:T(8,128)(2,1)S(1)}, bf16[23,80,128]{2,1,0:T(8,128)(2,1)S(1)}, u32[]{:S(2)}, u32[]{:S(2)}) collective-permute-start(bf16[23,80,128]{2,1,0:T(8,128)(2,1)S(1)} %constant_dynamic-slice_fusion.3), channel_id=1, source_target_pairs={{0,1},{1,0},{2,3},{3,2},{4,5},{5,4},{6,7},{7,6},{8,9},{9,8},{10,11... | collective-permute-start | bytes 1413128 | tf_op jit(solution)/shard_map/ppermute | solution.py:504
  49.7 6.6 %collective-permute-start.2 = (bf16[16,80,128]{2,1,0:T(8,128)(2,1)S(1)}, bf16[16,80,128]{2,1,0:T(8,128)(2,1)S(1)}, u32[]{:S(2)}, u32[]{:S(2)}) collective-permute-start(bf16[16,80,128]{2,1,0:T(8,128)(2,1)S(1)} %constant_dynamic-slice_fusion.2), channel_id=1, source_target_pairs={{0,1},{1,0},{2,3},{3,2},{4,5},{5,4},{6,7},{7,6},{8,9},{9,8},{10,11... | collective-permute-start | bytes 983048 | tf_op jit(solution)/shard_map/ppermute | solution.py:504
  49.9 6.4 %collective-permute-start.4 = (bf16[7,80,128]{2,1,0:T(8,128)(2,1)S(1)}, bf16[7,80,128]{2,1,0:T(8,128)(2,1)S(1)}, u32[]{:S(2)}, u32[]{:S(2)}) collective-permute-start(bf16[7,80,128]{2,1,0:T(8,128)(2,1)S(1)} %constant_dynamic-slice_fusion), channel_id=1, source_target_pairs={{1,32},{3,34},{5,36},{7,38},{9,40},{11,42},{13,44},{15,46},{17,48}... | collective-permute-start | bytes 430088 | tf_op jit(solution)/shard_map/ppermute | solution.py:504
  53.4 6.4 %collective-permute-start.3 = (bf16[7,80,128]{2,1,0:T(8,128)(2,1)S(1)}, bf16[7,80,128]{2,1,0:T(8,128)(2,1)S(1)}, u32[]{:S(2)}, u32[]{:S(2)}) collective-permute-start(bf16[7,80,128]{2,1,0:T(8,128)(2,1)S(1)} %constant_dynamic-slice_fusion.1), channel_id=1, source_target_pairs={{1,32},{3,34},{5,36},{7,38},{9,40},{11,42},{13,44},{15,46},{17,48}... | collective-permute-start | bytes 430088 | tf_op jit(solution)/shard_map/ppermute | solution.py:504
  75.5 0.8 copy-start.6
  76.3 4.0 %collective-permute-start.7 = (bf16[16,80,128]{2,1,0:T(8,128)(2,1)S(1)}, bf16[16,80,128]{2,1,0:T(8,128)(2,1)S(1)}, u32[]{:S(2)}, u32[]{:S(2)}) collective-permute-start(bf16[16,80,128]{2,1,0:T(8,128)(2,1)S(1)} %get-tuple-element.36.mixed), channel_id=1, source_target_pairs={{0,1},{1,0},{2,3},{3,2},{4,5},{5,4},{6,7},{7,6},{8,9},{9,8},{10,11... | collective-permute-start | bytes 983048 | tf_op jit(solution)/shard_map/ppermute | solution.py:504
  76.3 8.6 %collective-permute-start.6 = (bf16[7,160,128]{2,1,0:T(8,128)(2,1)S(1)}, bf16[7,160,128]{2,1,0:T(8,128)(2,1)S(1)}, u32[]{:S(2)}, u32[]{:S(2)}) collective-permute-start(bf16[7,160,128]{2,1,0:T(8,128)(2,1)S(1)} %get-tuple-element.35), channel_id=1, source_target_pairs={{1,32},{3,34},{5,36},{7,38},{9,40},{11,42},{13,44},{15,46},{17,48}... | collective-permute-start | bytes 860168 | tf_op jit(solution)/shard_map/ppermute | solution.py:504
  80.4 2.3 %copy-start.5 = (bf16[32,576,128]{2,1,0:T(8,128)(2,1)S(1)}, bf16[32,576,128]{2,1,0:T(8,128)(2,1)}, u32[]{:S(2)}) copy-start(bf16[32,576,128]{2,1,0:T(8,128)(2,1)} %all-gather.3.cloned.1.call-done) | copy-start | bytes 14155780
  82.8 2.2 %copy-start.7 = (bf16[23,80,128]{2,1,0:T(8,128)(2,1)S(1)}, bf16[23,80,128]{2,1,0:T(8,128)(2,1)}, u32[]{:S(2)}) copy-start(bf16[23,80,128]{2,1,0:T(8,128)(2,1)} %copy-done.6) | copy-start | bytes 1413124
  85.1 7.6 %collective-permute-start.8 = (bf16[23,80,128]{2,1,0:T(8,128)(2,1)S(1)}, bf16[23,80,128]{2,1,0:T(8,128)(2,1)S(1)}, u32[]{:S(2)}, u32[]{:S(2)}) collective-permute-start(bf16[23,80,128]{2,1,0:T(8,128)(2,1)S(1)} %get-tuple-element.42), channel_id=1, source_target_pairs={{0,1},{1,0},{2,3},{3,2},{4,5},{5,4},{6,7},{7,6},{8,9},{9,8},{10,11... | collective-permute-start | bytes 1413128 | tf_op jit(solution)/shard_map/ppermute | solution.py:504
  85.9 5.4 %collective-permute-start.5 = (bf16[16,80,128]{2,1,0:T(8,128)(2,1)S(1)}, bf16[16,80,128]{2,1,0:T(8,128)(2,1)S(1)}, u32[]{:S(2)}, u32[]{:S(2)}) collective-permute-start(bf16[16,80,128]{2,1,0:T(8,128)(2,1)S(1)} %get-tuple-element.32), channel_id=1, source_target_pairs={{0,1},{1,0},{2,3},{3,2},{4,5},{5,4},{6,7},{7,6},{8,9},{9,8},{10,11... | collective-permute-start | bytes 983048 | tf_op jit(solution)/shard_map/ppermute | solution.py:504
  86.0 5.3 %collective-permute-start.9 = (bf16[144,128]{1,0:T(8,128)(2,1)S(1)}, bf16[144,128]{1,0:T(8,128)(2,1)S(1)}, u32[]{:S(2)}, u32[]{:S(2)}) collective-permute-start(bf16[144,128]{1,0:T(8,128)(2,1)S(1)} %get-tuple-element.43), channel_id=1, source_target_pairs={{0,32},{1,33},{2,34},{3,35},{4,36},{5,37},{6,38},{7,39},{8,40},{9,... | collective-permute-start | bytes 110600 | tf_op jit(solution)/shard_map/ppermute | solution.py:504
  87.8 4.4 %collective-permute-start.10 = (bf16[144,128]{1,0:T(8,128)(2,1)S(1)}, bf16[144,128]{1,0:T(8,128)(2,1)S(1)}, u32[]{:S(2)}, u32[]{:S(2)}) collective-permute-start(bf16[144,128]{1,0:T(8,128)(2,1)S(1)} %get-tuple-element.44), channel_id=1, source_target_pairs={{0,64},{1,65},{2,66},{3,67},{4,68},{5,69},{6,70},{7,71},{8,72},{9,... | collective-permute-start | bytes 110600 | tf_op jit(solution)/shard_map/ppermute | solution.py:504
  89.6 3.1 %collective-permute-start.11 = (bf16[144,128]{1,0:T(8,128)(2,1)S(1)}, bf16[144,128]{1,0:T(8,128)(2,1)S(1)}, u32[]{:S(2)}, u32[]{:S(2)}) collective-permute-start(bf16[144,128]{1,0:T(8,128)(2,1)S(1)} %get-tuple-element.45), channel_id=1, source_target_pairs={{0,96},{1,97},{2,98},{3,99},{4,100},{5,101},{6,102},{7,103},{8,104... | collective-permute-start | bytes 110600 | tf_op jit(solution)/shard_map/ppermute | solution.py:504
  92.7 29.0 %copy-start.1 = (bf16[128,1152]{1,0:T(8,128)(2,1)S(1)}, bf16[128,1152]{1,0:T(8,128)(2,1)}, u32[]{:S(2)}) copy-start(bf16[128,1152]{1,0:T(8,128)(2,1)} %residual.1) | copy-start | bytes 884740
  93.1 28.7 %copy-start = (bf16[1152,1152]{1,0:T(8,128)(2,1)S(1)}, bf16[1152,1152]{1,0:T(8,128)(2,1)}, u32[]{:S(2)}) copy-start(bf16[1152,1152]{1,0:T(8,128)(2,1)} %weight.3) | copy-start | bytes 7962628
  93.1 28.7 %copy-start.2 = (f32[32,1152]{1,0:T(8,128)S(1)}, f32[32,1152]{1,0:T(8,128)}, u32[]{:S(2)}) copy-start(f32[32,1152]{1,0:T(8,128)} %gate.3) | copy-start | bytes 442372
  93.1 28.7 %copy-start.3 = (f32[1152]{0:T(1024)S(1)}, f32[1152]{0:T(1024)}, u32[]{:S(2)}) copy-start(f32[1152]{0:T(1024)} %bias.1) | copy-start | bytes 13828
  93.1 28.7 %copy-start.4 = (s32[128]{0:T(128)S(1)}, s32[128]{0:T(128)}, u32[]{:S(2)}) copy-start(s32[128]{0:T(128)} %tags.5) | copy-start | bytes 1540
Sparse Core Ops, SparseCore 0:
  17.1 63.3 all-gather.2

commit v11 on v10

--- a/solution.py
+++ b/solution.py
@@ -240,7 +240,7 @@
 
 def attend_body(
     own, near, asked, far_own, far_other,
-    mixed_ref, keep_asked_ref, give_asked_ref, keep_ref, give_ref, far_ref,
+    mixed_ref, keep_asked_ref, give_asked_ref, both_ref, far_ref,
     key_n, key_t, value_n, value_t, query_t, query_n, grad_t, grad_n, held, pulls, mixed_t, dq, dk, dv,
     clips, first_ref, count_ref,
 ):
@@ -312,6 +312,8 @@
         rows = token_rows(at)
         return [dk[rows, :].T[0:FULL] * SCALE, dv[rows, :].T[0:FULL]]
 
+    keep_ref, give_ref = both_ref.at[0:NEAR], both_ref.at[NEAR : 2 * NEAR]
+
     def hand_out(keep, give, block, wholes):
         first, second = halves(side, wholes)
         keep[block], give[block] = first.astype(BF), second.astype(BF)
@@ -329,15 +331,15 @@
 
 def attend(own, near, asked, far_own, far_other):
     whole = jax.ShapeDtypeStruct((SIDE, FULL, TOK), BF)
-    keys = jax.ShapeDtypeStruct((NEAR, FULL, TOK), BF)
+    both = jax.ShapeDtypeStruct((2 * NEAR, FULL, TOK), BF)
     edge = jax.ShapeDtypeStruct((EDGE, 2 * FULL, TOK), BF)
     row_form = pltpu.VMEM((ROOM * TOK, TOK), BF)
     column_form = pltpu.VMEM((ROOM, 80, TOK), BF)
     return pl.pallas_call(
         attend_body,
-        out_shape=(whole, whole, whole, keys, keys, edge),
+        out_shape=(whole, whole, whole, both, edge),
         in_specs=[WHOLE] * 5,
-        out_specs=(WHOLE,) * 6,
+        out_specs=(WHOLE,) * 5,
         cost_estimate=cost(20),
         scratch_shapes=[
             row_form, column_form, row_form, column_form,
@@ -408,8 +410,9 @@
     )(mixed, other, branch)
 
 
-def fold_body(keep, give, far, keep_ref, give_ref):
+def fold_body(both, far, keep_ref, give_ref):
     side = core()
+    keep, give = both.at[0:NEAR], both.at[NEAR : 2 * NEAR]
     keep_ref[...] = keep[...]
     give_ref[...] = give[...]
     for block in range(EDGE):
@@ -420,20 +423,39 @@
         give_ref[place] = (give[place].astype(F32) + second).astype(BF)
 
 
-def fold(keep, give, far):
+def fold(both, far):
     keys = jax.ShapeDtypeStruct((NEAR, FULL, TOK), BF)
     return pl.pallas_call(
         fold_body,
         out_shape=(keys, keys),
-        in_specs=[WHOLE] * 3,
+        in_specs=[WHOLE] * 2,
         out_specs=(WHOLE,) * 2,
         compiler_params=params(8),
         cost_estimate=cost(1),
         name="fold",
-    )(keep, give, far)
-
-
-def join_body(keep_asked, got_asked, keep, got, term, term1, term2, term3, out_ref, total, pairs):
+    )(both, far)
+
+
+def join_asked_body(keep, got, out_ref):
+    side = core()
+    for block in range(SIDE):
+        out_ref[SIDE * side + block] = keep[block]
+        out_ref[SIDE * (1 - side) + block] = got[block]
+
+
+def join_asked(keep, got):
+    return pl.pallas_call(
+        join_asked_body,
+        out_shape=jax.ShapeDtypeStruct((PLANE, FULL, TOK), BF),
+        in_specs=[WHOLE] * 2,
+        out_specs=WHOLE,
+        compiler_params=params(8),
+        cost_estimate=cost(1),
+        name="join_asked",
+    )(keep, got)
+
+
+def join_body(keep, got, term, term1, term2, term3, out_ref, total, pairs):
     side = core()
     total[0:SHARE] = sum(one[...].astype(F32) for one in (term, term1, term2, term3))
     total[SHARE:] = jnp.zeros((8, TOK), F32)
@@ -444,18 +466,16 @@
     for block in range(EDGE):
         pairs[others + (SIDE - EDGE) * side + block] += keep[SIDE + block].astype(F32)
         pairs[mine + (SIDE - EDGE) * (1 - side) + block] += got[SIDE + block].astype(F32)
-    for block in range(SIDE):
-        tail = total[block * FINAL : block * FINAL + 16, :]
-        for start, asked in ((mine, keep_asked), (others, got_asked)):
-            whole = [asked[block].astype(F32), pairs[start + block], tail]
-            out_ref[start + block] = jnp.concatenate(whole, 0).astype(BF)
+    for block in range(PLANE):
+        start = (block % SIDE) * FINAL
+        out_ref[block] = jnp.concatenate([pairs[block], total[start : start + 16, :]], 0).astype(BF)
 
 
 def join(*values):
     return pl.pallas_call(
         join_body,
-        out_shape=jax.ShapeDtypeStruct((PLANE, 2 * FULL + 16, TOK), BF),
-        in_specs=[WHOLE] * 8,
+        out_shape=jax.ShapeDtypeStruct((PLANE, FULL + 16, TOK), BF),
+        in_specs=[WHOLE] * 6,
         out_specs=WHOLE,
         scratch_shapes=[pltpu.VMEM((SHARE + 8, TOK), F32), pltpu.VMEM((PLANE, FULL, TOK), F32)],
         compiler_params=params(12),
@@ -464,39 +484,55 @@
     )(*values)
 
 
-def finish_body(packed, residual, tags, gate, weight, bias, out_ref, dq_ref, dk_ref, dv_ref, dw_ref):
-    def rows(at):
-        low = slice(at * HALF, (at + 1) * HALF)
-        high = slice(at * HALF, at * HALF + HEAD_DIM - HALF)
-        parts = []
-        for head in range(HEADS):
-            parts += [packed[2 * head].astype(F32)[low], packed[2 * head + 1].astype(F32)[high]]
-        return jnp.concatenate(parts, 0).T.astype(BF)
-
+def all_heads(packed, at):
+    low = slice(at * HALF, (at + 1) * HALF)
+    high = slice(at * HALF, at * HALF + HEAD_DIM - HALF)
+    parts = []
+    for head in range(HEADS):
+        parts += [packed[2 * head].astype(F32)[low], packed[2 * head + 1].astype(F32)[high]]
+    return jnp.concatenate(parts, 0).T.astype(BF)
+
+
+def finish_asked_body(packed, residual, tags, gate, weight, bias, out_ref, dq_ref):
     gate_rows = lax.dot_general(
         clip_onehot(tags), gate[...], (((0,), (0,)), ((), ())),
         precision=lax.Precision.HIGHEST, preferred_element_type=F32,
     )
-    projected = mm(rows(0), weight[...]) + bias[...].reshape(1, WIDTH)
+    projected = mm(all_heads(packed, 0), weight[...]) + bias[...].reshape(1, WIDTH)
     out_ref[...] = (residual[...].astype(F32) + gate_rows * projected).astype(BF)
-    dq_ref[...] = rows(1)
-    dk_ref[...] = rows(2)
-    dv_ref[...] = rows(3)
+    dq_ref[...] = all_heads(packed, 1)
+
+
+def finish_asked(packed, residual, tags, gate, weight, bias):
+    return pl.pallas_call(
+        finish_asked_body,
+        out_shape=(jax.ShapeDtypeStruct((TOK, WIDTH), BF),) * 2,
+        in_specs=[WHOLE] * 6,
+        out_specs=(WHOLE,) * 2,
+        compiler_params=params(16),
+        cost_estimate=cost(2),
+        name="finish_asked",
+    )(packed, residual, tags, gate, weight, bias)
+
+
+def finish_body(packed, dk_ref, dv_ref, dw_ref):
+    dk_ref[...] = all_heads(packed, 0)
+    dv_ref[...] = all_heads(packed, 1)
     source = lax.rem(lax.axis_index("dp"), PLANE) // SIDE
-    tails = [packed[2 * head + source, 2 * FULL :].astype(F32)[:, 0:HEAD_DIM] for head in range(HEADS)]
+    tails = [packed[2 * head + source, FULL:].astype(F32)[:, 0:HEAD_DIM] for head in range(HEADS)]
     dw_ref[...] = jnp.concatenate(tails, 1)[0:FINAL]
 
 
-def finish(packed, residual, tags, gate, weight, bias):
+def finish(packed):
     return pl.pallas_call(
         finish_body,
-        out_shape=(jax.ShapeDtypeStruct((TOK, WIDTH), BF),) * 4 + (jax.ShapeDtypeStruct((FINAL, WIDTH), F32),),
-        in_specs=[WHOLE] * 6,
-        out_specs=(WHOLE,) * 5,
+        out_shape=(jax.ShapeDtypeStruct((TOK, WIDTH), BF),) * 2 + (jax.ShapeDtypeStruct((FINAL, WIDTH), F32),),
+        in_specs=[WHOLE],
+        out_specs=(WHOLE,) * 3,
         compiler_params=params(16),
-        cost_estimate=cost(3),
+        cost_estimate=cost(1),
         name="finish",
-    )(packed, residual, tags, gate, weight, bias)
+    )(packed)
 
 
 def sent(values, target):
@@ -539,17 +575,19 @@
     asked = sent(some_blocks(own, SIDE * (1 - side), FULL, SIDE), other_core)
     far_other = sent(some_blocks(own, (PLANE - EDGE) * side, 0, EDGE), cross)
     far_own = sent(some_blocks(near, SIDE * side, 0, EDGE), cross)
-    mixed, keep_asked, give_asked, keep, give, far = attend(own, near, asked, far_own, far_other)
+    mixed, keep_asked, give_asked, both, far = attend(own, near, asked, far_own, far_other)
+    joined = join_asked(keep_asked, sent(give_asked, other_core))
+    asked_back = traded(joined)
     far = sent(far, cross)
-    mixed_other = sent(mixed, other_core)
-    got_asked = sent(give_asked, other_core)
+    mixed_other, _ = lax.optimization_barrier((sent(mixed, other_core), joined))
     term, *terms = weight_term(mixed, mixed_other, gathered)
     terms = [sent(one, planes_on(away + 1)) for away, one in enumerate(terms)]
     far, _ = lax.optimization_barrier((far, term))
-    keep, give = fold(keep, give, far)
+    keep, give = fold(both, far)
     got = sent(give, other_core)
-    packed = traded(join(keep_asked, got_asked, keep, got, term, *terms))
-    block_out, dq, dk, dv, dw = finish(packed, residual, tags, gate, weight, bias)
+    keys_back = traded(join(keep, got, term, *terms))
+    block_out, dq = finish_asked(asked_back, residual, tags, gate, weight, bias)
+    dk, dv, dw = finish(keys_back)
     return block_out, dq, dk, dv, dw.T
 
 

time: 131 us -> 131 us (level)
  blocking collectives: 28.6 us -> 0 us
  starting transfers between devices: 26 us -> 38.4 us
  waiting for transfers between devices: 29.9 us -> 41.9 us
  Pallas kernels: 28.6 us -> 32.1 us
    all_to_all x1 -> x0, blocking collectives: 28.6 us -> none  [traded(): lax.all_to_all(values, 'dp', 0, 0, axis_index_groups=groups, tiled=True)]
    all_to_all x1 -> x3, starting transfers between devices: 8.16 us -> 20.8 us  [traded(): lax.all_to_all(values, 'dp', 0, 0, axis_index_groups=groups, tiled=True)]
    all_to_all x1 -> x3, waiting for transfers between devices: 24 us -> 35.4 us  [traded(): lax.all_to_all(values, 'dp', 0, 0, axis_index_groups=groups, tiled=True)]
    pallas_call x3 -> x5, Pallas kernels: 16.2 us -> 19.5 us  [the longest x1 15.4 us: attend(): pl.pallas_call(attend_body, out_shape=(whole, whole, whole, both, edge),...]
  transfers between devices with their start and end apart: 14 -> 16, of which waited for: 5 -> 6; matrix products, arithmetic and copies ran while one was open for 0% -> 0% of each run, Pallas kernels for 18% -> 20%
where the time goes in v11:
time: 131 us
  waiting for transfers between devices  41.9 us (32%)
  starting transfers between devices  38.4 us (29%)
  Pallas kernels  32.1 us (25%)
  between operations  14.3 us (11%)
  local copies, waits for them, and re-layouts  4.37 us (3%)
    all_to_all x3, waiting for transfers between devices, traded(): lax.all_to_all(values, 'dp', 0, 0, axis_index_groups=groups, tiled=True)  35.4 us
    all_to_all x3, starting transfers between devices, traded(): lax.all_to_all(values, 'dp', 0, 0, axis_index_groups=groups, tiled=True)  20.8 us
    ppermute x12, starting transfers between devices, sent(): lax.ppermute(values, 'dp', [(i, j) for i, j in pairs if 0 <= j < DEVICES])  17.6 us
    pallas_call x1, Pallas kernels, attend(): pl.pallas_call(attend_body, out_shape=(whole, whole, whole, both, edge),...  15.4 us
    ppermute x12, waiting for transfers between devices, sent(): lax.ppermute(values, 'dp', [(i, j) for i, j in pairs if 0 <= j < DEVICES])  6.45 us
    pallas_call x1, Pallas kernels, pack(): pl.pallas_call(pack_body, out_shape=jax.ShapeDtypeStruct((PLANE, 2 * FULL...  5.06 us
    unnamed x16, local copies, waits for them, and re-layouts  4.28 us
  transfers between devices with their start and end apart: 16, of which 6 were waited for; matrix products, arithmetic and copies ran while one was open for 0% of the time, Pallas kernels for 20%

profile of v11, /device:TPU:1, one launch (start us, length us, event | category | flops | bytes accessed | tf_op | source)
XLA Modules:
  0.0 131.0 jit_solution(16452605501430997523)
XLA Ops:
  7.2 0.0 all-gather.3.cloned.1.call-start
  7.2 2.5 %branch_columns.1 = (bf16[1152,128]{1,0:T(8,128)(2,1)}, bf16[2,576,128]{2,1,0:T(8,128)(2,1)}, bf16[576,128]{1,0:T(8,128)(2,1)}) custom-call(bf16[128,1152]{1,0:T(8,128)(2,1)} %out_grad.1, s32[128]{0:T(128)} %tags.5, f32[32,1152]{1,0:T(8,128)} %gate.3), custom_call_target="tpu_custom_call" | custom-call | flops 800000000 | bytes 4000000 | tf_op jit(solution)/shard_map/branch_columns/pallas_call | solution.py:87
  9.8 1.4 %collective-permute-start = (bf16[576,128]{1,0:T(8,128)(2,1)}, bf16[576,128]{1,0:T(8,128)(2,1)S(1)}, u32[]{:S(2)}, u32[]{:S(2)}) collective-permute-start(bf16[576,128]{1,0:T(8,128)(2,1)} %get-tuple-element.28), channel_id=1, source_target_pairs={{0,1},{1,0},{2,3},{3,2},{4,5},{5,4},{6,7},{7,6},{8,9},{9,8},{10,11... | collective-permute-start | bytes 442376 | tf_op jit(solution)/shard_map/ppermute | solution.py:540
  11.2 5.1 %pack.1 = bf16[32,160,128]{2,1,0:T(8,128)(2,1)} custom-call(bf16[128,1152]{1,0:T(8,128)(2,1)} %query.1, bf16[128,1152]{1,0:T(8,128)(2,1)} %key.1, bf16[128,1152]{1,0:T(8,128)(2,1)} %value.1, bf16[1152,1152]{1,0:T(8,128)(2,1)} %weight.3, s32[128]{0:T(128)} %tags.5, bf16[1152,128]{1,0:T(8,128)(2,1)} %get-tuple-element.29.branch), custom_call_target="tpu_custom_call" | custom-call | flops 1600000000 | bytes 8000000 | tf_op jit(solution)/shard_map/pack/pallas_call | solution.py:150
  16.3 0.0 collective-permute-done.got
  16.3 0.7 fill.1
  16.9 0.0 all-gather.3.cloned.1.call-update
  17.0 8.2 %all-to-all-start = ((bf16[32,160,128]{2,1,0:T(8,128)(2,1)}), bf16[32,160,128]{2,1,0:T(8,128)(2,1)S(1)}, u32[]{:S(2)}, u32[]{:S(2)}) async-start(bf16[32,160,128]{2,1,0:T(8,128)(2,1)} %pack.1), calls=%async_computation | async-start | bytes 2621440 | tf_op jit(solution)/shard_map/all_to_all | solution.py:557
  25.1 24.0 %all-to-all-done.own = bf16[32,160,128]{2,1,0:T(8,128)(2,1)S(1)} async-done(((bf16[32,160,128]{2,1,0:T(8,128)(2,1)}), bf16[32,160,128]{2,1,0:T(8,128)(2,1)S(1)}, u32[]{:S(2)}, u32[]{:S(2)}) %all-to-all-start) | async-done | bytes 1310752 | tf_op jit(solution)/shard_map/all_to_all | solution.py:557
  49.2 0.6 collective-permute-start.1
  49.7 0.1 collective-permute-start.2
  49.9 3.5 %collective-permute-start.4 = (bf16[7,80,128]{2,1,0:T(8,128)(2,1)S(1)}, bf16[7,80,128]{2,1,0:T(8,128)(2,1)S(1)}, u32[]{:S(2)}, u32[]{:S(2)}) collective-permute-start(bf16[7,80,128]{2,1,0:T(8,128)(2,1)S(1)} %constant_dynamic-slice_fusion), channel_id=1, source_target_pairs={{1,32},{3,34},{5,36},{7,38},{9,40},{11,42},{13,44},{15,46},{17,48}... | collective-permute-start | bytes 430088 | tf_op jit(solution)/shard_map/ppermute | solution.py:540
  53.4 0.0 collective-permute-done.1.near
  53.5 2.0 %collective-permute-start.3 = (bf16[7,80,128]{2,1,0:T(8,128)(2,1)S(1)}, bf16[7,80,128]{2,1,0:T(8,128)(2,1)S(1)}, u32[]{:S(2)}, u32[]{:S(2)}) collective-permute-start(bf16[7,80,128]{2,1,0:T(8,128)(2,1)S(1)} %constant_dynamic-slice_fusion.1), channel_id=1, source_target_pairs={{1,32},{3,34},{5,36},{7,38},{9,40},{11,42},{13,44},{15,46},{17,48}... | collective-permute-start | bytes 430088 | tf_op jit(solution)/shard_map/ppermute | solution.py:540
  55.5 0.8 collective-permute-done.4.far_other
  56.3 0.0 collective-permute-done.2.asked
  56.3 3.6 %collective-permute-done.3.far_own = bf16[7,80,128]{2,1,0:T(8,128)(2,1)S(1)} collective-permute-done((bf16[7,80,128]{2,1,0:T(8,128)(2,1)S(1)}, bf16[7,80,128]{2,1,0:T(8,128)(2,1)S(1)}, u32[]{:S(2)}, u32[]{:S(2)}) %collective-permute-start.3) | collective-permute-done | bytes 143392 | tf_op jit(solution)/shard_map/ppermute | solution.py:540
  59.9 15.4 %attend.1 = (bf16[16,80,128]{2,1,0:T(8,128)(2,1)S(1)}, bf16[16,80,128]{2,1,0:T(8,128)(2,1)S(1)}, bf16[16,80,128]{2,1,0:T(8,128)(2,1)S(1)}, bf16[46,80,128]{2,1,0:T(8,128)(2,1)S(1)}, bf16[7,160,128]{2,1,0:T(8,128)(2,1)}) custom-call(bf16[32,160,128]{2,1,0:T(8,128)(2,1)S(1)} %all-to-all-done.own, bf16[23,80,128]{2,1,0:T(8,128)(2,1)S(1)} %collective-permute-done.1.near, ...), custom_call_target="tpu_custom_call" | custom-call | flops 8000000000 | bytes 40000000 | tf_op jit(solution)/shard_map/attend/pallas_call | solution.py:338
  75.3 1.0 copy-done.6
  76.3 0.0 collective-permute-start.5
  76.3 0.5 collective-permute-start.7
  76.8 4.8 %collective-permute-start.6 = (bf16[7,160,128]{2,1,0:T(8,128)(2,1)}, bf16[7,160,128]{2,1,0:T(8,128)(2,1)S(1)}, u32[]{:S(2)}, u32[]{:S(2)}) collective-permute-start(bf16[7,160,128]{2,1,0:T(8,128)(2,1)} %get-tuple-element.36), channel_id=1, source_target_pairs={{1,32},{3,34},{5,36},{7,38},{9,40},{11,42},{13,44},{15,46},{17,48}... | collective-permute-start | bytes 860168 | tf_op jit(solution)/shard_map/ppermute | solution.py:540
  81.6 0.0 collective-permute-done.5.got
  81.6 0.9 join_asked.1
  82.5 3.9 %all-to-all-start.1 = ((bf16[32,80,128]{2,1,0:T(8,128)(2,1)}), bf16[32,80,128]{2,1,0:T(8,128)(2,1)S(1)}, u32[]{:S(2)}, u32[]{:S(2)}) async-start(bf16[32,80,128]{2,1,0:T(8,128)(2,1)} %join_asked.1), calls=%async_computation.1 | async-start | bytes 1310720 | tf_op jit(solution)/shard_map/all_to_all | solution.py:557
  86.4 0.0 collective-permute-done.7.other
  86.4 0.0 all-gather.3.cloned.1.call-done
  86.4 2.3 %copy-done.5 = bf16[32,576,128]{2,1,0:T(8,128)(2,1)S(1)} copy-done((bf16[32,576,128]{2,1,0:T(8,128)(2,1)S(1)}, bf16[32,576,128]{2,1,0:T(8,128)(2,1)}, u32[]{:S(2)}) %copy-start.5) | copy-done | bytes 4718616
  88.8 2.2 %weight_term.1 = (bf16[144,128]{1,0:T(8,128)(2,1)S(1)}, bf16[144,128]{1,0:T(8,128)(2,1)S(1)}, bf16[144,128]{1,0:T(8,128)(2,1)S(1)}, bf16[144,128]{1,0:T(8,128)(2,1)S(1)}) custom-call(bf16[16,80,128]{2,1,0:T(8,128)(2,1)S(1)} %get-tuple-element.37.mixed, bf16[16,80,128]{2,1,0:T(8,128)(2,1)S(1)} %collective-permute-done.7.other, ...), custom_call_target="tpu_custom_call" | custom-call | flops 1600000000 | bytes 8000000 | tf_op jit(solution)/shard_map/weight_term/pallas_call | solution.py:400
  90.9 0.0 collective-permute-done.6.far
  90.9 0.2 fold.1
  91.1 0.1 collective-permute-start.8
  91.2 1.1 collective-permute-start.9
  92.3 2.4 %collective-permute-start.10 = (bf16[144,128]{1,0:T(8,128)(2,1)S(1)}, bf16[144,128]{1,0:T(8,128)(2,1)S(1)}, u32[]{:S(2)}, u32[]{:S(2)}) collective-permute-start(bf16[144,128]{1,0:T(8,128)(2,1)S(1)} %get-tuple-element.46), channel_id=1, source_target_pairs={{0,64},{1,65},{2,66},{3,67},{4,68},{5,69},{6,70},{7,71},{8,72},{9,... | collective-permute-start | bytes 110600 | tf_op jit(solution)/shard_map/ppermute | solution.py:540
  94.7 1.1 collective-permute-start.11
  95.7 0.0 collective-permute-done.9.term1
  95.7 1.5 %collective-permute-done.10.term2 = bf16[144,128]{1,0:T(8,128)(2,1)S(1)} collective-permute-done((bf16[144,128]{1,0:T(8,128)(2,1)S(1)}, bf16[144,128]{1,0:T(8,128)(2,1)S(1)}, u32[]{:S(2)}, u32[]{:S(2)}) %collective-permute-start.10) | collective-permute-done | bytes 36896 | tf_op jit(solution)/shard_map/ppermute | solution.py:540
  97.2 0.6 collective-permute-done.11.term3
  97.8 0.0 collective-permute-done.8.got
  97.8 0.0 copy-start.4
  97.8 1.1 join.1
  99.0 0.0 all-to-all-done.1.packed
  99.0 8.8 %all-to-all-start.2 = ((bf16[32,96,128]{2,1,0:T(8,128)(2,1)}), bf16[32,96,128]{2,1,0:T(8,128)(2,1)}, u32[]{:S(2)}, u32[]{:S(2)}) async-start(bf16[32,96,128]{2,1,0:T(8,128)(2,1)} %join.1), calls=%async_computation.2 | async-start | bytes 1572864 | tf_op jit(solution)/shard_map/all_to_all | solution.py:557
  107.8 0.0 copy-start.1
  107.8 1.0 copy-done.1
  108.8 1.9 %finish_asked.1 = (bf16[128,1152]{1,0:T(8,128)(2,1)}, bf16[128,1152]{1,0:T(8,128)(2,1)}) custom-call(bf16[32,80,128]{2,1,0:T(8,128)(2,1)S(1)} %all-to-all-done.1.packed, bf16[128,1152]{1,0:T(8,128)(2,1)S(1)} %copy-done.1, s32[128]{0:T(128)S(1)} %copy-done.4, f32[32,1152]{1,0:T(8,128)S(1)} %copy-done.2, bf16[1152,1152]{1,0:T(8,128)(2,1)S(1)} %copy-done, ...), custom_call_target="tpu_custom_call" | custom-call | flops 800000000 | bytes 4000000 | tf_op jit(solution)/shard_map/finish_asked/pallas_call | solution.py:507
  110.6 11.4 %all-to-all-done.2.packed = bf16[32,96,128]{2,1,0:T(8,128)(2,1)} async-done(((bf16[32,96,128]{2,1,0:T(8,128)(2,1)}), bf16[32,96,128]{2,1,0:T(8,128)(2,1)}, u32[]{:S(2)}, u32[]{:S(2)}) %all-to-all-start.2) | async-done | bytes 786464 | tf_op jit(solution)/shard_map/all_to_all | solution.py:557
  122.0 2.1 %finish.1 = (bf16[128,1152]{1,0:T(8,128)(2,1)}, bf16[128,1152]{1,0:T(8,128)(2,1)}, f32[9,1152]{1,0:T(8,128)}) custom-call(bf16[32,96,128]{2,1,0:T(8,128)(2,1)} %all-to-all-done.2.packed), custom_call_target="tpu_custom_call" | custom-call | flops 400000000 | bytes 2000000 | tf_op jit(solution)/shard_map/finish/pallas_call | solution.py:527
  (15 shorter events, 0.1 us)
Async XLA Ops:
  7.2 79.2 %all-gather.3.cloned.1.call-start = ((), (), s32[]{:S(2)}) async-start(), calls=%async_computation.3 | async-start | bytes 5013504 | tf_op jit(solution)/shard_map/all_gather | solution.py:572
  9.8 6.5 %collective-permute-start = (bf16[576,128]{1,0:T(8,128)(2,1)}, bf16[576,128]{1,0:T(8,128)(2,1)S(1)}, u32[]{:S(2)}, u32[]{:S(2)}) collective-permute-start(bf16[576,128]{1,0:T(8,128)(2,1)} %get-tuple-element.28), channel_id=1, source_target_pairs={{0,1},{1,0},{2,3},{3,2},{4,5},{5,4},{6,7},{7,6},{8,9},{9,8},{10,11... | collective-permute-start | bytes 442376 | tf_op jit(solution)/shard_map/ppermute | solution.py:540
  17.0 32.2 %all-to-all-start = ((bf16[32,160,128]{2,1,0:T(8,128)(2,1)}), bf16[32,160,128]{2,1,0:T(8,128)(2,1)S(1)}, u32[]{:S(2)}, u32[]{:S(2)}) async-start(bf16[32,160,128]{2,1,0:T(8,128)(2,1)} %pack.1), calls=%async_computation | async-start | bytes 2621440 | tf_op jit(solution)/shard_map/all_to_all | solution.py:557
  49.2 4.3 %collective-permute-start.1 = (bf16[23,80,128]{2,1,0:T(8,128)(2,1)S(1)}, bf16[23,80,128]{2,1,0:T(8,128)(2,1)S(1)}, u32[]{:S(2)}, u32[]{:S(2)}) collective-permute-start(bf16[23,80,128]{2,1,0:T(8,128)(2,1)S(1)} %constant_dynamic-slice_fusion.3), channel_id=1, source_target_pairs={{0,1},{1,0},{2,3},{3,2},{4,5},{5,4},{6,7},{7,6},{8,9},{9,8},{10,11... | collective-permute-start | bytes 1413128 | tf_op jit(solution)/shard_map/ppermute | solution.py:540
  49.7 6.6 %collective-permute-start.2 = (bf16[16,80,128]{2,1,0:T(8,128)(2,1)S(1)}, bf16[16,80,128]{2,1,0:T(8,128)(2,1)S(1)}, u32[]{:S(2)}, u32[]{:S(2)}) collective-permute-start(bf16[16,80,128]{2,1,0:T(8,128)(2,1)S(1)} %constant_dynamic-slice_fusion.2), channel_id=1, source_target_pairs={{0,1},{1,0},{2,3},{3,2},{4,5},{5,4},{6,7},{7,6},{8,9},{9,8},{10,11... | collective-permute-start | bytes 983048 | tf_op jit(solution)/shard_map/ppermute | solution.py:540
  49.9 6.4 %collective-permute-start.4 = (bf16[7,80,128]{2,1,0:T(8,128)(2,1)S(1)}, bf16[7,80,128]{2,1,0:T(8,128)(2,1)S(1)}, u32[]{:S(2)}, u32[]{:S(2)}) collective-permute-start(bf16[7,80,128]{2,1,0:T(8,128)(2,1)S(1)} %constant_dynamic-slice_fusion), channel_id=1, source_target_pairs={{1,32},{3,34},{5,36},{7,38},{9,40},{11,42},{13,44},{15,46},{17,48}... | collective-permute-start | bytes 430088 | tf_op jit(solution)/shard_map/ppermute | solution.py:540
  53.5 6.4 %collective-permute-start.3 = (bf16[7,80,128]{2,1,0:T(8,128)(2,1)S(1)}, bf16[7,80,128]{2,1,0:T(8,128)(2,1)S(1)}, u32[]{:S(2)}, u32[]{:S(2)}) collective-permute-start(bf16[7,80,128]{2,1,0:T(8,128)(2,1)S(1)} %constant_dynamic-slice_fusion.1), channel_id=1, source_target_pairs={{1,32},{3,34},{5,36},{7,38},{9,40},{11,42},{13,44},{15,46},{17,48}... | collective-permute-start | bytes 430088 | tf_op jit(solution)/shard_map/ppermute | solution.py:540
  75.3 1.0 copy-start.6
  76.3 5.3 %collective-permute-start.5 = (bf16[16,80,128]{2,1,0:T(8,128)(2,1)S(1)}, bf16[16,80,128]{2,1,0:T(8,128)(2,1)S(1)}, u32[]{:S(2)}, u32[]{:S(2)}) collective-permute-start(bf16[16,80,128]{2,1,0:T(8,128)(2,1)S(1)} %get-tuple-element.32), channel_id=1, source_target_pairs={{0,1},{1,0},{2,3},{3,2},{4,5},{5,4},{6,7},{7,6},{8,9},{9,8},{10,11... | collective-permute-start | bytes 983048 | tf_op jit(solution)/shard_map/ppermute | solution.py:540
  76.3 10.1 %collective-permute-start.7 = (bf16[16,80,128]{2,1,0:T(8,128)(2,1)S(1)}, bf16[16,80,128]{2,1,0:T(8,128)(2,1)S(1)}, u32[]{:S(2)}, u32[]{:S(2)}) collective-permute-start(bf16[16,80,128]{2,1,0:T(8,128)(2,1)S(1)} %get-tuple-element.37.mixed), channel_id=1, source_target_pairs={{0,1},{1,0},{2,3},{3,2},{4,5},{5,4},{6,7},{7,6},{8,9},{9,8},{10,11... | collective-permute-start | bytes 983048 | tf_op jit(solution)/shard_map/ppermute | solution.py:540
  76.8 14.2 %collective-permute-start.6 = (bf16[7,160,128]{2,1,0:T(8,128)(2,1)}, bf16[7,160,128]{2,1,0:T(8,128)(2,1)S(1)}, u32[]{:S(2)}, u32[]{:S(2)}) collective-permute-start(bf16[7,160,128]{2,1,0:T(8,128)(2,1)} %get-tuple-element.36), channel_id=1, source_target_pairs={{1,32},{3,34},{5,36},{7,38},{9,40},{11,42},{13,44},{15,46},{17,48}... | collective-permute-start | bytes 860168 | tf_op jit(solution)/shard_map/ppermute | solution.py:540
  82.5 16.5 %all-to-all-start.1 = ((bf16[32,80,128]{2,1,0:T(8,128)(2,1)}), bf16[32,80,128]{2,1,0:T(8,128)(2,1)S(1)}, u32[]{:S(2)}, u32[]{:S(2)}) async-start(bf16[32,80,128]{2,1,0:T(8,128)(2,1)} %join_asked.1), calls=%async_computation.1 | async-start | bytes 1310720 | tf_op jit(solution)/shard_map/all_to_all | solution.py:557
  86.4 2.3 %copy-start.5 = (bf16[32,576,128]{2,1,0:T(8,128)(2,1)S(1)}, bf16[32,576,128]{2,1,0:T(8,128)(2,1)}, u32[]{:S(2)}) copy-start(bf16[32,576,128]{2,1,0:T(8,128)(2,1)} %all-gather.3.cloned.1.call-done) | copy-start | bytes 14155780
  88.8 2.2 %copy-start.7 = (bf16[46,80,128]{2,1,0:T(8,128)(2,1)S(1)}, bf16[46,80,128]{2,1,0:T(8,128)(2,1)}, u32[]{:S(2)}) copy-start(bf16[46,80,128]{2,1,0:T(8,128)(2,1)} %copy-done.6) | copy-start | bytes 2826244
  91.1 6.7 %collective-permute-start.8 = (bf16[23,80,128]{2,1,0:T(8,128)(2,1)S(1)}, bf16[23,80,128]{2,1,0:T(8,128)(2,1)S(1)}, u32[]{:S(2)}, u32[]{:S(2)}) collective-permute-start(bf16[23,80,128]{2,1,0:T(8,128)(2,1)S(1)} %get-tuple-element.44), channel_id=1, source_target_pairs={{0,1},{1,0},{2,3},{3,2},{4,5},{5,4},{6,7},{7,6},{8,9},{9,8},{10,11... | collective-permute-start | bytes 1413128 | tf_op jit(solution)/shard_map/ppermute | solution.py:540
  91.2 4.5 %collective-permute-start.9 = (bf16[144,128]{1,0:T(8,128)(2,1)S(1)}, bf16[144,128]{1,0:T(8,128)(2,1)S(1)}, u32[]{:S(2)}, u32[]{:S(2)}) collective-permute-start(bf16[144,128]{1,0:T(8,128)(2,1)S(1)} %get-tuple-element.45), channel_id=1, source_target_pairs={{0,32},{1,33},{2,34},{3,35},{4,36},{5,37},{6,38},{7,39},{8,40},{9,... | collective-permute-start | bytes 110600 | tf_op jit(solution)/shard_map/ppermute | solution.py:540
  92.3 4.9 %collective-permute-start.10 = (bf16[144,128]{1,0:T(8,128)(2,1)S(1)}, bf16[144,128]{1,0:T(8,128)(2,1)S(1)}, u32[]{:S(2)}, u32[]{:S(2)}) collective-permute-start(bf16[144,128]{1,0:T(8,128)(2,1)S(1)} %get-tuple-element.46), channel_id=1, source_target_pairs={{0,64},{1,65},{2,66},{3,67},{4,68},{5,69},{6,70},{7,71},{8,72},{9,... | collective-permute-start | bytes 110600 | tf_op jit(solution)/shard_map/ppermute | solution.py:540
  94.7 3.1 %collective-permute-start.11 = (bf16[144,128]{1,0:T(8,128)(2,1)S(1)}, bf16[144,128]{1,0:T(8,128)(2,1)S(1)}, u32[]{:S(2)}, u32[]{:S(2)}) collective-permute-start(bf16[144,128]{1,0:T(8,128)(2,1)S(1)} %get-tuple-element.47), channel_id=1, source_target_pairs={{0,96},{1,97},{2,98},{3,99},{4,100},{5,101},{6,102},{7,103},{8,104... | collective-permute-start | bytes 110600 | tf_op jit(solution)/shard_map/ppermute | solution.py:540
  97.8 10.0 %copy-start = (bf16[1152,1152]{1,0:T(8,128)(2,1)S(1)}, bf16[1152,1152]{1,0:T(8,128)(2,1)}, u32[]{:S(2)}) copy-start(bf16[1152,1152]{1,0:T(8,128)(2,1)} %weight.3) | copy-start | bytes 7962628
  97.8 10.0 %copy-start.2 = (f32[32,1152]{1,0:T(8,128)S(1)}, f32[32,1152]{1,0:T(8,128)}, u32[]{:S(2)}) copy-start(f32[32,1152]{1,0:T(8,128)} %gate.3) | copy-start | bytes 442372
  97.8 10.0 %copy-start.3 = (f32[1152]{0:T(1024)S(1)}, f32[1152]{0:T(1024)}, u32[]{:S(2)}) copy-start(f32[1152]{0:T(1024)} %bias.1) | copy-start | bytes 13828
  97.8 10.0 %copy-start.4 = (s32[128]{0:T(128)S(1)}, s32[128]{0:T(128)}, u32[]{:S(2)}) copy-start(s32[128]{0:T(128)} %tags.5) | copy-start | bytes 1540
  99.0 23.1 %all-to-all-start.2 = ((bf16[32,96,128]{2,1,0:T(8,128)(2,1)}), bf16[32,96,128]{2,1,0:T(8,128)(2,1)}, u32[]{:S(2)}, u32[]{:S(2)}) async-start(bf16[32,96,128]{2,1,0:T(8,128)(2,1)} %join.1), calls=%async_computation.2 | async-start | bytes 1572864 | tf_op jit(solution)/shard_map/all_to_all | solution.py:557
  107.8 1.0 copy-start.1
Sparse Core Ops, SparseCore 0:
  17.1 63.3 all-gather.2

commit v12 on v10

--- a/solution.py
+++ b/solution.py
@@ -28,7 +28,7 @@
 FULL = 2 * HALF
 FINAL = WIDTH // DEVICES
 CHIPS = 4
-SHARE = WIDTH // PLANES // 2
+SHARE = WIDTH // PLANES
 CLIPS = 32
 SCALE = 1.0 / math.sqrt(HEAD_DIM)
 SCALE2 = SCALE / math.log(2.0)
@@ -65,77 +65,37 @@
     return jnp.where(jnp.full(first.shape, flag, jnp.int32) == 0, first, second)
 
 
-def branch_body(out_grad, tags, gate, branch_ref, mine_ref, theirs_ref):
+def pack_body(
+    query, key, value, out_grad, gate, weight, tags, chunk_ref, branch_ref,
+    query_here, key_here, value_here, out_grad_here, gate_here, weight_here, sems,
+):
+    loads = {}
+    for at, (name, source, here) in enumerate((
+        ("out_grad", out_grad, out_grad_here), ("gate", gate, gate_here), ("key", key, key_here),
+        ("value", value, value_here), ("query", query, query_here), ("weight", weight, weight_here),
+    )):
+        loads[name] = pltpu.make_async_copy(source, here, sems.at[at])
+        loads[name].start()
+    tag_rows = jnp.broadcast_to(tags[...].reshape(1, TOK).astype(F32) + 1.0, (8, TOK))
+    blank = jnp.zeros((8, TOK), F32)
+    onehot = clip_onehot(tags)
+    loads["out_grad"].wait()
+    out_grad_t = out_grad_here[...].astype(F32).T
+    loads["gate"].wait()
     gate_t = lax.dot_general(
-        gate[...], clip_onehot(tags), (((0,), (0,)), ((), ())),
+        gate_here[...], onehot, (((0,), (0,)), ((), ())),
         precision=lax.Precision.HIGHEST, preferred_element_type=F32,
     )
-    branch_t = (out_grad[...].astype(F32).T * gate_t).astype(BF)
-    branch_ref[...] = branch_t
-    wide = branch_t.astype(F32)
-    halves = []
-    for side in range(2):
-        starts = [(2 * plane + side) * SHARE for plane in range(PLANES)]
-        halves.append(jnp.concatenate([wide[start : start + SHARE] for start in starts], 0))
-    side = core()
-    mine_ref[0] = pick(side, halves[0], halves[1]).astype(BF)
-    mine_ref[1] = jnp.zeros((WIDTH // 2, TOK), BF)
-    theirs_ref[...] = pick(side, halves[1], halves[0]).astype(BF)
-
-
-def branch_columns(out_grad, tags, gate):
-    return pl.pallas_call(
-        branch_body,
-        out_shape=(
-            jax.ShapeDtypeStruct((WIDTH, TOK), BF),
-            jax.ShapeDtypeStruct((2, WIDTH // 2, TOK), BF),
-            jax.ShapeDtypeStruct((WIDTH // 2, TOK), BF),
-        ),
-        in_specs=[WHOLE] * 3,
-        out_specs=(WHOLE,) * 3,
-        compiler_params=params(56),
-        cost_estimate=cost(2),
-        name="branch_columns",
-    )(out_grad, tags, gate)
-
-
-def fill_body(_, got, out_ref, sem):
-    load = pltpu.make_async_copy(got, out_ref.at[1], sem)
-    load.start()
-    load.wait()
-
-
-def fill(branch, got):
-    return pl.pallas_call(
-        fill_body,
-        out_shape=jax.ShapeDtypeStruct(branch.shape, BF),
-        in_specs=[FAR_AWAY] * 2,
-        out_specs=FAR_AWAY,
-        input_output_aliases={0: 0},
-        scratch_shapes=[pltpu.SemaphoreType.DMA],
-        compiler_params=params(16),
-        cost_estimate=cost(1),
-        name="fill",
-    )(branch, got)
-
-
-def pack_body(query, key, value, weight, tags, branch, chunk_ref, query_here, key_here, value_here, weight_here, sems):
-    loads = []
-    for at, (source, here) in enumerate(
-        ((key, key_here), (value, value_here), (query, query_here), (weight, weight_here))
-    ):
-        loads.append(pltpu.make_async_copy(source, here, sems.at[at]))
-        loads[-1].start()
-    tag_rows = jnp.broadcast_to(tags[...].reshape(1, TOK).astype(F32) + 1.0, (8, TOK))
-    blank = jnp.zeros((8, TOK), F32)
-    loads[0].wait()
+    branch = (out_grad_t * gate_t).astype(BF)
+    branch_ref[...] = branch
+    loads["key"].wait()
     key_t = key_here[...].astype(F32).T
-    loads[1].wait()
+    loads["value"].wait()
     value_t = value_here[...].astype(F32).T
-    loads[2].wait()
+    loads["query"].wait()
     query_t = query_here[...].astype(F32).T
-    loads[3].wait()
-    grad_t = mm(weight_here[...], branch[...])
+    loads["weight"].wait()
+    grad_t = mm(weight_here[...], branch)
     for head in range(HEADS):
         start = head * HEAD_DIM
         low, high = slice(start, start + HALF), slice(start + HALF, start + HEAD_DIM)
@@ -145,18 +105,24 @@
         chunk_ref[2 * head + 1] = jnp.concatenate(whole, 0).astype(BF)
 
 
-def pack(query, key, value, tags, branch, weight):
+def pack(query, key, value, out_grad, gate, weight, tags):
     rows = pltpu.VMEM((TOK, WIDTH), BF)
     return pl.pallas_call(
         pack_body,
-        out_shape=jax.ShapeDtypeStruct((PLANE, 2 * FULL, TOK), BF),
-        in_specs=[FAR_AWAY] * 4 + [WHOLE] * 2,
-        out_specs=WHOLE,
-        scratch_shapes=[rows, rows, rows, pltpu.VMEM((WIDTH, WIDTH), BF), pltpu.SemaphoreType.DMA((4,))],
+        out_shape=(
+            jax.ShapeDtypeStruct((PLANE, 2 * FULL, TOK), BF),
+            jax.ShapeDtypeStruct((WIDTH, TOK), BF),
+        ),
+        in_specs=[FAR_AWAY] * 6 + [WHOLE],
+        out_specs=(WHOLE,) * 2,
+        scratch_shapes=[
+            rows, rows, rows, rows, pltpu.VMEM((CLIPS, WIDTH), F32), pltpu.VMEM((WIDTH, WIDTH), BF),
+            pltpu.SemaphoreType.DMA((6,)),
+        ],
         compiler_params=params(61),
-        cost_estimate=cost(4),
+        cost_estimate=cost(5),
         name="pack",
-    )(query, key, value, weight, tags, branch)
+    )(query, key, value, out_grad, gate, weight, tags)
 
 
 def filled(piece, extra):
@@ -363,13 +329,12 @@
     step = pl.program_id(0)
     side = core()
     left, right = [], []
-    for chip in range(CHIPS):
-        for at in range(2):
-            block = 2 * (CHIPS * step + chip) + (side if at == 0 else 1 - side)
-            place = lax.rem(block, SIDE)
-            foreign = jnp.where(block // SIDE == side, 0, 1)
-            right.append(pick(foreign, mixed[place].astype(F32), other[place].astype(F32)))
-            left.append(branch[chip, at])
+    for at in range(CHIPS):
+        chip = CHIPS * step + at
+        place = 2 * lax.rem(chip, HEADS // 2) + side
+        foreign = jnp.where(chip // (HEADS // 2) == side, 0, 1)
+        right.append(pick(foreign, mixed[place].astype(F32), other[place].astype(F32)))
+        left.append(branch[at])
     term = lax.dot_general(
         jnp.concatenate(left, 1), jnp.concatenate(right, 1).astype(BF), (((1,), (1,)), ((), ())),
         preferred_element_type=F32,
@@ -378,7 +343,7 @@
     @pl.when(step == 0)
     def _():
         total[:, 0:FULL] = term
-        total[:, FULL:] = jnp.zeros((WIDTH // 2, TOK - FULL), F32)
+        total[:, FULL:] = jnp.zeros((WIDTH, TOK - FULL), F32)
 
     @pl.when(step > 0)
     def _():
@@ -399,9 +364,9 @@
         weight_term_body,
         grid=(HEADS // CHIPS,),
         out_shape=(jax.ShapeDtypeStruct((SHARE, TOK), BF),) * PLANES,
-        in_specs=[held, held, pl.BlockSpec((CHIPS, 2, WIDTH // 2, TOK), lambda i: (i, 0, 0, 0))],
+        in_specs=[held, held, pl.BlockSpec((CHIPS, WIDTH, TOK), lambda i: (i, 0, 0))],
         out_specs=(share,) * PLANES,
-        scratch_shapes=[pltpu.VMEM((WIDTH // 2, TOK), F32)],
+        scratch_shapes=[pltpu.VMEM((WIDTH, TOK), F32)],
         compiler_params=params(16),
         cost_estimate=cost(4),
         name="weight_term",
@@ -445,10 +410,10 @@
         pairs[others + (SIDE - EDGE) * side + block] += keep[SIDE + block].astype(F32)
         pairs[mine + (SIDE - EDGE) * (1 - side) + block] += got[SIDE + block].astype(F32)
     for block in range(SIDE):
-        tail = total[block * FINAL : block * FINAL + 16, :]
         for start, asked in ((mine, keep_asked), (others, got_asked)):
-            whole = [asked[block].astype(F32), pairs[start + block], tail]
-            out_ref[start + block] = jnp.concatenate(whole, 0).astype(BF)
+            at = start + block
+            whole = [asked[block].astype(F32), pairs[at], total[pl.ds(at * FINAL, 16), :]]
+            out_ref[at] = jnp.concatenate(whole, 0).astype(BF)
 
 
 def join(*values):
@@ -482,8 +447,10 @@
     dq_ref[...] = rows(1)
     dk_ref[...] = rows(2)
     dv_ref[...] = rows(3)
-    source = lax.rem(lax.axis_index("dp"), PLANE) // SIDE
-    tails = [packed[2 * head + source, 2 * FULL :].astype(F32)[:, 0:HEAD_DIM] for head in range(HEADS)]
+    tails = []
+    for head in range(HEADS):
+        first, second = [packed[2 * head + at, 2 * FULL :].astype(F32) for at in range(2)]
+        tails.append((first + second)[:, 0:HEAD_DIM])
     dw_ref[...] = jnp.concatenate(tails, 1)[0:FINAL]
 
 
@@ -528,10 +495,7 @@
 def shards(query, key, value, residual, tags, gate, weight, bias, out_grad):
     me = lax.axis_index("dp")
     side = me % 2
-    whole_branch, branch, branch_away = branch_columns(out_grad, tags, gate)
-    chunk = pack(query, key, value, tags, whole_branch, weight)
-    branch_got, chunk = lax.optimization_barrier((sent(branch_away, other_core), chunk))
-    branch = fill(branch, branch_got)
+    chunk, branch = pack(query, key, value, out_grad, gate, weight, tags)
     cores = [[plane * PLANE + 2 * chip + at for chip in range(HEADS)] for plane in range(PLANES) for at in range(2)]
     gathered = lax.all_gather(branch, "dp", axis=0, axis_index_groups=cores, tiled=False)
     own = traded(chunk)

time: 131 us -> 129 us (0.985)
  Pallas kernels: 28.6 us -> 24.9 us
  waiting for transfers between devices: 29.9 us -> 31.4 us
    pallas_call x3 -> x1, Pallas kernels: 8.26 us -> 5.88 us  [pack(): pl.pallas_call(pack_body, out_shape=(jax.ShapeDtypeStruct((PLANE, 2 * FUL...]
    pallas_call x1, Pallas kernels: 15.7 us -> 14.1 us  [attend(): pl.pallas_call(attend_body, out_shape=(whole, whole, whole, keys, keys, e...]
    ppermute x12 -> x11, waiting for transfers between devices: 5.89 us -> 7.33 us  [sent(): lax.ppermute(values, 'dp', [(i, j) for i, j in pairs if 0 <= j < DEVICES])]
    ppermute x12 -> x11, starting transfers between devices: 17.8 us -> 17 us  [sent(): lax.ppermute(values, 'dp', [(i, j) for i, j in pairs if 0 <= j < DEVICES])]
  transfers between devices with their start and end apart: 14 -> 13, of which waited for: 5 -> 5; matrix products, arithmetic and copies ran while one was open for 0% -> 0% of each run, Pallas kernels for 18% -> 13%
where the time goes in v12:
time: 129 us
  waiting for transfers between devices  31.4 us (24%)
  blocking collectives  28.6 us (22%)
  starting transfers between devices  26.5 us (21%)
  Pallas kernels  24.9 us (19%)
  between operations  14.2 us (11%)
  local copies, waits for them, and re-layouts  3.22 us (2%)
    all_to_all x1, blocking collectives, traded(): lax.all_to_all(values, 'dp', 0, 0, axis_index_groups=groups, tiled=True)  28.6 us
    all_to_all x1, waiting for transfers between devices, traded(): lax.all_to_all(values, 'dp', 0, 0, axis_index_groups=groups, tiled=True)  24 us
    ppermute x11, starting transfers between devices, sent(): lax.ppermute(values, 'dp', [(i, j) for i, j in pairs if 0 <= j < DEVICES])  17 us
    pallas_call x1, Pallas kernels, attend(): pl.pallas_call(attend_body, out_shape=(whole, whole, whole, keys, keys, e...  14.1 us
    all_to_all x1, starting transfers between devices, traded(): lax.all_to_all(values, 'dp', 0, 0, axis_index_groups=groups, tiled=True)  9.44 us
    ppermute x11, waiting for transfers between devices, sent(): lax.ppermute(values, 'dp', [(i, j) for i, j in pairs if 0 <= j < DEVICES])  7.33 us
    pallas_call x1, Pallas kernels, pack(): pl.pallas_call(pack_body, out_shape=(jax.ShapeDtypeStruct((PLANE, 2 * FUL...  5.88 us
    unnamed x16, local copies, waits for them, and re-layouts  3.14 us
  transfers between devices with their start and end apart: 13, of which 5 were waited for; matrix products, arithmetic and copies ran while one was open for 0% of the time, Pallas kernels for 13%

profile of v12, /device:TPU:1, one launch (start us, length us, event | category | flops | bytes accessed | tf_op | source)
XLA Modules:
  0.0 128.8 jit_solution(15047888485544646121)
XLA Ops:
  7.2 0.0 all-gather.3.cloned.1.call-start
  7.2 5.9 %pack.1 = (bf16[32,160,128]{2,1,0:T(8,128)(2,1)}, bf16[1152,128]{1,0:T(8,128)(2,1)}) custom-call(bf16[128,1152]{1,0:T(8,128)(2,1)} %query.1, bf16[128,1152]{1,0:T(8,128)(2,1)} %key.1, bf16[128,1152]{1,0:T(8,128)(2,1)} %value.1, bf16[128,1152]{1,0:T(8,128)(2,1)} %out_grad.1, f32[32,1152]{1,0:T(8,128)} %gate.3, bf16[1152,1152]{1,0:T(8,128)(2,1)} %weight.3, ...), custom_call_target="tpu_custom_call" | custom-call | flops 2000000000 | bytes 10000000 | tf_op jit(solution)/shard_map/pack/pallas_call | solution.py:110
  13.1 0.0 all-gather.3.cloned.1.call-update
  13.1 9.4 %all-to-all-start = ((bf16[32,160,128]{2,1,0:T(8,128)(2,1)}), bf16[32,160,128]{2,1,0:T(8,128)(2,1)S(1)}, u32[]{:S(2)}, u32[]{:S(2)}) async-start(bf16[32,160,128]{2,1,0:T(8,128)(2,1)} %get-tuple-element.25), calls=%async_computation | async-start | bytes 2621440 | tf_op jit(solution)/shard_map/all_to_all | solution.py:488
  22.6 24.0 %all-to-all-done.own = bf16[32,160,128]{2,1,0:T(8,128)(2,1)S(1)} async-done(((bf16[32,160,128]{2,1,0:T(8,128)(2,1)}), bf16[32,160,128]{2,1,0:T(8,128)(2,1)S(1)}, u32[]{:S(2)}, u32[]{:S(2)}) %all-to-all-start) | async-done | bytes 1310752 | tf_op jit(solution)/shard_map/all_to_all | solution.py:488
  46.6 0.5 collective-permute-start
  47.2 0.1 collective-permute-start.1
  47.3 3.8 %collective-permute-start.3 = (bf16[7,80,128]{2,1,0:T(8,128)(2,1)S(1)}, bf16[7,80,128]{2,1,0:T(8,128)(2,1)S(1)}, u32[]{:S(2)}, u32[]{:S(2)}) collective-permute-start(bf16[7,80,128]{2,1,0:T(8,128)(2,1)S(1)} %constant_dynamic-slice_fusion), channel_id=1, source_target_pairs={{1,32},{3,34},{5,36},{7,38},{9,40},{11,42},{13,44},{15,46},{17,48}... | collective-permute-start | bytes 430088 | tf_op jit(solution)/shard_map/ppermute | solution.py:471
  51.1 0.0 collective-permute-done.near
  51.2 1.9 %collective-permute-start.2 = (bf16[7,80,128]{2,1,0:T(8,128)(2,1)S(1)}, bf16[7,80,128]{2,1,0:T(8,128)(2,1)S(1)}, u32[]{:S(2)}, u32[]{:S(2)}) collective-permute-start(bf16[7,80,128]{2,1,0:T(8,128)(2,1)S(1)} %constant_dynamic-slice_fusion.1), channel_id=1, source_target_pairs={{1,32},{3,34},{5,36},{7,38},{9,40},{11,42},{13,44},{15,46},{17,48}... | collective-permute-start | bytes 430088 | tf_op jit(solution)/shard_map/ppermute | solution.py:471
  53.1 0.8 collective-permute-done.3.far_other
  53.9 0.0 collective-permute-done.1.asked
  53.9 4.1 %collective-permute-done.2.far_own = bf16[7,80,128]{2,1,0:T(8,128)(2,1)S(1)} collective-permute-done((bf16[7,80,128]{2,1,0:T(8,128)(2,1)S(1)}, bf16[7,80,128]{2,1,0:T(8,128)(2,1)S(1)}, u32[]{:S(2)}, u32[]{:S(2)}) %collective-permute-start.2) | collective-permute-done | bytes 143392 | tf_op jit(solution)/shard_map/ppermute | solution.py:471
  58.0 14.1 %attend.1 = (bf16[16,80,128]{2,1,0:T(8,128)(2,1)S(1)}, bf16[16,80,128]{2,1,0:T(8,128)(2,1)S(1)}, bf16[16,80,128]{2,1,0:T(8,128)(2,1)S(1)}, bf16[23,80,128]{2,1,0...) custom-call(bf16[32,160,128]{2,1,0:T(8,128)(2,1)S(1)} %all-to-all-done.own, ...), custom_call_target="tpu_custom_call" | custom-call | flops 8000000000 | bytes 40000000 | tf_op jit(solution)/shard_map/attend/pallas_call | solution.py:302
  72.1 0.0 copy-start.6
  72.1 0.8 copy-done.6
  72.9 0.0 collective-permute-start.6
  72.9 5.0 %collective-permute-start.5 = (bf16[7,160,128]{2,1,0:T(8,128)(2,1)S(1)}, bf16[7,160,128]{2,1,0:T(8,128)(2,1)S(1)}, u32[]{:S(2)}, u32[]{:S(2)}) collective-permute-start(bf16[7,160,128]{2,1,0:T(8,128)(2,1)S(1)} %get-tuple-element.30), channel_id=1, source_target_pairs={{1,32},{3,34},{5,36},{7,38},{9,40},{11,42},{13,44},{15,46},{17,48}... | collective-permute-start | bytes 860168 | tf_op jit(solution)/shard_map/ppermute | solution.py:471
  77.9 0.0 collective-permute-done.6.other
  77.9 0.0 all-gather.3.cloned.1.call-done
  77.9 0.0 copy-start.5
  77.9 2.3 %copy-done.5 = bf16[18432,128]{1,0:T(8,128)(2,1)S(1)} copy-done((bf16[18432,128]{1,0:T(8,128)(2,1)S(1)}, bf16[18432,128]{1,0:T(8,128)(2,1)}, u32[]{:S(2)}) %copy-start.5) | copy-done | bytes 4718616
  80.3 2.3 %weight_term.1 = (bf16[288,128]{1,0:T(8,128)(2,1)S(1)}, bf16[288,128]{1,0:T(8,128)(2,1)S(1)}, bf16[288,128]{1,0:T(8,128)(2,1)S(1)}, bf16[288,128]{1,0:T(8,128)(2,1)S(1)}) custom-call(bf16[16,80,128]{2,1,0:T(8,128)(2,1)S(1)} %get-tuple-element.31.mixed, bf16[16,80,128]{2,1,0:T(8,128)(2,1)S(1)} %collective-permute-done.6.other, bf16[16,1152,128]{2,1,0:T(8,128)(2,1)S(1)} %bitcast.2), custom_call_target="tpu_custom_call" | custom-call | flops 1600000000 | bytes 8000000 | tf_op jit(solution)/shard_map/weight_term/pallas_call | solution.py:363
  82.5 0.0 collective-permute-done.5.far
  82.5 0.0 copy-done.7
  82.6 0.2 fold.1
  82.7 0.7 collective-permute-start.7
  83.5 0.1 collective-permute-start.4
  83.5 1.2 collective-permute-start.8
  84.8 2.4 %collective-permute-start.9 = (bf16[288,128]{1,0:T(8,128)(2,1)S(1)}, bf16[288,128]{1,0:T(8,128)(2,1)S(1)}, u32[]{:S(2)}, u32[]{:S(2)}) collective-permute-start(bf16[288,128]{1,0:T(8,128)(2,1)S(1)} %get-tuple-element.38), channel_id=1, source_target_pairs={{0,64},{1,65},{2,66},{3,67},{4,68},{5,69},{6,70},{7,71},{8,72},{9,... | collective-permute-start | bytes 221192 | tf_op jit(solution)/shard_map/ppermute | solution.py:471
  87.2 1.2 collective-permute-start.10
  88.4 0.0 collective-permute-done.4.got_asked
  88.4 0.0 collective-permute-done.8.term1
  88.4 2.1 %collective-permute-done.9.term2 = bf16[288,128]{1,0:T(8,128)(2,1)S(1)} collective-permute-done((bf16[288,128]{1,0:T(8,128)(2,1)S(1)}, bf16[288,128]{1,0:T(8,128)(2,1)S(1)}, u32[]{:S(2)}, u32[]{:S(2)}) %collective-permute-start.9) | collective-permute-done | bytes 73760 | tf_op jit(solution)/shard_map/ppermute | solution.py:471
  90.4 0.3 collective-permute-done.10.term3
  90.8 0.0 collective-permute-done.7.got
  90.8 0.4 join.1
  91.2 0.0 copy-start
  91.2 0.0 copy-start.2
  91.2 0.0 copy-start.3
  91.2 0.0 copy-start.4
  91.2 28.6 %all_to_all.10.packed = bf16[32,176,128]{2,1,0:T(8,128)(2,1)S(1)} all-to-all(bf16[32,176,128]{2,1,0:T(8,128)(2,1)S(1)} %join.1), channel_id=1, replica_groups={{0,1,2,3,4,5,6,7,8,9,10,11,12,13,14,15,16,17,18,19,20,21,22,23,24,25,26..., dimensions={0} | all-to-all | bytes 2883584 | tf_op jit(solution)/shard_map/all_to_all | solution.py:488
  119.8 0.0 copy-done.1
  119.8 0.0 copy-done
  119.8 0.0 copy-done.2
  119.8 0.0 copy-done.3
  119.8 0.0 copy-done.4
  119.8 2.1 %finish.1 = (bf16[128,1152]{1,0:T(8,128)(2,1)}, bf16[128,1152]{1,0:T(8,128)(2,1)}, bf16[128,1152]{1,0:T(8,128)(2,1)}, bf16[128,1152]{1,0:T(8,128)(2,1)}, f32[9,1152]{1,0:T(8,128)}) custom-call(bf16[32,176,128]{2,1,0:T(8,128)(2,1)S(1)} %all_to_all.10.packed, bf16[128,1152]{1,0:T(8,128)(2,1)S(1)} %copy-done.1, s32[128]{0:T(128)S(1)} %copy-done.4, ...), custom_call_target="tpu_custom_call" | custom-call | flops 1200000000 | bytes 6000000 | tf_op jit(solution)/shard_map/finish/pallas_call | solution.py:458
  (6 shorter events, 0.1 us)
Async XLA Ops:
  7.2 70.8 %all-gather.3.cloned.1.call-start = ((), (), s32[]{:S(2)}) async-start(), calls=%async_computation.2 | async-start | bytes 5013504 | tf_op jit(solution)/shard_map/all_gather | solution.py:500
  13.1 33.5 %all-to-all-start = ((bf16[32,160,128]{2,1,0:T(8,128)(2,1)}), bf16[32,160,128]{2,1,0:T(8,128)(2,1)S(1)}, u32[]{:S(2)}, u32[]{:S(2)}) async-start(bf16[32,160,128]{2,1,0:T(8,128)(2,1)} %get-tuple-element.25), calls=%async_computation | async-start | bytes 2621440 | tf_op jit(solution)/shard_map/all_to_all | solution.py:488
  46.6 4.5 %collective-permute-start = (bf16[23,80,128]{2,1,0:T(8,128)(2,1)S(1)}, bf16[23,80,128]{2,1,0:T(8,128)(2,1)S(1)}, u32[]{:S(2)}, u32[]{:S(2)}) collective-permute-start(bf16[23,80,128]{2,1,0:T(8,128)(2,1)S(1)} %constant_dynamic-slice_fusion.3), channel_id=1, source_target_pairs={{0,1},{1,0},{2,3},{3,2},{4,5},{5,4},{6,7},{7,6},{8,9},{9,8},{10,11... | collective-permute-start | bytes 1413128 | tf_op jit(solution)/shard_map/ppermute | solution.py:471
  47.2 6.7 %collective-permute-start.1 = (bf16[16,80,128]{2,1,0:T(8,128)(2,1)S(1)}, bf16[16,80,128]{2,1,0:T(8,128)(2,1)S(1)}, u32[]{:S(2)}, u32[]{:S(2)}) collective-permute-start(bf16[16,80,128]{2,1,0:T(8,128)(2,1)S(1)} %constant_dynamic-slice_fusion.2), channel_id=1, source_target_pairs={{0,1},{1,0},{2,3},{3,2},{4,5},{5,4},{6,7},{7,6},{8,9},{9,8},{10,11... | collective-permute-start | bytes 983048 | tf_op jit(solution)/shard_map/ppermute | solution.py:471
  47.3 6.6 %collective-permute-start.3 = (bf16[7,80,128]{2,1,0:T(8,128)(2,1)S(1)}, bf16[7,80,128]{2,1,0:T(8,128)(2,1)S(1)}, u32[]{:S(2)}, u32[]{:S(2)}) collective-permute-start(bf16[7,80,128]{2,1,0:T(8,128)(2,1)S(1)} %constant_dynamic-slice_fusion), channel_id=1, source_target_pairs={{1,32},{3,34},{5,36},{7,38},{9,40},{11,42},{13,44},{15,46},{17,48}... | collective-permute-start | bytes 430088 | tf_op jit(solution)/shard_map/ppermute | solution.py:471
  51.2 6.8 %collective-permute-start.2 = (bf16[7,80,128]{2,1,0:T(8,128)(2,1)S(1)}, bf16[7,80,128]{2,1,0:T(8,128)(2,1)S(1)}, u32[]{:S(2)}, u32[]{:S(2)}) collective-permute-start(bf16[7,80,128]{2,1,0:T(8,128)(2,1)S(1)} %constant_dynamic-slice_fusion.1), channel_id=1, source_target_pairs={{1,32},{3,34},{5,36},{7,38},{9,40},{11,42},{13,44},{15,46},{17,48}... | collective-permute-start | bytes 430088 | tf_op jit(solution)/shard_map/ppermute | solution.py:471
  72.1 0.8 copy-start.6
  72.9 5.0 %collective-permute-start.6 = (bf16[16,80,128]{2,1,0:T(8,128)(2,1)S(1)}, bf16[16,80,128]{2,1,0:T(8,128)(2,1)S(1)}, u32[]{:S(2)}, u32[]{:S(2)}) collective-permute-start(bf16[16,80,128]{2,1,0:T(8,128)(2,1)S(1)} %get-tuple-element.31.mixed), channel_id=1, source_target_pairs={{0,1},{1,0},{2,3},{3,2},{4,5},{5,4},{6,7},{7,6},{8,9},{9,8},{10,11... | collective-permute-start | bytes 983048 | tf_op jit(solution)/shard_map/ppermute | solution.py:471
  72.9 9.7 %collective-permute-start.5 = (bf16[7,160,128]{2,1,0:T(8,128)(2,1)S(1)}, bf16[7,160,128]{2,1,0:T(8,128)(2,1)S(1)}, u32[]{:S(2)}, u32[]{:S(2)}) collective-permute-start(bf16[7,160,128]{2,1,0:T(8,128)(2,1)S(1)} %get-tuple-element.30), channel_id=1, source_target_pairs={{1,32},{3,34},{5,36},{7,38},{9,40},{11,42},{13,44},{15,46},{17,48}... | collective-permute-start | bytes 860168 | tf_op jit(solution)/shard_map/ppermute | solution.py:471
  77.9 2.3 %copy-start.5 = (bf16[18432,128]{1,0:T(8,128)(2,1)S(1)}, bf16[18432,128]{1,0:T(8,128)(2,1)}, u32[]{:S(2)}) copy-start(bf16[18432,128]{1,0:T(8,128)(2,1)} %all-gather.3.cloned.1.call-done) | copy-start | bytes 14155780
  80.3 2.3 %copy-start.7 = (bf16[23,80,128]{2,1,0:T(8,128)(2,1)S(1)}, bf16[23,80,128]{2,1,0:T(8,128)(2,1)}, u32[]{:S(2)}) copy-start(bf16[23,80,128]{2,1,0:T(8,128)(2,1)} %copy-done.6) | copy-start | bytes 1413124
  82.7 8.1 %collective-permute-start.7 = (bf16[23,80,128]{2,1,0:T(8,128)(2,1)S(1)}, bf16[23,80,128]{2,1,0:T(8,128)(2,1)S(1)}, u32[]{:S(2)}, u32[]{:S(2)}) collective-permute-start(bf16[23,80,128]{2,1,0:T(8,128)(2,1)S(1)} %get-tuple-element.36), channel_id=1, source_target_pairs={{0,1},{1,0},{2,3},{3,2},{4,5},{5,4},{6,7},{7,6},{8,9},{9,8},{10,11... | collective-permute-start | bytes 1413128 | tf_op jit(solution)/shard_map/ppermute | solution.py:471
  83.5 4.9 %collective-permute-start.4 = (bf16[16,80,128]{2,1,0:T(8,128)(2,1)S(1)}, bf16[16,80,128]{2,1,0:T(8,128)(2,1)S(1)}, u32[]{:S(2)}, u32[]{:S(2)}) collective-permute-start(bf16[16,80,128]{2,1,0:T(8,128)(2,1)S(1)} %get-tuple-element.27), channel_id=1, source_target_pairs={{0,1},{1,0},{2,3},{3,2},{4,5},{5,4},{6,7},{7,6},{8,9},{9,8},{10,11... | collective-permute-start | bytes 983048 | tf_op jit(solution)/shard_map/ppermute | solution.py:471
  83.5 4.8 %collective-permute-start.8 = (bf16[288,128]{1,0:T(8,128)(2,1)S(1)}, bf16[288,128]{1,0:T(8,128)(2,1)S(1)}, u32[]{:S(2)}, u32[]{:S(2)}) collective-permute-start(bf16[288,128]{1,0:T(8,128)(2,1)S(1)} %get-tuple-element.37), channel_id=1, source_target_pairs={{0,32},{1,33},{2,34},{3,35},{4,36},{5,37},{6,38},{7,39},{8,40},{9,... | collective-permute-start | bytes 221192 | tf_op jit(solution)/shard_map/ppermute | solution.py:471
  84.8 5.7 %collective-permute-start.9 = (bf16[288,128]{1,0:T(8,128)(2,1)S(1)}, bf16[288,128]{1,0:T(8,128)(2,1)S(1)}, u32[]{:S(2)}, u32[]{:S(2)}) collective-permute-start(bf16[288,128]{1,0:T(8,128)(2,1)S(1)} %get-tuple-element.38), channel_id=1, source_target_pairs={{0,64},{1,65},{2,66},{3,67},{4,68},{5,69},{6,70},{7,71},{8,72},{9,... | collective-permute-start | bytes 221192 | tf_op jit(solution)/shard_map/ppermute | solution.py:471
  87.2 3.6 %collective-permute-start.10 = (bf16[288,128]{1,0:T(8,128)(2,1)S(1)}, bf16[288,128]{1,0:T(8,128)(2,1)S(1)}, u32[]{:S(2)}, u32[]{:S(2)}) collective-permute-start(bf16[288,128]{1,0:T(8,128)(2,1)S(1)} %get-tuple-element.39), channel_id=1, source_target_pairs={{0,96},{1,97},{2,98},{3,99},{4,100},{5,101},{6,102},{7,103},{8,104... | collective-permute-start | bytes 221192 | tf_op jit(solution)/shard_map/ppermute | solution.py:471
  90.8 29.0 %copy-start.1 = (bf16[128,1152]{1,0:T(8,128)(2,1)S(1)}, bf16[128,1152]{1,0:T(8,128)(2,1)}, u32[]{:S(2)}) copy-start(bf16[128,1152]{1,0:T(8,128)(2,1)} %residual.1) | copy-start | bytes 884740
  91.2 28.6 %copy-start = (bf16[1152,1152]{1,0:T(8,128)(2,1)S(1)}, bf16[1152,1152]{1,0:T(8,128)(2,1)}, u32[]{:S(2)}) copy-start(bf16[1152,1152]{1,0:T(8,128)(2,1)} %weight.3) | copy-start | bytes 7962628
  91.2 28.6 %copy-start.2 = (f32[32,1152]{1,0:T(8,128)S(1)}, f32[32,1152]{1,0:T(8,128)}, u32[]{:S(2)}) copy-start(f32[32,1152]{1,0:T(8,128)} %gate.3) | copy-start | bytes 442372
  91.2 28.6 %copy-start.3 = (f32[1152]{0:T(1024)S(1)}, f32[1152]{0:T(1024)}, u32[]{:S(2)}) copy-start(f32[1152]{0:T(1024)} %bias.1) | copy-start | bytes 13828
  91.2 28.6 %copy-start.4 = (s32[128]{0:T(128)S(1)}, s32[128]{0:T(128)}, u32[]{:S(2)}) copy-start(s32[128]{0:T(128)} %tags.3) | copy-start | bytes 1540
Sparse Core Ops, SparseCore 0:
  13.2 64.6 all-gather.2

commit v13 on v12

--- a/solution.py
+++ b/solution.py
@@ -353,7 +353,7 @@
     def _():
         plane = lax.axis_index("dp") // PLANE
         for away in range(PLANES):
-            start = pl.multiple_of(lax.rem(plane + away, PLANES) * SHARE, 8)
+            start = pl.multiple_of((plane ^ away) * SHARE, 8)
             out_refs[away][...] = total[pl.ds(start, SHARE), :].astype(BF)
 
 
@@ -479,8 +479,8 @@
     return device - PLANE + 1 if device % 2 == 0 else device + PLANE - 1
 
 
-def planes_on(count):
-    return lambda device: (device + count * PLANE) % DEVICES
+def plane_pair(bits):
+    return lambda device: device ^ (bits * PLANE)
 
 
 def traded(values):
@@ -508,7 +508,7 @@
     mixed_other = sent(mixed, other_core)
     got_asked = sent(give_asked, other_core)
     term, *terms = weight_term(mixed, mixed_other, gathered)
-    terms = [sent(one, planes_on(away + 1)) for away, one in enumerate(terms)]
+    terms = [sent(one, plane_pair(away + 1)) for away, one in enumerate(terms)]
     far, _ = lax.optimization_barrier((far, term))
     keep, give = fold(keep, give, far)
     got = sent(give, other_core)

time: 129 us -> 130 us (level)
  waiting for transfers between devices: 31.4 us -> 33.5 us
    ppermute x11, waiting for transfers between devices: 7.33 us -> 9.28 us  [sent(): lax.ppermute(values, 'dp', [(i, j) for i, j in pairs if 0 <= j < DEVICES])]
  transfers between devices with their start and end apart: 13 -> 13, of which waited for: 5 -> 6; matrix products, arithmetic and copies ran while one was open for 0% -> 0% of each run, Pallas kernels for 13% -> 13%
where the time goes in v13:
time: 130 us
  waiting for transfers between devices  33.5 us (26%)
  blocking collectives  28.4 us (22%)
  Pallas kernels  25.4 us (20%)
  starting transfers between devices  25.3 us (19%)
  between operations  14.2 us (11%)
  local copies, waits for them, and re-layouts  3.23 us (2%)
    all_to_all x1, blocking collectives, traded(): lax.all_to_all(values, 'dp', 0, 0, axis_index_groups=groups, tiled=True)  28.4 us
    all_to_all x1, waiting for transfers between devices, traded(): lax.all_to_all(values, 'dp', 0, 0, axis_index_groups=groups, tiled=True)  24 us
    ppermute x11, starting transfers between devices, sent(): lax.ppermute(values, 'dp', [(i, j) for i, j in pairs if 0 <= j < DEVICES])  15.8 us
    pallas_call x1, Pallas kernels, attend(): pl.pallas_call(attend_body, out_shape=(whole, whole, whole, keys, keys, e...  14.6 us
    all_to_all x1, starting transfers between devices, traded(): lax.all_to_all(values, 'dp', 0, 0, axis_index_groups=groups, tiled=True)  9.44 us
    ppermute x11, waiting for transfers between devices, sent(): lax.ppermute(values, 'dp', [(i, j) for i, j in pairs if 0 <= j < DEVICES])  9.28 us
    pallas_call x1, Pallas kernels, pack(): pl.pallas_call(pack_body, out_shape=(jax.ShapeDtypeStruct((PLANE, 2 * FUL...  5.88 us
    unnamed x16, local copies, waits for them, and re-layouts  3.15 us
  transfers between devices with their start and end apart: 13, of which 6 were waited for; matrix products, arithmetic and copies ran while one was open for 0% of the time, Pallas kernels for 13%

profile of v13, /device:TPU:1, one launch (start us, length us, event | category | flops | bytes accessed | tf_op | source)
XLA Modules:
  0.0 130.0 jit_solution(10789398968149860765)
XLA Ops:
  7.2 0.0 all-gather.3.cloned.1.call-start
  7.2 5.9 %pack.1 = (bf16[32,160,128]{2,1,0:T(8,128)(2,1)}, bf16[1152,128]{1,0:T(8,128)(2,1)}) custom-call(bf16[128,1152]{1,0:T(8,128)(2,1)} %query.1, bf16[128,1152]{1,0:T(8,128)(2,1)} %key.1, bf16[128,1152]{1,0:T(8,128)(2,1)} %value.1, bf16[128,1152]{1,0:T(8,128)(2,1)} %out_grad.1, f32[32,1152]{1,0:T(8,128)} %gate.3, bf16[1152,1152]{1,0:T(8,128)(2,1)} %weight.3, ...), custom_call_target="tpu_custom_call" | custom-call | flops 2000000000 | bytes 10000000 | tf_op jit(solution)/shard_map/pack/pallas_call | solution.py:110
  13.1 0.0 all-gather.3.cloned.1.call-update
  13.1 9.4 %all-to-all-start = ((bf16[32,160,128]{2,1,0:T(8,128)(2,1)}), bf16[32,160,128]{2,1,0:T(8,128)(2,1)S(1)}, u32[]{:S(2)}, u32[]{:S(2)}) async-start(bf16[32,160,128]{2,1,0:T(8,128)(2,1)} %get-tuple-element.25), calls=%async_computation | async-start | bytes 2621440 | tf_op jit(solution)/shard_map/all_to_all | solution.py:488
  22.6 24.0 %all-to-all-done.own = bf16[32,160,128]{2,1,0:T(8,128)(2,1)S(1)} async-done(((bf16[32,160,128]{2,1,0:T(8,128)(2,1)}), bf16[32,160,128]{2,1,0:T(8,128)(2,1)S(1)}, u32[]{:S(2)}, u32[]{:S(2)}) %all-to-all-start) | async-done | bytes 1310752 | tf_op jit(solution)/shard_map/all_to_all | solution.py:488
  46.6 0.5 collective-permute-start
  47.2 0.1 collective-permute-start.1
  47.3 3.8 %collective-permute-start.3 = (bf16[7,80,128]{2,1,0:T(8,128)(2,1)S(1)}, bf16[7,80,128]{2,1,0:T(8,128)(2,1)S(1)}, u32[]{:S(2)}, u32[]{:S(2)}) collective-permute-start(bf16[7,80,128]{2,1,0:T(8,128)(2,1)S(1)} %constant_dynamic-slice_fusion), channel_id=1, source_target_pairs={{1,32},{3,34},{5,36},{7,38},{9,40},{11,42},{13,44},{15,46},{17,48}... | collective-permute-start | bytes 430088 | tf_op jit(solution)/shard_map/ppermute | solution.py:471
  51.1 0.0 collective-permute-done.near
  51.2 1.9 %collective-permute-start.2 = (bf16[7,80,128]{2,1,0:T(8,128)(2,1)S(1)}, bf16[7,80,128]{2,1,0:T(8,128)(2,1)S(1)}, u32[]{:S(2)}, u32[]{:S(2)}) collective-permute-start(bf16[7,80,128]{2,1,0:T(8,128)(2,1)S(1)} %constant_dynamic-slice_fusion.1), channel_id=1, source_target_pairs={{1,32},{3,34},{5,36},{7,38},{9,40},{11,42},{13,44},{15,46},{17,48}... | collective-permute-start | bytes 430088 | tf_op jit(solution)/shard_map/ppermute | solution.py:471
  53.1 0.8 collective-permute-done.3.far_other
  53.9 0.0 collective-permute-done.1.asked
  53.9 4.1 %collective-permute-done.2.far_own = bf16[7,80,128]{2,1,0:T(8,128)(2,1)S(1)} collective-permute-done((bf16[7,80,128]{2,1,0:T(8,128)(2,1)S(1)}, bf16[7,80,128]{2,1,0:T(8,128)(2,1)S(1)}, u32[]{:S(2)}, u32[]{:S(2)}) %collective-permute-start.2) | collective-permute-done | bytes 143392 | tf_op jit(solution)/shard_map/ppermute | solution.py:471
  58.0 14.6 %attend.1 = (bf16[16,80,128]{2,1,0:T(8,128)(2,1)S(1)}, bf16[16,80,128]{2,1,0:T(8,128)(2,1)S(1)}, bf16[16,80,128]{2,1,0:T(8,128)(2,1)S(1)}, bf16[23,80,128]{2,1,0...) custom-call(bf16[32,160,128]{2,1,0:T(8,128)(2,1)S(1)} %all-to-all-done.own, ...), custom_call_target="tpu_custom_call" | custom-call | flops 8000000000 | bytes 40000000 | tf_op jit(solution)/shard_map/attend/pallas_call | solution.py:302
  72.6 0.0 copy-start.6
  72.6 0.8 copy-done.6
  73.4 0.0 collective-permute-start.6
  73.4 4.3 %collective-permute-start.5 = (bf16[7,160,128]{2,1,0:T(8,128)(2,1)S(1)}, bf16[7,160,128]{2,1,0:T(8,128)(2,1)S(1)}, u32[]{:S(2)}, u32[]{:S(2)}) collective-permute-start(bf16[7,160,128]{2,1,0:T(8,128)(2,1)S(1)} %get-tuple-element.30), channel_id=1, source_target_pairs={{1,32},{3,34},{5,36},{7,38},{9,40},{11,42},{13,44},{15,46},{17,48}... | collective-permute-start | bytes 860168 | tf_op jit(solution)/shard_map/ppermute | solution.py:471
  77.7 0.0 collective-permute-done.6.other
  77.7 0.2 all-gather.3.cloned.1.call-done
  77.9 0.0 copy-start.5
  77.9 2.3 %copy-done.5 = bf16[18432,128]{1,0:T(8,128)(2,1)S(1)} copy-done((bf16[18432,128]{1,0:T(8,128)(2,1)S(1)}, bf16[18432,128]{1,0:T(8,128)(2,1)}, u32[]{:S(2)}) %copy-start.5) | copy-done | bytes 4718616
  80.3 2.3 %weight_term.1 = (bf16[288,128]{1,0:T(8,128)(2,1)S(1)}, bf16[288,128]{1,0:T(8,128)(2,1)S(1)}, bf16[288,128]{1,0:T(8,128)(2,1)S(1)}, bf16[288,128]{1,0:T(8,128)(2,1)S(1)}) custom-call(bf16[16,80,128]{2,1,0:T(8,128)(2,1)S(1)} %get-tuple-element.31.mixed, bf16[16,80,128]{2,1,0:T(8,128)(2,1)S(1)} %collective-permute-done.6.other, bf16[16,1152,128]{2,1,0:T(8,128)(2,1)S(1)} %bitcast.2), custom_call_target="tpu_custom_call" | custom-call | flops 1600000000 | bytes 8000000 | tf_op jit(solution)/shard_map/weight_term/pallas_call | solution.py:363
  82.5 0.0 collective-permute-done.5.far
  82.5 0.0 copy-done.7
  82.5 0.2 fold.1
  82.7 0.8 collective-permute-start.7
  83.5 0.1 collective-permute-start.4
  83.5 1.9 %collective-permute-start.8 = (bf16[288,128]{1,0:T(8,128)(2,1)S(1)}, bf16[288,128]{1,0:T(8,128)(2,1)S(1)}, u32[]{:S(2)}, u32[]{:S(2)}) collective-permute-start(bf16[288,128]{1,0:T(8,128)(2,1)S(1)} %get-tuple-element.37), channel_id=1, source_target_pairs={{0,32},{1,33},{2,34},{3,35},{4,36},{5,37},{6,38},{7,39},{8,40},{9,... | collective-permute-start | bytes 221192 | tf_op jit(solution)/shard_map/ppermute | solution.py:471
  85.4 1.8 %collective-permute-start.9 = (bf16[288,128]{1,0:T(8,128)(2,1)S(1)}, bf16[288,128]{1,0:T(8,128)(2,1)S(1)}, u32[]{:S(2)}, u32[]{:S(2)}) collective-permute-start(bf16[288,128]{1,0:T(8,128)(2,1)S(1)} %get-tuple-element.38), channel_id=1, source_target_pairs={{0,64},{1,65},{2,66},{3,67},{4,68},{5,69},{6,70},{7,71},{8,72},{9,... | collective-permute-start | bytes 221192 | tf_op jit(solution)/shard_map/ppermute | solution.py:471
  87.2 0.6 collective-permute-start.10
  87.8 0.0 collective-permute-done.4.got_asked
  87.8 0.0 collective-permute-done.8.term1
  87.8 3.4 %collective-permute-done.9.term2 = bf16[288,128]{1,0:T(8,128)(2,1)S(1)} collective-permute-done((bf16[288,128]{1,0:T(8,128)(2,1)S(1)}, bf16[288,128]{1,0:T(8,128)(2,1)S(1)}, u32[]{:S(2)}, u32[]{:S(2)}) %collective-permute-start.9) | collective-permute-done | bytes 73760 | tf_op jit(solution)/shard_map/ppermute | solution.py:471
  91.2 1.0 collective-permute-done.10.term3
  92.2 0.0 collective-permute-done.7.got
  92.2 0.4 join.1
  92.5 0.0 copy-start
  92.6 0.0 copy-start.2
  92.6 0.0 copy-start.3
  92.6 0.0 copy-start.4
  92.6 28.4 %all_to_all.10.packed = bf16[32,176,128]{2,1,0:T(8,128)(2,1)S(1)} all-to-all(bf16[32,176,128]{2,1,0:T(8,128)(2,1)S(1)} %join.1), channel_id=1, replica_groups={{0,1,2,3,4,5,6,7,8,9,10,11,12,13,14,15,16,17,18,19,20,21,22,23,24,25,26..., dimensions={0} | all-to-all | bytes 2883584 | tf_op jit(solution)/shard_map/all_to_all | solution.py:488
  121.0 0.0 copy-done.1
  121.0 0.0 copy-done
  121.0 0.0 copy-done.2
  121.0 0.0 copy-done.3
  121.0 0.0 copy-done.4
  121.0 2.1 %finish.1 = (bf16[128,1152]{1,0:T(8,128)(2,1)}, bf16[128,1152]{1,0:T(8,128)(2,1)}, bf16[128,1152]{1,0:T(8,128)(2,1)}, bf16[128,1152]{1,0:T(8,128)(2,1)}, f32[9,1152]{1,0:T(8,128)}) custom-call(bf16[32,176,128]{2,1,0:T(8,128)(2,1)S(1)} %all_to_all.10.packed, bf16[128,1152]{1,0:T(8,128)(2,1)S(1)} %copy-done.1, s32[128]{0:T(128)S(1)} %copy-done.4, ...), custom_call_target="tpu_custom_call" | custom-call | flops 1200000000 | bytes 6000000 | tf_op jit(solution)/shard_map/finish/pallas_call | solution.py:458
  (6 shorter events, 0.1 us)
Async XLA Ops:
  7.2 70.7 %all-gather.3.cloned.1.call-start = ((), (), s32[]{:S(2)}) async-start(), calls=%async_computation.2 | async-start | bytes 5013504 | tf_op jit(solution)/shard_map/all_gather | solution.py:500
  13.1 33.5 %all-to-all-start = ((bf16[32,160,128]{2,1,0:T(8,128)(2,1)}), bf16[32,160,128]{2,1,0:T(8,128)(2,1)S(1)}, u32[]{:S(2)}, u32[]{:S(2)}) async-start(bf16[32,160,128]{2,1,0:T(8,128)(2,1)} %get-tuple-element.25), calls=%async_computation | async-start | bytes 2621440 | tf_op jit(solution)/shard_map/all_to_all | solution.py:488
  46.6 4.5 %collective-permute-start = (bf16[23,80,128]{2,1,0:T(8,128)(2,1)S(1)}, bf16[23,80,128]{2,1,0:T(8,128)(2,1)S(1)}, u32[]{:S(2)}, u32[]{:S(2)}) collective-permute-start(bf16[23,80,128]{2,1,0:T(8,128)(2,1)S(1)} %constant_dynamic-slice_fusion.3), channel_id=1, source_target_pairs={{0,1},{1,0},{2,3},{3,2},{4,5},{5,4},{6,7},{7,6},{8,9},{9,8},{10,11... | collective-permute-start | bytes 1413128 | tf_op jit(solution)/shard_map/ppermute | solution.py:471
  47.2 6.7 %collective-permute-start.1 = (bf16[16,80,128]{2,1,0:T(8,128)(2,1)S(1)}, bf16[16,80,128]{2,1,0:T(8,128)(2,1)S(1)}, u32[]{:S(2)}, u32[]{:S(2)}) collective-permute-start(bf16[16,80,128]{2,1,0:T(8,128)(2,1)S(1)} %constant_dynamic-slice_fusion.2), channel_id=1, source_target_pairs={{0,1},{1,0},{2,3},{3,2},{4,5},{5,4},{6,7},{7,6},{8,9},{9,8},{10,11... | collective-permute-start | bytes 983048 | tf_op jit(solution)/shard_map/ppermute | solution.py:471
  47.3 6.6 %collective-permute-start.3 = (bf16[7,80,128]{2,1,0:T(8,128)(2,1)S(1)}, bf16[7,80,128]{2,1,0:T(8,128)(2,1)S(1)}, u32[]{:S(2)}, u32[]{:S(2)}) collective-permute-start(bf16[7,80,128]{2,1,0:T(8,128)(2,1)S(1)} %constant_dynamic-slice_fusion), channel_id=1, source_target_pairs={{1,32},{3,34},{5,36},{7,38},{9,40},{11,42},{13,44},{15,46},{17,48}... | collective-permute-start | bytes 430088 | tf_op jit(solution)/shard_map/ppermute | solution.py:471
  51.2 6.8 %collective-permute-start.2 = (bf16[7,80,128]{2,1,0:T(8,128)(2,1)S(1)}, bf16[7,80,128]{2,1,0:T(8,128)(2,1)S(1)}, u32[]{:S(2)}, u32[]{:S(2)}) collective-permute-start(bf16[7,80,128]{2,1,0:T(8,128)(2,1)S(1)} %constant_dynamic-slice_fusion.1), channel_id=1, source_target_pairs={{1,32},{3,34},{5,36},{7,38},{9,40},{11,42},{13,44},{15,46},{17,48}... | collective-permute-start | bytes 430088 | tf_op jit(solution)/shard_map/ppermute | solution.py:471
  72.6 0.8 copy-start.6
  73.4 4.4 %collective-permute-start.6 = (bf16[16,80,128]{2,1,0:T(8,128)(2,1)S(1)}, bf16[16,80,128]{2,1,0:T(8,128)(2,1)S(1)}, u32[]{:S(2)}, u32[]{:S(2)}) collective-permute-start(bf16[16,80,128]{2,1,0:T(8,128)(2,1)S(1)} %get-tuple-element.31.mixed), channel_id=1, source_target_pairs={{0,1},{1,0},{2,3},{3,2},{4,5},{5,4},{6,7},{7,6},{8,9},{9,8},{10,11... | collective-permute-start | bytes 983048 | tf_op jit(solution)/shard_map/ppermute | solution.py:471
  73.4 9.1 %collective-permute-start.5 = (bf16[7,160,128]{2,1,0:T(8,128)(2,1)S(1)}, bf16[7,160,128]{2,1,0:T(8,128)(2,1)S(1)}, u32[]{:S(2)}, u32[]{:S(2)}) collective-permute-start(bf16[7,160,128]{2,1,0:T(8,128)(2,1)S(1)} %get-tuple-element.30), channel_id=1, source_target_pairs={{1,32},{3,34},{5,36},{7,38},{9,40},{11,42},{13,44},{15,46},{17,48}... | collective-permute-start | bytes 860168 | tf_op jit(solution)/shard_map/ppermute | solution.py:471
  77.9 2.3 %copy-start.5 = (bf16[18432,128]{1,0:T(8,128)(2,1)S(1)}, bf16[18432,128]{1,0:T(8,128)(2,1)}, u32[]{:S(2)}) copy-start(bf16[18432,128]{1,0:T(8,128)(2,1)} %all-gather.3.cloned.1.call-done) | copy-start | bytes 14155780
  80.3 2.3 %copy-start.7 = (bf16[23,80,128]{2,1,0:T(8,128)(2,1)S(1)}, bf16[23,80,128]{2,1,0:T(8,128)(2,1)}, u32[]{:S(2)}) copy-start(bf16[23,80,128]{2,1,0:T(8,128)(2,1)} %copy-done.6) | copy-start | bytes 1413124
  82.7 9.5 %collective-permute-start.7 = (bf16[23,80,128]{2,1,0:T(8,128)(2,1)S(1)}, bf16[23,80,128]{2,1,0:T(8,128)(2,1)S(1)}, u32[]{:S(2)}, u32[]{:S(2)}) collective-permute-start(bf16[23,80,128]{2,1,0:T(8,128)(2,1)S(1)} %get-tuple-element.36), channel_id=1, source_target_pairs={{0,1},{1,0},{2,3},{3,2},{4,5},{5,4},{6,7},{7,6},{8,9},{9,8},{10,11... | collective-permute-start | bytes 1413128 | tf_op jit(solution)/shard_map/ppermute | solution.py:471
  83.5 4.3 %collective-permute-start.4 = (bf16[16,80,128]{2,1,0:T(8,128)(2,1)S(1)}, bf16[16,80,128]{2,1,0:T(8,128)(2,1)S(1)}, u32[]{:S(2)}, u32[]{:S(2)}) collective-permute-start(bf16[16,80,128]{2,1,0:T(8,128)(2,1)S(1)} %get-tuple-element.27), channel_id=1, source_target_pairs={{0,1},{1,0},{2,3},{3,2},{4,5},{5,4},{6,7},{7,6},{8,9},{9,8},{10,11... | collective-permute-start | bytes 983048 | tf_op jit(solution)/shard_map/ppermute | solution.py:471
  83.5 4.3 %collective-permute-start.8 = (bf16[288,128]{1,0:T(8,128)(2,1)S(1)}, bf16[288,128]{1,0:T(8,128)(2,1)S(1)}, u32[]{:S(2)}, u32[]{:S(2)}) collective-permute-start(bf16[288,128]{1,0:T(8,128)(2,1)S(1)} %get-tuple-element.37), channel_id=1, source_target_pairs={{0,32},{1,33},{2,34},{3,35},{4,36},{5,37},{6,38},{7,39},{8,40},{9,... | collective-permute-start | bytes 221192 | tf_op jit(solution)/shard_map/ppermute | solution.py:471
  85.4 5.8 %collective-permute-start.9 = (bf16[288,128]{1,0:T(8,128)(2,1)S(1)}, bf16[288,128]{1,0:T(8,128)(2,1)S(1)}, u32[]{:S(2)}, u32[]{:S(2)}) collective-permute-start(bf16[288,128]{1,0:T(8,128)(2,1)S(1)} %get-tuple-element.38), channel_id=1, source_target_pairs={{0,64},{1,65},{2,66},{3,67},{4,68},{5,69},{6,70},{7,71},{8,72},{9,... | collective-permute-start | bytes 221192 | tf_op jit(solution)/shard_map/ppermute | solution.py:471
  87.2 5.0 %collective-permute-start.10 = (bf16[288,128]{1,0:T(8,128)(2,1)S(1)}, bf16[288,128]{1,0:T(8,128)(2,1)S(1)}, u32[]{:S(2)}, u32[]{:S(2)}) collective-permute-start(bf16[288,128]{1,0:T(8,128)(2,1)S(1)} %get-tuple-element.39), channel_id=1, source_target_pairs={{0,96},{1,97},{2,98},{3,99},{4,100},{5,101},{6,102},{7,103},{8,104... | collective-permute-start | bytes 221192 | tf_op jit(solution)/shard_map/ppermute | solution.py:471
  92.2 28.8 %copy-start.1 = (bf16[128,1152]{1,0:T(8,128)(2,1)S(1)}, bf16[128,1152]{1,0:T(8,128)(2,1)}, u32[]{:S(2)}) copy-start(bf16[128,1152]{1,0:T(8,128)(2,1)} %residual.1) | copy-start | bytes 884740
  92.5 28.4 %copy-start = (bf16[1152,1152]{1,0:T(8,128)(2,1)S(1)}, bf16[1152,1152]{1,0:T(8,128)(2,1)}, u32[]{:S(2)}) copy-start(bf16[1152,1152]{1,0:T(8,128)(2,1)} %weight.3) | copy-start | bytes 7962628
  92.6 28.4 %copy-start.2 = (f32[32,1152]{1,0:T(8,128)S(1)}, f32[32,1152]{1,0:T(8,128)}, u32[]{:S(2)}) copy-start(f32[32,1152]{1,0:T(8,128)} %gate.3) | copy-start | bytes 442372
  92.6 28.4 %copy-start.3 = (f32[1152]{0:T(1024)S(1)}, f32[1152]{0:T(1024)}, u32[]{:S(2)}) copy-start(f32[1152]{0:T(1024)} %bias.1) | copy-start | bytes 13828
  92.6 28.4 %copy-start.4 = (s32[128]{0:T(128)S(1)}, s32[128]{0:T(128)}, u32[]{:S(2)}) copy-start(s32[128]{0:T(128)} %tags.3) | copy-start | bytes 1540
Sparse Core Ops, SparseCore 0:
  13.2 64.6 all-gather.2

commit v14 on v12

--- a/solution.py
+++ b/solution.py
@@ -92,17 +92,22 @@
     key_t = key_here[...].astype(F32).T
     loads["value"].wait()
     value_t = value_here[...].astype(F32).T
+    halves_of = [
+        (slice(head * HEAD_DIM, head * HEAD_DIM + HALF), slice(head * HEAD_DIM + HALF, (head + 1) * HEAD_DIM))
+        for head in range(HEADS)
+    ]
+    for head, (low, high) in enumerate(halves_of):
+        chunk_ref[2 * head, 0:FULL] = jnp.concatenate([key_t[low], value_t[low]], 0).astype(BF)
+        whole = [key_t[high], tag_rows, value_t[high], blank]
+        chunk_ref[2 * head + 1, 0:FULL] = jnp.concatenate(whole, 0).astype(BF)
     loads["query"].wait()
     query_t = query_here[...].astype(F32).T
     loads["weight"].wait()
     grad_t = mm(weight_here[...], branch)
-    for head in range(HEADS):
-        start = head * HEAD_DIM
-        low, high = slice(start, start + HALF), slice(start + HALF, start + HEAD_DIM)
-        whole = [key_t[low], value_t[low], query_t[low], grad_t[low]]
-        chunk_ref[2 * head] = jnp.concatenate(whole, 0).astype(BF)
-        whole = [key_t[high], tag_rows, value_t[high], blank, query_t[high], blank, grad_t[high], blank]
-        chunk_ref[2 * head + 1] = jnp.concatenate(whole, 0).astype(BF)
+    for head, (low, high) in enumerate(halves_of):
+        chunk_ref[2 * head, FULL:] = jnp.concatenate([query_t[low], grad_t[low]], 0).astype(BF)
+        whole = [query_t[high], blank, grad_t[high], blank]
+        chunk_ref[2 * head + 1, FULL:] = jnp.concatenate(whole, 0).astype(BF)
 
 
 def pack(query, key, value, out_grad, gate, weight, tags):

time: 129 us -> 129 us (level)
  no operation moved by 1% of the time
where the time goes in v14:
time: 129 us
  waiting for transfers between devices  31.3 us (24%)
  blocking collectives  28.6 us (22%)
  starting transfers between devices  26.3 us (20%)
  Pallas kernels  25 us (19%)
  between operations  14.2 us (11%)
  local copies, waits for them, and re-layouts  3.22 us (2%)
    all_to_all x1, blocking collectives, traded(): lax.all_to_all(values, 'dp', 0, 0, axis_index_groups=groups, tiled=True)  28.6 us
    all_to_all x1, waiting for transfers between devices, traded(): lax.all_to_all(values, 'dp', 0, 0, axis_index_groups=groups, tiled=True)  24 us
    ppermute x11, starting transfers between devices, sent(): lax.ppermute(values, 'dp', [(i, j) for i, j in pairs if 0 <= j < DEVICES])  16.9 us
    pallas_call x1, Pallas kernels, attend(): pl.pallas_call(attend_body, out_shape=(whole, whole, whole, keys, keys, e...  14.3 us
    all_to_all x1, starting transfers between devices, traded(): lax.all_to_all(values, 'dp', 0, 0, axis_index_groups=groups, tiled=True)  9.45 us
    ppermute x11, waiting for transfers between devices, sent(): lax.ppermute(values, 'dp', [(i, j) for i, j in pairs if 0 <= j < DEVICES])  7.32 us
    pallas_call x1, Pallas kernels, pack(): pl.pallas_call(pack_body, out_shape=(jax.ShapeDtypeStruct((PLANE, 2 * FUL...  5.87 us
    unnamed x16, local copies, waits for them, and re-layouts  3.14 us
  transfers between devices with their start and end apart: 13, of which 5 were waited for; matrix products, arithmetic and copies ran while one was open for 0% of the time, Pallas kernels for 13%

profile of v14, /device:TPU:1, one launch (start us, length us, event | category | flops | bytes accessed | tf_op | source)
XLA Modules:
  0.0 128.8 jit_solution(9038831961303645984)
XLA Ops:
  7.2 0.0 all-gather.3.cloned.1.call-start
  7.2 5.9 %pack.1 = (bf16[32,160,128]{2,1,0:T(8,128)(2,1)}, bf16[1152,128]{1,0:T(8,128)(2,1)}) custom-call(bf16[128,1152]{1,0:T(8,128)(2,1)} %query.1, bf16[128,1152]{1,0:T(8,128)(2,1)} %key.1, bf16[128,1152]{1,0:T(8,128)(2,1)} %value.1, bf16[128,1152]{1,0:T(8,128)(2,1)} %out_grad.1, f32[32,1152]{1,0:T(8,128)} %gate.3, bf16[1152,1152]{1,0:T(8,128)(2,1)} %weight.3, ...), custom_call_target="tpu_custom_call" | custom-call | flops 2000000000 | bytes 10000000 | tf_op jit(solution)/shard_map/pack/pallas_call | solution.py:115
  13.1 0.0 all-gather.3.cloned.1.call-update
  13.1 9.4 %all-to-all-start = ((bf16[32,160,128]{2,1,0:T(8,128)(2,1)}), bf16[32,160,128]{2,1,0:T(8,128)(2,1)S(1)}, u32[]{:S(2)}, u32[]{:S(2)}) async-start(bf16[32,160,128]{2,1,0:T(8,128)(2,1)} %get-tuple-element.25), calls=%async_computation | async-start | bytes 2621440 | tf_op jit(solution)/shard_map/all_to_all | solution.py:493
  22.6 24.0 %all-to-all-done.own = bf16[32,160,128]{2,1,0:T(8,128)(2,1)S(1)} async-done(((bf16[32,160,128]{2,1,0:T(8,128)(2,1)}), bf16[32,160,128]{2,1,0:T(8,128)(2,1)S(1)}, u32[]{:S(2)}, u32[]{:S(2)}) %all-to-all-start) | async-done | bytes 1310752 | tf_op jit(solution)/shard_map/all_to_all | solution.py:493
  46.6 0.5 collective-permute-start
  47.2 0.1 collective-permute-start.1
  47.3 3.8 %collective-permute-start.3 = (bf16[7,80,128]{2,1,0:T(8,128)(2,1)S(1)}, bf16[7,80,128]{2,1,0:T(8,128)(2,1)S(1)}, u32[]{:S(2)}, u32[]{:S(2)}) collective-permute-start(bf16[7,80,128]{2,1,0:T(8,128)(2,1)S(1)} %constant_dynamic-slice_fusion), channel_id=1, source_target_pairs={{1,32},{3,34},{5,36},{7,38},{9,40},{11,42},{13,44},{15,46},{17,48}... | collective-permute-start | bytes 430088 | tf_op jit(solution)/shard_map/ppermute | solution.py:476
  51.1 0.0 collective-permute-done.near
  51.1 1.9 %collective-permute-start.2 = (bf16[7,80,128]{2,1,0:T(8,128)(2,1)S(1)}, bf16[7,80,128]{2,1,0:T(8,128)(2,1)S(1)}, u32[]{:S(2)}, u32[]{:S(2)}) collective-permute-start(bf16[7,80,128]{2,1,0:T(8,128)(2,1)S(1)} %constant_dynamic-slice_fusion.1), channel_id=1, source_target_pairs={{1,32},{3,34},{5,36},{7,38},{9,40},{11,42},{13,44},{15,46},{17,48}... | collective-permute-start | bytes 430088 | tf_op jit(solution)/shard_map/ppermute | solution.py:476
  53.1 0.8 collective-permute-done.3.far_other
  53.9 0.0 collective-permute-done.1.asked
  53.9 4.1 %collective-permute-done.2.far_own = bf16[7,80,128]{2,1,0:T(8,128)(2,1)S(1)} collective-permute-done((bf16[7,80,128]{2,1,0:T(8,128)(2,1)S(1)}, bf16[7,80,128]{2,1,0:T(8,128)(2,1)S(1)}, u32[]{:S(2)}, u32[]{:S(2)}) %collective-permute-start.2) | collective-permute-done | bytes 143392 | tf_op jit(solution)/shard_map/ppermute | solution.py:476
  58.0 14.3 %attend.1 = (bf16[16,80,128]{2,1,0:T(8,128)(2,1)S(1)}, bf16[16,80,128]{2,1,0:T(8,128)(2,1)S(1)}, bf16[16,80,128]{2,1,0:T(8,128)(2,1)S(1)}, bf16[23,80,128]{2,1,0...) custom-call(bf16[32,160,128]{2,1,0:T(8,128)(2,1)S(1)} %all-to-all-done.own, ...), custom_call_target="tpu_custom_call" | custom-call | flops 8000000000 | bytes 40000000 | tf_op jit(solution)/shard_map/attend/pallas_call | solution.py:307
  72.2 0.0 copy-start.6
  72.3 0.8 copy-done.6
  73.0 0.0 collective-permute-start.6
  73.0 4.8 %collective-permute-start.5 = (bf16[7,160,128]{2,1,0:T(8,128)(2,1)S(1)}, bf16[7,160,128]{2,1,0:T(8,128)(2,1)S(1)}, u32[]{:S(2)}, u32[]{:S(2)}) collective-permute-start(bf16[7,160,128]{2,1,0:T(8,128)(2,1)S(1)} %get-tuple-element.30), channel_id=1, source_target_pairs={{1,32},{3,34},{5,36},{7,38},{9,40},{11,42},{13,44},{15,46},{17,48}... | collective-permute-start | bytes 860168 | tf_op jit(solution)/shard_map/ppermute | solution.py:476
  77.9 0.0 collective-permute-done.6.other
  77.9 0.0 all-gather.3.cloned.1.call-done
  77.9 0.0 copy-start.5
  77.9 2.3 %copy-done.5 = bf16[18432,128]{1,0:T(8,128)(2,1)S(1)} copy-done((bf16[18432,128]{1,0:T(8,128)(2,1)S(1)}, bf16[18432,128]{1,0:T(8,128)(2,1)}, u32[]{:S(2)}) %copy-start.5) | copy-done | bytes 4718616
  80.3 2.3 %weight_term.1 = (bf16[288,128]{1,0:T(8,128)(2,1)S(1)}, bf16[288,128]{1,0:T(8,128)(2,1)S(1)}, bf16[288,128]{1,0:T(8,128)(2,1)S(1)}, bf16[288,128]{1,0:T(8,128)(2,1)S(1)}) custom-call(bf16[16,80,128]{2,1,0:T(8,128)(2,1)S(1)} %get-tuple-element.31.mixed, bf16[16,80,128]{2,1,0:T(8,128)(2,1)S(1)} %collective-permute-done.6.other, bf16[16,1152,128]{2,1,0:T(8,128)(2,1)S(1)} %bitcast.2), custom_call_target="tpu_custom_call" | custom-call | flops 1600000000 | bytes 8000000 | tf_op jit(solution)/shard_map/weight_term/pallas_call | solution.py:368
  82.5 0.0 collective-permute-done.5.far
  82.5 0.0 copy-done.7
  82.5 0.2 fold.1
  82.7 0.7 collective-permute-start.7
  83.4 0.1 collective-permute-start.4
  83.5 1.4 %collective-permute-start.8 = (bf16[288,128]{1,0:T(8,128)(2,1)S(1)}, bf16[288,128]{1,0:T(8,128)(2,1)S(1)}, u32[]{:S(2)}, u32[]{:S(2)}) collective-permute-start(bf16[288,128]{1,0:T(8,128)(2,1)S(1)} %get-tuple-element.37), channel_id=1, source_target_pairs={{0,32},{1,33},{2,34},{3,35},{4,36},{5,37},{6,38},{7,39},{8,40},{9,... | collective-permute-start | bytes 221192 | tf_op jit(solution)/shard_map/ppermute | solution.py:476
  84.9 2.3 %collective-permute-start.9 = (bf16[288,128]{1,0:T(8,128)(2,1)S(1)}, bf16[288,128]{1,0:T(8,128)(2,1)S(1)}, u32[]{:S(2)}, u32[]{:S(2)}) collective-permute-start(bf16[288,128]{1,0:T(8,128)(2,1)S(1)} %get-tuple-element.38), channel_id=1, source_target_pairs={{0,64},{1,65},{2,66},{3,67},{4,68},{5,69},{6,70},{7,71},{8,72},{9,... | collective-permute-start | bytes 221192 | tf_op jit(solution)/shard_map/ppermute | solution.py:476
  87.2 1.2 collective-permute-start.10
  88.4 0.0 collective-permute-done.4.got_asked
  88.4 0.0 collective-permute-done.8.term1
  88.4 2.1 %collective-permute-done.9.term2 = bf16[288,128]{1,0:T(8,128)(2,1)S(1)} collective-permute-done((bf16[288,128]{1,0:T(8,128)(2,1)S(1)}, bf16[288,128]{1,0:T(8,128)(2,1)S(1)}, u32[]{:S(2)}, u32[]{:S(2)}) %collective-permute-start.9) | collective-permute-done | bytes 73760 | tf_op jit(solution)/shard_map/ppermute | solution.py:476
  90.4 0.3 collective-permute-done.10.term3
  90.8 0.0 collective-permute-done.7.got
  90.8 0.4 join.1
  91.1 0.0 copy-start
  91.2 0.0 copy-start.2
  91.2 0.0 copy-start.3
  91.2 0.0 copy-start.4
  91.2 28.6 %all_to_all.10.packed = bf16[32,176,128]{2,1,0:T(8,128)(2,1)S(1)} all-to-all(bf16[32,176,128]{2,1,0:T(8,128)(2,1)S(1)} %join.1), channel_id=1, replica_groups={{0,1,2,3,4,5,6,7,8,9,10,11,12,13,14,15,16,17,18,19,20,21,22,23,24,25,26..., dimensions={0} | all-to-all | bytes 2883584 | tf_op jit(solution)/shard_map/all_to_all | solution.py:493
  119.8 0.0 copy-done.1
  119.8 0.0 copy-done
  119.8 0.0 copy-done.2
  119.8 0.0 copy-done.3
  119.8 0.0 copy-done.4
  119.8 2.1 %finish.1 = (bf16[128,1152]{1,0:T(8,128)(2,1)}, bf16[128,1152]{1,0:T(8,128)(2,1)}, bf16[128,1152]{1,0:T(8,128)(2,1)}, bf16[128,1152]{1,0:T(8,128)(2,1)}, f32[9,1152]{1,0:T(8,128)}) custom-call(bf16[32,176,128]{2,1,0:T(8,128)(2,1)S(1)} %all_to_all.10.packed, bf16[128,1152]{1,0:T(8,128)(2,1)S(1)} %copy-done.1, s32[128]{0:T(128)S(1)} %copy-done.4, ...), custom_call_target="tpu_custom_call" | custom-call | flops 1200000000 | bytes 6000000 | tf_op jit(solution)/shard_map/finish/pallas_call | solution.py:463
  (6 shorter events, 0.1 us)
Async XLA Ops:
  7.2 70.7 %all-gather.3.cloned.1.call-start = ((), (), s32[]{:S(2)}) async-start(), calls=%async_computation.2 | async-start | bytes 5013504 | tf_op jit(solution)/shard_map/all_gather | solution.py:505
  13.1 33.5 %all-to-all-start = ((bf16[32,160,128]{2,1,0:T(8,128)(2,1)}), bf16[32,160,128]{2,1,0:T(8,128)(2,1)S(1)}, u32[]{:S(2)}, u32[]{:S(2)}) async-start(bf16[32,160,128]{2,1,0:T(8,128)(2,1)} %get-tuple-element.25), calls=%async_computation | async-start | bytes 2621440 | tf_op jit(solution)/shard_map/all_to_all | solution.py:493
  46.6 4.5 %collective-permute-start = (bf16[23,80,128]{2,1,0:T(8,128)(2,1)S(1)}, bf16[23,80,128]{2,1,0:T(8,128)(2,1)S(1)}, u32[]{:S(2)}, u32[]{:S(2)}) collective-permute-start(bf16[23,80,128]{2,1,0:T(8,128)(2,1)S(1)} %constant_dynamic-slice_fusion.3), channel_id=1, source_target_pairs={{0,1},{1,0},{2,3},{3,2},{4,5},{5,4},{6,7},{7,6},{8,9},{9,8},{10,11... | collective-permute-start | bytes 1413128 | tf_op jit(solution)/shard_map/ppermute | solution.py:476
  47.2 6.7 %collective-permute-start.1 = (bf16[16,80,128]{2,1,0:T(8,128)(2,1)S(1)}, bf16[16,80,128]{2,1,0:T(8,128)(2,1)S(1)}, u32[]{:S(2)}, u32[]{:S(2)}) collective-permute-start(bf16[16,80,128]{2,1,0:T(8,128)(2,1)S(1)} %constant_dynamic-slice_fusion.2), channel_id=1, source_target_pairs={{0,1},{1,0},{2,3},{3,2},{4,5},{5,4},{6,7},{7,6},{8,9},{9,8},{10,11... | collective-permute-start | bytes 983048 | tf_op jit(solution)/shard_map/ppermute | solution.py:476
  47.3 6.6 %collective-permute-start.3 = (bf16[7,80,128]{2,1,0:T(8,128)(2,1)S(1)}, bf16[7,80,128]{2,1,0:T(8,128)(2,1)S(1)}, u32[]{:S(2)}, u32[]{:S(2)}) collective-permute-start(bf16[7,80,128]{2,1,0:T(8,128)(2,1)S(1)} %constant_dynamic-slice_fusion), channel_id=1, source_target_pairs={{1,32},{3,34},{5,36},{7,38},{9,40},{11,42},{13,44},{15,46},{17,48}... | collective-permute-start | bytes 430088 | tf_op jit(solution)/shard_map/ppermute | solution.py:476
  51.1 6.8 %collective-permute-start.2 = (bf16[7,80,128]{2,1,0:T(8,128)(2,1)S(1)}, bf16[7,80,128]{2,1,0:T(8,128)(2,1)S(1)}, u32[]{:S(2)}, u32[]{:S(2)}) collective-permute-start(bf16[7,80,128]{2,1,0:T(8,128)(2,1)S(1)} %constant_dynamic-slice_fusion.1), channel_id=1, source_target_pairs={{1,32},{3,34},{5,36},{7,38},{9,40},{11,42},{13,44},{15,46},{17,48}... | collective-permute-start | bytes 430088 | tf_op jit(solution)/shard_map/ppermute | solution.py:476
  72.2 0.8 copy-start.6
  73.0 4.8 %collective-permute-start.6 = (bf16[16,80,128]{2,1,0:T(8,128)(2,1)S(1)}, bf16[16,80,128]{2,1,0:T(8,128)(2,1)S(1)}, u32[]{:S(2)}, u32[]{:S(2)}) collective-permute-start(bf16[16,80,128]{2,1,0:T(8,128)(2,1)S(1)} %get-tuple-element.31.mixed), channel_id=1, source_target_pairs={{0,1},{1,0},{2,3},{3,2},{4,5},{5,4},{6,7},{7,6},{8,9},{9,8},{10,11... | collective-permute-start | bytes 983048 | tf_op jit(solution)/shard_map/ppermute | solution.py:476
  73.0 9.5 %collective-permute-start.5 = (bf16[7,160,128]{2,1,0:T(8,128)(2,1)S(1)}, bf16[7,160,128]{2,1,0:T(8,128)(2,1)S(1)}, u32[]{:S(2)}, u32[]{:S(2)}) collective-permute-start(bf16[7,160,128]{2,1,0:T(8,128)(2,1)S(1)} %get-tuple-element.30), channel_id=1, source_target_pairs={{1,32},{3,34},{5,36},{7,38},{9,40},{11,42},{13,44},{15,46},{17,48}... | collective-permute-start | bytes 860168 | tf_op jit(solution)/shard_map/ppermute | solution.py:476
  77.9 2.3 %copy-start.5 = (bf16[18432,128]{1,0:T(8,128)(2,1)S(1)}, bf16[18432,128]{1,0:T(8,128)(2,1)}, u32[]{:S(2)}) copy-start(bf16[18432,128]{1,0:T(8,128)(2,1)} %all-gather.3.cloned.1.call-done) | copy-start | bytes 14155780
  80.3 2.3 %copy-start.7 = (bf16[23,80,128]{2,1,0:T(8,128)(2,1)S(1)}, bf16[23,80,128]{2,1,0:T(8,128)(2,1)}, u32[]{:S(2)}) copy-start(bf16[23,80,128]{2,1,0:T(8,128)(2,1)} %copy-done.6) | copy-start | bytes 1413124
  82.7 8.1 %collective-permute-start.7 = (bf16[23,80,128]{2,1,0:T(8,128)(2,1)S(1)}, bf16[23,80,128]{2,1,0:T(8,128)(2,1)S(1)}, u32[]{:S(2)}, u32[]{:S(2)}) collective-permute-start(bf16[23,80,128]{2,1,0:T(8,128)(2,1)S(1)} %get-tuple-element.36), channel_id=1, source_target_pairs={{0,1},{1,0},{2,3},{3,2},{4,5},{5,4},{6,7},{7,6},{8,9},{9,8},{10,11... | collective-permute-start | bytes 1413128 | tf_op jit(solution)/shard_map/ppermute | solution.py:476
  83.4 4.9 %collective-permute-start.4 = (bf16[16,80,128]{2,1,0:T(8,128)(2,1)S(1)}, bf16[16,80,128]{2,1,0:T(8,128)(2,1)S(1)}, u32[]{:S(2)}, u32[]{:S(2)}) collective-permute-start(bf16[16,80,128]{2,1,0:T(8,128)(2,1)S(1)} %get-tuple-element.27), channel_id=1, source_target_pairs={{0,1},{1,0},{2,3},{3,2},{4,5},{5,4},{6,7},{7,6},{8,9},{9,8},{10,11... | collective-permute-start | bytes 983048 | tf_op jit(solution)/shard_map/ppermute | solution.py:476
  83.5 4.8 %collective-permute-start.8 = (bf16[288,128]{1,0:T(8,128)(2,1)S(1)}, bf16[288,128]{1,0:T(8,128)(2,1)S(1)}, u32[]{:S(2)}, u32[]{:S(2)}) collective-permute-start(bf16[288,128]{1,0:T(8,128)(2,1)S(1)} %get-tuple-element.37), channel_id=1, source_target_pairs={{0,32},{1,33},{2,34},{3,35},{4,36},{5,37},{6,38},{7,39},{8,40},{9,... | collective-permute-start | bytes 221192 | tf_op jit(solution)/shard_map/ppermute | solution.py:476
  84.9 5.5 %collective-permute-start.9 = (bf16[288,128]{1,0:T(8,128)(2,1)S(1)}, bf16[288,128]{1,0:T(8,128)(2,1)S(1)}, u32[]{:S(2)}, u32[]{:S(2)}) collective-permute-start(bf16[288,128]{1,0:T(8,128)(2,1)S(1)} %get-tuple-element.38), channel_id=1, source_target_pairs={{0,64},{1,65},{2,66},{3,67},{4,68},{5,69},{6,70},{7,71},{8,72},{9,... | collective-permute-start | bytes 221192 | tf_op jit(solution)/shard_map/ppermute | solution.py:476
  87.2 3.6 %collective-permute-start.10 = (bf16[288,128]{1,0:T(8,128)(2,1)S(1)}, bf16[288,128]{1,0:T(8,128)(2,1)S(1)}, u32[]{:S(2)}, u32[]{:S(2)}) collective-permute-start(bf16[288,128]{1,0:T(8,128)(2,1)S(1)} %get-tuple-element.39), channel_id=1, source_target_pairs={{0,96},{1,97},{2,98},{3,99},{4,100},{5,101},{6,102},{7,103},{8,104... | collective-permute-start | bytes 221192 | tf_op jit(solution)/shard_map/ppermute | solution.py:476
  90.8 29.0 %copy-start.1 = (bf16[128,1152]{1,0:T(8,128)(2,1)S(1)}, bf16[128,1152]{1,0:T(8,128)(2,1)}, u32[]{:S(2)}) copy-start(bf16[128,1152]{1,0:T(8,128)(2,1)} %residual.1) | copy-start | bytes 884740
  91.1 28.6 %copy-start = (bf16[1152,1152]{1,0:T(8,128)(2,1)S(1)}, bf16[1152,1152]{1,0:T(8,128)(2,1)}, u32[]{:S(2)}) copy-start(bf16[1152,1152]{1,0:T(8,128)(2,1)} %weight.3) | copy-start | bytes 7962628
  91.2 28.6 %copy-start.2 = (f32[32,1152]{1,0:T(8,128)S(1)}, f32[32,1152]{1,0:T(8,128)}, u32[]{:S(2)}) copy-start(f32[32,1152]{1,0:T(8,128)} %gate.3) | copy-start | bytes 442372
  91.2 28.6 %copy-start.3 = (f32[1152]{0:T(1024)S(1)}, f32[1152]{0:T(1024)}, u32[]{:S(2)}) copy-start(f32[1152]{0:T(1024)} %bias.1) | copy-start | bytes 13828
  91.2 28.6 %copy-start.4 = (s32[128]{0:T(128)S(1)}, s32[128]{0:T(128)}, u32[]{:S(2)}) copy-start(s32[128]{0:T(128)} %tags.3) | copy-start | bytes 1540
Sparse Core Ops, SparseCore 0:
  13.2 64.6 all-gather.2
